TPU v7x, 32 devices: a whole 2x2x4 slice. The times are simulated.
32 devices in a mesh: frame: 4 (over y, core), row: 4 (over z), head: 2 (over x).
Axes of the slice: x: 2, y: 2, z: 4, core: 2. Of those that a mesh axis runs over, the one named last changes fastest.
Arguments:
- queries: bfloat16 [8, 32, 16, 12, 128], P('frame', 'row', 'head'), may hold values from -6 to 6
- keys: bfloat16 [8, 32, 16, 12, 128], P('frame', 'row', 'head'), may hold values from -6 to 6
- values: bfloat16 [8, 32, 16, 12, 128], P('frame', 'row', 'head'), may hold values from -6 to 6
- out_grad: bfloat16 [8, 32, 16, 12, 128], P('frame', 'row', 'head'), may hold values from -6 to 6
- active: int32 [8, 4, 2, 27], replicated, may hold values from 0 to 1, as said below
Outputs:
- attended: bfloat16 [8, 32, 16, 12, 128], P('frame', 'row', 'head')
- query_grad: bfloat16 [8, 32, 16, 12, 128], P('frame', 'row', 'head')
- key_grad: bfloat16 [8, 32, 16, 12, 128], P('frame', 'row', 'head')
- value_grad: bfloat16 [8, 32, 16, 12, 128], P('frame', 'row', 'head')
Inputs may be any that keep to these rules, and one draw needn't show every extreme that they name: `active`: entry 13 (the tile with itself) is 1 for every tile; all other entries are 0 or 1.
All inputs are finite; a program needn't handle non-finite values.
Results may differ from a plain program's by a relative error of at most 0.011.
Values may be sent and summed in bfloat16 or wider, within the bound.
No kernel may reach another device: no remote copies, remote signals or barrier semaphores. Data moves between devices by JAX's collectives and lax.ppermute only.
A program may use at most 64 MiB of HBM per device.

v0:
```python
import jax
import jax.numpy as jnp
from jax import lax
from jax.sharding import PartitionSpec as P

TF = 1
TR = 8
TC = 8


def padded(shard, sides, width):
    for axis, dim in sides:
        size, length = (lax.axis_size(axis), shard.shape[dim])
        up = [(i, (i + 1) % size) for i in range(size - 1)]
        down = [(j, i) for i, j in up]
        last = lax.slice_in_dim(shard, length - width, length, axis=dim)
        initial = lax.slice_in_dim(shard, 0, width, axis=dim)
        before = lax.ppermute(last, axis, up)
        after = lax.ppermute(initial, axis, down)
        shard = jnp.concatenate([before, shard, after], axis=dim)
    return shard


def product(form, left, right):
    return jnp.einsum(form, left, right, preferred_element_type=jnp.float32)


def slot_masks(act_ext, one_ext, frame_tiles, row_tiles, sign):
    col_tiles = act_ext.shape[2]
    own = jnp.arange(col_tiles, dtype=jnp.int32)[:, None]
    other = jnp.arange(col_tiles, dtype=jnp.int32)[None, :]
    offsets = jnp.arange(3, dtype=jnp.int32) - 1
    matches = (((other - own) * sign)[:, :, None] == offsets[None, None, :]).astype(jnp.float32)
    layers = []
    for offset in range(9):
        frame_step = offset // 3 - 1
        row_step = offset % 3 - 1
        if sign > 0:
            chosen = act_ext[1 : 1 + frame_tiles, 1 : 1 + row_tiles, :, 3 * offset : 3 * offset + 3]
            inside = one_ext[
                1 + frame_step : 1 + frame_step + frame_tiles,
                1 + row_step : 1 + row_step + row_tiles,
            ]
        else:
            chosen = act_ext[
                1 - frame_step : 1 - frame_step + frame_tiles,
                1 - row_step : 1 - row_step + row_tiles,
                :,
                3 * offset : 3 * offset + 3,
            ]
            inside = jnp.ones((frame_tiles, row_tiles), jnp.float32)
        layers.append(
            jnp.einsum("abio,ijo->abij", chosen.astype(jnp.float32), matches)
            * inside[:, :, None, None]
        )
    tiles = jnp.stack(layers, axis=3).reshape(frame_tiles, row_tiles, col_tiles, 9 * col_tiles)
    slab = TF * TR * col_tiles * TC
    query_pos = lax.broadcasted_iota(jnp.int32, (slab, col_tiles), 0)
    query_tile = lax.broadcasted_iota(jnp.int32, (slab, col_tiles), 1)
    query_cols = (query_pos % (col_tiles * TC) // TC == query_tile).astype(jnp.float32)
    key_pos = lax.broadcasted_iota(jnp.int32, (9 * col_tiles, 9 * slab), 1)
    key_tile = lax.broadcasted_iota(jnp.int32, (9 * col_tiles, 9 * slab), 0)
    key_code = key_pos // slab * col_tiles + key_pos % slab % (col_tiles * TC) // TC
    key_cols = (key_code == key_tile).astype(jnp.float32)
    spread_rows = jnp.einsum("qi,abik->abqk", query_cols, tiles)
    spread = jnp.einsum("abqj,jk->abqk", spread_rows, key_cols)
    return spread > 0.5


def gather_bands(wide, frame_tiles, row_tiles, sign):
    parts = []
    for offset in range(9):
        frame_step = sign * (offset // 3 - 1)
        row_step = sign * (offset % 3 - 1)
        parts.append(
            wide[
                1 + frame_step : 1 + frame_step + frame_tiles,
                1 + row_step : 1 + row_step + row_tiles,
            ]
        )
    stacked = jnp.stack(parts, axis=2)
    return stacked.reshape((frame_tiles, row_tiles, 9 * wide.shape[2]) + wide.shape[3:])


def query_side(query_slab, key_wide, value_wide, grad_slab, allowed, scaling):
    frame_tiles, row_tiles = (query_slab.shape[0], query_slab.shape[1])
    key_band = gather_bands(key_wide, frame_tiles, row_tiles, 1)
    value_band = gather_bands(value_wide, frame_tiles, row_tiles, 1)
    scores = product("abqd,abkd->abqk", query_slab, key_band) * scaling
    scores = jnp.where(allowed, scores, -jnp.inf)
    highest = jnp.max(scores, axis=-1, keepdims=True)
    log_total = highest + jnp.log(jnp.sum(jnp.exp(scores - highest), axis=-1, keepdims=True))
    weights = jnp.where(allowed, jnp.exp(scores - log_total), 0.0).astype(jnp.bfloat16)
    weights = lax.optimization_barrier(weights)
    attended = product("abqk,abkd->abqd", weights, value_band).astype(jnp.bfloat16)
    attended = lax.optimization_barrier(attended)
    grad_dot = jnp.sum(grad_slab.astype(jnp.float32) * attended.astype(jnp.float32), axis=-1)
    grad_probs = product("abqd,abkd->abqk", grad_slab, value_band)
    grad_scores = (
        weights.astype(jnp.float32) * (grad_probs - grad_dot[..., None]) * scaling
    ).astype(jnp.bfloat16)
    query_grad = product("abqk,abkd->abqd", grad_scores, key_band).astype(jnp.bfloat16)
    return (attended, query_grad, log_total[..., 0], grad_dot)


def key_side(key_slab, value_slab, query_wide, grad_wide, total_wide, dot_wide, allowed, scaling):
    frame_tiles, row_tiles = (key_slab.shape[0], key_slab.shape[1])
    query_band = gather_bands(query_wide, frame_tiles, row_tiles, -1)
    grad_band = gather_bands(grad_wide, frame_tiles, row_tiles, -1)
    total_band = gather_bands(total_wide, frame_tiles, row_tiles, -1)
    dot_band = gather_bands(dot_wide, frame_tiles, row_tiles, -1)
    scores = product("abkd,abqd->abkq", key_slab, query_band) * scaling
    weights = jnp.where(allowed, jnp.exp(scores - total_band[:, :, None, :]), 0.0).astype(
        jnp.bfloat16
    )
    weights = lax.optimization_barrier(weights)
    grad_probs = product("abkd,abqd->abkq", value_slab, grad_band)
    grad_scores = (
        weights.astype(jnp.float32) * (grad_probs - dot_band[:, :, None, :]) * scaling
    ).astype(jnp.bfloat16)
    key_grad = product("abkq,abqd->abkd", grad_scores, query_band).astype(jnp.bfloat16)
    value_grad = product("abkq,abqd->abkd", weights, grad_band).astype(jnp.bfloat16)
    return (key_grad, value_grad)


def on_device(queries, keys, values, out_grad, active):
    frames_here, rows_here, cols_here, heads_all, head_dim = queries.shape
    head_count = lax.axis_size("head")
    groups = heads_all // head_count
    columns = cols_here * head_count
    frame_tiles = frames_here // TF
    row_tiles = rows_here // TR
    scaling = head_dim ** (-0.5)
    frame_at = lax.axis_index("frame")
    row_at = lax.axis_index("row")
    padded_active = jnp.pad(active, ((1, 1), (1, 1), (0, 0), (0, 0)))
    padded_ones = jnp.pad(jnp.ones((active.shape[0], active.shape[1]), jnp.float32), 1)
    act_ext = lax.dynamic_slice(
        padded_active,
        (frame_at * frame_tiles, row_at * row_tiles, 0, 0),
        (frame_tiles + 2, row_tiles + 2, active.shape[2], active.shape[3]),
    )
    one_ext = lax.dynamic_slice(
        padded_ones, (frame_at * frame_tiles, row_at * row_tiles), (frame_tiles + 2, row_tiles + 2)
    )
    front_mask = slot_masks(act_ext, one_ext, frame_tiles, row_tiles, 1)
    back_mask = slot_masks(act_ext, one_ext, frame_tiles, row_tiles, -1)

    def split_heads(tensor):
        return tensor.reshape(frames_here, rows_here, cols_here, head_count, groups, head_dim)

    def to_slabs(tensor):
        count = tensor.shape[3]
        shaped = tensor.reshape(frame_tiles, TF, row_tiles, TR, columns, count, head_dim)
        return jnp.transpose(shaped, (5, 0, 2, 1, 3, 4, 6)).reshape(
            count, frame_tiles, row_tiles, TF * TR * columns, head_dim
        )

    def from_slabs(result):
        count = result.shape[0]
        shaped = result.reshape(count, frame_tiles, row_tiles, TF, TR, columns, head_dim)
        return jnp.transpose(shaped, (1, 3, 2, 4, 5, 0, 6)).reshape(
            frames_here, rows_here, columns, 1, count, head_dim
        )

    query_slab = to_slabs(
        lax.all_to_all(split_heads(queries), "head", split_axis=3, concat_axis=2, tiled=True)[
            :, :, :, 0
        ]
    )
    key_slab = to_slabs(
        lax.all_to_all(split_heads(keys), "head", split_axis=3, concat_axis=2, tiled=True)[
            :, :, :, 0
        ]
    )
    value_slab = to_slabs(
        lax.all_to_all(split_heads(values), "head", split_axis=3, concat_axis=2, tiled=True)[
            :, :, :, 0
        ]
    )
    grad_slab = to_slabs(
        lax.all_to_all(split_heads(out_grad), "head", split_axis=3, concat_axis=2, tiled=True)[
            :, :, :, 0
        ]
    )
    pair_rims = padded(jnp.stack([key_slab, value_slab]), (("frame", 2), ("row", 3)), 1)
    key_wide = pair_rims[0]
    value_wide = pair_rims[1]

    def front(parts):
        return query_side(parts[0], parts[1], parts[2], parts[3], front_mask, scaling)

    attended, query_grad, log_total, grad_dot = lax.map(
        front, (query_slab, key_wide, value_wide, grad_slab)
    )
    other_rims = padded(jnp.stack([query_slab, grad_slab]), (("frame", 2), ("row", 3)), 1)
    query_wide = other_rims[0]
    grad_wide = other_rims[1]
    stats = padded(jnp.stack([log_total, grad_dot]), (("frame", 2), ("row", 3)), 1)

    def back(parts):
        return key_side(
            parts[0], parts[1], parts[2], parts[3], parts[4], parts[5], back_mask, scaling
        )

    key_grad, value_grad = lax.map(
        back, (key_slab, value_slab, query_wide, grad_wide, stats[0], stats[1])
    )
    returned = (
        lax.all_to_all(from_slabs(attended), "head", split_axis=2, concat_axis=3, tiled=True),
        lax.all_to_all(from_slabs(query_grad), "head", split_axis=2, concat_axis=3, tiled=True),
        lax.all_to_all(from_slabs(key_grad), "head", split_axis=2, concat_axis=3, tiled=True),
        lax.all_to_all(from_slabs(value_grad), "head", split_axis=2, concat_axis=3, tiled=True),
    )
    return tuple(
        (
            tensor.reshape(frames_here, rows_here, cols_here, heads_all, head_dim)
            for tensor in returned
        )
    )


def solution(mesh):
    in_specs = (
        P("frame", "row", "head", None, None),
        P("frame", "row", "head", None, None),
        P("frame", "row", "head", None, None),
        P("frame", "row", "head", None, None),
        P(),
    )
    out_specs = (
        P("frame", "row", "head", None, None),
        P("frame", "row", "head", None, None),
        P("frame", "row", "head", None, None),
        P("frame", "row", "head", None, None),
    )
    return jax.shard_map(
        on_device, mesh=mesh, in_specs=in_specs, out_specs=out_specs, check_vma=False
    )
```

profile of v0, /device:TPU:9, one launch (start us, length us, event | category | flops | bytes accessed | tf_op | source)
XLA Modules:
  0.0 232.6 jit_solution(6505473238960770135)
XLA Ops:
  2.5 3.5 %all-to-all-start.1 = ((bf16[2,8,8,2,6,128]{5,2,4,1,0,3:T(8,128)(2,1)}), bf16[2,8,8,2,6,128]{5,2,4,1,0,3:T(8,128)(2,1)S(1)}, u32[]{:S(2)}, u32[]{:S(2)}) async-start(bf16[2,8,8,2,6,128]{5,2,4,1,0,3:T(8,128)(2,1)} %copy.737), calls=%async_computation.1 | async-start | bytes 786432 | tf_op jit(solution)/shard_map/all_to_all | solution.py:172
  13.4 3.5 %all-to-all-start.2 = ((bf16[2,8,8,2,6,128]{5,2,4,1,0,3:T(8,128)(2,1)}), bf16[2,8,8,2,6,128]{5,2,4,1,0,3:T(8,128)(2,1)S(1)}, u32[]{:S(2)}, u32[]{:S(2)}) async-start(bf16[2,8,8,2,6,128]{5,2,4,1,0,3:T(8,128)(2,1)} %copy.740), calls=%async_computation.2 | async-start | bytes 786432 | tf_op jit(solution)/shard_map/all_to_all | solution.py:177
  17.1 5.8 %all-to-all-done.2 = bf16[2,8,8,2,6,128]{5,2,4,1,0,3:T(8,128)(2,1)S(1)} async-done(((bf16[2,8,8,2,6,128]{5,2,4,1,0,3:T(8,128)(2,1)}), bf16[2,8,8,2,6,128]{5,2,4,1,0,3:T(8,128)(2,1)S(1)}, u32[]{:S(2)}, u32[]{:S(2)}) %all-to-all-start.2) | async-done | bytes 393248 | tf_op jit(solution)/shard_map/all_to_all | solution.py:177
  22.9 3.5 %all-to-all-start = ((bf16[2,8,8,2,6,128]{5,2,4,1,0,3:T(8,128)(2,1)}), bf16[2,8,8,2,6,128]{5,2,4,1,0,3:T(8,128)(2,1)S(1)}, u32[]{:S(2)}, u32[]{:S(2)}) async-start(bf16[2,8,8,2,6,128]{5,2,4,1,0,3:T(8,128)(2,1)} %copy.734), calls=%async_computation | async-start | bytes 786432 | tf_op jit(solution)/shard_map/all_to_all | solution.py:167
  26.6 4.6 %collective-permute-start = (bf16[2,6,1,1,128,128]{5,4,2,1,3,0:T(8,128)(2,1)S(1)}, bf16[2,6,1,1,128,128]{5,4,2,1,3,0:T(8,128)(2,1)S(1)}, u32[]{:S(2)}, u32[]{:S(2)}) collective-permute-start(bf16[2,6,1,1,128,128]{5,4,2,1,3,0:T(8,128)(2,1)S(1)} %get-tuple-element.232), channel_id=1, source_target_pairs={{0,8},{8,16},{16,24},{1,9},{9,17},{17,25},{2,10},{10,18},{18,26},{... | collective-permute-start | bytes 1179656 | tf_op jit(solution)/shard_map/ppermute | solution.py:18
  33.1 2.7 %collective-permute-done = bf16[2,6,1,1,128,128]{5,4,2,1,3,0:T(8,128)(2,1)S(1)} collective-permute-done((bf16[2,6,1,1,128,128]{5,4,2,1,3,0:T(8,128)(2,1)S(1)}, bf16[2,6,1,1,128,128]{5,4,2,1,3,0:T(8,128)(2,1)S(1)}, u32[]{:S(2)}, u32[]{:S(2)}) %collective-permute-start) | collective-permute-done | bytes 393248 | tf_op jit(solution)/shard_map/ppermute | solution.py:18
  35.9 4.4 %collective-permute-done.1 = bf16[2,6,1,1,128,128]{5,4,2,1,3,0:T(8,128)(2,1)S(1)} collective-permute-done((bf16[2,6,1,1,128,128]{5,4,2,1,3,0:T(8,128)(2,1)S(1)}, bf16[2,6,1,1,128,128]{5,4,2,1,3,0:T(8,128)(2,1)S(1)}, u32[]{:S(2)}, u32[]{:S(2)}) %collective-permute-start.1) | collective-permute-done | bytes 393248 | tf_op jit(solution)/shard_map/ppermute | solution.py:19
  41.6 3.2 %collective-permute-start.2 = (bf16[2,6,4,1,128,128]{5,4,2,1,3,0:T(8,128)(2,1)}, bf16[2,6,4,1,128,128]{5,4,2,1,3,0:T(8,128)(2,1)}, u32[]{:S(2)}, u32[]{:S(2)}) collective-permute-start(bf16[2,6,4,1,128,128]{5,4,2,1,3,0:T(8,128)(2,1)} %pad_maximum_fusion.2), channel_id=1, source_target_pairs={{0,2},{2,4},{4,6},{1,3},{3,5},{5,7},{8,10},{10,12},{12,14},{9,11},... | collective-permute-start | bytes 4718600 | tf_op jit(solution)/shard_map/ppermute | solution.py:18
  44.8 3.2 %collective-permute-start.3 = (bf16[2,6,4,1,128,128]{5,4,2,1,3,0:T(8,128)(2,1)}, bf16[2,6,4,1,128,128]{5,4,2,1,3,0:T(8,128)(2,1)}, u32[]{:S(2)}, u32[]{:S(2)}) collective-permute-start(bf16[2,6,4,1,128,128]{5,4,2,1,3,0:T(8,128)(2,1)} %pad_maximum_fusion.2), channel_id=1, source_target_pairs={{2,0},{4,2},{6,4},{3,1},{5,3},{7,5},{10,8},{12,10},{14,12},{11,9},... | collective-permute-start | bytes 4718600 | tf_op jit(solution)/shard_map/ppermute | solution.py:19
  49.4 3.5 %all-to-all-start.3 = ((bf16[2,8,8,2,6,128]{5,2,4,1,0,3:T(8,128)(2,1)}), bf16[2,8,8,2,6,128]{5,2,4,1,0,3:T(8,128)(2,1)S(1)}, u32[]{:S(2)}, u32[]{:S(2)}) async-start(bf16[2,8,8,2,6,128]{5,2,4,1,0,3:T(8,128)(2,1)} %copy.743), calls=%async_computation.3 | async-start | bytes 786432 | tf_op jit(solution)/shard_map/all_to_all | solution.py:182
  53.0 5.2 %all-to-all-done.3 = bf16[2,8,8,2,6,128]{5,2,4,1,0,3:T(8,128)(2,1)S(1)} async-done(((bf16[2,8,8,2,6,128]{5,2,4,1,0,3:T(8,128)(2,1)}), bf16[2,8,8,2,6,128]{5,2,4,1,0,3:T(8,128)(2,1)S(1)}, u32[]{:S(2)}, u32[]{:S(2)}) %all-to-all-start.3) | async-done | bytes 393248 | tf_op jit(solution)/shard_map/all_to_all | solution.py:182
  59.3 2.8 %collective-permute-start.4 = (bf16[2,6,1,1,128,128]{5,4,2,1,3,0:T(8,128)(2,1)}, bf16[2,6,1,1,128,128]{5,4,2,1,3,0:T(8,128)(2,1)S(1)}, u32[]{:S(2)}, u32[]{:S(2)}) collective-permute-start(bf16[2,6,1,1,128,128]{5,4,2,1,3,0:T(8,128)(2,1)} %get-tuple-element.230), channel_id=1, source_target_pairs={{0,8},{8,16},{16,24},{1,9},{9,17},{17,25},{2,10},{10,18},{18,26},{... | collective-permute-start | bytes 1179656 | tf_op jit(solution)/shard_map/ppermute | solution.py:18
  67.1 4.7 %collective-permute-done.5 = bf16[2,6,1,1,128,128]{5,4,2,1,3,0:T(8,128)(2,1)S(1)} collective-permute-done((bf16[2,6,1,1,128,128]{5,4,2,1,3,0:T(8,128)(2,1)}, bf16[2,6,1,1,128,128]{5,4,2,1,3,0:T(8,128)(2,1)S(1)}, u32[]{:S(2)}, u32[]{:S(2)}) %collective-permute-start.5) | collective-permute-done | bytes 393248 | tf_op jit(solution)/shard_map/ppermute | solution.py:19
  75.2 4.4 %collective-permute-start.7 = (bf16[2,6,4,1,128,128]{5,4,2,1,3,0:T(8,128)(2,1)}, bf16[2,6,4,1,128,128]{5,4,2,1,3,0:T(8,128)(2,1)}, u32[]{:S(2)}, u32[]{:S(2)}) collective-permute-start(bf16[2,6,4,1,128,128]{5,4,2,1,3,0:T(8,128)(2,1)} %pad_maximum_fusion.3), channel_id=1, source_target_pairs={{2,0},{4,2},{6,4},{3,1},{5,3},{7,5},{10,8},{12,10},{14,12},{11,9},... | collective-permute-start | bytes 4718600 | tf_op jit(solution)/shard_map/ppermute | solution.py:19
  81.7 2.8 %pad_maximum_fusion = bf16[2,6,4,3,128,128]{5,4,2,1,3,0:T(8,128)(2,1)S(1)} fusion(bf16[2,6,4,1,128,128]{5,4,2,1,3,0:T(8,128)(2,1)} %collective-permute-done.3, bf16[2,6,1,1,128,128]{5,4,2,1,3,0:T(8,128)(2,1)S(1)} %collective-permute-done.1, bf16[1,6,2,1,128,128]{5,4,2,1,3,0:T(8,128)(2,1)S(1)} %bitcast.940, ...), kind=kLoop, calls=%fused_computation.140 | loop fusion | flops 11796480 | bytes 9437184 | tf_op jit(solution)/shard_map/concatenate | solution.py:20
  84.5 3.2 %slice_bitcast_fusion.38 = (bf16[6,4,3,128,128]{4,3,1,0,2:T(8,128)(2,1)}, bf16[6,4,3,128,128]{4,3,1,0,2:T(8,128)(2,1)}) fusion(bf16[2,6,4,3,128,128]{5,4,2,1,3,0:T(8,128)(2,1)S(1)} %pad_maximum_fusion), kind=kLoop, calls=%fused_computation.146 | loop fusion | bytes 9437184 | tf_op jit(solution)/shard_map/squeeze | solution.py:188
  89.3 29.2 %while.28 = (s32[]{:T(128)}, bf16[6,2,1,128,128]{4,3,1,2,0:T(8,128)(2,1)}, bf16[6,2,1,128,128]{4,3,1,2,0:T(8,128)(2,1)}, f32[6,2,1,128]{3,1,2,0:T(2,128)S(1)}, f...) while((s32[]{:T(128)}, ...), condition=%wide.region_4.5_spmd, body=%wide.region_0.4_spmd.sunk | while | flops 306019840 | bytes 12727937 | solution.py:193
  120.5 2.4 %collective-permute-start.9 = (f32[2,6,1,1,128]{4,2,3,1,0:T(1,128)S(1)}, f32[2,6,1,1,128]{4,2,3,1,0:T(1,128)S(1)}, u32[]{:S(2)}, u32[]{:S(2)}) collective-permute-start(f32[2,6,1,1,128]{4,2,3,1,0:T(1,128)S(1)} %get-tuple-element.254), channel_id=1, source_target_pairs={{8,0},{16,8},{24,16},{9,1},{17,9},{25,17},{10,2},{18,10},{26,18},{... | collective-permute-start | bytes 18440 | tf_op jit(solution)/shard_map/ppermute | solution.py:19
  122.9 3.0 %pad_maximum_fusion.1 = bf16[2,6,4,3,128,128]{5,4,2,1,3,0:T(8,128)(2,1)S(1)} fusion(bf16[2,6,4,1,128,128]{5,4,2,1,3,0:T(8,128)(2,1)} %collective-permute-done.7, bf16[2,6,1,1,128,128]{5,4,2,1,3,0:T(8,128)(2,1)} %copy-done.3, bf16[1,6,2,1,128,128]{5,4,2,1,3,0:T(8,128)(2,1)S(1)} %bitcast.933, bf16[1,6,2,1,128,128]{5,4,2,1,3,0:T(8,128)(2,1)S(1)} %bitcast.929, ...), kind=kLoop, calls=%fused_computation.141 | loop fusion | flops 11796480 | bytes 9437184 | tf_op jit(solution)/shard_map/concatenate | solution.py:20
  126.0 2.9 %collective-permute-start.10 = (f32[2,6,4,1,128]{4,2,3,1,0:T(4,128)S(1)}, f32[2,6,4,1,128]{4,2,3,1,0:T(4,128)S(1)}, u32[]{:S(2)}, u32[]{:S(2)}) collective-permute-start(f32[2,6,4,1,128]{4,2,3,1,0:T(4,128)S(1)} %pad_maximum_fusion.7), channel_id=1, source_target_pairs={{0,2},{2,4},{4,6},{1,3},{3,5},{5,7},{8,10},{10,12},{12,14},{9,11},... | collective-permute-start | bytes 73736 | tf_op jit(solution)/shard_map/ppermute | solution.py:18
  128.9 2.5 %collective-permute-start.11 = (f32[2,6,4,1,128]{4,2,3,1,0:T(4,128)S(1)}, f32[2,6,4,1,128]{4,2,3,1,0:T(4,128)S(1)}, u32[]{:S(2)}, u32[]{:S(2)}) collective-permute-start(f32[2,6,4,1,128]{4,2,3,1,0:T(4,128)S(1)} %pad_maximum_fusion.7), channel_id=1, source_target_pairs={{2,0},{4,2},{6,4},{3,1},{5,3},{7,5},{10,8},{12,10},{14,12},{11,9},... | collective-permute-start | bytes 73736 | tf_op jit(solution)/shard_map/ppermute | solution.py:19
  131.4 2.4 %slice_bitcast_fusion.36 = (bf16[6,4,3,128,128]{4,3,1,0,2:T(8,128)(2,1)S(1)}, bf16[6,4,3,128,128]{4,3,1,0,2:T(8,128)(2,1)}) fusion(bf16[2,6,4,3,128,128]{5,4,2,1,3,0:T(8,128)(2,1)S(1)} %pad_maximum_fusion.1), kind=kLoop, calls=%fused_computation.144 | loop fusion | bytes 9437184 | tf_op jit(solution)/shard_map/squeeze | solution.py:198
  134.7 4.8 %all-to-all-start.4 = ((bf16[2,8,16,1,6,128]{5,1,0,4,3,2:T(8,128)(2,1)}), bf16[2,8,16,1,6,128]{5,1,0,4,3,2:T(8,128)(2,1)S(1)}, u32[]{:S(2)}, u32[]{:S(2)}) async-start(bf16[2,8,16,1,6,128]{5,1,0,4,3,2:T(8,128)(2,1)} %copy.750), calls=%async_computation.4 | async-start | bytes 786432 | tf_op jit(solution)/shard_map/all_to_all | solution.py:210
  141.0 6.2 %all-to-all-done.4 = bf16[2,8,16,1,6,128]{5,1,0,4,3,2:T(8,128)(2,1)S(1)} async-done(((bf16[2,8,16,1,6,128]{5,1,0,4,3,2:T(8,128)(2,1)}), bf16[2,8,16,1,6,128]{5,1,0,4,3,2:T(8,128)(2,1)S(1)}, u32[]{:S(2)}, u32[]{:S(2)}) %all-to-all-start.4) | async-done | bytes 393248 | tf_op jit(solution)/shard_map/all_to_all | solution.py:210
  147.2 4.2 %all-to-all-start.5 = ((bf16[2,8,16,1,6,128]{5,1,0,4,3,2:T(8,128)(2,1)}), bf16[2,8,16,1,6,128]{5,1,0,4,3,2:T(8,128)(2,1)}, u32[]{:S(2)}, u32[]{:S(2)}) async-start(bf16[2,8,16,1,6,128]{5,1,0,4,3,2:T(8,128)(2,1)} %copy.753), calls=%async_computation.5 | async-start | bytes 786432 | tf_op jit(solution)/shard_map/all_to_all | solution.py:211
  153.0 58.4 %while.29 = (s32[]{:T(128)}, bf16[6,2,1,128,128]{4,3,1,2,0:T(8,128)(2,1)}, bf16[6,2,1,128,128]{4,3,1,2,0:T(8,128)(2,1)}, pred[2,1,128,1152]{3,2,0,1:T(32,128)(4,...) while((s32[]{:T(128)}, ...), condition=%wide.region_6.7_spmd, body=%wide.region_5.6_spmd.sunk | while | flops 304709632 | bytes 11133073 | solution.py:206
  170.2 2.3 fusion.334
  189.7 2.3 fusion.334
  209.2 2.3 fusion.334
  213.4 3.5 %all-to-all-start.6 = ((bf16[2,8,16,1,6,128]{5,1,0,4,3,2:T(8,128)(2,1)}), bf16[2,8,16,1,6,128]{5,1,0,4,3,2:T(8,128)(2,1)S(1)}, u32[]{:S(2)}, u32[]{:S(2)}) async-start(bf16[2,8,16,1,6,128]{5,1,0,4,3,2:T(8,128)(2,1)} %copy.783), calls=%async_computation.6 | async-start | bytes 786432 | tf_op jit(solution)/shard_map/all_to_all | solution.py:212
  217.7 5.3 %all-to-all-done.6 = bf16[2,8,16,1,6,128]{5,1,0,4,3,2:T(8,128)(2,1)S(1)} async-done(((bf16[2,8,16,1,6,128]{5,1,0,4,3,2:T(8,128)(2,1)}), bf16[2,8,16,1,6,128]{5,1,0,4,3,2:T(8,128)(2,1)S(1)}, u32[]{:S(2)}, u32[]{:S(2)}) %all-to-all-start.6) | async-done | bytes 393248 | tf_op jit(solution)/shard_map/all_to_all | solution.py:212
  223.0 3.5 %all-to-all-start.7 = ((bf16[2,8,16,1,6,128]{5,1,0,4,3,2:T(8,128)(2,1)}), bf16[2,8,16,1,6,128]{5,1,0,4,3,2:T(8,128)(2,1)S(1)}, u32[]{:S(2)}, u32[]{:S(2)}) async-start(bf16[2,8,16,1,6,128]{5,1,0,4,3,2:T(8,128)(2,1)} %copy.786), calls=%async_computation.7 | async-start | bytes 786432 | tf_op jit(solution)/shard_map/all_to_all | solution.py:213
  (502 shorter events, 121.6 us)
Async XLA Ops:
  0.6 5.6 %copy-start.12 = (s32[8,4,2,27]{3,2,1,0:T(2,128)S(1)}, s32[8,4,2,27]{3,2,1,0:T(2,128)}, u32[]{:S(2)}) copy-start(s32[8,4,2,27]{3,2,1,0:T(2,128)} %param.13) | copy-start | bytes 20740
  0.6 8.7 %copy-start.9 = (bf16[2,8,8,12,128]{4,2,3,1,0:T(8,128)(2,1)S(1)}, bf16[2,8,8,12,128]{4,2,3,1,0:T(8,128)(2,1)}, u32[]{:S(2)}) copy-start(bf16[2,8,8,12,128]{4,2,3,1,0:T(8,128)(2,1)} %param.11) | copy-start | bytes 1179652
  0.7 9.4 %copy-start.10 = (bf16[2,8,8,12,128]{4,2,3,1,0:T(8,128)(2,1)S(1)}, bf16[2,8,8,12,128]{4,2,3,1,0:T(8,128)(2,1)}, u32[]{:S(2)}) copy-start(bf16[2,8,8,12,128]{4,2,3,1,0:T(8,128)(2,1)} %param.9) | copy-start | bytes 1179652
  2.5 10.9 %all-to-all-start.1 = ((bf16[2,8,8,2,6,128]{5,2,4,1,0,3:T(8,128)(2,1)}), bf16[2,8,8,2,6,128]{5,2,4,1,0,3:T(8,128)(2,1)S(1)}, u32[]{:S(2)}, u32[]{:S(2)}) async-start(bf16[2,8,8,2,6,128]{5,2,4,1,0,3:T(8,128)(2,1)} %copy.737), calls=%async_computation.1 | async-start | bytes 786432 | tf_op jit(solution)/shard_map/all_to_all | solution.py:172
  13.4 9.4 %all-to-all-start.2 = ((bf16[2,8,8,2,6,128]{5,2,4,1,0,3:T(8,128)(2,1)}), bf16[2,8,8,2,6,128]{5,2,4,1,0,3:T(8,128)(2,1)S(1)}, u32[]{:S(2)}, u32[]{:S(2)}) async-start(bf16[2,8,8,2,6,128]{5,2,4,1,0,3:T(8,128)(2,1)} %copy.740), calls=%async_computation.2 | async-start | bytes 786432 | tf_op jit(solution)/shard_map/all_to_all | solution.py:177
  17.1 64.6 %copy-start = (bf16[6,2,1,1,8,16,128]{6,5,4,1,0,3,2:T(8,128)(2,1)}, bf16[6,2,1,1,8,16,128]{6,5,4,1,0,3,2:T(8,128)(2,1)S(1)}, u32[]{:S(2)}) copy-start(bf16[6,2,1,1,8,16,128]{6,5,4,1,0,3,2:T(8,128)(2,1)S(1)} %copy.739) | copy-start | bytes 1179652
  22.9 26.5 %all-to-all-start = ((bf16[2,8,8,2,6,128]{5,2,4,1,0,3:T(8,128)(2,1)}), bf16[2,8,8,2,6,128]{5,2,4,1,0,3:T(8,128)(2,1)S(1)}, u32[]{:S(2)}, u32[]{:S(2)}) async-start(bf16[2,8,8,2,6,128]{5,2,4,1,0,3:T(8,128)(2,1)} %copy.734), calls=%async_computation | async-start | bytes 786432 | tf_op jit(solution)/shard_map/all_to_all | solution.py:167
  26.5 55.2 %copy-start.1 = (bf16[6,2,1,1,8,16,128]{6,5,4,1,0,3,2:T(8,128)(2,1)}, bf16[6,2,1,1,8,16,128]{6,5,4,1,0,3,2:T(8,128)(2,1)S(1)}, u32[]{:S(2)}) copy-start(bf16[6,2,1,1,8,16,128]{6,5,4,1,0,3,2:T(8,128)(2,1)S(1)} %copy.742) | copy-start | bytes 1179652
  26.6 9.3 %collective-permute-start = (bf16[2,6,1,1,128,128]{5,4,2,1,3,0:T(8,128)(2,1)S(1)}, bf16[2,6,1,1,128,128]{5,4,2,1,3,0:T(8,128)(2,1)S(1)}, u32[]{:S(2)}, u32[]{:S(2)}) collective-permute-start(bf16[2,6,1,1,128,128]{5,4,2,1,3,0:T(8,128)(2,1)S(1)} %get-tuple-element.232), channel_id=1, source_target_pairs={{0,8},{8,16},{16,24},{1,9},{9,17},{17,25},{2,10},{10,18},{18,26},{... | collective-permute-start | bytes 1179656 | tf_op jit(solution)/shard_map/ppermute | solution.py:18
  31.2 9.1 %collective-permute-start.1 = (bf16[2,6,1,1,128,128]{5,4,2,1,3,0:T(8,128)(2,1)S(1)}, bf16[2,6,1,1,128,128]{5,4,2,1,3,0:T(8,128)(2,1)S(1)}, u32[]{:S(2)}, u32[]{:S(2)}) collective-permute-start(bf16[2,6,1,1,128,128]{5,4,2,1,3,0:T(8,128)(2,1)S(1)} %get-tuple-element.233), channel_id=1, source_target_pairs={{8,0},{16,8},{24,16},{9,1},{17,9},{25,17},{10,2},{18,10},{26,18},{... | collective-permute-start | bytes 1179656 | tf_op jit(solution)/shard_map/ppermute | solution.py:19
  33.1 15.3 %copy-start.11 = (bf16[2,8,8,12,128]{4,2,3,1,0:T(8,128)(2,1)S(1)}, bf16[2,8,8,12,128]{4,2,3,1,0:T(8,128)(2,1)}, u32[]{:S(2)}) copy-start(bf16[2,8,8,12,128]{4,2,3,1,0:T(8,128)(2,1)} %param.12) | copy-start | bytes 1179652
  41.6 38.0 %collective-permute-start.2 = (bf16[2,6,4,1,128,128]{5,4,2,1,3,0:T(8,128)(2,1)}, bf16[2,6,4,1,128,128]{5,4,2,1,3,0:T(8,128)(2,1)}, u32[]{:S(2)}, u32[]{:S(2)}) collective-permute-start(bf16[2,6,4,1,128,128]{5,4,2,1,3,0:T(8,128)(2,1)} %pad_maximum_fusion.2), channel_id=1, source_target_pairs={{0,2},{2,4},{4,6},{1,3},{3,5},{5,7},{8,10},{10,12},{12,14},{9,11},... | collective-permute-start | bytes 4718600 | tf_op jit(solution)/shard_map/ppermute | solution.py:18
  44.8 36.8 %collective-permute-start.3 = (bf16[2,6,4,1,128,128]{5,4,2,1,3,0:T(8,128)(2,1)}, bf16[2,6,4,1,128,128]{5,4,2,1,3,0:T(8,128)(2,1)}, u32[]{:S(2)}, u32[]{:S(2)}) collective-permute-start(bf16[2,6,4,1,128,128]{5,4,2,1,3,0:T(8,128)(2,1)} %pad_maximum_fusion.2), channel_id=1, source_target_pairs={{2,0},{4,2},{6,4},{3,1},{5,3},{7,5},{10,8},{12,10},{14,12},{11,9},... | collective-permute-start | bytes 4718600 | tf_op jit(solution)/shard_map/ppermute | solution.py:19
  49.4 8.9 %all-to-all-start.3 = ((bf16[2,8,8,2,6,128]{5,2,4,1,0,3:T(8,128)(2,1)}), bf16[2,8,8,2,6,128]{5,2,4,1,0,3:T(8,128)(2,1)S(1)}, u32[]{:S(2)}, u32[]{:S(2)}) async-start(bf16[2,8,8,2,6,128]{5,2,4,1,0,3:T(8,128)(2,1)} %copy.743), calls=%async_computation.3 | async-start | bytes 786432 | tf_op jit(solution)/shard_map/all_to_all | solution.py:182
  59.3 7.8 %collective-permute-start.4 = (bf16[2,6,1,1,128,128]{5,4,2,1,3,0:T(8,128)(2,1)}, bf16[2,6,1,1,128,128]{5,4,2,1,3,0:T(8,128)(2,1)S(1)}, u32[]{:S(2)}, u32[]{:S(2)}) collective-permute-start(bf16[2,6,1,1,128,128]{5,4,2,1,3,0:T(8,128)(2,1)} %get-tuple-element.230), channel_id=1, source_target_pairs={{0,8},{8,16},{16,24},{1,9},{9,17},{17,25},{2,10},{10,18},{18,26},{... | collective-permute-start | bytes 1179656 | tf_op jit(solution)/shard_map/ppermute | solution.py:18
  62.1 9.7 %collective-permute-start.5 = (bf16[2,6,1,1,128,128]{5,4,2,1,3,0:T(8,128)(2,1)}, bf16[2,6,1,1,128,128]{5,4,2,1,3,0:T(8,128)(2,1)S(1)}, u32[]{:S(2)}, u32[]{:S(2)}) collective-permute-start(bf16[2,6,1,1,128,128]{5,4,2,1,3,0:T(8,128)(2,1)} %get-tuple-element.231), channel_id=1, source_target_pairs={{8,0},{16,8},{24,16},{9,1},{17,9},{25,17},{10,2},{18,10},{26,18},{... | collective-permute-start | bytes 1179656 | tf_op jit(solution)/shard_map/ppermute | solution.py:19
  67.1 6.0 %copy-start.2 = (bf16[2,6,1,1,128,128]{5,4,2,1,3,0:T(8,128)(2,1)}, bf16[2,6,1,1,128,128]{5,4,2,1,3,0:T(8,128)(2,1)S(1)}, u32[]{:S(2)}) copy-start(bf16[2,6,1,1,128,128]{5,4,2,1,3,0:T(8,128)(2,1)S(1)} %collective-permute-done.4) | copy-start | bytes 1179652
  73.2 49.7 %collective-permute-start.6 = (bf16[2,6,4,1,128,128]{5,4,2,1,3,0:T(8,128)(2,1)}, bf16[2,6,4,1,128,128]{5,4,2,1,3,0:T(8,128)(2,1)}, u32[]{:S(2)}, u32[]{:S(2)}) collective-permute-start(bf16[2,6,4,1,128,128]{5,4,2,1,3,0:T(8,128)(2,1)} %pad_maximum_fusion.3), channel_id=1, source_target_pairs={{0,2},{2,4},{4,6},{1,3},{3,5},{5,7},{8,10},{10,12},{12,14},{9,11},... | collective-permute-start | bytes 4718600 | tf_op jit(solution)/shard_map/ppermute | solution.py:18
  75.2 47.7 %collective-permute-start.7 = (bf16[2,6,4,1,128,128]{5,4,2,1,3,0:T(8,128)(2,1)}, bf16[2,6,4,1,128,128]{5,4,2,1,3,0:T(8,128)(2,1)}, u32[]{:S(2)}, u32[]{:S(2)}) collective-permute-start(bf16[2,6,4,1,128,128]{5,4,2,1,3,0:T(8,128)(2,1)} %pad_maximum_fusion.3), channel_id=1, source_target_pairs={{2,0},{4,2},{6,4},{3,1},{5,3},{7,5},{10,8},{12,10},{14,12},{11,9},... | collective-permute-start | bytes 4718600 | tf_op jit(solution)/shard_map/ppermute | solution.py:19
  118.5 7.4 %collective-permute-start.8 = (f32[2,6,1,1,128]{4,2,3,1,0:T(1,128)S(1)}, f32[2,6,1,1,128]{4,2,3,1,0:T(1,128)S(1)}, u32[]{:S(2)}, u32[]{:S(2)}) collective-permute-start(f32[2,6,1,1,128]{4,2,3,1,0:T(1,128)S(1)} %get-tuple-element.253), channel_id=1, source_target_pairs={{0,8},{8,16},{16,24},{1,9},{9,17},{17,25},{2,10},{10,18},{18,26},{... | collective-permute-start | bytes 18440 | tf_op jit(solution)/shard_map/ppermute | solution.py:18
  120.5 5.5 %collective-permute-start.9 = (f32[2,6,1,1,128]{4,2,3,1,0:T(1,128)S(1)}, f32[2,6,1,1,128]{4,2,3,1,0:T(1,128)S(1)}, u32[]{:S(2)}, u32[]{:S(2)}) collective-permute-start(f32[2,6,1,1,128]{4,2,3,1,0:T(1,128)S(1)} %get-tuple-element.254), channel_id=1, source_target_pairs={{8,0},{16,8},{24,16},{9,1},{17,9},{25,17},{10,2},{18,10},{26,18},{... | collective-permute-start | bytes 18440 | tf_op jit(solution)/shard_map/ppermute | solution.py:19
  126.0 7.8 %copy-start.6 = (bf16[6,2,1,128,128]{4,3,1,2,0:T(8,128)(2,1)S(1)}, bf16[6,2,1,128,128]{4,3,1,2,0:T(8,128)(2,1)}, u32[]{:S(2)}) copy-start(bf16[6,2,1,128,128]{4,3,1,2,0:T(8,128)(2,1)} %get-tuple-element.112) | copy-start | bytes 1179652
  126.0 14.3 %collective-permute-start.10 = (f32[2,6,4,1,128]{4,2,3,1,0:T(4,128)S(1)}, f32[2,6,4,1,128]{4,2,3,1,0:T(4,128)S(1)}, u32[]{:S(2)}, u32[]{:S(2)}) collective-permute-start(f32[2,6,4,1,128]{4,2,3,1,0:T(4,128)S(1)} %pad_maximum_fusion.7), channel_id=1, source_target_pairs={{0,2},{2,4},{4,6},{1,3},{3,5},{5,7},{8,10},{10,12},{12,14},{9,11},... | collective-permute-start | bytes 73736 | tf_op jit(solution)/shard_map/ppermute | solution.py:18
  128.9 11.5 %collective-permute-start.11 = (f32[2,6,4,1,128]{4,2,3,1,0:T(4,128)S(1)}, f32[2,6,4,1,128]{4,2,3,1,0:T(4,128)S(1)}, u32[]{:S(2)}, u32[]{:S(2)}) collective-permute-start(f32[2,6,4,1,128]{4,2,3,1,0:T(4,128)S(1)} %pad_maximum_fusion.7), channel_id=1, source_target_pairs={{2,0},{4,2},{6,4},{3,1},{5,3},{7,5},{10,8},{12,10},{14,12},{11,9},... | collective-permute-start | bytes 73736 | tf_op jit(solution)/shard_map/ppermute | solution.py:19
  133.8 5.7 %copy-start.7 = (bf16[6,2,1,128,128]{4,3,1,2,0:T(8,128)(2,1)S(1)}, bf16[6,2,1,128,128]{4,3,1,2,0:T(8,128)(2,1)}, u32[]{:S(2)}) copy-start(bf16[6,2,1,128,128]{4,3,1,2,0:T(8,128)(2,1)} %get-tuple-element.113) | copy-start | bytes 1179652
  134.7 12.6 %all-to-all-start.4 = ((bf16[2,8,16,1,6,128]{5,1,0,4,3,2:T(8,128)(2,1)}), bf16[2,8,16,1,6,128]{5,1,0,4,3,2:T(8,128)(2,1)S(1)}, u32[]{:S(2)}, u32[]{:S(2)}) async-start(bf16[2,8,16,1,6,128]{5,1,0,4,3,2:T(8,128)(2,1)} %copy.750), calls=%async_computation.4 | async-start | bytes 786432 | tf_op jit(solution)/shard_map/all_to_all | solution.py:210
  147.2 5.8 %copy-start.4 = (bf16[2,8,16,1,6,128]{5,1,0,4,3,2:T(8,128)(2,1)}, bf16[2,8,16,1,6,128]{5,1,0,4,3,2:T(8,128)(2,1)S(1)}, u32[]{:S(2)}) copy-start(bf16[2,8,16,1,6,128]{5,1,0,4,3,2:T(8,128)(2,1)S(1)} %all-to-all-done.4) | copy-start | bytes 1179652
  147.2 66.1 %all-to-all-start.5 = ((bf16[2,8,16,1,6,128]{5,1,0,4,3,2:T(8,128)(2,1)}), bf16[2,8,16,1,6,128]{5,1,0,4,3,2:T(8,128)(2,1)}, u32[]{:S(2)}, u32[]{:S(2)}) async-start(bf16[2,8,16,1,6,128]{5,1,0,4,3,2:T(8,128)(2,1)} %copy.753), calls=%async_computation.5 | async-start | bytes 786432 | tf_op jit(solution)/shard_map/all_to_all | solution.py:211
  211.4 5.4 %copy-start.8 = (bf16[6,2,1,128,128]{4,3,1,2,0:T(8,128)(2,1)S(1)}, bf16[6,2,1,128,128]{4,3,1,2,0:T(8,128)(2,1)}, u32[]{:S(2)}) copy-start(bf16[6,2,1,128,128]{4,3,1,2,0:T(8,128)(2,1)} %get-tuple-element.117) | copy-start | bytes 1179652
  211.4 15.0 %copy-start.5 = (bf16[2,8,16,1,6,128]{5,1,0,4,3,2:T(8,128)(2,1)S(1)}, bf16[2,8,16,1,6,128]{5,1,0,4,3,2:T(8,128)(2,1)}, u32[]{:S(2)}) copy-start(bf16[2,8,16,1,6,128]{5,1,0,4,3,2:T(8,128)(2,1)} %copy-done.4) | copy-start | bytes 1179652
  213.4 9.6 %all-to-all-start.6 = ((bf16[2,8,16,1,6,128]{5,1,0,4,3,2:T(8,128)(2,1)}), bf16[2,8,16,1,6,128]{5,1,0,4,3,2:T(8,128)(2,1)S(1)}, u32[]{:S(2)}, u32[]{:S(2)}) async-start(bf16[2,8,16,1,6,128]{5,1,0,4,3,2:T(8,128)(2,1)} %copy.783), calls=%async_computation.6 | async-start | bytes 786432 | tf_op jit(solution)/shard_map/all_to_all | solution.py:212
  223.0 8.7 %all-to-all-start.7 = ((bf16[2,8,16,1,6,128]{5,1,0,4,3,2:T(8,128)(2,1)}), bf16[2,8,16,1,6,128]{5,1,0,4,3,2:T(8,128)(2,1)S(1)}, u32[]{:S(2)}, u32[]{:S(2)}) async-start(bf16[2,8,16,1,6,128]{5,1,0,4,3,2:T(8,128)(2,1)} %copy.786), calls=%async_computation.7 | async-start | bytes 786432 | tf_op jit(solution)/shard_map/all_to_all | solution.py:213
  (7 other events, 6.4 us)
where the time goes:
time: 237 us; the launch traced here: 233 us
  local copies, waits for them, and re-layouts  67 us (28%)
  starting transfers between devices  63.6 us (27%)
  matrix products  45.4 us (19%)
  waiting for transfers between devices  39.1 us (16%)
  other arithmetic  14.8 us (6%)
    dot_general x36, matrix products, product(): return jnp.einsum(form, left, right, preferred_element_type=jnp.float32)  40.2 us
    ppermute x6, starting transfers between devices, padded(): before = lax.ppermute(last, axis, up)  17.4 us
    ppermute x6, starting transfers between devices, padded(): after = lax.ppermute(initial, axis, down)  16.4 us
    squeeze x12, local copies, waits for them, and re-layouts, on_device(): lax.map(front, (query_slab, key_wide, value_wide, grad_slab))  13.5 us
    ppermute x6, waiting for transfers between devices, padded(): after = lax.ppermute(initial, axis, down)  11.1 us
    another operation x36, local copies, waits for them, and re-layouts, gather_bands(): stacked = jnp.stack(parts, axis=2)  9.01 us
    concatenate x6, other arithmetic, padded(): shard = jnp.concatenate([before, shard, after], axis=dim)  8.67 us
    while x216, local copies, waits for them, and re-layouts  6.43 us
  transfers between devices with their start and end apart: 20, of which 10 were waited for; matrix products, arithmetic and copies ran while one was open for 53% of the time, Pallas kernels for 0%

commit v1 on v0

v1 whole, which is shorter than its diff:
```python
import functools

import jax
import jax.numpy as jnp
from jax import lax
from jax.experimental import pallas as pl
from jax.experimental.pallas import tpu as pltpu
from jax.sharding import PartitionSpec as P

TF = 1
TR = 8
TC = 8
MASKED = -1e30
NT = (((1,), (1,)), ((), ()))
NN = (((1,), (0,)), ((), ()))


def dot(left, right, dims):
    return lax.dot_general(left, right, dims, preferred_element_type=jnp.float32)


def spread(bias, tokens):
    blocks, width = bias.shape
    return jnp.broadcast_to(bias[:, None, :], (blocks, tokens // blocks, width)).reshape(tokens, width)


def fill_band(own, before, after, low, high, first, second):
    frames, tokens = own.shape[1], own.shape[3]
    for at in range(frames + 2):
        for row, beside in enumerate((before, own, after)):
            place = pl.ds((3 * at + row) * tokens, tokens)
            for which, band in enumerate((first, second)):
                if at == 0:
                    band[place, :] = low[row, which, 0]
                elif at == frames + 1:
                    band[place, :] = high[row, which, 0]
                else:
                    band[place, :] = beside[which, at - 1, 0]


def front_kernel(
    scaling, pair, own, before, after, low, high, bias, attended, query_grad, stats, key_all, value_all
):
    frames, tokens = own.shape[1], own.shape[3]
    fill_band(own, before, after, low, high, key_all, value_all)
    for at in range(frames):
        window = pl.ds(3 * at * tokens, 9 * tokens)
        key_band = key_all[window, :]
        value_band = value_all[window, :]
        scores = dot(pair[0, at, 0], key_band, NT) * scaling + spread(bias[at], tokens)
        highest = jnp.max(scores, axis=1, keepdims=True)
        raised = jnp.exp(scores - highest)
        total = jnp.sum(raised, axis=1, keepdims=True)
        weights = (raised * (1.0 / total)).astype(jnp.bfloat16)
        out = dot(weights, value_band, NN).astype(jnp.bfloat16)
        grad = pair[1, at, 0]
        grad_dot = jnp.sum(grad.astype(jnp.float32) * out.astype(jnp.float32), axis=1, keepdims=True)
        grad_probs = dot(grad, value_band, NT)
        grad_scores = (weights.astype(jnp.float32) * (grad_probs - grad_dot)).astype(jnp.bfloat16)
        attended[at, 0] = out
        query_grad[at, 0] = (dot(grad_scores, key_band, NN) * scaling).astype(jnp.bfloat16)
        lane = lax.broadcasted_iota(jnp.int32, (tokens, 128), 1)
        both = jnp.where(lane == 0, highest + jnp.log(total), grad_dot)
        stats[at, 0] = jnp.transpose(both)[:2]


def back_kernel(
    scaling, pair, own, before, after, low, high, own_st, before_st, after_st, low_st, high_st, bias,
    key_grad, value_grad, query_all, grad_all
):
    frames, tokens = own.shape[1], own.shape[3]
    fill_band(own, before, after, low, high, query_all, grad_all)

    def stat_row(at, row, which):
        if at == 0:
            return low_st[row, 0, which : which + 1]
        if at == frames + 1:
            return high_st[row, 0, which : which + 1]
        return (before_st, own_st, after_st)[row][at - 1, 0, which : which + 1]

    def stat_band(at, which):
        rows = [stat_row(at + step, row, which) for step in range(3) for row in range(3)]
        return jnp.concatenate(rows, axis=1)

    for at in range(frames):
        window = pl.ds(3 * at * tokens, 9 * tokens)
        query_band = query_all[window, :]
        grad_band = grad_all[window, :]
        shift = bias[at] - stat_band(at, 0)
        weights = jnp.exp(dot(pair[0, at, 0], query_band, NT) * scaling + spread(shift, tokens))
        weights = weights.astype(jnp.bfloat16)
        grad_probs = dot(pair[1, at, 0], grad_band, NT)
        grad_scores = weights.astype(jnp.float32) * (grad_probs - stat_band(at, 1))
        key_grad[at, 0] = (dot(grad_scores.astype(jnp.bfloat16), query_band, NN) * scaling).astype(jnp.bfloat16)
        value_grad[at, 0] = dot(weights, grad_band, NN).astype(jnp.bfloat16)


def pair_spec(frames, tokens, dim):
    return pl.BlockSpec((2, frames, 1, tokens, dim), lambda head: (0, 0, head, 0, 0))


def edge_spec(tokens, dim):
    return pl.BlockSpec((3, 2, 1, tokens, dim), lambda head: (0, 0, head, 0, 0))


def whole_spec(shape):
    return pl.BlockSpec(shape, lambda head: (0,) * len(shape))


def head_spec(count, rows, dim):
    return pl.BlockSpec((count, 1, rows, dim), lambda head: (0, head, 0, 0))


def cost(frames, groups, tokens, dim):
    return pl.CostEstimate(
        flops=frames * groups * 8 * tokens * 9 * tokens * dim,
        bytes_accessed=groups * (frames + 2) * 3 * 2 * tokens * dim * 2,
        transcendentals=frames * groups * tokens * 9 * tokens,
    )


def front(pair, halo, bias, scaling):
    _, frames, groups, tokens, dim = pair.shape
    grad = jax.ShapeDtypeStruct((frames, groups, tokens, dim), jnp.bfloat16)
    near = pair_spec(frames, tokens, dim)
    edge = edge_spec(tokens, dim)
    return pl.pallas_call(
        functools.partial(front_kernel, scaling),
        grid=(groups,),
        out_shape=(grad, grad, jax.ShapeDtypeStruct((frames, groups, 2, tokens), jnp.float32)),
        in_specs=[near, near, near, near, edge, edge, whole_spec(bias.shape)],
        out_specs=(
            head_spec(frames, tokens, dim),
            head_spec(frames, tokens, dim),
            head_spec(frames, 2, tokens),
        ),
        scratch_shapes=[pltpu.VMEM((3 * (frames + 2) * tokens, dim), jnp.bfloat16)] * 2,
        compiler_params=pltpu.CompilerParams(vmem_limit_bytes=32 * 2**20),
        cost_estimate=cost(frames, groups, tokens, dim),
    )(pair, *halo, bias)


def back(pair, halo, stats, bias, scaling):
    _, frames, groups, tokens, dim = pair.shape
    grad = jax.ShapeDtypeStruct((frames, groups, tokens, dim), jnp.bfloat16)
    near = pair_spec(frames, tokens, dim)
    edge = edge_spec(tokens, dim)
    near_st = head_spec(frames, 2, tokens)
    edge_st = head_spec(3, 2, tokens)
    return pl.pallas_call(
        functools.partial(back_kernel, scaling),
        grid=(groups,),
        out_shape=(grad, grad),
        in_specs=[near, near, near, near, edge, edge]
        + [near_st, near_st, near_st, edge_st, edge_st, whole_spec(bias.shape)],
        out_specs=(head_spec(frames, tokens, dim), head_spec(frames, tokens, dim)),
        scratch_shapes=[pltpu.VMEM((3 * (frames + 2) * tokens, dim), jnp.bfloat16)] * 2,
        compiler_params=pltpu.CompilerParams(vmem_limit_bytes=32 * 2**20),
        cost_estimate=cost(frames, groups, tokens, dim),
    )(pair, *halo, *stats, bias)


def step_along(tensor, axis, sign):
    size = lax.axis_size(axis)
    return lax.ppermute(tensor, axis, [(i, i + sign) for i in range(size) if 0 <= i + sign < size])


def turn(tensor, shift):
    size = lax.axis_size("head")
    return lax.ppermute(tensor, "head", [(i, (i + shift) % size) for i in range(size)])


def surroundings(own, frame_dim):
    before = step_along(own, "row", 1)
    after = step_along(own, "row", -1)

    def edge(at):
        parts = [lax.index_in_dim(part, at, frame_dim, keepdims=False) for part in (before, own, after)]
        return jnp.stack(parts)

    low = step_along(edge(own.shape[frame_dim] - 1), "frame", 1)
    high = step_along(edge(0), "frame", -1)
    return own, before, after, low, high


def tile_biases(active, frames, columns_here, tokens):
    size = lax.axis_size("head")
    me = lax.axis_index("head")
    frame_at = lax.axis_index("frame") * frames
    row_at = lax.axis_index("row")
    all_frames, all_rows, count, slots = active.shape
    padded = jnp.pad(active.astype(jnp.float32), ((1, 1), (1, 1), (0, 0), (0, 0)))
    near = lax.dynamic_slice(padded, (frame_at, row_at, 0, 0), (frames + 2, 3, count, slots))
    near = near.reshape(frames + 2, 3, count, 9, 3)
    frame_ids = frame_at - 1 + jnp.arange(frames + 2)
    row_ids = row_at - 1 + jnp.arange(3)
    inside = ((frame_ids >= 0) & (frame_ids < all_frames))[:, None] & ((row_ids >= 0) & (row_ids < all_rows))
    inside = inside.astype(jnp.float32)
    tile_of = ((me + jnp.arange(size)) % size * columns_here) // TC

    def layers(own_tile, other_tile):
        shift = other_tile - own_tile
        if abs(shift) > 1:
            nothing = jnp.zeros((frames, 9), jnp.float32)
            return nothing, nothing
        ahead, behind = [], []
        for offset in range(9):
            frame_step, row_step = offset // 3, offset % 3
            chosen = near[1 : 1 + frames, 1, own_tile, offset, shift + 1]
            ahead.append(chosen * inside[frame_step : frame_step + frames, row_step])
            behind.append(near[frame_step : frame_step + frames, row_step, own_tile, 8 - offset, 1 - shift])
        return jnp.stack(ahead, 1), jnp.stack(behind, 1)

    table = [[layers(i, j) for j in range(count)] for i in range(count)]
    biases = []
    for which in range(2):
        tiles = jnp.stack([jnp.stack([table[i][j][which] for j in range(count)]) for i in range(count)])
        chosen = jnp.zeros((size, size, frames, 9), jnp.float32)
        for i in range(count):
            for j in range(count):
                here = ((tile_of == i)[:, None] & (tile_of == j)[None, :])[:, :, None, None]
                chosen = jnp.where(here, tiles[i, j], chosen)
        bias = jnp.where(chosen > 0.5, 0.0, MASKED).transpose(2, 0, 3, 1)
        bias = jnp.broadcast_to(bias[..., None], (frames, size, 9, size, tokens // size))
        biases.append(bias.reshape(frames, size, 9 * tokens))
    return biases


def on_device(queries, keys, values, out_grad, active):
    frames, rows, columns_here, heads, dim = queries.shape
    size = lax.axis_size("head")
    me = lax.axis_index("head")
    groups = heads // size
    cells = rows * columns_here
    tokens = cells * size
    scaling = dim ** (-0.5)

    def to_heads(tensors):
        moved = [t.reshape(frames, cells, heads, dim).transpose(0, 2, 1, 3) for t in tensors]
        stacked = jnp.stack(moved)

        def group(shift):
            return lax.dynamic_slice_in_dim(stacked, (me + shift) % size * groups, groups, 2)

        parts = [group(0)] + [turn(group(size - b), size - b) for b in range(1, size)]
        return jnp.concatenate(parts, axis=3)

    def from_heads(tensors):
        stacked = jnp.stack(tensors)

        def block(b):
            return lax.slice_in_dim(stacked, b * cells, (b + 1) * cells, axis=3)

        whole = jnp.zeros((len(tensors), frames, heads, cells, dim), jnp.bfloat16)
        for b in range(size):
            piece = block(0) if b == 0 else turn(block(b), b)
            whole = lax.dynamic_update_slice_in_dim(whole, piece, (me + size - b) % size * groups, 2)
        whole = whole.reshape(len(tensors), frames, heads, rows, columns_here, dim).transpose(0, 1, 3, 4, 2, 5)
        return [whole[i] for i in range(len(tensors))]

    front_bias, back_bias = tile_biases(active, frames, columns_here, tokens)
    key_value = to_heads((keys, values))
    query_grad_out = to_heads((queries, out_grad))
    key_halo = surroundings(key_value, 1)
    query_halo = surroundings(query_grad_out, 1)
    attended, query_grad, stats = front(query_grad_out, key_halo, front_bias, scaling)
    stat_halo = surroundings(stats, 0)
    key_grad, value_grad = back(key_value, query_halo, stat_halo, back_bias, scaling)
    attended, query_grad = from_heads((attended, query_grad))
    key_grad, value_grad = from_heads((key_grad, value_grad))
    return attended, query_grad, key_grad, value_grad


def solution(mesh):
    spec = P("frame", "row", "head", None, None)
    return jax.shard_map(
        on_device, mesh=mesh, in_specs=(spec,) * 4 + (P(),), out_specs=(spec,) * 4, check_vma=False
    )
```

time: 237 us -> 116 us (0.49)
  local copies, waits for them, and re-layouts: 67 us -> 20.6 us
  matrix products: 45.4 us -> 0 us
  waiting for transfers between devices: 39.1 us -> 19 us
  Pallas kernels: 0 us -> 19.5 us
  starting transfers between devices: 63.6 us -> 44.5 us
  other arithmetic: 14.8 us -> 8.6 us
    dot_general x56 -> x0, matrix products: 45.4 us -> none  [the longest x36 40.2 us: product(): return jnp.einsum(form, left, right, preferred_element_type=jnp.float32)]
    all_to_all x8 -> x0, starting transfers between devices: 29.8 us -> none  [the longest x1 4.84 us: on_device(): lax.all_to_all(from_slabs(attended), 'head', split_axis=2, concat_axis=3,...]
    squeeze x21 -> x6, local copies, waits for them, and re-layouts: 24.3 us -> 0.3 us  [the longest x2 0.18 us: layers(): chosen = near[1:1 + frames, 1, own_tile, offset, shift + 1]]
    all_to_all x8 -> x0, waiting for transfers between devices: 24 us -> none  [the longest x1 6.21 us: on_device(): lax.all_to_all(from_slabs(attended), 'head', split_axis=2, concat_axis=3,...]
    pallas_call x0 -> x2, Pallas kernels: none -> 19.5 us  [the longest x1 12.2 us: front(): pl.pallas_call(functools.partial(front_kernel, scaling), grid=(groups,),...]
    ppermute x12 -> x16, starting transfers between devices: 33.8 us -> 44.5 us  [the longest x12 40.9 us: step_along(): lax.ppermute(tensor, axis, [(i, i + sign) for i in range(size) if 0 <= i...]
    reshape x8 -> x2, local copies, waits for them, and re-layouts: 8.65 us -> 0.21 us  [tile_biases(): biases.append(bias.reshape(frames, size, 9 * tokens))]
    concatenate x6 -> x2, other arithmetic: 8.67 us -> 1.16 us  [to_heads(): return jnp.concatenate(parts, axis=3)]
  transfers between devices with their start and end apart: 20 -> 16, of which waited for: 10 -> 5; matrix products, arithmetic and copies ran while one was open for 53% -> 22% of each run, Pallas kernels for 0% -> 17%
where the time goes in v1:
time: 116 us; the launch traced here: 114 us
  starting transfers between devices  44.5 us (38%)
  local copies, waits for them, and re-layouts  20.6 us (18%)
  Pallas kernels  19.5 us (17%)
  waiting for transfers between devices  19 us (16%)
  other arithmetic  8.6 us (7%)
  between operations  1.31 us (1%)
    ppermute x12, starting transfers between devices, step_along(): lax.ppermute(tensor, axis, [(i, i + sign) for i in range(size) if 0 <= i...  40.9 us
    pallas_call x1, Pallas kernels, front(): pl.pallas_call(functools.partial(front_kernel, scaling), grid=(groups,),...  12.2 us
    ppermute x4, waiting for transfers between devices, turn(): lax.ppermute(tensor, 'head', [(i, (i + shift) % size) for i in range(size)])  10.4 us
    ppermute x12, waiting for transfers between devices, step_along(): lax.ppermute(tensor, axis, [(i, i + sign) for i in range(size) if 0 <= i...  8.67 us
    pallas_call x1, Pallas kernels, back(): pl.pallas_call(functools.partial(back_kernel, scaling), grid=(groups,), o...  7.35 us
    another operation x9, other arithmetic, edge(): return jnp.stack(parts)  5.84 us
    unnamed x22, local copies, waits for them, and re-layouts  4.11 us
    another operation x44, local copies, waits for them, and re-layouts, layers(): return (jnp.stack(ahead, 1), jnp.stack(behind, 1))  4.1 us
  transfers between devices with their start and end apart: 16, of which 5 were waited for; matrix products, arithmetic and copies ran while one was open for 22% of the time, Pallas kernels for 17%

profile of v1, /device:TPU:9, one launch (start us, length us, event | category | flops | bytes accessed | tf_op | source)
XLA Modules:
  0.0 113.6 jit_solution(12166957900002758214)
XLA Ops:
  0.7 1.3 %copy_bitcast_fusion = (bf16[1,2,12,64,128]{4,3,2,1,0:T(8,128)(2,1)S(1)}, bf16[1,2,12,64,128]{4,3,2,1,0:T(8,128)(2,1)S(1)}) fusion(bf16[2,8,8,12,128]{4,2,3,1,0:T(8,128)(2,1)} %param.7, bf16[2,8,8,12,128]{4,2,3,1,0:T(8,128)(2,1)} %param.6), kind=kLoop, calls=%fused_computation.53 | loop fusion | bytes 1572864 | tf_op jit(solution)/shard_map/stack | solution.py:240
  2.1 1.3 %collective-permute-start.1 = (bf16[2,2,6,64,128]{4,3,2,1,0:T(8,128)(2,1)S(1)}, bf16[2,2,6,64,128]{4,3,2,1,0:T(8,128)(2,1)S(1)}, u32[]{:S(2)}, u32[]{:S(2)}) collective-permute-start(bf16[2,2,6,64,128]{4,3,2,1,0:T(8,128)(2,1)S(1)} %get-tuple-element.41), channel_id=1, source_target_pairs={{0,1},{1,0},{2,3},{3,2},{4,5},{5,4},{6,7},{7,6},{8,9},{9,8},{10,11... | collective-permute-start | bytes 1179656 | tf_op jit(solution)/shard_map/ppermute | solution.py:170
  13.2 3.2 %collective-permute-start.2 = (bf16[2,2,6,128,128]{4,3,2,0,1:T(8,128)(2,1)S(1)}, bf16[2,2,6,128,128]{4,3,2,0,1:T(8,128)(2,1)S(1)}, u32[]{:S(2)}, u32[]{:S(2)}) collective-permute-start(bf16[2,2,6,128,128]{4,3,2,0,1:T(8,128)(2,1)S(1)} %copy.60), channel_id=1, source_target_pairs={{0,2},{2,4},{4,6},{1,3},{3,5},{5,7},{8,10},{10,12},{12,14},{9,11},... | collective-permute-start | bytes 2359304 | tf_op jit(solution)/shard_map/ppermute | solution.py:165
  16.4 2.1 %collective-permute-start.3 = (bf16[2,2,6,128,128]{4,3,2,0,1:T(8,128)(2,1)S(1)}, bf16[2,2,6,128,128]{4,3,2,0,1:T(8,128)(2,1)S(1)}, u32[]{:S(2)}, u32[]{:S(2)}) collective-permute-start(bf16[2,2,6,128,128]{4,3,2,0,1:T(8,128)(2,1)S(1)} %copy.60), channel_id=1, source_target_pairs={{2,0},{4,2},{6,4},{3,1},{5,3},{7,5},{10,8},{12,10},{14,12},{11,9},... | collective-permute-start | bytes 2359304 | tf_op jit(solution)/shard_map/ppermute | solution.py:165
  18.6 2.0 %collective-permute-done = bf16[2,2,6,64,128]{4,3,2,0,1:T(8,128)(2,1)S(1)} collective-permute-done((bf16[2,2,6,64,128]{4,3,2,0,1:T(8,128)(2,1)S(1)}, bf16[2,2,6,64,128]{4,3,2,0,1:T(8,128)(2,1)S(1)}, u32[]{:S(2)}, u32[]{:S(2)}) %collective-permute-start) | collective-permute-done | bytes 393248 | tf_op jit(solution)/shard_map/ppermute | solution.py:170
  20.6 1.1 pad_maximum_fusion.4
  21.7 3.2 %collective-permute-start.7 = (bf16[2,2,6,128,128]{4,3,2,0,1:T(8,128)(2,1)}, bf16[2,2,6,128,128]{4,3,2,0,1:T(8,128)(2,1)}, u32[]{:S(2)}, u32[]{:S(2)}) collective-permute-start(bf16[2,2,6,128,128]{4,3,2,0,1:T(8,128)(2,1)} %pad_maximum_fusion.4), channel_id=1, source_target_pairs={{0,2},{2,4},{4,6},{1,3},{3,5},{5,7},{8,10},{10,12},{12,14},{9,11},... | collective-permute-start | bytes 2359304 | tf_op jit(solution)/shard_map/ppermute | solution.py:165
  24.9 3.0 %collective-permute-start.8 = (bf16[2,2,6,128,128]{4,3,2,0,1:T(8,128)(2,1)}, bf16[2,2,6,128,128]{4,3,2,0,1:T(8,128)(2,1)}, u32[]{:S(2)}, u32[]{:S(2)}) collective-permute-start(bf16[2,2,6,128,128]{4,3,2,0,1:T(8,128)(2,1)} %pad_maximum_fusion.4), channel_id=1, source_target_pairs={{2,0},{4,2},{6,4},{3,1},{5,3},{7,5},{10,8},{12,10},{14,12},{11,9},... | collective-permute-start | bytes 2359304 | tf_op jit(solution)/shard_map/ppermute | solution.py:165
  27.9 4.4 %collective-permute-done.2 = bf16[2,2,6,128,128]{4,3,2,0,1:T(8,128)(2,1)S(1)} collective-permute-done((bf16[2,2,6,128,128]{4,3,2,0,1:T(8,128)(2,1)S(1)}, bf16[2,2,6,128,128]{4,3,2,0,1:T(8,128)(2,1)S(1)}, u32[]{:S(2)}, u32[]{:S(2)}) %collective-permute-start.2) | collective-permute-done | bytes 786464 | tf_op jit(solution)/shard_map/ppermute | solution.py:165
  32.4 2.9 %collective-permute-done.3 = bf16[2,2,6,128,128]{4,3,2,0,1:T(8,128)(2,1)S(1)} collective-permute-done((bf16[2,2,6,128,128]{4,3,2,0,1:T(8,128)(2,1)S(1)}, bf16[2,2,6,128,128]{4,3,2,0,1:T(8,128)(2,1)S(1)}, u32[]{:S(2)}, u32[]{:S(2)}) %collective-permute-start.3) | collective-permute-done | bytes 786464 | tf_op jit(solution)/shard_map/ppermute | solution.py:165
  36.1 1.1 pad_maximum_fusion.1
  37.3 7.5 %collective-permute-start.5 = (bf16[3,2,6,128,128]{4,3,2,1,0:T(8,128)(2,1)}, bf16[3,2,6,128,128]{4,3,2,1,0:T(8,128)(2,1)S(1)}, u32[]{:S(2)}, u32[]{:S(2)}) collective-permute-start(bf16[3,2,6,128,128]{4,3,2,1,0:T(8,128)(2,1)} %pad_maximum_fusion.1), channel_id=1, source_target_pairs={{8,0},{16,8},{24,16},{9,1},{17,9},{25,17},{10,2},{18,10},{26,18},{... | collective-permute-start | bytes 3538952 | tf_op jit(solution)/shard_map/ppermute | solution.py:165
  44.8 1.1 %pad_maximum_fusion = bf16[3,2,6,128,128]{4,3,2,1,0:T(8,128)(2,1)} fusion(bf16[1,2,6,128,128]{4,3,2,1,0:T(8,128)(2,1)S(1)} %get-tuple-element.39, bf16[1,2,6,128,128]{4,3,2,1,0:T(8,128)(2,1)S(1)} %slice_bitcast_fusion.11, bf16[1,2,6,128,128]{4,3,2,1,0:T(8,128)(2,1)S(1)} %get-tuple-element.37), kind=kLoop, calls=%fused_computation | loop fusion | flops 1179648 | bytes 2359296 | tf_op jit(solution)/shard_map/stack | solution.py:179
  45.9 3.0 %collective-permute-start.4 = (bf16[3,2,6,128,128]{4,3,2,1,0:T(8,128)(2,1)}, bf16[3,2,6,128,128]{4,3,2,1,0:T(8,128)(2,1)}, u32[]{:S(2)}, u32[]{:S(2)}) collective-permute-start(bf16[3,2,6,128,128]{4,3,2,1,0:T(8,128)(2,1)} %pad_maximum_fusion), channel_id=1, source_target_pairs={{0,8},{8,16},{16,24},{1,9},{9,17},{17,25},{2,10},{10,18},{18,26},{... | collective-permute-start | bytes 3538952 | tf_op jit(solution)/shard_map/ppermute | solution.py:165
  50.0 1.2 %copy.100.pair.own = bf16[2,2,6,128,128]{4,3,2,1,0:T(8,128)(2,1)S(1)} copy(bf16[2,2,6,128,128]{4,3,2,0,1:T(8,128)(2,1)} %pad_maximum_fusion.4) | data formatting | bytes 1572864 | tf_op jit(solution)/shard_map/concatenate | solution.py:246
  51.2 1.1 fusion.13
  52.3 1.2 %slice_bitcast_fusion.3 = (bf16[1,2,6,128,128]{4,3,2,1,0:T(8,128)(2,1)S(1)}, bf16[1,2,6,128,128]{4,3,2,1,0:T(8,128)(2,1)S(1)}) fusion(bf16[2,2,6,128,128]{4,3,2,0,1:T(8,128)(2,1)} %collective-permute-done.7), kind=kLoop, calls=%fused_computation.42 | loop fusion | bytes 1572864 | tf_op jit(solution)/shard_map/stack;squeeze | solution.py:179
  53.5 1.2 %slice_bitcast_fusion.2 = (bf16[1,2,6,128,128]{4,3,2,1,0:T(8,128)(2,1)S(1)}, bf16[1,2,6,128,128]{4,3,2,1,0:T(8,128)(2,1)S(1)}) fusion(bf16[2,2,6,128,128]{4,3,2,0,1:T(8,128)(2,1)} %collective-permute-done.8), kind=kLoop, calls=%fused_computation.41 | loop fusion | bytes 1572864 | tf_op jit(solution)/shard_map/stack;squeeze | solution.py:179
  54.7 1.2 %pad_maximum_fusion.3 = bf16[3,2,6,128,128]{4,3,2,1,0:T(8,128)(2,1)} fusion(bf16[1,2,6,128,128]{4,3,2,1,0:T(8,128)(2,1)S(1)} %get-tuple-element.30, bf16[1,2,6,128,128]{4,3,2,1,0:T(8,128)(2,1)S(1)} %get-tuple-element.28, bf16[1,2,6,128,128]{4,3,2,1,0:T(8,128)(2,1)S(1)} %get-tuple-element.26), kind=kLoop, calls=%fused_computation.3 | loop fusion | flops 1179648 | bytes 2359296 | tf_op jit(solution)/shard_map/stack | solution.py:179
  55.8 3.6 %collective-permute-start.10 = (bf16[3,2,6,128,128]{4,3,2,1,0:T(8,128)(2,1)}, bf16[3,2,6,128,128]{4,3,2,1,0:T(8,128)(2,1)}, u32[]{:S(2)}, u32[]{:S(2)}) collective-permute-start(bf16[3,2,6,128,128]{4,3,2,1,0:T(8,128)(2,1)} %pad_maximum_fusion.3), channel_id=1, source_target_pairs={{8,0},{16,8},{24,16},{9,1},{17,9},{25,17},{10,2},{18,10},{26,18},{... | collective-permute-start | bytes 3538952 | tf_op jit(solution)/shard_map/ppermute | solution.py:165
  59.5 1.2 %pad_maximum_fusion.2 = bf16[3,2,6,128,128]{4,3,2,1,0:T(8,128)(2,1)} fusion(bf16[1,2,6,128,128]{4,3,2,1,0:T(8,128)(2,1)S(1)} %get-tuple-element.31, bf16[1,2,6,128,128]{4,3,2,1,0:T(8,128)(2,1)S(1)} %get-tuple-element.29, bf16[1,2,6,128,128]{4,3,2,1,0:T(8,128)(2,1)S(1)} %get-tuple-element.27), kind=kLoop, calls=%fused_computation.2 | loop fusion | flops 1179648 | bytes 2359296 | tf_op jit(solution)/shard_map/stack | solution.py:179
  60.7 3.2 %collective-permute-start.9 = (bf16[3,2,6,128,128]{4,3,2,1,0:T(8,128)(2,1)}, bf16[3,2,6,128,128]{4,3,2,1,0:T(8,128)(2,1)}, u32[]{:S(2)}, u32[]{:S(2)}) collective-permute-start(bf16[3,2,6,128,128]{4,3,2,1,0:T(8,128)(2,1)} %pad_maximum_fusion.2), channel_id=1, source_target_pairs={{0,8},{8,16},{16,24},{1,9},{9,17},{17,25},{2,10},{10,18},{18,26},{... | collective-permute-start | bytes 3538952 | tf_op jit(solution)/shard_map/ppermute | solution.py:165
  64.1 12.2 %shard_map.84 = (bf16[2,6,128,128]{3,2,1,0:T(8,128)(2,1)S(1)}, bf16[2,6,128,128]{3,2,1,0:T(8,128)(2,1)S(1)}, f32[2,6,2,128]{3,2,1,0:T(2,128)S(1)}) custom-call(bf16[2,2,6,128,128]{4,3,2,1,0:T(8,128)(2,1)S(1)} %copy.100.pair.own, bf16[2,2,6,128,128]{4,3,2,1,0:T(8,128)(2,1)S(1)} %pad_maximum_fusion.5.own.pair, bf16[2,2,6,128,128]{4,3,2,1,0:T(8,128)(2,1)S(1)} %copy.101.before, ...), custom_call_target="tpu_custom_call" | custom-call | flops 1811939328 | bytes 4718592 | tf_op jit(solution)/shard_map/pallas_call | solution.py:127
  76.3 3.2 %collective-permute-start.11 = (f32[2,6,2,128]{3,2,1,0:T(2,128)S(1)}, f32[2,6,2,128]{3,2,1,0:T(2,128)S(1)}, u32[]{:S(2)}, u32[]{:S(2)}) collective-permute-start(f32[2,6,2,128]{3,2,1,0:T(2,128)S(1)} %get-tuple-element.11.own_st), channel_id=1, source_target_pairs={{0,2},{2,4},{4,6},{1,3},{3,5},{5,7},{8,10},{10,12},{12,14},{9,11},... | collective-permute-start | bytes 36872 | tf_op jit(solution)/shard_map/ppermute | solution.py:165
  79.5 2.1 %collective-permute-start.12 = (f32[2,6,2,128]{3,2,1,0:T(2,128)S(1)}, f32[2,6,2,128]{3,2,1,0:T(2,128)S(1)}, u32[]{:S(2)}, u32[]{:S(2)}) collective-permute-start(f32[2,6,2,128]{3,2,1,0:T(2,128)S(1)} %get-tuple-element.11.own_st), channel_id=1, source_target_pairs={{2,0},{4,2},{6,4},{3,1},{5,3},{7,5},{10,8},{12,10},{14,12},{11,9},... | collective-permute-start | bytes 36872 | tf_op jit(solution)/shard_map/ppermute | solution.py:165
  82.5 1.4 %collective-permute-done.12.after_st = f32[2,6,2,128]{3,2,1,0:T(2,128)S(1)} collective-permute-done((f32[2,6,2,128]{3,2,1,0:T(2,128)S(1)}, f32[2,6,2,128]{3,2,1,0:T(2,128)S(1)}, u32[]{:S(2)}, u32[]{:S(2)}) %collective-permute-start.12) | collective-permute-done | bytes 12320 | tf_op jit(solution)/shard_map/ppermute | solution.py:165
  83.9 3.7 %collective-permute-start.14 = (f32[3,6,2,128]{3,2,1,0:T(2,128)S(1)}, f32[3,6,2,128]{3,2,1,0:T(2,128)S(1)}, u32[]{:S(2)}, u32[]{:S(2)}) collective-permute-start(f32[3,6,2,128]{3,2,1,0:T(2,128)S(1)} %pad_maximum_fusion.9), channel_id=1, source_target_pairs={{8,0},{16,8},{24,16},{9,1},{17,9},{25,17},{10,2},{18,10},{26,18},{... | collective-permute-start | bytes 55304 | tf_op jit(solution)/shard_map/ppermute | solution.py:165
  87.7 3.1 %collective-permute-start.13 = (f32[3,6,2,128]{3,2,1,0:T(2,128)S(1)}, f32[3,6,2,128]{3,2,1,0:T(2,128)S(1)}, u32[]{:S(2)}, u32[]{:S(2)}) collective-permute-start(f32[3,6,2,128]{3,2,1,0:T(2,128)S(1)} %pad_maximum_fusion.8), channel_id=1, source_target_pairs={{0,8},{8,16},{16,24},{1,9},{9,17},{17,25},{2,10},{10,18},{18,26},{... | collective-permute-start | bytes 55304 | tf_op jit(solution)/shard_map/ppermute | solution.py:165
  91.0 1.2 %copy.140.before = bf16[2,2,6,128,128]{4,3,2,1,0:T(8,128)(2,1)S(1)} copy(bf16[2,2,6,128,128]{4,3,2,0,1:T(8,128)(2,1)} %collective-permute-done.7) | data formatting | bytes 1572864 | tf_op jit(solution)/shard_map/ppermute | solution.py:165
  92.2 1.2 %copy.141.after = bf16[2,2,6,128,128]{4,3,2,1,0:T(8,128)(2,1)S(1)} copy(bf16[2,2,6,128,128]{4,3,2,0,1:T(8,128)(2,1)} %collective-permute-done.8) | data formatting | bytes 1572864 | tf_op jit(solution)/shard_map/ppermute | solution.py:165
  93.5 7.4 %shard_map.85 = (bf16[2,6,128,128]{3,2,1,0:T(8,128)(2,1)S(1)}, bf16[2,6,128,128]{3,2,1,0:T(8,128)(2,1)S(1)}) custom-call(bf16[2,2,6,128,128]{4,3,2,1,0:T(8,128)(2,1)S(1)} %pad_maximum_fusion.5.own.pair, bf16[2,2,6,128,128]{4,3,2,1,0:T(8,128)(2,1)S(1)} %copy.100.pair.own, bf16[2,2,6,128,128]{4,3,2,1,0:T(8,128)(2,1)S(1)} %copy.140.before, ...), custom_call_target="tpu_custom_call" | custom-call | flops 1811939328 | bytes 4718592 | tf_op jit(solution)/shard_map/pallas_call | solution.py:150
  103.5 8.4 %collective-permute-done.15 = bf16[2,2,6,64,128]{4,3,2,1,0:T(8,128)(2,1)S(1)} collective-permute-done((bf16[2,2,6,64,128]{4,3,2,1,0:T(8,128)(2,1)S(1)}, bf16[2,2,6,64,128]{4,3,2,1,0:T(8,128)(2,1)S(1)}, u32[]{:S(2)}, u32[]{:S(2)}) %collective-permute-start.15) | collective-permute-done | bytes 393248 | tf_op jit(solution)/shard_map/ppermute | solution.py:170
  (165 shorter events, 17.4 us)
Async XLA Ops:
  2.0 1.4 %copy-start.5 = (bf16[2,8,8,12,128]{4,2,3,1,0:T(8,128)(2,1)S(1)}, bf16[2,8,8,12,128]{4,2,3,1,0:T(8,128)(2,1)}, u32[]{:S(2)}) copy-start(bf16[2,8,8,12,128]{4,2,3,1,0:T(8,128)(2,1)} %param.8) | copy-start | bytes 1179652
  2.0 1.4 %copy-start.6 = (bf16[2,8,8,12,128]{4,2,3,1,0:T(8,128)(2,1)S(1)}, bf16[2,8,8,12,128]{4,2,3,1,0:T(8,128)(2,1)}, u32[]{:S(2)}) copy-start(bf16[2,8,8,12,128]{4,2,3,1,0:T(8,128)(2,1)} %param.5) | copy-start | bytes 1179652
  2.1 10.9 %collective-permute-start.1 = (bf16[2,2,6,64,128]{4,3,2,1,0:T(8,128)(2,1)S(1)}, bf16[2,2,6,64,128]{4,3,2,1,0:T(8,128)(2,1)S(1)}, u32[]{:S(2)}, u32[]{:S(2)}) collective-permute-start(bf16[2,2,6,64,128]{4,3,2,1,0:T(8,128)(2,1)S(1)} %get-tuple-element.41), channel_id=1, source_target_pairs={{0,1},{1,0},{2,3},{3,2},{4,5},{5,4},{6,7},{7,6},{8,9},{9,8},{10,11... | collective-permute-start | bytes 1179656 | tf_op jit(solution)/shard_map/ppermute | solution.py:170
  3.6 1.1 copy-start.8
  3.7 16.9 %collective-permute-start = (bf16[2,2,6,64,128]{4,3,2,0,1:T(8,128)(2,1)S(1)}, bf16[2,2,6,64,128]{4,3,2,0,1:T(8,128)(2,1)S(1)}, u32[]{:S(2)}, u32[]{:S(2)}) collective-permute-start(bf16[2,2,6,64,128]{4,3,2,0,1:T(8,128)(2,1)S(1)} %get-tuple-element.43), channel_id=1, source_target_pairs={{0,1},{1,0},{2,3},{3,2},{4,5},{5,4},{6,7},{7,6},{8,9},{9,8},{10,11... | collective-permute-start | bytes 1179656 | tf_op jit(solution)/shard_map/ppermute | solution.py:170
  13.2 19.1 %collective-permute-start.2 = (bf16[2,2,6,128,128]{4,3,2,0,1:T(8,128)(2,1)S(1)}, bf16[2,2,6,128,128]{4,3,2,0,1:T(8,128)(2,1)S(1)}, u32[]{:S(2)}, u32[]{:S(2)}) collective-permute-start(bf16[2,2,6,128,128]{4,3,2,0,1:T(8,128)(2,1)S(1)} %copy.60), channel_id=1, source_target_pairs={{0,2},{2,4},{4,6},{1,3},{3,5},{5,7},{8,10},{10,12},{12,14},{9,11},... | collective-permute-start | bytes 2359304 | tf_op jit(solution)/shard_map/ppermute | solution.py:165
  16.4 18.8 %collective-permute-start.3 = (bf16[2,2,6,128,128]{4,3,2,0,1:T(8,128)(2,1)S(1)}, bf16[2,2,6,128,128]{4,3,2,0,1:T(8,128)(2,1)S(1)}, u32[]{:S(2)}, u32[]{:S(2)}) collective-permute-start(bf16[2,2,6,128,128]{4,3,2,0,1:T(8,128)(2,1)S(1)} %copy.60), channel_id=1, source_target_pairs={{2,0},{4,2},{6,4},{3,1},{5,3},{7,5},{10,8},{12,10},{14,12},{11,9},... | collective-permute-start | bytes 2359304 | tf_op jit(solution)/shard_map/ppermute | solution.py:165
  20.6 7.3 %copy-start.4 = (bf16[2,2,6,64,128]{4,3,2,0,1:T(8,128)(2,1)}, bf16[2,2,6,64,128]{4,3,2,0,1:T(8,128)(2,1)S(1)}, u32[]{:S(2)}) copy-start(bf16[2,2,6,64,128]{4,3,2,0,1:T(8,128)(2,1)S(1)} %collective-permute-done) | copy-start | bytes 1179652
  21.7 30.6 %collective-permute-start.7 = (bf16[2,2,6,128,128]{4,3,2,0,1:T(8,128)(2,1)}, bf16[2,2,6,128,128]{4,3,2,0,1:T(8,128)(2,1)}, u32[]{:S(2)}, u32[]{:S(2)}) collective-permute-start(bf16[2,2,6,128,128]{4,3,2,0,1:T(8,128)(2,1)} %pad_maximum_fusion.4), channel_id=1, source_target_pairs={{0,2},{2,4},{4,6},{1,3},{3,5},{5,7},{8,10},{10,12},{12,14},{9,11},... | collective-permute-start | bytes 2359304 | tf_op jit(solution)/shard_map/ppermute | solution.py:165
  24.9 28.6 %collective-permute-start.8 = (bf16[2,2,6,128,128]{4,3,2,0,1:T(8,128)(2,1)}, bf16[2,2,6,128,128]{4,3,2,0,1:T(8,128)(2,1)}, u32[]{:S(2)}, u32[]{:S(2)}) collective-permute-start(bf16[2,2,6,128,128]{4,3,2,0,1:T(8,128)(2,1)} %pad_maximum_fusion.4), channel_id=1, source_target_pairs={{2,0},{4,2},{6,4},{3,1},{5,3},{7,5},{10,8},{12,10},{14,12},{11,9},... | collective-permute-start | bytes 2359304 | tf_op jit(solution)/shard_map/ppermute | solution.py:165
  32.3 3.0 %copy-start = (bf16[2,2,6,128,128]{4,3,2,0,1:T(8,128)(2,1)}, bf16[2,2,6,128,128]{4,3,2,0,1:T(8,128)(2,1)S(1)}, u32[]{:S(2)}) copy-start(bf16[2,2,6,128,128]{4,3,2,0,1:T(8,128)(2,1)S(1)} %collective-permute-done.2) | copy-start | bytes 2359300
  35.3 0.9 copy-start.2
  37.3 26.8 %collective-permute-start.5 = (bf16[3,2,6,128,128]{4,3,2,1,0:T(8,128)(2,1)}, bf16[3,2,6,128,128]{4,3,2,1,0:T(8,128)(2,1)S(1)}, u32[]{:S(2)}, u32[]{:S(2)}) collective-permute-start(bf16[3,2,6,128,128]{4,3,2,1,0:T(8,128)(2,1)} %pad_maximum_fusion.1), channel_id=1, source_target_pairs={{8,0},{16,8},{24,16},{9,1},{17,9},{25,17},{10,2},{18,10},{26,18},{... | collective-permute-start | bytes 3538952 | tf_op jit(solution)/shard_map/ppermute | solution.py:165
  45.9 18.2 %collective-permute-start.4 = (bf16[3,2,6,128,128]{4,3,2,1,0:T(8,128)(2,1)}, bf16[3,2,6,128,128]{4,3,2,1,0:T(8,128)(2,1)}, u32[]{:S(2)}, u32[]{:S(2)}) collective-permute-start(bf16[3,2,6,128,128]{4,3,2,1,0:T(8,128)(2,1)} %pad_maximum_fusion), channel_id=1, source_target_pairs={{0,8},{8,16},{16,24},{1,9},{9,17},{17,25},{2,10},{10,18},{18,26},{... | collective-permute-start | bytes 3538952 | tf_op jit(solution)/shard_map/ppermute | solution.py:165
  55.8 37.6 %collective-permute-start.10 = (bf16[3,2,6,128,128]{4,3,2,1,0:T(8,128)(2,1)}, bf16[3,2,6,128,128]{4,3,2,1,0:T(8,128)(2,1)}, u32[]{:S(2)}, u32[]{:S(2)}) collective-permute-start(bf16[3,2,6,128,128]{4,3,2,1,0:T(8,128)(2,1)} %pad_maximum_fusion.3), channel_id=1, source_target_pairs={{8,0},{16,8},{24,16},{9,1},{17,9},{25,17},{10,2},{18,10},{26,18},{... | collective-permute-start | bytes 3538952 | tf_op jit(solution)/shard_map/ppermute | solution.py:165
  59.5 4.4 %copy-start.1 = (bf16[2,2,6,128,128]{4,3,2,0,1:T(8,128)(2,1)S(1)}, bf16[2,2,6,128,128]{4,3,2,0,1:T(8,128)(2,1)}, u32[]{:S(2)}) copy-start(bf16[2,2,6,128,128]{4,3,2,0,1:T(8,128)(2,1)} %copy-done) | copy-start | bytes 2359300
  60.7 3.3 %copy-start.3 = (bf16[2,2,6,128,128]{4,3,2,0,1:T(8,128)(2,1)S(1)}, bf16[2,2,6,128,128]{4,3,2,0,1:T(8,128)(2,1)}, u32[]{:S(2)}) copy-start(bf16[2,2,6,128,128]{4,3,2,0,1:T(8,128)(2,1)} %copy-done.2) | copy-start | bytes 2359300
  60.7 32.7 %collective-permute-start.9 = (bf16[3,2,6,128,128]{4,3,2,1,0:T(8,128)(2,1)}, bf16[3,2,6,128,128]{4,3,2,1,0:T(8,128)(2,1)}, u32[]{:S(2)}, u32[]{:S(2)}) collective-permute-start(bf16[3,2,6,128,128]{4,3,2,1,0:T(8,128)(2,1)} %pad_maximum_fusion.2), channel_id=1, source_target_pairs={{0,8},{8,16},{16,24},{1,9},{9,17},{17,25},{2,10},{10,18},{18,26},{... | collective-permute-start | bytes 3538952 | tf_op jit(solution)/shard_map/ppermute | solution.py:165
  76.3 6.3 %collective-permute-start.11 = (f32[2,6,2,128]{3,2,1,0:T(2,128)S(1)}, f32[2,6,2,128]{3,2,1,0:T(2,128)S(1)}, u32[]{:S(2)}, u32[]{:S(2)}) collective-permute-start(f32[2,6,2,128]{3,2,1,0:T(2,128)S(1)} %get-tuple-element.11.own_st), channel_id=1, source_target_pairs={{0,2},{2,4},{4,6},{1,3},{3,5},{5,7},{8,10},{10,12},{12,14},{9,11},... | collective-permute-start | bytes 36872 | tf_op jit(solution)/shard_map/ppermute | solution.py:165
  79.5 4.4 %collective-permute-start.12 = (f32[2,6,2,128]{3,2,1,0:T(2,128)S(1)}, f32[2,6,2,128]{3,2,1,0:T(2,128)S(1)}, u32[]{:S(2)}, u32[]{:S(2)}) collective-permute-start(f32[2,6,2,128]{3,2,1,0:T(2,128)S(1)} %get-tuple-element.11.own_st), channel_id=1, source_target_pairs={{2,0},{4,2},{6,4},{3,1},{5,3},{7,5},{10,8},{12,10},{14,12},{11,9},... | collective-permute-start | bytes 36872 | tf_op jit(solution)/shard_map/ppermute | solution.py:165
  81.6 9.2 %copy-start.7 = (f32[2,2,9,2]{3,2,1,0:T(8,128)S(1)}, f32[2,2,9,2]{3,2,1,0:T(8,128)}, u32[]{:S(2)}) copy-start(f32[2,2,9,2]{3,2,1,0:T(8,128)} %get-tuple-element.122) | copy-start | bytes 868
  81.9 19.9 %collective-permute-start.6 = (bf16[2,2,6,64,128]{4,3,2,1,0:T(8,128)(2,1)S(1)}, bf16[2,2,6,64,128]{4,3,2,1,0:T(8,128)(2,1)S(1)}, u32[]{:S(2)}, u32[]{:S(2)}) collective-permute-start(bf16[2,2,6,64,128]{4,3,2,1,0:T(8,128)(2,1)S(1)} %get-tuple-element.34), channel_id=1, source_target_pairs={{0,1},{1,0},{2,3},{3,2},{4,5},{5,4},{6,7},{7,6},{8,9},{9,8},{10,11... | collective-permute-start | bytes 1179656 | tf_op jit(solution)/shard_map/ppermute | solution.py:170
  83.9 9.5 %collective-permute-start.14 = (f32[3,6,2,128]{3,2,1,0:T(2,128)S(1)}, f32[3,6,2,128]{3,2,1,0:T(2,128)S(1)}, u32[]{:S(2)}, u32[]{:S(2)}) collective-permute-start(f32[3,6,2,128]{3,2,1,0:T(2,128)S(1)} %pad_maximum_fusion.9), channel_id=1, source_target_pairs={{8,0},{16,8},{24,16},{9,1},{17,9},{25,17},{10,2},{18,10},{26,18},{... | collective-permute-start | bytes 55304 | tf_op jit(solution)/shard_map/ppermute | solution.py:165
  87.7 5.8 %collective-permute-start.13 = (f32[3,6,2,128]{3,2,1,0:T(2,128)S(1)}, f32[3,6,2,128]{3,2,1,0:T(2,128)S(1)}, u32[]{:S(2)}, u32[]{:S(2)}) collective-permute-start(f32[3,6,2,128]{3,2,1,0:T(2,128)S(1)} %pad_maximum_fusion.8), channel_id=1, source_target_pairs={{0,8},{8,16},{16,24},{1,9},{9,17},{17,25},{2,10},{10,18},{18,26},{... | collective-permute-start | bytes 55304 | tf_op jit(solution)/shard_map/ppermute | solution.py:165
  101.1 10.8 %collective-permute-start.15 = (bf16[2,2,6,64,128]{4,3,2,1,0:T(8,128)(2,1)S(1)}, bf16[2,2,6,64,128]{4,3,2,1,0:T(8,128)(2,1)S(1)}, u32[]{:S(2)}, u32[]{:S(2)}) collective-permute-start(bf16[2,2,6,64,128]{4,3,2,1,0:T(8,128)(2,1)S(1)} %get-tuple-element.24), channel_id=1, source_target_pairs={{0,1},{1,0},{2,3},{3,2},{4,5},{5,4},{6,7},{7,6},{8,9},{9,8},{10,11... | collective-permute-start | bytes 1179656 | tf_op jit(solution)/shard_map/ppermute | solution.py:170

commit v2 on v1

v2 whole, which is shorter than its diff:
```python
import functools

import jax
import jax.numpy as jnp
import numpy as np
from jax import lax
from jax.experimental import pallas as pl
from jax.experimental.pallas import tpu as pltpu
from jax.sharding import PartitionSpec as P

TF = 1
TR = 8
TC = 8
MASKED = -1e30
LOG2E = 1.4426950408889634
NT = (((1,), (1,)), ((), ()))
NN = (((1,), (0,)), ((), ()))


def dot(left, right, dims):
    return lax.dot_general(left, right, dims, preferred_element_type=jnp.float32)


def flat(tiles):
    return tiles.reshape(tiles.shape[-4] * tiles.shape[-2], tiles.shape[-1])


def spread(bias, tokens):
    columns, width = bias.shape
    return jnp.broadcast_to(bias[None], (tokens // columns, columns, width)).reshape(tokens, width)


def fill_band(own, before, after, low, high, bands):
    frames = own.shape[0]
    tokens = own.shape[2] * own.shape[4]
    for at in range(frames + 2):
        for row, beside in enumerate((before, own, after)):
            place = pl.ds((3 * at + row) * tokens, tokens)
            for which, band in enumerate(bands):
                if at == 0:
                    band[place, :] = flat(low[row, which])
                elif at == frames + 1:
                    band[place, :] = flat(high[row, which])
                else:
                    band[place, :] = flat(beside[at - 1, which])


def front_kernel(scaling, pair, own, before, after, low, high, bias, grads, stats, key_all, value_all):
    frames, _, rows, _, columns, dim = pair.shape
    tokens = rows * columns
    fill_band(own, before, after, low, high, (key_all, value_all))
    windows = [pl.ds(3 * at * tokens, 9 * tokens) for at in range(frames)]
    scores = [
        dot(flat(pair[at, 0]), key_all[windows[at], :], NT) * (scaling * LOG2E) + spread(bias[at], tokens)
        for at in range(frames)
    ]
    grad_probs = [dot(flat(pair[at, 1]), value_all[windows[at], :], NT) for at in range(frames)]
    highest = [jnp.max(part, axis=1, keepdims=True) for part in scores]
    raised = [jnp.exp2(part - top) for part, top in zip(scores, highest)]
    total = [jnp.sum(part, axis=1, keepdims=True) for part in raised]
    weights = [part.astype(jnp.bfloat16) for part in raised]
    for at in range(frames):
        share = 1.0 / total[at]
        out = (dot(weights[at], value_all[windows[at], :], NN) * share).astype(jnp.bfloat16)
        grad = flat(pair[at, 1]).astype(jnp.float32)
        grad_dot = jnp.sum(grad * out.astype(jnp.float32), axis=1, keepdims=True)
        grad_scores = (weights[at].astype(jnp.float32) * (grad_probs[at] - grad_dot)).astype(jnp.bfloat16)
        query_grad = dot(grad_scores, key_all[windows[at], :], NN) * (share * scaling)
        grads[0, at, :, 0] = out.reshape(rows, columns, dim)
        grads[1, at, :, 0] = query_grad.astype(jnp.bfloat16).reshape(rows, columns, dim)
        lane = lax.broadcasted_iota(jnp.int32, (tokens, 128), 1)
        both = jnp.where(lane == 0, highest[at] + jnp.log2(total[at]), grad_dot)
        stats[at, 0] = jnp.transpose(both)[:2]


def back_kernel(
    scaling, pair, own, before, after, low, high, own_st, before_st, after_st, low_st, high_st, bias,
    grads, query_all, grad_all
):
    frames, _, rows, _, columns, dim = pair.shape
    tokens = rows * columns
    fill_band(own, before, after, low, high, (query_all, grad_all))

    def stat_row(at, row, which):
        if at == 0:
            return low_st[row, 0, which : which + 1]
        if at == frames + 1:
            return high_st[row, 0, which : which + 1]
        return (before_st, own_st, after_st)[row][at - 1, 0, which : which + 1]

    def stat_band(at, which):
        parts = [stat_row(at + step, row, which) for step in range(3) for row in range(3)]
        return jnp.concatenate(parts, axis=1)

    windows = [pl.ds(3 * at * tokens, 9 * tokens) for at in range(frames)]
    scores = [dot(flat(pair[at, 0]), query_all[windows[at], :], NT) for at in range(frames)]
    grad_probs = [dot(flat(pair[at, 1]), grad_all[windows[at], :], NT) for at in range(frames)]
    for at in range(frames):
        shift = spread(bias[at] - stat_band(at, 0), tokens)
        weights = jnp.exp2(scores[at] * (scaling * LOG2E) + shift).astype(jnp.bfloat16)
        grad_scores = weights.astype(jnp.float32) * (grad_probs[at] - stat_band(at, 1))
        key_grad = dot(grad_scores.astype(jnp.bfloat16), query_all[windows[at], :], NN) * scaling
        value_grad = dot(weights, grad_all[windows[at], :], NN)
        grads[0, at, :, 0] = key_grad.astype(jnp.bfloat16).reshape(rows, columns, dim)
        grads[1, at, :, 0] = value_grad.astype(jnp.bfloat16).reshape(rows, columns, dim)


def slab_spec(shape, first):
    lead, pairs, rows, _, columns, dim = shape
    return pl.BlockSpec((lead, pairs, rows, 1, columns, dim), lambda head: (0, 0, 0, head + first, 0, 0))


def stat_spec(shape, first):
    lead, _, pairs, tokens = shape
    return pl.BlockSpec((lead, 1, pairs, tokens), lambda head: (0, head + first, 0, 0))


def whole_spec(shape):
    return pl.BlockSpec(shape, lambda head: (0,) * len(shape))


def run(kernel, scaling, pair, halo, stats, bias, first, count):
    frames, _, rows, _, columns, dim = pair.shape
    tokens = rows * columns
    grads = jax.ShapeDtypeStruct((2, frames, rows, count, columns, dim), jnp.bfloat16)
    outs = [grads]
    out_specs = [slab_spec(grads.shape, 0)]
    if stats is None:
        outs.append(jax.ShapeDtypeStruct((frames, count, 2, tokens), jnp.float32))
        out_specs.append(stat_spec(outs[-1].shape, 0))
    stats = () if stats is None else stats
    return pl.pallas_call(
        functools.partial(kernel, scaling),
        grid=(count,),
        out_shape=tuple(outs),
        in_specs=[slab_spec(part.shape, first) for part in (pair,) + halo]
        + [stat_spec(part.shape, first) for part in stats]
        + [whole_spec(bias.shape)],
        out_specs=tuple(out_specs),
        scratch_shapes=[pltpu.VMEM((3 * (frames + 2) * tokens, dim), jnp.bfloat16)] * 2,
        compiler_params=pltpu.CompilerParams(vmem_limit_bytes=32 * 2**20),
        cost_estimate=pl.CostEstimate(
            flops=frames * count * 8 * tokens * 9 * tokens * dim,
            bytes_accessed=count * (frames + 2) * 3 * 2 * tokens * dim * 2,
            transcendentals=frames * count * tokens * 9 * tokens,
        ),
    )(pair, *halo, *stats, bias)


def step_along(tensor, axis, sign):
    size = lax.axis_size(axis)
    return lax.ppermute(tensor, axis, [(i, i + sign) for i in range(size) if 0 <= i + sign < size])


def turn(tensor, shift):
    size = lax.axis_size("head")
    return lax.ppermute(tensor, "head", [(i, (i + shift) % size) for i in range(size)])


def frame_edges(before, own, after):
    last = own.shape[0] - 1
    low = step_along(jnp.stack([before[last], own[last], after[last]]), "frame", 1)
    high = step_along(jnp.stack([before[0], own[0], after[0]]), "frame", -1)
    return low, high


def row_sides(own):
    return step_along(own, "row", 1), step_along(own, "row", -1)


def tile_biases(active, frames, rows, columns_here):
    size = lax.axis_size("head")
    me = lax.axis_index("head")
    frame_at = lax.axis_index("frame") * frames
    row_at = lax.axis_index("row")
    all_frames, all_rows, count, slots = active.shape
    padded = jnp.pad(active.astype(jnp.float32), ((1, 1), (1, 1), (0, 0), (0, 0)))
    near = lax.dynamic_slice(padded, (frame_at, row_at, 0, 0), (frames + 2, 3, count, slots))
    near = near.reshape(frames + 2, 3, count, 9, 3)
    steps = jnp.arange(3, dtype=jnp.int32) - 1
    frame_ids = frame_at + jnp.arange(frames, dtype=jnp.int32)[:, None] + steps
    frame_in = (frame_ids >= 0) & (frame_ids < all_frames)
    row_in = (row_at + steps >= 0) & (row_at + steps < all_rows)
    inside = (frame_in[:, :, None] & row_in).reshape(frames, 9).astype(jnp.float32)
    ahead = near[1 : 1 + frames, 1] * inside[:, None, :, None]
    pick = np.zeros((frames + 2, 3, 9, frames, 9), np.float32)
    for at in range(frames):
        for offset in range(9):
            pick[at + offset // 3, offset % 3, 8 - offset, at, offset] = 1.0
    behind = jnp.einsum("xyioc,xyofq->fiqc", near, pick)
    place = jnp.arange(size * columns_here, dtype=jnp.int32)
    tile = ((me + place // columns_here) % size * columns_here + place % columns_here) // TC
    biases = []
    for table, sign in ((ahead, 1), (behind, -1)):
        owner = tile[None] == jnp.arange(count, dtype=jnp.int32)[:, None]
        shift = (sign * (tile[None, :] - tile[:, None]))[None] == steps[:, None, None]
        chosen = (owner[:, None, :, None] & shift[None]).astype(jnp.float32)
        allowed = jnp.einsum("fioc,icpk->fpok", table, chosen)
        bias = jnp.where(allowed > 0.5, 0.0, MASKED)[:, :, :, None, :]
        bias = jnp.broadcast_to(bias, bias.shape[:3] + (rows,) + bias.shape[4:])
        biases.append(bias.reshape(frames, place.shape[0], -1))
    return biases


def on_device(queries, keys, values, out_grad, active):
    frames, rows, columns_here, heads, dim = queries.shape
    size = lax.axis_size("head")
    me = lax.axis_index("head")
    groups = heads // size
    scaling = dim ** (-0.5)

    def group_of(tensors, shift):
        start = (me + shift) % size * groups
        parts = [
            lax.dynamic_slice_in_dim(jnp.transpose(t, (0, 1, 3, 2, 4)), start, groups, 2) for t in tensors
        ]
        return jnp.stack(parts, 1)

    def send_columns(tensors):
        return [group_of(tensors, size - b) for b in range(1, size)]

    def from_heads(grads):
        whole = jnp.zeros((2, frames, rows, heads, columns_here, dim), jnp.bfloat16)
        for b in range(size):
            piece = lax.slice_in_dim(grads, b * columns_here, (b + 1) * columns_here, axis=4)
            piece = piece if b == 0 else turn(piece, b)
            whole = lax.dynamic_update_slice_in_dim(whole, piece, (me + size - b) % size * groups, 3)
        whole = jnp.transpose(whole, (0, 1, 2, 4, 3, 5))
        return whole[0], whole[1]

    front_bias, back_bias = tile_biases(active, frames, rows, columns_here)
    own_kv = group_of((keys, values), 0)
    moved_kv = [turn(part, size - 1 - at) for at, part in enumerate(send_columns((keys, values)))]
    sent_qg = send_columns((queries, out_grad))
    sent_qg, moved_kv = lax.optimization_barrier((sent_qg, moved_kv))
    kv = jnp.concatenate([own_kv] + moved_kv, axis=4)
    kv_before, kv_after = row_sides(kv)
    moved_qg = [turn(part, size - 1 - at) for at, part in enumerate(sent_qg)]
    qg = jnp.concatenate([group_of((queries, out_grad), 0)] + moved_qg, axis=4)
    qg, kv_before, kv_after = lax.optimization_barrier((qg, kv_before, kv_after))
    kv_low, kv_high = frame_edges(kv_before, kv, kv_after)
    qg_before, qg_after = row_sides(qg)
    key_halo = (kv, kv_before, kv_after, kv_low, kv_high)
    front_grads, stats = run(front_kernel, scaling, qg, key_halo, None, front_bias, 0, groups)
    st_before, st_after = row_sides(stats)
    qg_low, qg_high = frame_edges(qg_before, qg, qg_after)
    st_low, st_high = frame_edges(st_before, stats, st_after)
    query_halo = (qg, qg_before, qg_after, qg_low, qg_high)
    stat_halo = (stats, st_before, st_after, st_low, st_high)
    (back_grads,) = run(back_kernel, scaling, kv, query_halo, stat_halo, back_bias, 0, groups)
    return from_heads(front_grads) + from_heads(back_grads)


def solution(mesh):
    spec = P("frame", "row", "head", None, None)
    return jax.shard_map(
        on_device, mesh=mesh, in_specs=(spec,) * 4 + (P(),), out_specs=(spec,) * 4, check_vma=False
    )
```

time: 116 us -> 113 us (0.974)
  waiting for transfers between devices: 19 us -> 29.3 us
  Pallas kernels: 19.5 us -> 15.3 us
  other arithmetic: 8.6 us -> 4.43 us
  starting transfers between devices: 44.5 us -> 40.4 us
  local copies, waits for them, and re-layouts: 20.6 us -> 18 us
  matrix products: 0 us -> 2.44 us
    ppermute x4, waiting for transfers between devices: 10.4 us -> 17.4 us  [turn(): lax.ppermute(tensor, 'head', [(i, (i + shift) % size) for i in range(size)])]
    another operation x52 -> x4, local copies, waits for them, and re-layouts: 8.46 us -> 2.38 us  [the longest x2 2.15 us: group_of(): return jnp.stack(parts, 1)]
    ppermute x12, starting transfers between devices: 40.9 us -> 35.3 us  [step_along(): lax.ppermute(tensor, axis, [(i, i + sign) for i in range(size) if 0 <= i...]
    pallas_call x2, Pallas kernels: 19.5 us -> 15.3 us  [run(): pl.pallas_call(functools.partial(kernel, scaling), grid=(count,), out_sha...]
    another operation x17 -> x8, other arithmetic: 6.21 us -> 2.64 us  [the longest x3 1.29 us: frame_edges(): jnp.stack([before[last], own[last], after[last]])]
    mul x36 -> x0, local copies, waits for them, and re-layouts: 3.32 us -> none  [layers(): ahead.append(chosen * inside[frame_step:frame_step + frames, row_step])]
    ppermute x12, waiting for transfers between devices: 8.67 us -> 12 us  [step_along(): lax.ppermute(tensor, axis, [(i, i + sign) for i in range(size) if 0 <= i...]
    reshape x2 -> x3, local copies, waits for them, and re-layouts: 0.21 us -> 3.49 us  [the longest x2 3.23 us: tile_biases(): biases.append(bias.reshape(frames, place.shape[0], -1))]
  transfers between devices with their start and end apart: 16 -> 16, of which waited for: 5 -> 8; matrix products, arithmetic and copies ran while one was open for 22% -> 18% of each run, Pallas kernels for 17% -> 14%
where the time goes in v2:
time: 113 us; the launch traced here: 111 us
  starting transfers between devices  40.4 us (36%)
  waiting for transfers between devices  29.3 us (26%)
  local copies, waits for them, and re-layouts  18 us (16%)
  Pallas kernels  15.3 us (14%)
  other arithmetic  4.43 us (4%)
  matrix products  2.44 us (2%)
    ppermute x12, starting transfers between devices, step_along(): lax.ppermute(tensor, axis, [(i, i + sign) for i in range(size) if 0 <= i...  35.3 us
    ppermute x4, waiting for transfers between devices, turn(): lax.ppermute(tensor, 'head', [(i, (i + shift) % size) for i in range(size)])  17.4 us
    pallas_call x2, Pallas kernels, run(): pl.pallas_call(functools.partial(kernel, scaling), grid=(count,), out_sha...  15.3 us
    ppermute x12, waiting for transfers between devices, step_along(): lax.ppermute(tensor, axis, [(i, i + sign) for i in range(size) if 0 <= i...  12 us
    ppermute x4, starting transfers between devices, turn(): lax.ppermute(tensor, 'head', [(i, (i + shift) % size) for i in range(size)])  5.06 us
    reshape x2, local copies, waits for them, and re-layouts, tile_biases(): biases.append(bias.reshape(frames, place.shape[0], -1))  3.23 us
    broadcast_in_dim x2, local copies, waits for them, and re-layouts, tile_biases(): bias = jnp.broadcast_to(bias, bias.shape[:3] + (rows,) + bias.shape[4:])  3.21 us
    dot_general x2, matrix products, tile_biases(): allowed = jnp.einsum('fioc,icpk->fpok', table, chosen)  2.44 us
  transfers between devices with their start and end apart: 16, of which 8 were waited for; matrix products, arithmetic and copies ran while one was open for 18% of the time, Pallas kernels for 14%

profile of v2, /device:TPU:9, one launch (start us, length us, event | category | flops | bytes accessed | tf_op | source)
XLA Modules:
  0.0 111.0 jit_solution(14360401499165397524)
XLA Ops:
  0.7 1.3 %dynamic-slice_bitcast_fusion = (bf16[2,1,8,6,8,128]{5,4,3,2,1,0:T(8,128)(2,1)S(1)}, bf16[2,1,8,6,8,128]{5,4,3,2,1,0:T(8,128)(2,1)S(1)}, bf16[2,1,8,6,8,128]{5,4...) fusion(bf16[2,8,8,12,128]{4,2,3,1,0:T(8,128)(2,1)} %param.8, s32[]{:T(128)S(6)} %select_n.113, s32[]{:T(128)S(6)} %select_n.115, ...), kind=kLoop, calls=%fused_computation.23 | loop fusion | bytes 1572872 | tf_op jit(solution)/shard_map/stack | solution.py:217
  2.1 1.3 %collective-permute-start = (bf16[2,2,8,6,8,128]{5,4,3,2,1,0:T(8,128)(2,1)S(1)}, bf16[2,2,8,6,8,128]{5,4,3,2,1,0:T(8,128)(2,1)S(1)}, u32[]{:S(2)}, u32[]{:S(2)}) collective-permute-start(bf16[2,2,8,6,8,128]{5,4,3,2,1,0:T(8,128)(2,1)S(1)} %pad_maximum_fusion.7), channel_id=1, source_target_pairs={{0,1},{1,0},{2,3},{3,2},{4,5},{5,4},{6,7},{7,6},{8,9},{9,8},{10,11... | collective-permute-start | bytes 1179656 | tf_op jit(solution)/shard_map/ppermute | solution.py:157
  5.2 6.9 %collective-permute-done = bf16[2,2,8,6,8,128]{5,4,3,2,1,0:T(8,128)(2,1)S(1)} collective-permute-done((bf16[2,2,8,6,8,128]{5,4,3,2,1,0:T(8,128)(2,1)S(1)}, bf16[2,2,8,6,8,128]{5,4,3,2,1,0:T(8,128)(2,1)S(1)}, u32[]{:S(2)}, u32[]{:S(2)}) %collective-permute-start) | collective-permute-done | bytes 393248 | tf_op jit(solution)/shard_map/ppermute | solution.py:157
  12.3 3.2 %collective-permute-start.2 = (bf16[2,2,8,6,16,128]{5,4,3,2,1,0:T(8,128)(2,1)S(1)}, bf16[2,2,8,6,16,128]{5,4,3,2,1,0:T(8,128)(2,1)S(1)}, u32[]{:S(2)}, u32[]{:S(2)}) collective-permute-start(bf16[2,2,8,6,16,128]{5,4,3,2,1,0:T(8,128)(2,1)S(1)} %pad_maximum_fusion.5.own.pair), channel_id=1, source_target_pairs={{0,2},{2,4},{4,6},{1,3},{3,5},{5,7},{8,10},{10,12},{12,14},{9,11},... | collective-permute-start | bytes 2359304 | tf_op jit(solution)/shard_map/ppermute | solution.py:152
  15.5 2.1 %collective-permute-start.3 = (bf16[2,2,8,6,16,128]{5,4,3,2,1,0:T(8,128)(2,1)S(1)}, bf16[2,2,8,6,16,128]{5,4,3,2,1,0:T(8,128)(2,1)S(1)}, u32[]{:S(2)}, u32[]{:S(2)}) collective-permute-start(bf16[2,2,8,6,16,128]{5,4,3,2,1,0:T(8,128)(2,1)S(1)} %pad_maximum_fusion.5.own.pair), channel_id=1, source_target_pairs={{2,0},{4,2},{6,4},{3,1},{5,3},{7,5},{10,8},{12,10},{14,12},{11,9},... | collective-permute-start | bytes 2359304 | tf_op jit(solution)/shard_map/ppermute | solution.py:152
  20.6 1.6 %reshape.265.bias = f32[2,16,1152]{2,1,0:T(8,128)S(1)} reshape(f32[2,16,9,8,16]{4,3,2,1,0:T(8,128)} %broadcast_in_dim.14) | data formatting | bytes 294912 | tf_op jit(solution)/shard_map/reshape | solution.py:201
  22.7 3.6 %collective-permute-done.1 = bf16[2,2,8,6,8,128]{5,4,3,2,1,0:T(8,128)(2,1)} collective-permute-done((bf16[2,2,8,6,8,128]{5,4,3,2,1,0:T(8,128)(2,1)S(1)}, bf16[2,2,8,6,8,128]{5,4,3,2,1,0:T(8,128)(2,1)}, u32[]{:S(2)}, u32[]{:S(2)}) %collective-permute-start.1) | collective-permute-done | bytes 393248 | tf_op jit(solution)/shard_map/ppermute | solution.py:157
  26.3 1.3 %pad_maximum_fusion.4.pair.own = bf16[2,2,8,6,16,128]{5,4,3,2,1,0:T(8,128)(2,1)S(1)} fusion(bf16[2,2,8,6,8,128]{5,4,3,2,1,0:T(8,128)(2,1)} %collective-permute-done.1, bf16[2,1,8,6,8,128]{5,4,3,2,1,0:T(8,128)(2,1)} %get-tuple-element.44, bf16[2,1,8,6,8,128]{5,4,3,2,1,0:T(8,128)(2,1)} %get-tuple-element.59), kind=kLoop, calls=%fused_computation.13 | loop fusion | flops 2359296 | bytes 1572864 | tf_op jit(solution)/shard_map/concatenate | solution.py:239
  27.6 4.1 %collective-permute-done.2.before = bf16[2,2,8,6,16,128]{5,4,3,2,1,0:T(8,128)(2,1)S(1)} collective-permute-done((bf16[2,2,8,6,16,128]{5,4,3,2,1,0:T(8,128)(2,1)S(1)}, bf16[2,2,8,6,16,128]{5,4,3,2,1,0:T(8,128)(2,1)S(1)}, u32[]{:S(2)}, u32[]{:S(2)}) %collective-permute-start.2) | collective-permute-done | bytes 786464 | tf_op jit(solution)/shard_map/ppermute | solution.py:152
  32.6 2.0 %collective-permute-done.3.after = bf16[2,2,8,6,16,128]{5,4,3,2,1,0:T(8,128)(2,1)S(1)} collective-permute-done((bf16[2,2,8,6,16,128]{5,4,3,2,1,0:T(8,128)(2,1)S(1)}, bf16[2,2,8,6,16,128]{5,4,3,2,1,0:T(8,128)(2,1)S(1)}, u32[]{:S(2)}, u32[]{:S(2)}) %collective-permute-start.3) | collective-permute-done | bytes 786464 | tf_op jit(solution)/shard_map/ppermute | solution.py:152
  35.5 3.3 %collective-permute-start.7 = (bf16[2,2,8,6,16,128]{5,4,3,2,1,0:T(8,128)(2,1)S(1)}, bf16[2,2,8,6,16,128]{5,4,3,2,1,0:T(8,128)(2,1)S(1)}, u32[]{:S(2)}, u32[]{:S(2)}) collective-permute-start(bf16[2,2,8,6,16,128]{5,4,3,2,1,0:T(8,128)(2,1)S(1)} %pad_maximum_fusion.4.pair.own), channel_id=1, source_target_pairs={{0,2},{2,4},{4,6},{1,3},{3,5},{5,7},{8,10},{10,12},{12,14},{9,11},... | collective-permute-start | bytes 2359304 | tf_op jit(solution)/shard_map/ppermute | solution.py:152
  38.8 2.1 %collective-permute-start.8 = (bf16[2,2,8,6,16,128]{5,4,3,2,1,0:T(8,128)(2,1)S(1)}, bf16[2,2,8,6,16,128]{5,4,3,2,1,0:T(8,128)(2,1)S(1)}, u32[]{:S(2)}, u32[]{:S(2)}) collective-permute-start(bf16[2,2,8,6,16,128]{5,4,3,2,1,0:T(8,128)(2,1)S(1)} %pad_maximum_fusion.4.pair.own), channel_id=1, source_target_pairs={{2,0},{4,2},{6,4},{3,1},{5,3},{7,5},{10,8},{12,10},{14,12},{11,9},... | collective-permute-start | bytes 2359304 | tf_op jit(solution)/shard_map/ppermute | solution.py:152
  43.5 6.3 %collective-permute-start.4 = (bf16[3,2,8,6,16,128]{5,4,3,2,1,0:T(8,128)(2,1)}, bf16[3,2,8,6,16,128]{5,4,3,2,1,0:T(8,128)(2,1)}, u32[]{:S(2)}, u32[]{:S(2)}) collective-permute-start(bf16[3,2,8,6,16,128]{5,4,3,2,1,0:T(8,128)(2,1)} %pad_maximum_fusion), channel_id=1, source_target_pairs={{0,8},{8,16},{16,24},{1,9},{9,17},{17,25},{2,10},{10,18},{18,26},{... | collective-permute-start | bytes 3538952 | tf_op jit(solution)/shard_map/ppermute | solution.py:152
  51.0 1.9 %collective-permute-start.5 = (bf16[3,2,8,6,16,128]{5,4,3,2,1,0:T(8,128)(2,1)}, bf16[3,2,8,6,16,128]{5,4,3,2,1,0:T(8,128)(2,1)}, u32[]{:S(2)}, u32[]{:S(2)}) collective-permute-start(bf16[3,2,8,6,16,128]{5,4,3,2,1,0:T(8,128)(2,1)} %pad_maximum_fusion.1), channel_id=1, source_target_pairs={{8,0},{16,8},{24,16},{9,1},{17,9},{25,17},{10,2},{18,10},{26,18},{... | collective-permute-start | bytes 3538952 | tf_op jit(solution)/shard_map/ppermute | solution.py:152
  52.9 2.1 %fusion.5 = f32[2,16,9,16]{2,3,0,1:T(8,128)} fusion(bf16[4,3,2,9,3,1]{3,4,1,0,2,5:T(4,128)(2,1)S(1)} %copy.20, bf16[4,3,9,2,9,1]{4,2,1,0,5,3:T(8,128)(2,1)} %constant.182, pred[3,16,16]{2,0,1:T(4,128)(4,1)S(1)} %get-tuple-element.52, pred[2,16]{0,1:T(8,128)(4,1)S(1)} %iota_compare_fusion), kind=kOutput, calls=%fused_computation.11 | convolution fusion | flops 89376 | bytes 24416 | tf_op jit(solution)/shard_map/fioc,icpk->fpok/dot_general | solution.py:198
  55.0 1.9 %copy.17 = f32[2,16,9,16]{3,2,1,0:T(8,128)} copy(f32[2,16,9,16]{2,3,0,1:T(8,128)} %fusion.5) | data formatting | bytes 36864 | tf_op jit(solution)/shard_map/jit(_where)/select_n | solution.py:199
  56.9 2.1 %broadcast_in_dim.17 = f32[2,16,9,8,16]{4,3,2,1,0:T(8,128)} broadcast(f32[2,16,9,16]{3,2,1,0:T(8,128)} %copy.17), dimensions={0,1,2,4} | broadcast | bytes 165888 | tf_op jit(solution)/shard_map/broadcast_in_dim | solution.py:200
  59.0 1.6 %reshape.266.bias = f32[2,16,1152]{2,1,0:T(8,128)S(1)} reshape(f32[2,16,9,8,16]{4,3,2,1,0:T(8,128)} %broadcast_in_dim.17) | data formatting | bytes 294912 | tf_op jit(solution)/shard_map/reshape | solution.py:201
  61.2 3.6 %collective-permute-start.9 = (bf16[3,2,8,6,16,128]{5,4,3,2,1,0:T(8,128)(2,1)S(1)}, bf16[3,2,8,6,16,128]{5,4,3,2,1,0:T(8,128)(2,1)S(1)}, u32[]{:S(2)}, u32[]{:S(2)}) collective-permute-start(bf16[3,2,8,6,16,128]{5,4,3,2,1,0:T(8,128)(2,1)S(1)} %pad_maximum_fusion.2), channel_id=1, source_target_pairs={{0,8},{8,16},{16,24},{1,9},{9,17},{17,25},{2,10},{10,18},{18,26},{... | collective-permute-start | bytes 3538952 | tf_op jit(solution)/shard_map/ppermute | solution.py:152
  65.1 2.1 %collective-permute-start.10 = (bf16[3,2,8,6,16,128]{5,4,3,2,1,0:T(8,128)(2,1)S(1)}, bf16[3,2,8,6,16,128]{5,4,3,2,1,0:T(8,128)(2,1)S(1)}, u32[]{:S(2)}, u32[]{:S(2)}) collective-permute-start(bf16[3,2,8,6,16,128]{5,4,3,2,1,0:T(8,128)(2,1)S(1)} %pad_maximum_fusion.3), channel_id=1, source_target_pairs={{8,0},{16,8},{24,16},{9,1},{17,9},{25,17},{10,2},{18,10},{26,18},{... | collective-permute-start | bytes 3538952 | tf_op jit(solution)/shard_map/ppermute | solution.py:152
  67.1 1.7 %collective-permute-done.5.high = bf16[3,2,8,6,16,128]{5,4,3,2,1,0:T(8,128)(2,1)} collective-permute-done((bf16[3,2,8,6,16,128]{5,4,3,2,1,0:T(8,128)(2,1)}, bf16[3,2,8,6,16,128]{5,4,3,2,1,0:T(8,128)(2,1)}, u32[]{:S(2)}, u32[]{:S(2)}) %collective-permute-start.5) | collective-permute-done | bytes 1179680 | tf_op jit(solution)/shard_map/ppermute | solution.py:152
  68.8 9.6 %shard_map.93 = (bf16[2,2,8,6,16,128]{5,4,3,2,1,0:T(8,128)(2,1)S(1)}, f32[2,6,2,128]{3,2,1,0:T(2,128)S(1)}) custom-call(bf16[2,2,8,6,16,128]{5,4,3,2,1,0:T(8,128)(2,1)S(1)} %pad_maximum_fusion.4.pair.own, bf16[2,2,8,6,16,128]{5,4,3,2,1,0:T(8,128)(2,1)S(1)} %pad_maximum_fusion.5.own.pair, bf16[2,2,8,6,16,128]{5,4,3,2,1,0:T(8,128)(2,1)S(1)} %copy-done.2, ...), custom_call_target="tpu_custom_call" | custom-call | flops 1811939328 | bytes 4718592 | tf_op jit(solution)/shard_map/pallas_call | solution.py:132
  78.4 3.2 %collective-permute-start.11 = (f32[2,6,2,128]{3,2,1,0:T(2,128)S(1)}, f32[2,6,2,128]{3,2,1,0:T(2,128)S(1)}, u32[]{:S(2)}, u32[]{:S(2)}) collective-permute-start(f32[2,6,2,128]{3,2,1,0:T(2,128)S(1)} %get-tuple-element.17.own_st), channel_id=1, source_target_pairs={{0,2},{2,4},{4,6},{1,3},{3,5},{5,7},{8,10},{10,12},{12,14},{9,11},... | collective-permute-start | bytes 36872 | tf_op jit(solution)/shard_map/ppermute | solution.py:152
  81.6 2.1 %collective-permute-start.12 = (f32[2,6,2,128]{3,2,1,0:T(2,128)S(1)}, f32[2,6,2,128]{3,2,1,0:T(2,128)S(1)}, u32[]{:S(2)}, u32[]{:S(2)}) collective-permute-start(f32[2,6,2,128]{3,2,1,0:T(2,128)S(1)} %get-tuple-element.17.own_st), channel_id=1, source_target_pairs={{2,0},{4,2},{6,4},{3,1},{5,3},{7,5},{10,8},{12,10},{14,12},{11,9},... | collective-permute-start | bytes 36872 | tf_op jit(solution)/shard_map/ppermute | solution.py:152
  83.7 2.3 %collective-permute-done.12.after_st = f32[2,6,2,128]{3,2,1,0:T(2,128)S(1)} collective-permute-done((f32[2,6,2,128]{3,2,1,0:T(2,128)S(1)}, f32[2,6,2,128]{3,2,1,0:T(2,128)S(1)}, u32[]{:S(2)}, u32[]{:S(2)}) %collective-permute-start.12) | collective-permute-done | bytes 12320 | tf_op jit(solution)/shard_map/ppermute | solution.py:152
  86.0 3.4 %collective-permute-start.13 = (f32[3,6,2,128]{3,2,1,0:T(2,128)S(1)}, f32[3,6,2,128]{3,2,1,0:T(2,128)S(1)}, u32[]{:S(2)}, u32[]{:S(2)}) collective-permute-start(f32[3,6,2,128]{3,2,1,0:T(2,128)S(1)} %pad_maximum_fusion.8), channel_id=1, source_target_pairs={{0,8},{8,16},{16,24},{1,9},{9,17},{17,25},{2,10},{10,18},{18,26},{... | collective-permute-start | bytes 55304 | tf_op jit(solution)/shard_map/ppermute | solution.py:152
  89.5 1.9 %collective-permute-start.14 = (f32[3,6,2,128]{3,2,1,0:T(2,128)S(1)}, f32[3,6,2,128]{3,2,1,0:T(2,128)S(1)}, u32[]{:S(2)}, u32[]{:S(2)}) collective-permute-start(f32[3,6,2,128]{3,2,1,0:T(2,128)S(1)} %pad_maximum_fusion.9), channel_id=1, source_target_pairs={{8,0},{16,8},{24,16},{9,1},{17,9},{25,17},{10,2},{18,10},{26,18},{... | collective-permute-start | bytes 55304 | tf_op jit(solution)/shard_map/ppermute | solution.py:152
  91.7 1.3 %collective-permute-start.6 = (bf16[2,2,8,6,8,128]{5,4,3,2,1,0:T(8,128)(2,1)S(1)}, bf16[2,2,8,6,8,128]{5,4,3,2,1,0:T(8,128)(2,1)S(1)}, u32[]{:S(2)}, u32[]{:S(2)}) collective-permute-start(bf16[2,2,8,6,8,128]{5,4,3,2,1,0:T(8,128)(2,1)S(1)} %get-tuple-element.30), channel_id=1, source_target_pairs={{0,1},{1,0},{2,3},{3,2},{4,5},{5,4},{6,7},{7,6},{8,9},{9,8},{10,11... | collective-permute-start | bytes 1179656 | tf_op jit(solution)/shard_map/ppermute | solution.py:157
  93.0 1.9 %collective-permute-done.14.high_st = f32[3,6,2,128]{3,2,1,0:T(2,128)S(1)} collective-permute-done((f32[3,6,2,128]{3,2,1,0:T(2,128)S(1)}, f32[3,6,2,128]{3,2,1,0:T(2,128)S(1)}, u32[]{:S(2)}, u32[]{:S(2)}) %collective-permute-start.14) | collective-permute-done | bytes 18464 | tf_op jit(solution)/shard_map/ppermute | solution.py:152
  94.9 5.7 %shard_map.94 = bf16[2,2,8,6,16,128]{5,4,3,2,1,0:T(8,128)(2,1)S(1)} custom-call(bf16[2,2,8,6,16,128]{5,4,3,2,1,0:T(8,128)(2,1)S(1)} %pad_maximum_fusion.5.own.pair, bf16[2,2,8,6,16,128]{5,4,3,2,1,0:T(8,128)(2,1)S(1)} %pad_maximum_fusion.4.pair.own, bf16[2,2,8,6,16,128]{5,4,3,2,1,0:T(8,128)(2,1)S(1)} %collective-permute-done.7.before, ...), custom_call_target="tpu_custom_call" | custom-call | flops 1811939328 | bytes 4718592 | tf_op jit(solution)/shard_map/pallas_call | solution.py:132
  100.9 1.3 %collective-permute-start.15 = (bf16[2,2,8,6,8,128]{5,4,3,2,1,0:T(8,128)(2,1)S(1)}, bf16[2,2,8,6,8,128]{5,4,3,2,1,0:T(8,128)(2,1)S(1)}, u32[]{:S(2)}, u32[]{:S(2)}) collective-permute-start(bf16[2,2,8,6,8,128]{5,4,3,2,1,0:T(8,128)(2,1)S(1)} %get-tuple-element.20), channel_id=1, source_target_pairs={{0,1},{1,0},{2,3},{3,2},{4,5},{5,4},{6,7},{7,6},{8,9},{9,8},{10,11... | collective-permute-start | bytes 1179656 | tf_op jit(solution)/shard_map/ppermute | solution.py:157
  103.2 6.8 %collective-permute-done.15 = bf16[2,2,8,6,8,128]{5,4,3,2,1,0:T(8,128)(2,1)S(1)} collective-permute-done((bf16[2,2,8,6,8,128]{5,4,3,2,1,0:T(8,128)(2,1)S(1)}, bf16[2,2,8,6,8,128]{5,4,3,2,1,0:T(8,128)(2,1)S(1)}, u32[]{:S(2)}, u32[]{:S(2)}) %collective-permute-start.15) | collective-permute-done | bytes 393248 | tf_op jit(solution)/shard_map/ppermute | solution.py:157
  (75 shorter events, 14.1 us)
Async XLA Ops:
  0.7 2.8 %copy-start.7 = (s32[8,4,2,27]{3,2,1,0:T(2,128)S(1)}, s32[8,4,2,27]{3,2,1,0:T(2,128)}, u32[]{:S(2)}) copy-start(s32[8,4,2,27]{3,2,1,0:T(2,128)} %param.10) | copy-start | bytes 20740
  0.7 3.6 %copy-start.5 = (bf16[2,8,8,12,128]{4,2,3,1,0:T(8,128)(2,1)S(1)}, bf16[2,8,8,12,128]{4,2,3,1,0:T(8,128)(2,1)}, u32[]{:S(2)}) copy-start(bf16[2,8,8,12,128]{4,2,3,1,0:T(8,128)(2,1)} %param.9) | copy-start | bytes 1179652
  0.7 3.6 %copy-start.6 = (bf16[2,8,8,12,128]{4,2,3,1,0:T(8,128)(2,1)S(1)}, bf16[2,8,8,12,128]{4,2,3,1,0:T(8,128)(2,1)}, u32[]{:S(2)}) copy-start(bf16[2,8,8,12,128]{4,2,3,1,0:T(8,128)(2,1)} %param.6) | copy-start | bytes 1179652
  2.1 10.0 %collective-permute-start = (bf16[2,2,8,6,8,128]{5,4,3,2,1,0:T(8,128)(2,1)S(1)}, bf16[2,2,8,6,8,128]{5,4,3,2,1,0:T(8,128)(2,1)S(1)}, u32[]{:S(2)}, u32[]{:S(2)}) collective-permute-start(bf16[2,2,8,6,8,128]{5,4,3,2,1,0:T(8,128)(2,1)S(1)} %pad_maximum_fusion.7), channel_id=1, source_target_pairs={{0,1},{1,0},{2,3},{3,2},{4,5},{5,4},{6,7},{7,6},{8,9},{9,8},{10,11... | collective-permute-start | bytes 1179656 | tf_op jit(solution)/shard_map/ppermute | solution.py:157
  12.3 19.4 %collective-permute-start.2 = (bf16[2,2,8,6,16,128]{5,4,3,2,1,0:T(8,128)(2,1)S(1)}, bf16[2,2,8,6,16,128]{5,4,3,2,1,0:T(8,128)(2,1)S(1)}, u32[]{:S(2)}, u32[]{:S(2)}) collective-permute-start(bf16[2,2,8,6,16,128]{5,4,3,2,1,0:T(8,128)(2,1)S(1)} %pad_maximum_fusion.5.own.pair), channel_id=1, source_target_pairs={{0,2},{2,4},{4,6},{1,3},{3,5},{5,7},{8,10},{10,12},{12,14},{9,11},... | collective-permute-start | bytes 2359304 | tf_op jit(solution)/shard_map/ppermute | solution.py:152
  15.5 19.1 %collective-permute-start.3 = (bf16[2,2,8,6,16,128]{5,4,3,2,1,0:T(8,128)(2,1)S(1)}, bf16[2,2,8,6,16,128]{5,4,3,2,1,0:T(8,128)(2,1)S(1)}, u32[]{:S(2)}, u32[]{:S(2)}) collective-permute-start(bf16[2,2,8,6,16,128]{5,4,3,2,1,0:T(8,128)(2,1)S(1)} %pad_maximum_fusion.5.own.pair), channel_id=1, source_target_pairs={{2,0},{4,2},{6,4},{3,1},{5,3},{7,5},{10,8},{12,10},{14,12},{11,9},... | collective-permute-start | bytes 2359304 | tf_op jit(solution)/shard_map/ppermute | solution.py:152
  17.7 8.6 %collective-permute-start.1 = (bf16[2,2,8,6,8,128]{5,4,3,2,1,0:T(8,128)(2,1)S(1)}, bf16[2,2,8,6,8,128]{5,4,3,2,1,0:T(8,128)(2,1)}, u32[]{:S(2)}, u32[]{:S(2)}) collective-permute-start(bf16[2,2,8,6,8,128]{5,4,3,2,1,0:T(8,128)(2,1)S(1)} %pad_maximum_fusion.6), channel_id=1, source_target_pairs={{0,1},{1,0},{2,3},{3,2},{4,5},{5,4},{6,7},{7,6},{8,9},{9,8},{10,11... | collective-permute-start | bytes 1179656 | tf_op jit(solution)/shard_map/ppermute | solution.py:157
  31.7 0.9 copy-start
  34.6 0.9 copy-start.3
  35.5 6.7 %copy-start.1 = (bf16[2,2,8,6,16,128]{5,4,3,2,1,0:T(8,128)(2,1)S(1)}, bf16[2,2,8,6,16,128]{5,4,3,2,1,0:T(8,128)(2,1)}, u32[]{:S(2)}) copy-start(bf16[2,2,8,6,16,128]{5,4,3,2,1,0:T(8,128)(2,1)} %copy-done) | copy-start | bytes 2359300
  35.5 25.5 %collective-permute-start.7 = (bf16[2,2,8,6,16,128]{5,4,3,2,1,0:T(8,128)(2,1)S(1)}, bf16[2,2,8,6,16,128]{5,4,3,2,1,0:T(8,128)(2,1)S(1)}, u32[]{:S(2)}, u32[]{:S(2)}) collective-permute-start(bf16[2,2,8,6,16,128]{5,4,3,2,1,0:T(8,128)(2,1)S(1)} %pad_maximum_fusion.4.pair.own), channel_id=1, source_target_pairs={{0,2},{2,4},{4,6},{1,3},{3,5},{5,7},{8,10},{10,12},{12,14},{9,11},... | collective-permute-start | bytes 2359304 | tf_op jit(solution)/shard_map/ppermute | solution.py:152
  38.8 22.0 %collective-permute-start.8 = (bf16[2,2,8,6,16,128]{5,4,3,2,1,0:T(8,128)(2,1)S(1)}, bf16[2,2,8,6,16,128]{5,4,3,2,1,0:T(8,128)(2,1)S(1)}, u32[]{:S(2)}, u32[]{:S(2)}) collective-permute-start(bf16[2,2,8,6,16,128]{5,4,3,2,1,0:T(8,128)(2,1)S(1)} %pad_maximum_fusion.4.pair.own), channel_id=1, source_target_pairs={{2,0},{4,2},{6,4},{3,1},{5,3},{7,5},{10,8},{12,10},{14,12},{11,9},... | collective-permute-start | bytes 2359304 | tf_op jit(solution)/shard_map/ppermute | solution.py:152
  43.5 23.6 %collective-permute-start.4 = (bf16[3,2,8,6,16,128]{5,4,3,2,1,0:T(8,128)(2,1)}, bf16[3,2,8,6,16,128]{5,4,3,2,1,0:T(8,128)(2,1)}, u32[]{:S(2)}, u32[]{:S(2)}) collective-permute-start(bf16[3,2,8,6,16,128]{5,4,3,2,1,0:T(8,128)(2,1)} %pad_maximum_fusion), channel_id=1, source_target_pairs={{0,8},{8,16},{16,24},{1,9},{9,17},{17,25},{2,10},{10,18},{18,26},{... | collective-permute-start | bytes 3538952 | tf_op jit(solution)/shard_map/ppermute | solution.py:152
  51.0 17.8 %collective-permute-start.5 = (bf16[3,2,8,6,16,128]{5,4,3,2,1,0:T(8,128)(2,1)}, bf16[3,2,8,6,16,128]{5,4,3,2,1,0:T(8,128)(2,1)}, u32[]{:S(2)}, u32[]{:S(2)}) collective-permute-start(bf16[3,2,8,6,16,128]{5,4,3,2,1,0:T(8,128)(2,1)} %pad_maximum_fusion.1), channel_id=1, source_target_pairs={{8,0},{16,8},{24,16},{9,1},{17,9},{25,17},{10,2},{18,10},{26,18},{... | collective-permute-start | bytes 3538952 | tf_op jit(solution)/shard_map/ppermute | solution.py:152
  61.2 33.6 %collective-permute-start.9 = (bf16[3,2,8,6,16,128]{5,4,3,2,1,0:T(8,128)(2,1)S(1)}, bf16[3,2,8,6,16,128]{5,4,3,2,1,0:T(8,128)(2,1)S(1)}, u32[]{:S(2)}, u32[]{:S(2)}) collective-permute-start(bf16[3,2,8,6,16,128]{5,4,3,2,1,0:T(8,128)(2,1)S(1)} %pad_maximum_fusion.2), channel_id=1, source_target_pairs={{0,8},{8,16},{16,24},{1,9},{9,17},{17,25},{2,10},{10,18},{18,26},{... | collective-permute-start | bytes 3538952 | tf_op jit(solution)/shard_map/ppermute | solution.py:152
  64.9 3.9 %copy-start.2 = (bf16[2,2,8,6,16,128]{5,4,3,2,1,0:T(8,128)(2,1)S(1)}, bf16[2,2,8,6,16,128]{5,4,3,2,1,0:T(8,128)(2,1)}, u32[]{:S(2)}) copy-start(bf16[2,2,8,6,16,128]{5,4,3,2,1,0:T(8,128)(2,1)} %copy-done) | copy-start | bytes 2359300
  64.9 3.9 %copy-start.4 = (bf16[2,2,8,6,16,128]{5,4,3,2,1,0:T(8,128)(2,1)S(1)}, bf16[2,2,8,6,16,128]{5,4,3,2,1,0:T(8,128)(2,1)}, u32[]{:S(2)}) copy-start(bf16[2,2,8,6,16,128]{5,4,3,2,1,0:T(8,128)(2,1)} %copy-done.3) | copy-start | bytes 2359300
  65.1 29.8 %collective-permute-start.10 = (bf16[3,2,8,6,16,128]{5,4,3,2,1,0:T(8,128)(2,1)S(1)}, bf16[3,2,8,6,16,128]{5,4,3,2,1,0:T(8,128)(2,1)S(1)}, u32[]{:S(2)}, u32[]{:S(2)}) collective-permute-start(bf16[3,2,8,6,16,128]{5,4,3,2,1,0:T(8,128)(2,1)S(1)} %pad_maximum_fusion.3), channel_id=1, source_target_pairs={{8,0},{16,8},{24,16},{9,1},{17,9},{25,17},{10,2},{18,10},{26,18},{... | collective-permute-start | bytes 3538952 | tf_op jit(solution)/shard_map/ppermute | solution.py:152
  78.4 7.6 %collective-permute-start.11 = (f32[2,6,2,128]{3,2,1,0:T(2,128)S(1)}, f32[2,6,2,128]{3,2,1,0:T(2,128)S(1)}, u32[]{:S(2)}, u32[]{:S(2)}) collective-permute-start(f32[2,6,2,128]{3,2,1,0:T(2,128)S(1)} %get-tuple-element.17.own_st), channel_id=1, source_target_pairs={{0,2},{2,4},{4,6},{1,3},{3,5},{5,7},{8,10},{10,12},{12,14},{9,11},... | collective-permute-start | bytes 36872 | tf_op jit(solution)/shard_map/ppermute | solution.py:152
  81.6 4.4 %collective-permute-start.12 = (f32[2,6,2,128]{3,2,1,0:T(2,128)S(1)}, f32[2,6,2,128]{3,2,1,0:T(2,128)S(1)}, u32[]{:S(2)}, u32[]{:S(2)}) collective-permute-start(f32[2,6,2,128]{3,2,1,0:T(2,128)S(1)} %get-tuple-element.17.own_st), channel_id=1, source_target_pairs={{2,0},{4,2},{6,4},{3,1},{5,3},{7,5},{10,8},{12,10},{14,12},{11,9},... | collective-permute-start | bytes 36872 | tf_op jit(solution)/shard_map/ppermute | solution.py:152
  86.0 7.0 %collective-permute-start.13 = (f32[3,6,2,128]{3,2,1,0:T(2,128)S(1)}, f32[3,6,2,128]{3,2,1,0:T(2,128)S(1)}, u32[]{:S(2)}, u32[]{:S(2)}) collective-permute-start(f32[3,6,2,128]{3,2,1,0:T(2,128)S(1)} %pad_maximum_fusion.8), channel_id=1, source_target_pairs={{0,8},{8,16},{16,24},{1,9},{9,17},{17,25},{2,10},{10,18},{18,26},{... | collective-permute-start | bytes 55304 | tf_op jit(solution)/shard_map/ppermute | solution.py:152
  89.5 5.4 %collective-permute-start.14 = (f32[3,6,2,128]{3,2,1,0:T(2,128)S(1)}, f32[3,6,2,128]{3,2,1,0:T(2,128)S(1)}, u32[]{:S(2)}, u32[]{:S(2)}) collective-permute-start(f32[3,6,2,128]{3,2,1,0:T(2,128)S(1)} %pad_maximum_fusion.9), channel_id=1, source_target_pairs={{8,0},{16,8},{24,16},{9,1},{17,9},{25,17},{10,2},{18,10},{26,18},{... | collective-permute-start | bytes 55304 | tf_op jit(solution)/shard_map/ppermute | solution.py:152
  91.7 10.5 %collective-permute-start.6 = (bf16[2,2,8,6,8,128]{5,4,3,2,1,0:T(8,128)(2,1)S(1)}, bf16[2,2,8,6,8,128]{5,4,3,2,1,0:T(8,128)(2,1)S(1)}, u32[]{:S(2)}, u32[]{:S(2)}) collective-permute-start(bf16[2,2,8,6,8,128]{5,4,3,2,1,0:T(8,128)(2,1)S(1)} %get-tuple-element.30), channel_id=1, source_target_pairs={{0,1},{1,0},{2,3},{3,2},{4,5},{5,4},{6,7},{7,6},{8,9},{9,8},{10,11... | collective-permute-start | bytes 1179656 | tf_op jit(solution)/shard_map/ppermute | solution.py:157
  100.9 9.1 %collective-permute-start.15 = (bf16[2,2,8,6,8,128]{5,4,3,2,1,0:T(8,128)(2,1)S(1)}, bf16[2,2,8,6,8,128]{5,4,3,2,1,0:T(8,128)(2,1)S(1)}, u32[]{:S(2)}, u32[]{:S(2)}) collective-permute-start(bf16[2,2,8,6,8,128]{5,4,3,2,1,0:T(8,128)(2,1)S(1)} %get-tuple-element.20), channel_id=1, source_target_pairs={{0,1},{1,0},{2,3},{3,2},{4,5},{5,4},{6,7},{7,6},{8,9},{9,8},{10,11... | collective-permute-start | bytes 1179656 | tf_op jit(solution)/shard_map/ppermute | solution.py:157

commit v3 on v2

v3 whole, which is shorter than its diff:
```python
import functools

import jax
import jax.numpy as jnp
import numpy as np
from jax import lax
from jax.experimental import pallas as pl
from jax.experimental.pallas import tpu as pltpu
from jax.sharding import PartitionSpec as P

TF = 1
TR = 8
TC = 8
MASKED = -1e30
LOG2E = 1.4426950408889634
NT = (((1,), (1,)), ((), ()))
NN = (((1,), (0,)), ((), ()))


def dot(left, right, dims):
    return lax.dot_general(left, right, dims, preferred_element_type=jnp.float32)


def flat(tiles):
    return tiles.reshape(tiles.shape[-4] * tiles.shape[-2], tiles.shape[-1])


def spread(bias, tokens):
    columns, width = bias.shape
    return jnp.broadcast_to(bias[None], (tokens // columns, columns, width)).reshape(tokens, width)


def fill_band(band, own, before, after, low, high, at_of):
    frames = own.shape[0]
    tokens = own.shape[-4] * own.shape[-2]
    for at in range(frames + 2):
        for row, beside in enumerate((before, own, after)):
            if at == 0:
                tiles = low[at_of(row)]
            elif at == frames + 1:
                tiles = high[at_of(row)]
            else:
                tiles = beside[at_of(at - 1)]
            band[pl.ds((3 * at + row) * tokens, tokens), :] = flat(tiles)


def single(at):
    return at


def attend_kernel(scaling, pair, *refs):
    keys, values = refs[:5], refs[5:10]
    bias, attended, stats, key_all, value_all = refs[10:]
    frames, _, rows, _, columns, dim = pair.shape
    tokens = rows * columns
    fill_band(key_all, *keys, single)
    fill_band(value_all, *values, single)
    windows = [pl.ds(3 * at * tokens, 9 * tokens) for at in range(frames)]
    scores = [
        dot(flat(pair[at, 0]), key_all[windows[at], :], NT) * (scaling * LOG2E) + spread(bias[at], tokens)
        for at in range(frames)
    ]
    highest = [jnp.max(part, axis=1, keepdims=True) for part in scores]
    raised = [jnp.exp2(part - top) for part, top in zip(scores, highest)]
    total = [jnp.sum(part, axis=1, keepdims=True) for part in raised]
    sums = [dot(raised[at].astype(jnp.bfloat16), value_all[windows[at], :], NN) for at in range(frames)]
    for at in range(frames):
        out = (sums[at] * (1.0 / total[at])).astype(jnp.bfloat16)
        grad = flat(pair[at, 1]).astype(jnp.float32)
        grad_dot = jnp.sum(grad * out.astype(jnp.float32), axis=1, keepdims=True)
        attended[at, :, 0] = out.reshape(rows, columns, dim)
        lane = lax.broadcasted_iota(jnp.int32, (tokens, 128), 1)
        both = jnp.where(lane == 0, highest[at] + jnp.log2(total[at]), grad_dot)
        stats[at, 0] = jnp.transpose(both)[:2]


def query_kernel(scaling, pair, *refs):
    keys, values = refs[:5], refs[5:10]
    attended, stats, bias, grads, key_all, value_all = refs[10:]
    frames, _, rows, _, columns, dim = pair.shape
    tokens = rows * columns
    fill_band(key_all, *keys, single)
    fill_band(value_all, *values, single)
    windows = [pl.ds(3 * at * tokens, 9 * tokens) for at in range(frames)]

    def column(at, which):
        wide = jnp.broadcast_to(stats[at, 0, which : which + 1], (128, tokens))
        return jnp.transpose(wide)[:, :1]

    scores = [dot(flat(pair[at, 0]), key_all[windows[at], :], NT) for at in range(frames)]
    grad_probs = [dot(flat(pair[at, 1]), value_all[windows[at], :], NT) for at in range(frames)]
    for at in range(frames):
        shift = spread(bias[at], tokens) - column(at, 0)
        weights = jnp.exp2(scores[at] * (scaling * LOG2E) + shift)
        grad_scores = (weights * (grad_probs[at] - column(at, 1))).astype(jnp.bfloat16)
        query_grad = dot(grad_scores, key_all[windows[at], :], NN) * scaling
        grads[0, at, :, 0] = attended[at, :, 0]
        grads[1, at, :, 0] = query_grad.astype(jnp.bfloat16).reshape(rows, columns, dim)


def back_kernel(
    scaling, keys, values, own, before, after, low, high, own_st, before_st, after_st, low_st, high_st, bias,
    grads, query_all, grad_all
):
    frames, rows, _, columns, dim = keys.shape
    tokens = rows * columns
    halo = (own, before, after, low, high)
    fill_band(query_all, *halo, lambda at: (at, 0))
    fill_band(grad_all, *halo, lambda at: (at, 1))

    def stat_row(at, row, which):
        if at == 0:
            return low_st[row, 0, which : which + 1]
        if at == frames + 1:
            return high_st[row, 0, which : which + 1]
        return (before_st, own_st, after_st)[row][at - 1, 0, which : which + 1]

    def stat_band(at, which):
        parts = [stat_row(at + step, row, which) for step in range(3) for row in range(3)]
        return jnp.concatenate(parts, axis=1)

    windows = [pl.ds(3 * at * tokens, 9 * tokens) for at in range(frames)]
    scores = [dot(flat(keys[at]), query_all[windows[at], :], NT) for at in range(frames)]
    grad_probs = [dot(flat(values[at]), grad_all[windows[at], :], NT) for at in range(frames)]
    for at in range(frames):
        shift = spread(bias[at] - stat_band(at, 0), tokens)
        weights = jnp.exp2(scores[at] * (scaling * LOG2E) + shift).astype(jnp.bfloat16)
        grad_scores = weights.astype(jnp.float32) * (grad_probs[at] - stat_band(at, 1))
        key_grad = dot(grad_scores.astype(jnp.bfloat16), query_all[windows[at], :], NN) * scaling
        value_grad = dot(weights, grad_all[windows[at], :], NN)
        grads[0, at, :, 0] = key_grad.astype(jnp.bfloat16).reshape(rows, columns, dim)
        grads[1, at, :, 0] = value_grad.astype(jnp.bfloat16).reshape(rows, columns, dim)


def head_spec(shape, dim, first):
    block = shape[:dim] + (1,) + shape[dim + 1 :]
    return pl.BlockSpec(block, lambda head: (0,) * dim + (head + first,) + (0,) * (len(shape) - dim - 1))


def whole_spec(shape):
    return pl.BlockSpec(shape, lambda head: (0,) * len(shape))


def run(kernel, scaling, tiles, stats, bias, outs, first, count, products):
    rows, _, columns, dim = tiles[0].shape[-4:]
    frames = tiles[0].shape[0]
    tokens = rows * columns
    return pl.pallas_call(
        functools.partial(kernel, scaling),
        grid=(count,),
        out_shape=tuple(outs),
        in_specs=[head_spec(part.shape, part.ndim - 3, first) for part in tuple(tiles) + tuple(stats)]
        + [whole_spec(bias.shape)],
        out_specs=tuple(head_spec(out.shape, len(out.shape) - 3, 0) for out in outs),
        scratch_shapes=[pltpu.VMEM((3 * (frames + 2) * tokens, dim), jnp.bfloat16)] * 2,
        compiler_params=pltpu.CompilerParams(vmem_limit_bytes=32 * 2**20),
        cost_estimate=pl.CostEstimate(
            flops=frames * count * 2 * products * tokens * 9 * tokens * dim,
            bytes_accessed=count * (frames + 2) * 3 * 2 * tokens * dim * 2,
            transcendentals=frames * count * tokens * 9 * tokens,
        ),
    )(*tiles, *stats, bias)


def step_along(tensor, axis, sign):
    size = lax.axis_size(axis)
    return lax.ppermute(tensor, axis, [(i, i + sign) for i in range(size) if 0 <= i + sign < size])


def turn(tensor, shift):
    size = lax.axis_size("head")
    return lax.ppermute(tensor, "head", [(i, (i + shift) % size) for i in range(size)])


def frame_edges(before, own, after):
    last = own.shape[0] - 1
    low = step_along(jnp.stack([before[last], own[last], after[last]]), "frame", 1)
    high = step_along(jnp.stack([before[0], own[0], after[0]]), "frame", -1)
    return low, high


def row_sides(own):
    return step_along(own, "row", 1), step_along(own, "row", -1)


def tile_biases(active, frames, rows, columns_here):
    size = lax.axis_size("head")
    me = lax.axis_index("head")
    frame_at = lax.axis_index("frame") * frames
    row_at = lax.axis_index("row")
    all_frames, all_rows, count, slots = active.shape
    padded = jnp.pad(active.astype(jnp.float32), ((1, 1), (1, 1), (0, 0), (0, 0)))
    near = lax.dynamic_slice(padded, (frame_at, row_at, 0, 0), (frames + 2, 3, count, slots))
    near = near.reshape(frames + 2, 3, count, 9, 3)
    steps = jnp.arange(3, dtype=jnp.int32) - 1
    frame_ids = frame_at + jnp.arange(frames, dtype=jnp.int32)[:, None] + steps
    frame_in = (frame_ids >= 0) & (frame_ids < all_frames)
    row_in = (row_at + steps >= 0) & (row_at + steps < all_rows)
    inside = (frame_in[:, :, None] & row_in).reshape(frames, 9).astype(jnp.float32)
    ahead = near[1 : 1 + frames, 1] * inside[:, None, :, None]
    pick = np.zeros((frames + 2, 3, 9, frames, 9), np.float32)
    for at in range(frames):
        for offset in range(9):
            pick[at + offset // 3, offset % 3, 8 - offset, at, offset] = 1.0
    behind = jnp.einsum("xyioc,xyofq->fiqc", near, pick)
    place = jnp.arange(size * columns_here, dtype=jnp.int32)
    tile = ((me + place // columns_here) % size * columns_here + place % columns_here) // TC
    repeat = np.kron(np.eye(9), np.kron(np.ones((1, rows)), np.eye(place.shape[0])))
    spread_out = jnp.asarray(repeat, jnp.bfloat16)
    smalls = []
    for table, sign in ((ahead, 1), (behind, -1)):
        owner = tile[None] == jnp.arange(count, dtype=jnp.int32)[:, None]
        shift = (sign * (tile[None, :] - tile[:, None]))[None] == steps[:, None, None]
        chosen = (owner[:, None, :, None] & shift[None]).astype(jnp.float32)
        smalls.append(jnp.einsum("fioc,icpk->fpok", table, chosen))
    small = jnp.stack(smalls).reshape(2 * frames * place.shape[0], -1).astype(jnp.bfloat16)
    allowed = jnp.dot(small, spread_out, preferred_element_type=jnp.float32)
    bias = jnp.where(allowed > 0.5, 0.0, MASKED).reshape(2, frames, place.shape[0], -1)
    return bias[0], bias[1]


def on_device(queries, keys, values, out_grad, active):
    frames, rows, columns_here, heads, dim = queries.shape
    size = lax.axis_size("head")
    me = lax.axis_index("head")
    groups = heads // size
    scaling = dim ** (-0.5)

    def group_of(tensor, shift):
        start = (me + shift) % size * groups
        return lax.dynamic_slice_in_dim(jnp.transpose(tensor, (0, 1, 3, 2, 4)), start, groups, 2)

    def pair_of(first, second, shift):
        return jnp.stack([group_of(first, shift), group_of(second, shift)], 1)

    def gather_columns(pick):
        moved = [turn(pick(size - b), size - b) for b in range(1, size)]
        return jnp.concatenate([pick(0)] + moved, axis=-2)

    def from_heads(parts):
        whole = jnp.zeros((2, frames, rows, heads, columns_here, dim), jnp.bfloat16)
        for first, grads in parts:
            for b in range(size):
                piece = lax.slice_in_dim(grads, b * columns_here, (b + 1) * columns_here, axis=4)
                piece = piece if b == 0 else turn(piece, b)
                start = (me + size - b) % size * groups + first
                whole = lax.dynamic_update_slice_in_dim(whole, piece, start, 3)
        whole = jnp.transpose(whole, (0, 1, 2, 4, 3, 5))
        return whole[0], whole[1]

    front_bias, back_bias = tile_biases(active, frames, rows, columns_here)
    held = [pair_of(queries, out_grad, shift) for shift in range(size)]
    key = gather_columns(lambda shift: group_of(keys, shift))
    value = gather_columns(lambda shift: group_of(values, shift))
    held, key = lax.optimization_barrier((held, key))
    pair = gather_columns(lambda shift: held[shift])
    columns = columns_here * size
    tokens = rows * columns

    def surround(own):
        sides = row_sides(own)
        return (own,) + sides + frame_edges(sides[0], own, sides[1])

    def out_shape(lead, count):
        return jax.ShapeDtypeStruct(lead + (frames, rows, count, columns, dim), jnp.bfloat16)

    stat_shape = jax.ShapeDtypeStruct((frames, groups, 2, tokens), jnp.float32)
    key_sides = row_sides(key)
    pair, key_sides = lax.optimization_barrier((pair, key_sides))
    around = (key,) + key_sides + frame_edges(key_sides[0], key, key_sides[1]) + surround(value)
    attended, stats = run(
        attend_kernel, scaling, (pair,) + around, (), front_bias, [out_shape((), groups), stat_shape], 0, groups, 2
    )
    (front_grads,) = run(
        query_kernel, scaling, (pair,) + around + (attended,), (stats,), front_bias, [out_shape((2,), groups)],
        0, groups, 3
    )
    pair_around = surround(pair)
    stats_around = surround(stats)
    halves = [(0, groups - groups // 2), (groups - groups // 2, groups // 2)]
    parts = []
    for first, count in halves:
        (back_grads,) = run(
            back_kernel, scaling, (key, value) + pair_around, stats_around, back_bias, [out_shape((2,), count)],
            first, count, 4
        )
        parts.append((first, back_grads))
    return from_heads([(0, front_grads)]) + from_heads(parts)


def solution(mesh):
    spec = P("frame", "row", "head", None, None)
    return jax.shard_map(
        on_device, mesh=mesh, in_specs=(spec,) * 4 + (P(),), out_specs=(spec,) * 4, check_vma=False
    )
```

time: 113 us -> 115 us (1.018)
  starting transfers between devices: 40.4 us -> 53.2 us
  waiting for transfers between devices: 29.3 us -> 16.7 us
  Pallas kernels: 15.3 us -> 20.9 us
  local copies, waits for them, and re-layouts: 18 us -> 14.8 us
  other arithmetic: 4.43 us -> 5.99 us
  matrix products: 2.44 us -> 1.07 us
    ppermute x4 -> x6, waiting for transfers between devices: 17.4 us -> 4.8 us  [turn(): lax.ppermute(tensor, 'head', [(i, (i + shift) % size) for i in range(size)])]
    ppermute x12 -> x16, starting transfers between devices: 35.3 us -> 47.3 us  [step_along(): lax.ppermute(tensor, axis, [(i, i + sign) for i in range(size) if 0 <= i...]
    pallas_call x2 -> x4, Pallas kernels: 15.3 us -> 20.9 us  [run(): pl.pallas_call(functools.partial(kernel, scaling), grid=(count,), out_sha...]
    unnamed x16 -> x44, local copies, waits for them, and re-layouts: 1.81 us -> 5.42 us
    reshape x2 -> x0, local copies, waits for them, and re-layouts: 3.23 us -> none  [tile_biases(): biases.append(bias.reshape(frames, place.shape[0], -1))]
    broadcast_in_dim x2 -> x0, local copies, waits for them, and re-layouts: 3.21 us -> none  [tile_biases(): bias = jnp.broadcast_to(bias, bias.shape[:3] + (rows,) + bias.shape[4:])]
    select_n x2 -> x0, local copies, waits for them, and re-layouts: 2.18 us -> none  [tile_biases(): bias = jnp.where(allowed > 0.5, 0.0, MASKED)[:, :, :, None, :]]
    dynamic_slice x0 -> x2, local copies, waits for them, and re-layouts: none -> 2.11 us  [group_of(): lax.dynamic_slice_in_dim(jnp.transpose(tensor, (0, 1, 3, 2, 4)), start, g...]
  transfers between devices with their start and end apart: 16 -> 22, of which waited for: 8 -> 6; matrix products, arithmetic and copies ran while one was open for 18% -> 13% of each run, Pallas kernels for 14% -> 18%
where the time goes in v3:
time: 115 us; the launch traced here: 114 us
  starting transfers between devices  53.2 us (46%)
  Pallas kernels  20.9 us (18%)
  waiting for transfers between devices  16.7 us (15%)
  local copies, waits for them, and re-layouts  14.8 us (13%)
  other arithmetic  5.99 us (5%)
  between operations  1.37 us (1%)
    ppermute x16, starting transfers between devices, step_along(): lax.ppermute(tensor, axis, [(i, i + sign) for i in range(size) if 0 <= i...  47.3 us
    pallas_call x4, Pallas kernels, run(): pl.pallas_call(functools.partial(kernel, scaling), grid=(count,), out_sha...  20.9 us
    ppermute x16, waiting for transfers between devices, step_along(): lax.ppermute(tensor, axis, [(i, i + sign) for i in range(size) if 0 <= i...  11.9 us
    ppermute x6, starting transfers between devices, turn(): lax.ppermute(tensor, 'head', [(i, (i + shift) % size) for i in range(size)])  5.95 us
    unnamed x44, local copies, waits for them, and re-layouts  5.42 us
    ppermute x6, waiting for transfers between devices, turn(): lax.ppermute(tensor, 'head', [(i, (i + shift) % size) for i in range(size)])  4.8 us
    another operation x4, other arithmetic, frame_edges(): high = step_along(jnp.stack([before[0], own[0], after[0]]), 'frame', -1)  3.01 us
  transfers between devices with their start and end apart: 22, of which 6 were waited for; matrix products, arithmetic and copies ran while one was open for 13% of the time, Pallas kernels for 18%

profile of v3, /device:TPU:9, one launch (start us, length us, event | category | flops | bytes accessed | tf_op | source)
XLA Modules:
  0.0 114.1 jit_solution(15266206601742984082)
XLA Ops:
  0.7 1.1 dynamic-slice_bitcast_fusion.3
  1.8 1.3 %collective-permute-start = (bf16[2,8,6,8,128]{4,3,2,1,0:T(8,128)(2,1)S(1)}, bf16[2,8,6,8,128]{4,3,2,1,0:T(8,128)(2,1)S(1)}, u32[]{:S(2)}, u32[]{:S(2)}) collective-permute-start(bf16[2,8,6,8,128]{4,3,2,1,0:T(8,128)(2,1)S(1)} %get-tuple-element.51), channel_id=1, source_target_pairs={{0,1},{1,0},{2,3},{3,2},{4,5},{5,4},{6,7},{7,6},{8,9},{9,8},{10,11... | collective-permute-start | bytes 589832 | tf_op jit(solution)/shard_map/ppermute | solution.py:172
  8.1 3.2 %collective-permute-start.2 = (bf16[2,8,6,16,128]{4,3,2,1,0:T(8,128)(2,1)S(1)}, bf16[2,8,6,16,128]{4,3,2,1,0:T(8,128)(2,1)S(1)}, u32[]{:S(2)}, u32[]{:S(2)}) collective-permute-start(bf16[2,8,6,16,128]{4,3,2,1,0:T(8,128)(2,1)S(1)} %pad_maximum_fusion.10.refs_0_.keys), channel_id=1, source_target_pairs={{0,2},{2,4},{4,6},{1,3},{3,5},{5,7},{8,10},{10,12},{12,14},{9,11},... | collective-permute-start | bytes 1179656 | tf_op jit(solution)/shard_map/ppermute | solution.py:167
  11.3 2.1 %collective-permute-start.3 = (bf16[2,8,6,16,128]{4,3,2,1,0:T(8,128)(2,1)S(1)}, bf16[2,8,6,16,128]{4,3,2,1,0:T(8,128)(2,1)S(1)}, u32[]{:S(2)}, u32[]{:S(2)}) collective-permute-start(bf16[2,8,6,16,128]{4,3,2,1,0:T(8,128)(2,1)S(1)} %pad_maximum_fusion.10.refs_0_.keys), channel_id=1, source_target_pairs={{2,0},{4,2},{6,4},{3,1},{5,3},{7,5},{10,8},{12,10},{14,12},{11,9},... | collective-permute-start | bytes 1179656 | tf_op jit(solution)/shard_map/ppermute | solution.py:167
  13.4 1.3 %collective-permute-start.1 = (bf16[2,2,8,6,8,128]{5,4,3,2,1,0:T(8,128)(2,1)S(1)}, bf16[2,2,8,6,8,128]{5,4,3,2,1,0:T(8,128)(2,1)S(1)}, u32[]{:S(2)}, u32[]{:S(2)}) collective-permute-start(bf16[2,2,8,6,8,128]{5,4,3,2,1,0:T(8,128)(2,1)S(1)} %pad_maximum_fusion.9), channel_id=1, source_target_pairs={{0,1},{1,0},{2,3},{3,2},{4,5},{5,4},{6,7},{7,6},{8,9},{9,8},{10,11... | collective-permute-start | bytes 1179656 | tf_op jit(solution)/shard_map/ppermute | solution.py:172
  14.8 3.2 %collective-permute-start.7 = (bf16[2,8,6,16,128]{4,3,2,1,0:T(8,128)(2,1)S(1)}, bf16[2,8,6,16,128]{4,3,2,1,0:T(8,128)(2,1)S(1)}, u32[]{:S(2)}, u32[]{:S(2)}) collective-permute-start(bf16[2,8,6,16,128]{4,3,2,1,0:T(8,128)(2,1)S(1)} %pad_maximum_fusion.7.refs_5_.values), channel_id=1, source_target_pairs={{0,2},{2,4},{4,6},{1,3},{3,5},{5,7},{8,10},{10,12},{12,14},{9,11},... | collective-permute-start | bytes 1179656 | tf_op jit(solution)/shard_map/ppermute | solution.py:167
  18.0 2.1 %collective-permute-start.8 = (bf16[2,8,6,16,128]{4,3,2,1,0:T(8,128)(2,1)S(1)}, bf16[2,8,6,16,128]{4,3,2,1,0:T(8,128)(2,1)S(1)}, u32[]{:S(2)}, u32[]{:S(2)}) collective-permute-start(bf16[2,8,6,16,128]{4,3,2,1,0:T(8,128)(2,1)S(1)} %pad_maximum_fusion.7.refs_5_.values), channel_id=1, source_target_pairs={{2,0},{4,2},{6,4},{3,1},{5,3},{7,5},{10,8},{12,10},{14,12},{11,9},... | collective-permute-start | bytes 1179656 | tf_op jit(solution)/shard_map/ppermute | solution.py:167
  20.2 1.1 collective-permute-done.1
  21.4 3.2 %collective-permute-start.12 = (bf16[2,2,8,6,16,128]{5,4,3,2,1,0:T(8,128)(2,1)S(1)}, bf16[2,2,8,6,16,128]{5,4,3,2,1,0:T(8,128)(2,1)S(1)}, u32[]{:S(2)}, u32[]{:S(2)}) collective-permute-start(bf16[2,2,8,6,16,128]{5,4,3,2,1,0:T(8,128)(2,1)S(1)} %pad_maximum_fusion.2.pair.own), channel_id=1, source_target_pairs={{0,2},{2,4},{4,6},{1,3},{3,5},{5,7},{8,10},{10,12},{12,14},{9,11},... | collective-permute-start | bytes 2359304 | tf_op jit(solution)/shard_map/ppermute | solution.py:167
  24.6 2.1 %collective-permute-start.13 = (bf16[2,2,8,6,16,128]{5,4,3,2,1,0:T(8,128)(2,1)S(1)}, bf16[2,2,8,6,16,128]{5,4,3,2,1,0:T(8,128)(2,1)S(1)}, u32[]{:S(2)}, u32[]{:S(2)}) collective-permute-start(bf16[2,2,8,6,16,128]{5,4,3,2,1,0:T(8,128)(2,1)S(1)} %pad_maximum_fusion.2.pair.own), channel_id=1, source_target_pairs={{2,0},{4,2},{6,4},{3,1},{5,3},{7,5},{10,8},{12,10},{14,12},{11,9},... | collective-permute-start | bytes 2359304 | tf_op jit(solution)/shard_map/ppermute | solution.py:167
  26.9 8.6 %collective-permute-start.4 = (bf16[3,8,6,16,128]{4,3,2,1,0:T(8,128)(2,1)S(1)}, bf16[3,8,6,16,128]{4,3,2,1,0:T(8,128)(2,1)S(1)}, u32[]{:S(2)}, u32[]{:S(2)}) collective-permute-start(bf16[3,8,6,16,128]{4,3,2,1,0:T(8,128)(2,1)S(1)} %pad_maximum_fusion.3), channel_id=1, source_target_pairs={{0,8},{8,16},{16,24},{1,9},{9,17},{17,25},{2,10},{10,18},{18,26},{... | collective-permute-start | bytes 1769480 | tf_op jit(solution)/shard_map/ppermute | solution.py:167
  36.4 1.9 %collective-permute-start.5 = (bf16[3,8,6,16,128]{4,3,2,1,0:T(8,128)(2,1)}, bf16[3,8,6,16,128]{4,3,2,1,0:T(8,128)(2,1)}, u32[]{:S(2)}, u32[]{:S(2)}) collective-permute-start(bf16[3,8,6,16,128]{4,3,2,1,0:T(8,128)(2,1)} %pad_maximum_fusion.4), channel_id=1, source_target_pairs={{8,0},{16,8},{24,16},{9,1},{17,9},{25,17},{10,2},{18,10},{26,18},{... | collective-permute-start | bytes 1769480 | tf_op jit(solution)/shard_map/ppermute | solution.py:167
  39.4 3.6 %collective-permute-start.9 = (bf16[3,8,6,16,128]{4,3,2,1,0:T(8,128)(2,1)}, bf16[3,8,6,16,128]{4,3,2,1,0:T(8,128)(2,1)}, u32[]{:S(2)}, u32[]{:S(2)}) collective-permute-start(bf16[3,8,6,16,128]{4,3,2,1,0:T(8,128)(2,1)} %pad_maximum_fusion.5), channel_id=1, source_target_pairs={{0,8},{8,16},{16,24},{1,9},{9,17},{17,25},{2,10},{10,18},{18,26},{... | collective-permute-start | bytes 1769480 | tf_op jit(solution)/shard_map/ppermute | solution.py:167
  44.7 1.9 %collective-permute-start.10 = (bf16[3,8,6,16,128]{4,3,2,1,0:T(8,128)(2,1)}, bf16[3,8,6,16,128]{4,3,2,1,0:T(8,128)(2,1)}, u32[]{:S(2)}, u32[]{:S(2)}) collective-permute-start(bf16[3,8,6,16,128]{4,3,2,1,0:T(8,128)(2,1)} %pad_maximum_fusion.6), channel_id=1, source_target_pairs={{8,0},{16,8},{24,16},{9,1},{17,9},{25,17},{10,2},{18,10},{26,18},{... | collective-permute-start | bytes 1769480 | tf_op jit(solution)/shard_map/ppermute | solution.py:167
  48.1 2.0 %collective-permute-done.9.refs_8_ = bf16[3,8,6,16,128]{4,3,2,1,0:T(8,128)(2,1)} collective-permute-done((bf16[3,8,6,16,128]{4,3,2,1,0:T(8,128)(2,1)}, bf16[3,8,6,16,128]{4,3,2,1,0:T(8,128)(2,1)}, u32[]{:S(2)}, u32[]{:S(2)}) %collective-permute-start.9) | collective-permute-done | bytes 589856 | tf_op jit(solution)/shard_map/ppermute | solution.py:167
  50.1 6.1 %collective-permute-done.10.refs_9_ = bf16[3,8,6,16,128]{4,3,2,1,0:T(8,128)(2,1)} collective-permute-done((bf16[3,8,6,16,128]{4,3,2,1,0:T(8,128)(2,1)}, bf16[3,8,6,16,128]{4,3,2,1,0:T(8,128)(2,1)}, u32[]{:S(2)}, u32[]{:S(2)}) %collective-permute-start.10) | collective-permute-done | bytes 589856 | tf_op jit(solution)/shard_map/ppermute | solution.py:167
  56.3 1.1 copy-done.7
  57.3 6.7 %shard_map.102 = (bf16[2,8,6,16,128]{4,3,2,1,0:T(8,128)(2,1)S(1)}, f32[2,6,2,128]{3,2,1,0:T(2,128)S(1)}) custom-call(bf16[2,2,8,6,16,128]{5,4,3,2,1,0:T(8,128)(2,1)S(1)} %pad_maximum_fusion.2.pair.own, bf16[2,8,6,16,128]{4,3,2,1,0:T(8,128)(2,1)S(1)} %pad_maximum_fusion.10.refs_0_.keys, bf16[2,8,6,16,128]{4,3,2,1,0:T(8,128)(2,1)S(1)} %collective-permute-done.2.refs_1_, ...), custom_call_target="tpu_custom_call" | custom-call | flops 905969664 | bytes 4718592 | tf_op jit(solution)/shard_map/pallas_call | solution.py:148
  64.0 3.1 %collective-permute-start.16 = (f32[2,6,2,128]{3,2,1,0:T(2,128)S(1)}, f32[2,6,2,128]{3,2,1,0:T(2,128)S(1)}, u32[]{:S(2)}, u32[]{:S(2)}) collective-permute-start(f32[2,6,2,128]{3,2,1,0:T(2,128)S(1)} %get-tuple-element.19.refs_11_.own_st), channel_id=1, source_target_pairs={{0,2},{2,4},{4,6},{1,3},{3,5},{5,7},{8,10},{10,12},{12,14},{9,11},... | collective-permute-start | bytes 36872 | tf_op jit(solution)/shard_map/ppermute | solution.py:167
  67.2 2.1 %collective-permute-start.17 = (f32[2,6,2,128]{3,2,1,0:T(2,128)S(1)}, f32[2,6,2,128]{3,2,1,0:T(2,128)S(1)}, u32[]{:S(2)}, u32[]{:S(2)}) collective-permute-start(f32[2,6,2,128]{3,2,1,0:T(2,128)S(1)} %get-tuple-element.19.refs_11_.own_st), channel_id=1, source_target_pairs={{2,0},{4,2},{6,4},{3,1},{5,3},{7,5},{10,8},{12,10},{14,12},{11,9},... | collective-permute-start | bytes 36872 | tf_op jit(solution)/shard_map/ppermute | solution.py:167
  69.6 1.1 %pad_maximum_fusion = bf16[3,2,8,6,16,128]{5,4,3,2,1,0:T(8,128)(2,1)} fusion(bf16[1,2,8,6,16,128]{5,4,3,2,1,0:T(8,128)(2,1)S(1)} %get-tuple-element.27, bf16[1,2,8,6,16,128]{5,4,3,2,1,0:T(8,128)(2,1)S(1)} %get-tuple-element.25, bf16[1,2,8,6,16,128]{5,4,3,2,1,0:T(8,128)(2,1)S(1)} %get-tuple-element.23), kind=kLoop, calls=%fused_computation.2 | loop fusion | flops 1179648 | bytes 2359296 | tf_op jit(solution)/shard_map/stack | solution.py:177
  70.8 2.3 %collective-permute-start.14 = (bf16[3,2,8,6,16,128]{5,4,3,2,1,0:T(8,128)(2,1)}, bf16[3,2,8,6,16,128]{5,4,3,2,1,0:T(8,128)(2,1)}, u32[]{:S(2)}, u32[]{:S(2)}) collective-permute-start(bf16[3,2,8,6,16,128]{5,4,3,2,1,0:T(8,128)(2,1)} %pad_maximum_fusion), channel_id=1, source_target_pairs={{0,8},{8,16},{16,24},{1,9},{9,17},{17,25},{2,10},{10,18},{18,26},{... | collective-permute-start | bytes 3538952 | tf_op jit(solution)/shard_map/ppermute | solution.py:167
  73.1 1.2 %pad_maximum_fusion.1 = bf16[3,2,8,6,16,128]{5,4,3,2,1,0:T(8,128)(2,1)} fusion(bf16[1,2,8,6,16,128]{5,4,3,2,1,0:T(8,128)(2,1)S(1)} %get-tuple-element.26, bf16[1,2,8,6,16,128]{5,4,3,2,1,0:T(8,128)(2,1)S(1)} %get-tuple-element.24, bf16[1,2,8,6,16,128]{5,4,3,2,1,0:T(8,128)(2,1)S(1)} %get-tuple-element.22), kind=kLoop, calls=%fused_computation.3 | loop fusion | flops 1179648 | bytes 2359296 | tf_op jit(solution)/shard_map/stack | solution.py:178
  74.3 3.0 %collective-permute-start.15 = (bf16[3,2,8,6,16,128]{5,4,3,2,1,0:T(8,128)(2,1)}, bf16[3,2,8,6,16,128]{5,4,3,2,1,0:T(8,128)(2,1)}, u32[]{:S(2)}, u32[]{:S(2)}) collective-permute-start(bf16[3,2,8,6,16,128]{5,4,3,2,1,0:T(8,128)(2,1)} %pad_maximum_fusion.1), channel_id=1, source_target_pairs={{8,0},{16,8},{24,16},{9,1},{17,9},{25,17},{10,2},{18,10},{26,18},{... | collective-permute-start | bytes 3538952 | tf_op jit(solution)/shard_map/ppermute | solution.py:167
  77.4 6.4 %shard_map.103 = bf16[2,2,8,6,16,128]{5,4,3,2,1,0:T(8,128)(2,1)S(1)} custom-call(bf16[2,2,8,6,16,128]{5,4,3,2,1,0:T(8,128)(2,1)S(1)} %pad_maximum_fusion.2.pair.own, bf16[2,8,6,16,128]{4,3,2,1,0:T(8,128)(2,1)S(1)} %pad_maximum_fusion.10.refs_0_.keys, bf16[2,8,6,16,128]{4,3,2,1,0:T(8,128)(2,1)S(1)} %collective-permute-done.2.refs_1_, ...), custom_call_target="tpu_custom_call" | custom-call | flops 1358954496 | bytes 4718592 | tf_op jit(solution)/shard_map/pallas_call | solution.py:148
  84.8 2.2 %collective-permute-start.11 = (bf16[2,2,8,6,8,128]{5,4,3,2,1,0:T(8,128)(2,1)}, bf16[2,2,8,6,8,128]{5,4,3,2,1,0:T(8,128)(2,1)}, u32[]{:S(2)}, u32[]{:S(2)}) collective-permute-start(bf16[2,2,8,6,8,128]{5,4,3,2,1,0:T(8,128)(2,1)} %get-tuple-element.30), channel_id=1, source_target_pairs={{0,1},{1,0},{2,3},{3,2},{4,5},{5,4},{6,7},{7,6},{8,9},{9,8},{10,11... | collective-permute-start | bytes 1179656 | tf_op jit(solution)/shard_map/ppermute | solution.py:172
  88.2 2.8 %collective-permute-start.18 = (f32[3,6,2,128]{3,2,1,0:T(2,128)S(1)}, f32[3,6,2,128]{3,2,1,0:T(2,128)S(1)}, u32[]{:S(2)}, u32[]{:S(2)}) collective-permute-start(f32[3,6,2,128]{3,2,1,0:T(2,128)S(1)} %pad_maximum_fusion.12), channel_id=1, source_target_pairs={{0,8},{8,16},{16,24},{1,9},{9,17},{17,25},{2,10},{10,18},{18,26},{... | collective-permute-start | bytes 55304 | tf_op jit(solution)/shard_map/ppermute | solution.py:167
  91.0 1.9 %collective-permute-start.19 = (f32[3,6,2,128]{3,2,1,0:T(2,128)S(1)}, f32[3,6,2,128]{3,2,1,0:T(2,128)S(1)}, u32[]{:S(2)}, u32[]{:S(2)}) collective-permute-start(f32[3,6,2,128]{3,2,1,0:T(2,128)S(1)} %pad_maximum_fusion.13), channel_id=1, source_target_pairs={{8,0},{16,8},{24,16},{9,1},{17,9},{25,17},{10,2},{18,10},{26,18},{... | collective-permute-start | bytes 55304 | tf_op jit(solution)/shard_map/ppermute | solution.py:167
  92.9 3.2 %collective-permute-done.19.high_st = f32[3,6,2,128]{3,2,1,0:T(2,128)S(1)} collective-permute-done((f32[3,6,2,128]{3,2,1,0:T(2,128)S(1)}, f32[3,6,2,128]{3,2,1,0:T(2,128)S(1)}, u32[]{:S(2)}, u32[]{:S(2)}) %collective-permute-start.19) | collective-permute-done | bytes 18464 | tf_op jit(solution)/shard_map/ppermute | solution.py:167
  97.5 3.9 %shard_map.104 = bf16[2,2,8,3,16,128]{5,4,3,2,1,0:T(8,128)(2,1)S(1)} custom-call(bf16[2,8,6,16,128]{4,3,2,1,0:T(8,128)(2,1)S(1)} %pad_maximum_fusion.10.refs_0_.keys, bf16[2,8,6,16,128]{4,3,2,1,0:T(8,128)(2,1)S(1)} %pad_maximum_fusion.7.refs_5_.values, bf16[2,2,8,6,16,128]{5,4,3,2,1,0:T(8,128)(2,1)S(1)} %pad_maximum_fusion.2.pair.own, ...), custom_call_target="tpu_custom_call" | custom-call | flops 905969664 | bytes 2359296 | tf_op jit(solution)/shard_map/pallas_call | solution.py:148
  103.6 3.9 %shard_map.105 = bf16[2,2,8,3,16,128]{5,4,3,2,1,0:T(8,128)(2,1)S(1)} custom-call(bf16[2,8,6,16,128]{4,3,2,1,0:T(8,128)(2,1)S(1)} %pad_maximum_fusion.10.refs_0_.keys, bf16[2,8,6,16,128]{4,3,2,1,0:T(8,128)(2,1)S(1)} %pad_maximum_fusion.7.refs_5_.values, bf16[2,2,8,6,16,128]{5,4,3,2,1,0:T(8,128)(2,1)S(1)} %pad_maximum_fusion.2.pair.own, ...), custom_call_target="tpu_custom_call" | custom-call | flops 905969664 | bytes 2359296 | tf_op jit(solution)/shard_map/pallas_call | solution.py:148
  109.4 3.7 %collective-permute-done.21 = bf16[2,2,8,3,8,128]{5,4,3,2,1,0:T(8,128)(2,1)S(1)} collective-permute-done((bf16[2,2,8,3,8,128]{5,4,3,2,1,0:T(8,128)(2,1)S(1)}, bf16[2,2,8,3,8,128]{5,4,3,2,1,0:T(8,128)(2,1)S(1)}, u32[]{:S(2)}, u32[]{:S(2)}) %collective-permute-start.21) | collective-permute-done | bytes 196640 | tf_op jit(solution)/shard_map/ppermute | solution.py:172
  (125 shorter events, 19.3 us)
Async XLA Ops:
  0.6 5.5 %copy-start.20 = (bf16[4,3,9,2,9,1]{4,2,1,0,5,3:T(8,128)(2,1)S(1)}, bf16[4,3,9,2,9,1]{4,2,1,0,5,3:T(8,128)(2,1)}, u32[]{:S(2)}) copy-start(bf16[4,3,9,2,9,1]{4,2,1,0,5,3:T(8,128)(2,1)} %constant.214) | copy-start | bytes 11668
  1.8 6.3 %collective-permute-start = (bf16[2,8,6,8,128]{4,3,2,1,0:T(8,128)(2,1)S(1)}, bf16[2,8,6,8,128]{4,3,2,1,0:T(8,128)(2,1)S(1)}, u32[]{:S(2)}, u32[]{:S(2)}) collective-permute-start(bf16[2,8,6,8,128]{4,3,2,1,0:T(8,128)(2,1)S(1)} %get-tuple-element.51), channel_id=1, source_target_pairs={{0,1},{1,0},{2,3},{3,2},{4,5},{5,4},{6,7},{7,6},{8,9},{9,8},{10,11... | collective-permute-start | bytes 589832 | tf_op jit(solution)/shard_map/ppermute | solution.py:172
  4.1 10.6 %collective-permute-start.6 = (bf16[2,8,6,8,128]{4,3,2,1,0:T(8,128)(2,1)S(1)}, bf16[2,8,6,8,128]{4,3,2,1,0:T(8,128)(2,1)S(1)}, u32[]{:S(2)}, u32[]{:S(2)}) collective-permute-start(bf16[2,8,6,8,128]{4,3,2,1,0:T(8,128)(2,1)S(1)} %get-tuple-element.43), channel_id=1, source_target_pairs={{0,1},{1,0},{2,3},{3,2},{4,5},{5,4},{6,7},{7,6},{8,9},{9,8},{10,11... | collective-permute-start | bytes 589832 | tf_op jit(solution)/shard_map/ppermute | solution.py:172
  8.1 13.3 %collective-permute-start.2 = (bf16[2,8,6,16,128]{4,3,2,1,0:T(8,128)(2,1)S(1)}, bf16[2,8,6,16,128]{4,3,2,1,0:T(8,128)(2,1)S(1)}, u32[]{:S(2)}, u32[]{:S(2)}) collective-permute-start(bf16[2,8,6,16,128]{4,3,2,1,0:T(8,128)(2,1)S(1)} %pad_maximum_fusion.10.refs_0_.keys), channel_id=1, source_target_pairs={{0,2},{2,4},{4,6},{1,3},{3,5},{5,7},{8,10},{10,12},{12,14},{9,11},... | collective-permute-start | bytes 1179656 | tf_op jit(solution)/shard_map/ppermute | solution.py:167
  11.3 10.1 %collective-permute-start.3 = (bf16[2,8,6,16,128]{4,3,2,1,0:T(8,128)(2,1)S(1)}, bf16[2,8,6,16,128]{4,3,2,1,0:T(8,128)(2,1)S(1)}, u32[]{:S(2)}, u32[]{:S(2)}) collective-permute-start(bf16[2,8,6,16,128]{4,3,2,1,0:T(8,128)(2,1)S(1)} %pad_maximum_fusion.10.refs_0_.keys), channel_id=1, source_target_pairs={{2,0},{4,2},{6,4},{3,1},{5,3},{7,5},{10,8},{12,10},{14,12},{11,9},... | collective-permute-start | bytes 1179656 | tf_op jit(solution)/shard_map/ppermute | solution.py:167
  13.4 7.9 %collective-permute-start.1 = (bf16[2,2,8,6,8,128]{5,4,3,2,1,0:T(8,128)(2,1)S(1)}, bf16[2,2,8,6,8,128]{5,4,3,2,1,0:T(8,128)(2,1)S(1)}, u32[]{:S(2)}, u32[]{:S(2)}) collective-permute-start(bf16[2,2,8,6,8,128]{5,4,3,2,1,0:T(8,128)(2,1)S(1)} %pad_maximum_fusion.9), channel_id=1, source_target_pairs={{0,1},{1,0},{2,3},{3,2},{4,5},{5,4},{6,7},{7,6},{8,9},{9,8},{10,11... | collective-permute-start | bytes 1179656 | tf_op jit(solution)/shard_map/ppermute | solution.py:172
  14.8 23.6 %collective-permute-start.7 = (bf16[2,8,6,16,128]{4,3,2,1,0:T(8,128)(2,1)S(1)}, bf16[2,8,6,16,128]{4,3,2,1,0:T(8,128)(2,1)S(1)}, u32[]{:S(2)}, u32[]{:S(2)}) collective-permute-start(bf16[2,8,6,16,128]{4,3,2,1,0:T(8,128)(2,1)S(1)} %pad_maximum_fusion.7.refs_5_.values), channel_id=1, source_target_pairs={{0,2},{2,4},{4,6},{1,3},{3,5},{5,7},{8,10},{10,12},{12,14},{9,11},... | collective-permute-start | bytes 1179656 | tf_op jit(solution)/shard_map/ppermute | solution.py:167
  18.0 18.5 %collective-permute-start.8 = (bf16[2,8,6,16,128]{4,3,2,1,0:T(8,128)(2,1)S(1)}, bf16[2,8,6,16,128]{4,3,2,1,0:T(8,128)(2,1)S(1)}, u32[]{:S(2)}, u32[]{:S(2)}) collective-permute-start(bf16[2,8,6,16,128]{4,3,2,1,0:T(8,128)(2,1)S(1)} %pad_maximum_fusion.7.refs_5_.values), channel_id=1, source_target_pairs={{2,0},{4,2},{6,4},{3,1},{5,3},{7,5},{10,8},{12,10},{14,12},{11,9},... | collective-permute-start | bytes 1179656 | tf_op jit(solution)/shard_map/ppermute | solution.py:167
  21.4 5.5 %copy-start = (bf16[2,8,6,16,128]{4,3,2,1,0:T(8,128)(2,1)}, bf16[2,8,6,16,128]{4,3,2,1,0:T(8,128)(2,1)S(1)}, u32[]{:S(2)}) copy-start(bf16[2,8,6,16,128]{4,3,2,1,0:T(8,128)(2,1)S(1)} %collective-permute-done.3.refs_2_) | copy-start | bytes 1179652
  21.4 48.0 %collective-permute-start.12 = (bf16[2,2,8,6,16,128]{5,4,3,2,1,0:T(8,128)(2,1)S(1)}, bf16[2,2,8,6,16,128]{5,4,3,2,1,0:T(8,128)(2,1)S(1)}, u32[]{:S(2)}, u32[]{:S(2)}) collective-permute-start(bf16[2,2,8,6,16,128]{5,4,3,2,1,0:T(8,128)(2,1)S(1)} %pad_maximum_fusion.2.pair.own), channel_id=1, source_target_pairs={{0,2},{2,4},{4,6},{1,3},{3,5},{5,7},{8,10},{10,12},{12,14},{9,11},... | collective-permute-start | bytes 2359304 | tf_op jit(solution)/shard_map/ppermute | solution.py:167
  24.6 44.7 %collective-permute-start.13 = (bf16[2,2,8,6,16,128]{5,4,3,2,1,0:T(8,128)(2,1)S(1)}, bf16[2,2,8,6,16,128]{5,4,3,2,1,0:T(8,128)(2,1)S(1)}, u32[]{:S(2)}, u32[]{:S(2)}) collective-permute-start(bf16[2,2,8,6,16,128]{5,4,3,2,1,0:T(8,128)(2,1)S(1)} %pad_maximum_fusion.2.pair.own), channel_id=1, source_target_pairs={{2,0},{4,2},{6,4},{3,1},{5,3},{7,5},{10,8},{12,10},{14,12},{11,9},... | collective-permute-start | bytes 2359304 | tf_op jit(solution)/shard_map/ppermute | solution.py:167
  26.9 16.9 %collective-permute-start.4 = (bf16[3,8,6,16,128]{4,3,2,1,0:T(8,128)(2,1)S(1)}, bf16[3,8,6,16,128]{4,3,2,1,0:T(8,128)(2,1)S(1)}, u32[]{:S(2)}, u32[]{:S(2)}) collective-permute-start(bf16[3,8,6,16,128]{4,3,2,1,0:T(8,128)(2,1)S(1)} %pad_maximum_fusion.3), channel_id=1, source_target_pairs={{0,8},{8,16},{16,24},{1,9},{9,17},{17,25},{2,10},{10,18},{18,26},{... | collective-permute-start | bytes 1769480 | tf_op jit(solution)/shard_map/ppermute | solution.py:167
  36.4 11.7 %collective-permute-start.5 = (bf16[3,8,6,16,128]{4,3,2,1,0:T(8,128)(2,1)}, bf16[3,8,6,16,128]{4,3,2,1,0:T(8,128)(2,1)}, u32[]{:S(2)}, u32[]{:S(2)}) collective-permute-start(bf16[3,8,6,16,128]{4,3,2,1,0:T(8,128)(2,1)} %pad_maximum_fusion.4), channel_id=1, source_target_pairs={{8,0},{16,8},{24,16},{9,1},{17,9},{25,17},{10,2},{18,10},{26,18},{... | collective-permute-start | bytes 1769480 | tf_op jit(solution)/shard_map/ppermute | solution.py:167
  38.4 5.5 %copy-start.2 = (bf16[2,8,6,16,128]{4,3,2,1,0:T(8,128)(2,1)}, bf16[2,8,6,16,128]{4,3,2,1,0:T(8,128)(2,1)S(1)}, u32[]{:S(2)}) copy-start(bf16[2,8,6,16,128]{4,3,2,1,0:T(8,128)(2,1)S(1)} %collective-permute-done.7.refs_6_) | copy-start | bytes 1179652
  39.4 10.8 %collective-permute-start.9 = (bf16[3,8,6,16,128]{4,3,2,1,0:T(8,128)(2,1)}, bf16[3,8,6,16,128]{4,3,2,1,0:T(8,128)(2,1)}, u32[]{:S(2)}, u32[]{:S(2)}) collective-permute-start(bf16[3,8,6,16,128]{4,3,2,1,0:T(8,128)(2,1)} %pad_maximum_fusion.5), channel_id=1, source_target_pairs={{0,8},{8,16},{16,24},{1,9},{9,17},{17,25},{2,10},{10,18},{18,26},{... | collective-permute-start | bytes 1769480 | tf_op jit(solution)/shard_map/ppermute | solution.py:167
  44.7 11.5 %collective-permute-start.10 = (bf16[3,8,6,16,128]{4,3,2,1,0:T(8,128)(2,1)}, bf16[3,8,6,16,128]{4,3,2,1,0:T(8,128)(2,1)}, u32[]{:S(2)}, u32[]{:S(2)}) collective-permute-start(bf16[3,8,6,16,128]{4,3,2,1,0:T(8,128)(2,1)} %pad_maximum_fusion.6), channel_id=1, source_target_pairs={{8,0},{16,8},{24,16},{9,1},{17,9},{25,17},{10,2},{18,10},{26,18},{... | collective-permute-start | bytes 1769480 | tf_op jit(solution)/shard_map/ppermute | solution.py:167
  47.4 8.9 %copy-start.1 = (bf16[2,8,6,16,128]{4,3,2,1,0:T(8,128)(2,1)S(1)}, bf16[2,8,6,16,128]{4,3,2,1,0:T(8,128)(2,1)}, u32[]{:S(2)}) copy-start(bf16[2,8,6,16,128]{4,3,2,1,0:T(8,128)(2,1)} %copy-done) | copy-start | bytes 1179652
  47.4 8.9 %copy-start.3 = (bf16[2,8,6,16,128]{4,3,2,1,0:T(8,128)(2,1)S(1)}, bf16[2,8,6,16,128]{4,3,2,1,0:T(8,128)(2,1)}, u32[]{:S(2)}) copy-start(bf16[2,8,6,16,128]{4,3,2,1,0:T(8,128)(2,1)} %copy-done.2) | copy-start | bytes 1179652
  47.4 8.9 %copy-start.5 = (bf16[2,8,6,16,128]{4,3,2,1,0:T(8,128)(2,1)S(1)}, bf16[2,8,6,16,128]{4,3,2,1,0:T(8,128)(2,1)}, u32[]{:S(2)}) copy-start(bf16[2,8,6,16,128]{4,3,2,1,0:T(8,128)(2,1)} %copy-done.4) | copy-start | bytes 1179652
  47.4 8.9 %copy-start.10 = (f32[32,1152]{1,0:T(8,128)S(1)}, f32[32,1152]{1,0:T(8,128)}, u32[]{:S(2)}) copy-start(f32[32,1152]{1,0:T(8,128)} %get-tuple-element.57) | copy-start | bytes 442372
  64.0 22.9 %collective-permute-start.16 = (f32[2,6,2,128]{3,2,1,0:T(2,128)S(1)}, f32[2,6,2,128]{3,2,1,0:T(2,128)S(1)}, u32[]{:S(2)}, u32[]{:S(2)}) collective-permute-start(f32[2,6,2,128]{3,2,1,0:T(2,128)S(1)} %get-tuple-element.19.refs_11_.own_st), channel_id=1, source_target_pairs={{0,2},{2,4},{4,6},{1,3},{3,5},{5,7},{8,10},{10,12},{12,14},{9,11},... | collective-permute-start | bytes 36872 | tf_op jit(solution)/shard_map/ppermute | solution.py:167
  67.2 19.8 %collective-permute-start.17 = (f32[2,6,2,128]{3,2,1,0:T(2,128)S(1)}, f32[2,6,2,128]{3,2,1,0:T(2,128)S(1)}, u32[]{:S(2)}, u32[]{:S(2)}) collective-permute-start(f32[2,6,2,128]{3,2,1,0:T(2,128)S(1)} %get-tuple-element.19.refs_11_.own_st), channel_id=1, source_target_pairs={{2,0},{4,2},{6,4},{3,1},{5,3},{7,5},{10,8},{12,10},{14,12},{11,9},... | collective-permute-start | bytes 36872 | tf_op jit(solution)/shard_map/ppermute | solution.py:167
  70.8 25.3 %collective-permute-start.14 = (bf16[3,2,8,6,16,128]{5,4,3,2,1,0:T(8,128)(2,1)}, bf16[3,2,8,6,16,128]{5,4,3,2,1,0:T(8,128)(2,1)}, u32[]{:S(2)}, u32[]{:S(2)}) collective-permute-start(bf16[3,2,8,6,16,128]{5,4,3,2,1,0:T(8,128)(2,1)} %pad_maximum_fusion), channel_id=1, source_target_pairs={{0,8},{8,16},{16,24},{1,9},{9,17},{17,25},{2,10},{10,18},{18,26},{... | collective-permute-start | bytes 3538952 | tf_op jit(solution)/shard_map/ppermute | solution.py:167
  73.1 4.3 %copy-start.8 = (bf16[3,8,6,16,128]{4,3,2,1,0:T(8,128)(2,1)S(1)}, bf16[3,8,6,16,128]{4,3,2,1,0:T(8,128)(2,1)}, u32[]{:S(2)}) copy-start(bf16[3,8,6,16,128]{4,3,2,1,0:T(8,128)(2,1)} %copy-done.6) | copy-start | bytes 1769476
  74.3 21.8 %collective-permute-start.15 = (bf16[3,2,8,6,16,128]{5,4,3,2,1,0:T(8,128)(2,1)}, bf16[3,2,8,6,16,128]{5,4,3,2,1,0:T(8,128)(2,1)}, u32[]{:S(2)}, u32[]{:S(2)}) collective-permute-start(bf16[3,2,8,6,16,128]{5,4,3,2,1,0:T(8,128)(2,1)} %pad_maximum_fusion.1), channel_id=1, source_target_pairs={{8,0},{16,8},{24,16},{9,1},{17,9},{25,17},{10,2},{18,10},{26,18},{... | collective-permute-start | bytes 3538952 | tf_op jit(solution)/shard_map/ppermute | solution.py:167
  83.7 12.4 %copy-start.9 = (f32[32,1152]{1,0:T(8,128)S(1)}, f32[32,1152]{1,0:T(8,128)}, u32[]{:S(2)}) copy-start(f32[32,1152]{1,0:T(8,128)} %get-tuple-element.56) | copy-start | bytes 442372
  84.8 6.2 %copy-start.15 = (bf16[2,2,8,12,8,128]{5,4,3,2,1,0:T(8,128)(2,1)}, bf16[2,2,8,12,8,128]{5,4,3,2,1,0:T(8,128)(2,1)S(1)}, u32[]{:S(2)}) copy-start(bf16[2,2,8,12,8,128]{5,4,3,2,1,0:T(8,128)(2,1)S(1)} %get-tuple-element.31) | copy-start | bytes 2359300
  84.8 17.1 %collective-permute-start.11 = (bf16[2,2,8,6,8,128]{5,4,3,2,1,0:T(8,128)(2,1)}, bf16[2,2,8,6,8,128]{5,4,3,2,1,0:T(8,128)(2,1)}, u32[]{:S(2)}, u32[]{:S(2)}) collective-permute-start(bf16[2,2,8,6,8,128]{5,4,3,2,1,0:T(8,128)(2,1)} %get-tuple-element.30), channel_id=1, source_target_pairs={{0,1},{1,0},{2,3},{3,2},{4,5},{5,4},{6,7},{7,6},{8,9},{9,8},{10,11... | collective-permute-start | bytes 1179656 | tf_op jit(solution)/shard_map/ppermute | solution.py:172
  88.2 4.8 %collective-permute-start.18 = (f32[3,6,2,128]{3,2,1,0:T(2,128)S(1)}, f32[3,6,2,128]{3,2,1,0:T(2,128)S(1)}, u32[]{:S(2)}, u32[]{:S(2)}) collective-permute-start(f32[3,6,2,128]{3,2,1,0:T(2,128)S(1)} %pad_maximum_fusion.12), channel_id=1, source_target_pairs={{0,8},{8,16},{16,24},{1,9},{9,17},{17,25},{2,10},{10,18},{18,26},{... | collective-permute-start | bytes 55304 | tf_op jit(solution)/shard_map/ppermute | solution.py:167
  91.0 5.1 %collective-permute-start.19 = (f32[3,6,2,128]{3,2,1,0:T(2,128)S(1)}, f32[3,6,2,128]{3,2,1,0:T(2,128)S(1)}, u32[]{:S(2)}, u32[]{:S(2)}) collective-permute-start(f32[3,6,2,128]{3,2,1,0:T(2,128)S(1)} %pad_maximum_fusion.13), channel_id=1, source_target_pairs={{8,0},{16,8},{24,16},{9,1},{17,9},{25,17},{10,2},{18,10},{26,18},{... | collective-permute-start | bytes 55304 | tf_op jit(solution)/shard_map/ppermute | solution.py:167
  101.7 5.9 %collective-permute-start.20 = (bf16[2,2,8,3,8,128]{5,4,3,2,1,0:T(8,128)(2,1)S(1)}, bf16[2,2,8,3,8,128]{5,4,3,2,1,0:T(8,128)(2,1)S(1)}, u32[]{:S(2)}, u32[]{:S(2)}) collective-permute-start(bf16[2,2,8,3,8,128]{5,4,3,2,1,0:T(8,128)(2,1)S(1)} %get-tuple-element.34), channel_id=1, source_target_pairs={{0,1},{1,0},{2,3},{3,2},{4,5},{5,4},{6,7},{7,6},{8,9},{9,8},{10,11... | collective-permute-start | bytes 589832 | tf_op jit(solution)/shard_map/ppermute | solution.py:172
  107.7 5.4 %collective-permute-start.21 = (bf16[2,2,8,3,8,128]{5,4,3,2,1,0:T(8,128)(2,1)S(1)}, bf16[2,2,8,3,8,128]{5,4,3,2,1,0:T(8,128)(2,1)S(1)}, u32[]{:S(2)}, u32[]{:S(2)}) collective-permute-start(bf16[2,2,8,3,8,128]{5,4,3,2,1,0:T(8,128)(2,1)S(1)} %get-tuple-element.32), channel_id=1, source_target_pairs={{0,1},{1,0},{2,3},{3,2},{4,5},{5,4},{6,7},{7,6},{8,9},{9,8},{10,11... | collective-permute-start | bytes 589832 | tf_op jit(solution)/shard_map/ppermute | solution.py:172
  (12 other events, 20.2 us)

commit v4 on v3

--- a/solution.py
+++ b/solution.py
@@ -30,31 +30,30 @@
     return jnp.broadcast_to(bias[None], (tokens // columns, columns, width)).reshape(tokens, width)
 
 
-def fill_band(band, own, before, after, low, high, at_of):
+def fill_band(band, own, before, after, low, high, side, edge):
     frames = own.shape[0]
     tokens = own.shape[-4] * own.shape[-2]
     for at in range(frames + 2):
         for row, beside in enumerate((before, own, after)):
             if at == 0:
-                tiles = low[at_of(row)]
+                tiles = low[edge(row)]
             elif at == frames + 1:
-                tiles = high[at_of(row)]
+                tiles = high[edge(row)]
             else:
-                tiles = beside[at_of(at - 1)]
+                tiles = beside[side(at - 1)]
             band[pl.ds((3 * at + row) * tokens, tokens), :] = flat(tiles)
 
 
-def single(at):
-    return at
+def fill_halo(halo, key_all, value_all):
+    fill_band(key_all, *halo[:3], *halo[6:], lambda at: at, lambda row: (row, 0))
+    fill_band(value_all, *halo[3:6], *halo[6:], lambda at: at, lambda row: (row, 1))
 
 
 def attend_kernel(scaling, pair, *refs):
-    keys, values = refs[:5], refs[5:10]
-    bias, attended, stats, key_all, value_all = refs[10:]
+    bias, attended, stats, key_all, value_all = refs[8:]
     frames, _, rows, _, columns, dim = pair.shape
     tokens = rows * columns
-    fill_band(key_all, *keys, single)
-    fill_band(value_all, *values, single)
+    fill_halo(refs[:8], key_all, value_all)
     windows = [pl.ds(3 * at * tokens, 9 * tokens) for at in range(frames)]
     scores = [
         dot(flat(pair[at, 0]), key_all[windows[at], :], NT) * (scaling * LOG2E) + spread(bias[at], tokens)
@@ -75,12 +74,10 @@
 
 
 def query_kernel(scaling, pair, *refs):
-    keys, values = refs[:5], refs[5:10]
-    attended, stats, bias, grads, key_all, value_all = refs[10:]
+    attended, stats, bias, grads, key_all, value_all = refs[8:]
     frames, _, rows, _, columns, dim = pair.shape
     tokens = rows * columns
-    fill_band(key_all, *keys, single)
-    fill_band(value_all, *values, single)
+    fill_halo(refs[:8], key_all, value_all)
     windows = [pl.ds(3 * at * tokens, 9 * tokens) for at in range(frames)]
 
     def column(at, which):
@@ -98,22 +95,17 @@
         grads[1, at, :, 0] = query_grad.astype(jnp.bfloat16).reshape(rows, columns, dim)
 
 
-def back_kernel(
-    scaling, keys, values, own, before, after, low, high, own_st, before_st, after_st, low_st, high_st, bias,
-    grads, query_all, grad_all
-):
+def back_kernel(scaling, spots, keys, values, own, before, after, low, high, *refs):
+    stats, (bias, grads, query_all, grad_all) = refs[:9], refs[9:]
     frames, rows, _, columns, dim = keys.shape
     tokens = rows * columns
     halo = (own, before, after, low, high)
-    fill_band(query_all, *halo, lambda at: (at, 0))
-    fill_band(grad_all, *halo, lambda at: (at, 1))
+    fill_band(query_all, *halo, lambda at: (at, 0), lambda row: (row, 0))
+    fill_band(grad_all, *halo, lambda at: (at, 1), lambda row: (row, 1))
 
     def stat_row(at, row, which):
-        if at == 0:
-            return low_st[row, 0, which : which + 1]
-        if at == frames + 1:
-            return high_st[row, 0, which : which + 1]
-        return (before_st, own_st, after_st)[row][at - 1, 0, which : which + 1]
+        device = 0 if at == 0 else 2 if at == frames + 1 else 1
+        return stats[3 * device + row][0, 0, (at - 1) % frames, 0, which : which + 1]
 
     def stat_band(at, which):
         parts = [stat_row(at + step, row, which) for step in range(3) for row in range(3)]
@@ -134,32 +126,43 @@
 
 def head_spec(shape, dim, first):
     block = shape[:dim] + (1,) + shape[dim + 1 :]
-    return pl.BlockSpec(block, lambda head: (0,) * dim + (head + first,) + (0,) * (len(shape) - dim - 1))
-
-
-def whole_spec(shape):
-    return pl.BlockSpec(shape, lambda head: (0,) * len(shape))
-
-
-def run(kernel, scaling, tiles, stats, bias, outs, first, count, products):
+    return pl.BlockSpec(block, lambda head, *_: (0,) * dim + (head + first,) + (0,) * (len(shape) - dim - 1))
+
+
+def near_spec(shape, first, at):
+    block = (1, 1, shape[2], 1) + shape[4:]
+    frame, row = at // 3, at % 3
+    return pl.BlockSpec(block, lambda head, spots: (spots[0, frame], spots[1, row], 0, head + first, 0, 0))
+
+
+def run(kernel, scaling, tiles, stats, bias, outs, first, count, products, spots=None):
     rows, _, columns, dim = tiles[0].shape[-4:]
     frames = tiles[0].shape[0]
     tokens = rows * columns
+    bias_spec = pl.BlockSpec(bias.shape, lambda head, *_: (0,) * bias.ndim)
+    in_specs = [head_spec(part.shape, part.ndim - 3, first) for part in tiles]
+    prefetched = () if spots is None else (spots,)
+    if spots is None:
+        in_specs += [head_spec(part.shape, part.ndim - 3, first) for part in stats]
+    else:
+        in_specs += [near_spec(part.shape, first, at) for at, part in enumerate(stats)]
     return pl.pallas_call(
         functools.partial(kernel, scaling),
-        grid=(count,),
+        grid_spec=pltpu.PrefetchScalarGridSpec(
+            num_scalar_prefetch=len(prefetched),
+            grid=(count,),
+            in_specs=in_specs + [bias_spec],
+            out_specs=tuple(head_spec(out.shape, len(out.shape) - 3, 0) for out in outs),
+            scratch_shapes=[pltpu.VMEM((3 * (frames + 2) * tokens, dim), jnp.bfloat16)] * 2,
+        ),
         out_shape=tuple(outs),
-        in_specs=[head_spec(part.shape, part.ndim - 3, first) for part in tuple(tiles) + tuple(stats)]
-        + [whole_spec(bias.shape)],
-        out_specs=tuple(head_spec(out.shape, len(out.shape) - 3, 0) for out in outs),
-        scratch_shapes=[pltpu.VMEM((3 * (frames + 2) * tokens, dim), jnp.bfloat16)] * 2,
         compiler_params=pltpu.CompilerParams(vmem_limit_bytes=32 * 2**20),
         cost_estimate=pl.CostEstimate(
             flops=frames * count * 2 * products * tokens * 9 * tokens * dim,
             bytes_accessed=count * (frames + 2) * 3 * 2 * tokens * dim * 2,
             transcendentals=frames * count * tokens * 9 * tokens,
         ),
-    )(*tiles, *stats, bias)
+    )(*prefetched, *tiles, *stats, bias)
 
 
 def step_along(tensor, axis, sign):
@@ -173,10 +176,14 @@
 
 
 def frame_edges(before, own, after):
-    last = own.shape[0] - 1
-    low = step_along(jnp.stack([before[last], own[last], after[last]]), "frame", 1)
-    high = step_along(jnp.stack([before[0], own[0], after[0]]), "frame", -1)
-    return low, high
+    return step_along(jnp.stack([before[-1], own[-1], after[-1]]), "frame", 1), step_along(
+        jnp.stack([before[0], own[0], after[0]]), "frame", -1
+    )
+
+
+def near_places(axis):
+    at = lax.axis_index(axis) + jnp.arange(3, dtype=jnp.int32) - 1
+    return jnp.clip(at, 0, lax.axis_size(axis) - 1)
 
 
 def row_sides(own):
@@ -257,17 +264,19 @@
     columns = columns_here * size
     tokens = rows * columns
 
-    def surround(own):
-        sides = row_sides(own)
-        return (own,) + sides + frame_edges(sides[0], own, sides[1])
-
     def out_shape(lead, count):
         return jax.ShapeDtypeStruct(lead + (frames, rows, count, columns, dim), jnp.bfloat16)
 
     stat_shape = jax.ShapeDtypeStruct((frames, groups, 2, tokens), jnp.float32)
     key_sides = row_sides(key)
     pair, key_sides = lax.optimization_barrier((pair, key_sides))
-    around = (key,) + key_sides + frame_edges(key_sides[0], key, key_sides[1]) + surround(value)
+    value_sides = row_sides(value)
+    key_rows = (key_sides[0], key, key_sides[1])
+    value_rows = (value_sides[0], value, value_sides[1])
+    low, high = frame_edges(*[jnp.stack(two, 1) for two in zip(key_rows, value_rows)])
+    around = (key,) + key_sides + (value,) + value_sides + (low, high)
+    pair_sides = row_sides(pair)
+    pair_around = (pair,) + pair_sides + frame_edges(pair_sides[0], pair, pair_sides[1])
     attended, stats = run(
         attend_kernel, scaling, (pair,) + around, (), front_bias, [out_shape((), groups), stat_shape], 0, groups, 2
     )
@@ -275,14 +284,14 @@
         query_kernel, scaling, (pair,) + around + (attended,), (stats,), front_bias, [out_shape((2,), groups)],
         0, groups, 3
     )
-    pair_around = surround(pair)
-    stats_around = surround(stats)
+    gathered = lax.all_gather(stats, ("frame", "row")).reshape((lax.axis_size("frame"), lax.axis_size("row")) + stats.shape)
+    spots = jnp.stack([near_places("frame"), near_places("row")])
     halves = [(0, groups - groups // 2), (groups - groups // 2, groups // 2)]
     parts = []
     for first, count in halves:
         (back_grads,) = run(
-            back_kernel, scaling, (key, value) + pair_around, stats_around, back_bias, [out_shape((2,), count)],
-            first, count, 4
+            back_kernel, scaling, (key, value) + pair_around, (gathered,) * 9, back_bias,
+            [out_shape((2,), count)], first, count, 4, spots
         )
         parts.append((first, back_grads))
     return from_heads([(0, front_grads)]) + from_heads(parts)

time: 115 us -> 126 us (1.096)
  the two profiles are of different devices: /device:TPU:9 before, /device:TPU:0 now
where the time goes in v4:
time: 126 us
  blocking collectives  33.6 us (27%)
  starting transfers between devices  30.2 us (24%)
  waiting for transfers between devices  22.1 us (18%)
  Pallas kernels  19.8 us (16%)
  local copies, waits for them, and re-layouts  11.5 us (9%)
  other arithmetic  5.63 us (4%)
  matrix products  1.79 us (1%)
    all_gather x1, blocking collectives, on_device(): lax.all_gather(stats, ('frame', 'row'))  33.6 us
    ppermute x10, starting transfers between devices, step_along(): lax.ppermute(tensor, axis, [(i, i + sign) for i in range(size) if 0 <= i...  23.2 us
    pallas_call x4, Pallas kernels, run(): pl.pallas_call(functools.partial(kernel, scaling), grid_spec=pltpu.Prefet...  19.8 us
    ppermute x10, waiting for transfers between devices, step_along(): lax.ppermute(tensor, axis, [(i, i + sign) for i in range(size) if 0 <= i...  14.6 us
    ppermute x6, waiting for transfers between devices, turn(): lax.ppermute(tensor, 'head', [(i, (i + shift) % size) for i in range(size)])  7.52 us
    ppermute x6, starting transfers between devices, turn(): lax.ppermute(tensor, 'head', [(i, (i + shift) % size) for i in range(size)])  6.99 us
    ppermute x2, local copies, waits for them, and re-layouts, step_along(): lax.ppermute(tensor, axis, [(i, i + sign) for i in range(size) if 0 <= i...  3.07 us
  transfers between devices with their start and end apart: 16, of which 7 were waited for; matrix products, arithmetic and copies ran while one was open for 13% of the time, Pallas kernels for 16%

profile of v4, /device:TPU:0, one launch (start us, length us, event | category | flops | bytes accessed | tf_op | source)
XLA Modules:
  0.0 125.9 jit_solution(16687823834285458564)
XLA Ops:
  0.7 1.1 dynamic-slice_bitcast_fusion.3
  1.8 3.0 %collective-permute-start = (bf16[2,8,6,8,128]{4,3,2,1,0:T(8,128)(2,1)S(1)}, bf16[2,8,6,8,128]{4,3,2,1,0:T(8,128)(2,1)S(1)}, u32[]{:S(2)}, u32[]{:S(2)}) collective-permute-start(bf16[2,8,6,8,128]{4,3,2,1,0:T(8,128)(2,1)S(1)} %get-tuple-element.41), channel_id=1, source_target_pairs={{0,1},{1,0},{2,3},{3,2},{4,5},{5,4},{6,7},{7,6},{8,9},{9,8},{10,11... | collective-permute-start | bytes 589832 | tf_op jit(solution)/shard_map/ppermute | solution.py:175
  4.8 1.1 dynamic-slice_bitcast_fusion.1
  10.6 4.1 %collective-permute-start.2 = (bf16[2,8,6,16,128]{4,3,2,1,0:T(8,128)(2,1)S(1)}, bf16[2,8,6,16,128]{4,3,2,1,0:T(8,128)(2,1)S(1)}, u32[]{:S(2)}, u32[]{:S(2)}) collective-permute-start(bf16[2,8,6,16,128]{4,3,2,1,0:T(8,128)(2,1)S(1)} %pad_maximum_fusion.7.refs_0_.keys), channel_id=1, source_target_pairs={{0,2},{2,4},{4,6},{1,3},{3,5},{5,7},{8,10},{10,12},{12,14},{9,11},... | collective-permute-start | bytes 1179656 | tf_op jit(solution)/shard_map/ppermute | solution.py:170
  14.6 1.3 %collective-permute-start.3 = (bf16[2,8,6,16,128]{4,3,2,1,0:T(8,128)(2,1)S(1)}, bf16[2,8,6,16,128]{4,3,2,1,0:T(8,128)(2,1)S(1)}, u32[]{:S(2)}, u32[]{:S(2)}) collective-permute-start(bf16[2,8,6,16,128]{4,3,2,1,0:T(8,128)(2,1)S(1)} %pad_maximum_fusion.7.refs_0_.keys), channel_id=1, source_target_pairs={{2,0},{4,2},{6,4},{3,1},{5,3},{7,5},{10,8},{12,10},{14,12},{11,9},... | collective-permute-start | bytes 1179656 | tf_op jit(solution)/shard_map/ppermute | solution.py:170
  15.9 1.6 %collective-permute-start.1 = (bf16[2,2,8,6,8,128]{5,4,3,2,1,0:T(8,128)(2,1)S(1)}, bf16[2,2,8,6,8,128]{5,4,3,2,1,0:T(8,128)(2,1)S(1)}, u32[]{:S(2)}, u32[]{:S(2)}) collective-permute-start(bf16[2,2,8,6,8,128]{5,4,3,2,1,0:T(8,128)(2,1)S(1)} %pad_maximum_fusion.6), channel_id=1, source_target_pairs={{0,1},{1,0},{2,3},{3,2},{4,5},{5,4},{6,7},{7,6},{8,9},{9,8},{10,11... | collective-permute-start | bytes 1179656 | tf_op jit(solution)/shard_map/ppermute | solution.py:175
  17.6 4.6 %collective-permute-start.5 = (bf16[2,8,6,16,128]{4,3,2,1,0:T(8,128)(2,1)S(1)}, bf16[2,8,6,16,128]{4,3,2,1,0:T(8,128)(2,1)S(1)}, u32[]{:S(2)}, u32[]{:S(2)}) collective-permute-start(bf16[2,8,6,16,128]{4,3,2,1,0:T(8,128)(2,1)S(1)} %get-tuple-element.37.refs_3_.values), channel_id=1, source_target_pairs={{0,2},{2,4},{4,6},{1,3},{3,5},{5,7},{8,10},{10,12},{12,14},{9,11},... | collective-permute-start | bytes 1179656 | tf_op jit(solution)/shard_map/ppermute | solution.py:170
  22.2 1.3 %collective-permute-start.6 = (bf16[2,8,6,16,128]{4,3,2,1,0:T(8,128)(2,1)S(1)}, bf16[2,8,6,16,128]{4,3,2,1,0:T(8,128)(2,1)S(1)}, u32[]{:S(2)}, u32[]{:S(2)}) collective-permute-start(bf16[2,8,6,16,128]{4,3,2,1,0:T(8,128)(2,1)S(1)} %get-tuple-element.37.refs_3_.values), channel_id=1, source_target_pairs={{2,0},{4,2},{6,4},{3,1},{5,3},{7,5},{10,8},{12,10},{14,12},{11,9},... | collective-permute-start | bytes 1179656 | tf_op jit(solution)/shard_map/ppermute | solution.py:170
  25.3 2.0 %collective-permute-done.3.refs_2_ = bf16[2,8,6,16,128]{4,3,2,1,0:T(8,128)(2,1)S(1)} collective-permute-done((bf16[2,8,6,16,128]{4,3,2,1,0:T(8,128)(2,1)S(1)}, bf16[2,8,6,16,128]{4,3,2,1,0:T(8,128)(2,1)S(1)}, u32[]{:S(2)}, u32[]{:S(2)}) %collective-permute-start.3) | collective-permute-done | bytes 393248 | tf_op jit(solution)/shard_map/ppermute | solution.py:170
  27.4 3.5 %collective-permute-start.10 = (bf16[2,2,8,6,16,128]{5,4,3,2,1,0:T(8,128)(2,1)S(1)}, bf16[2,2,8,6,16,128]{5,4,3,2,1,0:T(8,128)(2,1)S(1)}, u32[]{:S(2)}, u32[]{:S(2)}) collective-permute-start(bf16[2,2,8,6,16,128]{5,4,3,2,1,0:T(8,128)(2,1)S(1)} %pad_maximum_fusion.4.pair.own), channel_id=1, source_target_pairs={{0,2},{2,4},{4,6},{1,3},{3,5},{5,7},{8,10},{10,12},{12,14},{9,11},... | collective-permute-start | bytes 2359304 | tf_op jit(solution)/shard_map/ppermute | solution.py:170
  30.9 1.3 %collective-permute-start.11 = (bf16[2,2,8,6,16,128]{5,4,3,2,1,0:T(8,128)(2,1)S(1)}, bf16[2,2,8,6,16,128]{5,4,3,2,1,0:T(8,128)(2,1)S(1)}, u32[]{:S(2)}, u32[]{:S(2)}) collective-permute-start(bf16[2,2,8,6,16,128]{5,4,3,2,1,0:T(8,128)(2,1)S(1)} %pad_maximum_fusion.4.pair.own), channel_id=1, source_target_pairs={{2,0},{4,2},{6,4},{3,1},{5,3},{7,5},{10,8},{12,10},{14,12},{11,9},... | collective-permute-start | bytes 2359304 | tf_op jit(solution)/shard_map/ppermute | solution.py:170
  32.2 3.9 %collective-permute-done.6.refs_5_ = bf16[2,8,6,16,128]{4,3,2,1,0:T(8,128)(2,1)S(1)} collective-permute-done((bf16[2,8,6,16,128]{4,3,2,1,0:T(8,128)(2,1)S(1)}, bf16[2,8,6,16,128]{4,3,2,1,0:T(8,128)(2,1)S(1)}, u32[]{:S(2)}, u32[]{:S(2)}) %collective-permute-start.6) | collective-permute-done | bytes 393248 | tf_op jit(solution)/shard_map/ppermute | solution.py:170
  36.2 1.2 pad_maximum_fusion.1
  37.4 2.3 %collective-permute-start.7 = (bf16[3,2,8,6,16,128]{5,4,3,2,0,1:T(8,128)(2,1)}, bf16[3,2,8,6,16,128]{5,4,3,2,0,1:T(8,128)(2,1)}, u32[]{:S(2)}, u32[]{:S(2)}) collective-permute-start(bf16[3,2,8,6,16,128]{5,4,3,2,0,1:T(8,128)(2,1)} %pad_maximum_fusion.1), channel_id=1, source_target_pairs={{0,8},{8,16},{16,24},{1,9},{9,17},{17,25},{2,10},{10,18},{18,26},{... | collective-permute-start | bytes 3538952 | tf_op jit(solution)/shard_map/ppermute | solution.py:170
  39.7 1.2 fusion.8
  40.9 1.3 %collective-permute-start.8 = (bf16[3,2,8,6,16,128]{5,4,3,2,0,1:T(8,128)(2,1)}, bf16[3,2,8,6,16,128]{5,4,3,2,0,1:T(8,128)(2,1)}, u32[]{:S(2)}, u32[]{:S(2)}) collective-permute-start(bf16[3,2,8,6,16,128]{5,4,3,2,0,1:T(8,128)(2,1)} %fusion.8), channel_id=1, source_target_pairs={{8,0},{16,8},{24,16},{9,1},{17,9},{25,17},{10,2},{18,10},{26,18},{... | collective-permute-start | bytes 3538952 | tf_op jit(solution)/shard_map/ppermute | solution.py:170
  42.4 8.6 %collective-permute-done.11.after = bf16[2,2,8,6,16,128]{5,4,3,2,1,0:T(8,128)(2,1)S(1)} collective-permute-done((bf16[2,2,8,6,16,128]{5,4,3,2,1,0:T(8,128)(2,1)S(1)}, bf16[2,2,8,6,16,128]{5,4,3,2,1,0:T(8,128)(2,1)S(1)}, u32[]{:S(2)}, u32[]{:S(2)}) %collective-permute-start.11) | collective-permute-done | bytes 786464 | tf_op jit(solution)/shard_map/ppermute | solution.py:170
  51.3 1.1 pad_maximum_fusion.2
  52.4 2.3 %collective-permute-start.12 = (bf16[3,2,8,6,16,128]{5,4,3,2,1,0:T(8,128)(2,1)}, bf16[3,2,8,6,16,128]{5,4,3,2,1,0:T(8,128)(2,1)}, u32[]{:S(2)}, u32[]{:S(2)}) collective-permute-start(bf16[3,2,8,6,16,128]{5,4,3,2,1,0:T(8,128)(2,1)} %pad_maximum_fusion.2), channel_id=1, source_target_pairs={{0,8},{8,16},{16,24},{1,9},{9,17},{17,25},{2,10},{10,18},{18,26},{... | collective-permute-start | bytes 3538952 | tf_op jit(solution)/shard_map/ppermute | solution.py:170
  54.8 1.2 pad_maximum_fusion.3
  55.9 1.3 %collective-permute-start.13 = (bf16[3,2,8,6,16,128]{5,4,3,2,1,0:T(8,128)(2,1)}, bf16[3,2,8,6,16,128]{5,4,3,2,1,0:T(8,128)(2,1)}, u32[]{:S(2)}, u32[]{:S(2)}) collective-permute-start(bf16[3,2,8,6,16,128]{5,4,3,2,1,0:T(8,128)(2,1)} %pad_maximum_fusion.3), channel_id=1, source_target_pairs={{8,0},{16,8},{24,16},{9,1},{17,9},{25,17},{10,2},{18,10},{26,18},{... | collective-permute-start | bytes 3538952 | tf_op jit(solution)/shard_map/ppermute | solution.py:170
  57.3 1.0 fusion.40
  58.3 1.5 %copy.31.refs_6_ = bf16[3,2,8,6,16,128]{5,4,3,2,1,0:T(8,128)(2,1)S(1)} copy(bf16[3,2,8,6,16,128]{5,4,3,2,0,1:T(8,128)(2,1)} %collective-permute-done.7) | data formatting | bytes 2359296 | tf_op jit(solution)/shard_map/ppermute | solution.py:170
  59.8 1.6 %copy.32.refs_7_ = bf16[3,2,8,6,16,128]{5,4,3,2,1,0:T(8,128)(2,1)S(1)} copy(bf16[3,2,8,6,16,128]{5,4,3,2,0,1:T(8,128)(2,1)} %collective-permute-done.8) | data formatting | bytes 2359296 | tf_op jit(solution)/shard_map/ppermute | solution.py:170
  61.5 5.7 %shard_map.102 = (bf16[2,8,6,16,128]{4,3,2,1,0:T(8,128)(2,1)S(1)}, f32[2,6,2,128]{3,2,1,0:T(2,128)S(1)}) custom-call(bf16[2,2,8,6,16,128]{5,4,3,2,1,0:T(8,128)(2,1)S(1)} %pad_maximum_fusion.4.pair.own, bf16[2,8,6,16,128]{4,3,2,1,0:T(8,128)(2,1)S(1)} %pad_maximum_fusion.7.refs_0_.keys, bf16[2,8,6,16,128]{4,3,2,1,0:T(8,128)(2,1)S(1)} %collective-permute-done.2.refs_1_, ...), custom_call_target="tpu_custom_call" | custom-call | flops 905969664 | bytes 4718592 | tf_op jit(solution)/shard_map/pallas_call | solution.py:149
  67.2 5.0 %shard_map.103 = bf16[2,2,8,6,16,128]{5,4,3,2,1,0:T(8,128)(2,1)S(1)} custom-call(bf16[2,2,8,6,16,128]{5,4,3,2,1,0:T(8,128)(2,1)S(1)} %pad_maximum_fusion.4.pair.own, bf16[2,8,6,16,128]{4,3,2,1,0:T(8,128)(2,1)S(1)} %pad_maximum_fusion.7.refs_0_.keys, bf16[2,8,6,16,128]{4,3,2,1,0:T(8,128)(2,1)S(1)} %collective-permute-done.2.refs_1_, ...), custom_call_target="tpu_custom_call" | custom-call | flops 1358954496 | bytes 4718592 | tf_op jit(solution)/shard_map/pallas_call | solution.py:149
  72.5 1.6 %collective-permute-start.9 = (bf16[2,2,8,6,8,128]{5,4,3,2,1,0:T(8,128)(2,1)S(1)}, bf16[2,2,8,6,8,128]{5,4,3,2,1,0:T(8,128)(2,1)S(1)}, u32[]{:S(2)}, u32[]{:S(2)}) collective-permute-start(bf16[2,2,8,6,8,128]{5,4,3,2,1,0:T(8,128)(2,1)S(1)} %get-tuple-element.30), channel_id=1, source_target_pairs={{0,1},{1,0},{2,3},{3,2},{4,5},{5,4},{6,7},{7,6},{8,9},{9,8},{10,11... | collective-permute-start | bytes 1179656 | tf_op jit(solution)/shard_map/ppermute | solution.py:175
  74.0 33.6 %all-gather = f32[32,6,2,128]{3,2,1,0:T(2,128)S(1)} all-gather(f32[2,6,2,128]{3,2,1,0:T(2,128)S(1)} %get-tuple-element.19.refs_9_), channel_id=2, replica_groups=mesh['frame'=4,'row'=4,'head'=2] {'frame','row'}, dimensions={0}, use_global_device_ids=true | all-gather | bytes 208896 | tf_op jit(solution)/shard_map/all_gather | solution.py:287
  107.6 4.6 %shard_map.104 = bf16[2,2,8,3,16,128]{5,4,3,2,1,0:T(8,128)(2,1)S(1)} custom-call(s32[2,3]{1,0:T(2,128)S(1)} %pad_add_fusion.spots, bf16[2,8,6,16,128]{4,3,2,1,0:T(8,128)(2,1)S(1)} %pad_maximum_fusion.7.refs_0_.keys, bf16[2,8,6,16,128]{4,3,2,1,0:T(8,128)(2,1)S(1)} %get-tuple-element.37.refs_3_.values, ...), custom_call_target="tpu_custom_call" | custom-call | flops 905969664 | bytes 2359296 | tf_op jit(solution)/shard_map/pallas_call | solution.py:149
  113.1 4.6 %shard_map.105 = bf16[2,2,8,3,16,128]{5,4,3,2,1,0:T(8,128)(2,1)S(1)} custom-call(s32[2,3]{1,0:T(2,128)S(1)} %pad_add_fusion.spots, bf16[2,8,6,16,128]{4,3,2,1,0:T(8,128)(2,1)S(1)} %pad_maximum_fusion.7.refs_0_.keys, bf16[2,8,6,16,128]{4,3,2,1,0:T(8,128)(2,1)S(1)} %get-tuple-element.37.refs_3_.values, ...), custom_call_target="tpu_custom_call" | custom-call | flops 905969664 | bytes 2359296 | tf_op jit(solution)/shard_map/pallas_call | solution.py:149
  117.7 1.4 %collective-permute-done.14 = bf16[2,2,8,3,8,128]{5,4,3,2,1,0:T(8,128)(2,1)S(1)} collective-permute-done((bf16[2,2,8,3,8,128]{5,4,3,2,1,0:T(8,128)(2,1)S(1)}, bf16[2,2,8,3,8,128]{5,4,3,2,1,0:T(8,128)(2,1)S(1)}, u32[]{:S(2)}, u32[]{:S(2)}) %collective-permute-start.14) | collective-permute-done | bytes 196640 | tf_op jit(solution)/shard_map/ppermute | solution.py:175
  120.3 4.7 %collective-permute-done.15 = bf16[2,2,8,3,8,128]{5,4,3,2,1,0:T(8,128)(2,1)S(1)} collective-permute-done((bf16[2,2,8,3,8,128]{5,4,3,2,1,0:T(8,128)(2,1)S(1)}, bf16[2,2,8,3,8,128]{5,4,3,2,1,0:T(8,128)(2,1)S(1)}, u32[]{:S(2)}, u32[]{:S(2)}) %collective-permute-start.15) | collective-permute-done | bytes 196640 | tf_op jit(solution)/shard_map/ppermute | solution.py:175
  (88 shorter events, 10.5 us)
Async XLA Ops:
  0.6 7.0 %copy-start.10 = (bf16[4,3,9,2,9,1]{4,2,1,0,5,3:T(8,128)(2,1)S(1)}, bf16[4,3,9,2,9,1]{4,2,1,0,5,3:T(8,128)(2,1)}, u32[]{:S(2)}) copy-start(bf16[4,3,9,2,9,1]{4,2,1,0,5,3:T(8,128)(2,1)} %constant.239) | copy-start | bytes 11668
  0.6 5.5 %copy-start.11 = (s32[8,4,2,27]{3,2,1,0:T(2,128)S(1)}, s32[8,4,2,27]{3,2,1,0:T(2,128)}, u32[]{:S(2)}) copy-start(s32[8,4,2,27]{3,2,1,0:T(2,128)} %param.11) | copy-start | bytes 20740
  1.8 8.7 %collective-permute-start = (bf16[2,8,6,8,128]{4,3,2,1,0:T(8,128)(2,1)S(1)}, bf16[2,8,6,8,128]{4,3,2,1,0:T(8,128)(2,1)S(1)}, u32[]{:S(2)}, u32[]{:S(2)}) collective-permute-start(bf16[2,8,6,8,128]{4,3,2,1,0:T(8,128)(2,1)S(1)} %get-tuple-element.41), channel_id=1, source_target_pairs={{0,1},{1,0},{2,3},{3,2},{4,5},{5,4},{6,7},{7,6},{8,9},{9,8},{10,11... | collective-permute-start | bytes 589832 | tf_op jit(solution)/shard_map/ppermute | solution.py:175
  5.8 3.7 %copy-start.6 = (bf16[2,8,8,12,128]{4,2,3,1,0:T(8,128)(2,1)S(1)}, bf16[2,8,8,12,128]{4,2,3,1,0:T(8,128)(2,1)}, u32[]{:S(2)}) copy-start(bf16[2,8,8,12,128]{4,2,3,1,0:T(8,128)(2,1)} %param.10) | copy-start | bytes 1179652
  5.8 3.7 %copy-start.7 = (bf16[2,8,8,12,128]{4,2,3,1,0:T(8,128)(2,1)S(1)}, bf16[2,8,8,12,128]{4,2,3,1,0:T(8,128)(2,1)}, u32[]{:S(2)}) copy-start(bf16[2,8,8,12,128]{4,2,3,1,0:T(8,128)(2,1)} %param.7) | copy-start | bytes 1179652
  5.8 11.7 %collective-permute-start.4 = (bf16[2,8,6,8,128]{4,3,2,1,0:T(8,128)(2,1)S(1)}, bf16[2,8,6,8,128]{4,3,2,1,0:T(8,128)(2,1)S(1)}, u32[]{:S(2)}, u32[]{:S(2)}) collective-permute-start(bf16[2,8,6,8,128]{4,3,2,1,0:T(8,128)(2,1)S(1)} %get-tuple-element.39), channel_id=1, source_target_pairs={{0,1},{1,0},{2,3},{3,2},{4,5},{5,4},{6,7},{7,6},{8,9},{9,8},{10,11... | collective-permute-start | bytes 589832 | tf_op jit(solution)/shard_map/ppermute | solution.py:175
  9.7 13.8 %copy-start.8 = (bf16[144,1152]{1,0:T(8,128)(2,1)S(1)}, bf16[144,1152]{1,0:T(8,128)(2,1)}, u32[]{:S(2)}) copy-start(bf16[144,1152]{1,0:T(8,128)(2,1)} %constant.143.clone) | copy-start | bytes 995332
  9.7 13.8 %copy-start.9 = (bf16[64,144]{0,1:T(8,128)(2,1)S(1)}, bf16[64,144]{0,1:T(8,128)(2,1)}, u32[]{:S(2)}) copy-start(bf16[64,144]{0,1:T(8,128)(2,1)} %convert_element_type.20) | copy-start | bytes 55300
  10.6 14.8 %collective-permute-start.2 = (bf16[2,8,6,16,128]{4,3,2,1,0:T(8,128)(2,1)S(1)}, bf16[2,8,6,16,128]{4,3,2,1,0:T(8,128)(2,1)S(1)}, u32[]{:S(2)}, u32[]{:S(2)}) collective-permute-start(bf16[2,8,6,16,128]{4,3,2,1,0:T(8,128)(2,1)S(1)} %pad_maximum_fusion.7.refs_0_.keys), channel_id=1, source_target_pairs={{0,2},{2,4},{4,6},{1,3},{3,5},{5,7},{8,10},{10,12},{12,14},{9,11},... | collective-permute-start | bytes 1179656 | tf_op jit(solution)/shard_map/ppermute | solution.py:170
  14.6 12.7 %collective-permute-start.3 = (bf16[2,8,6,16,128]{4,3,2,1,0:T(8,128)(2,1)S(1)}, bf16[2,8,6,16,128]{4,3,2,1,0:T(8,128)(2,1)S(1)}, u32[]{:S(2)}, u32[]{:S(2)}) collective-permute-start(bf16[2,8,6,16,128]{4,3,2,1,0:T(8,128)(2,1)S(1)} %pad_maximum_fusion.7.refs_0_.keys), channel_id=1, source_target_pairs={{2,0},{4,2},{6,4},{3,1},{5,3},{7,5},{10,8},{12,10},{14,12},{11,9},... | collective-permute-start | bytes 1179656 | tf_op jit(solution)/shard_map/ppermute | solution.py:170
  15.9 9.3 %collective-permute-start.1 = (bf16[2,2,8,6,8,128]{5,4,3,2,1,0:T(8,128)(2,1)S(1)}, bf16[2,2,8,6,8,128]{5,4,3,2,1,0:T(8,128)(2,1)S(1)}, u32[]{:S(2)}, u32[]{:S(2)}) collective-permute-start(bf16[2,2,8,6,8,128]{5,4,3,2,1,0:T(8,128)(2,1)S(1)} %pad_maximum_fusion.6), channel_id=1, source_target_pairs={{0,1},{1,0},{2,3},{3,2},{4,5},{5,4},{6,7},{7,6},{8,9},{9,8},{10,11... | collective-permute-start | bytes 1179656 | tf_op jit(solution)/shard_map/ppermute | solution.py:175
  17.6 18.6 %collective-permute-start.5 = (bf16[2,8,6,16,128]{4,3,2,1,0:T(8,128)(2,1)S(1)}, bf16[2,8,6,16,128]{4,3,2,1,0:T(8,128)(2,1)S(1)}, u32[]{:S(2)}, u32[]{:S(2)}) collective-permute-start(bf16[2,8,6,16,128]{4,3,2,1,0:T(8,128)(2,1)S(1)} %get-tuple-element.37.refs_3_.values), channel_id=1, source_target_pairs={{0,2},{2,4},{4,6},{1,3},{3,5},{5,7},{8,10},{10,12},{12,14},{9,11},... | collective-permute-start | bytes 1179656 | tf_op jit(solution)/shard_map/ppermute | solution.py:170
  22.2 13.9 %collective-permute-start.6 = (bf16[2,8,6,16,128]{4,3,2,1,0:T(8,128)(2,1)S(1)}, bf16[2,8,6,16,128]{4,3,2,1,0:T(8,128)(2,1)S(1)}, u32[]{:S(2)}, u32[]{:S(2)}) collective-permute-start(bf16[2,8,6,16,128]{4,3,2,1,0:T(8,128)(2,1)S(1)} %get-tuple-element.37.refs_3_.values), channel_id=1, source_target_pairs={{2,0},{4,2},{6,4},{3,1},{5,3},{7,5},{10,8},{12,10},{14,12},{11,9},... | collective-permute-start | bytes 1179656 | tf_op jit(solution)/shard_map/ppermute | solution.py:170
  27.4 12.4 %copy-start = (bf16[2,8,6,16,128]{4,3,2,1,0:T(8,128)(2,1)}, bf16[2,8,6,16,128]{4,3,2,1,0:T(8,128)(2,1)S(1)}, u32[]{:S(2)}) copy-start(bf16[2,8,6,16,128]{4,3,2,1,0:T(8,128)(2,1)S(1)} %collective-permute-done.3.refs_2_) | copy-start | bytes 1179652
  27.4 23.8 %collective-permute-start.10 = (bf16[2,2,8,6,16,128]{5,4,3,2,1,0:T(8,128)(2,1)S(1)}, bf16[2,2,8,6,16,128]{5,4,3,2,1,0:T(8,128)(2,1)S(1)}, u32[]{:S(2)}, u32[]{:S(2)}) collective-permute-start(bf16[2,2,8,6,16,128]{5,4,3,2,1,0:T(8,128)(2,1)S(1)} %pad_maximum_fusion.4.pair.own), channel_id=1, source_target_pairs={{0,2},{2,4},{4,6},{1,3},{3,5},{5,7},{8,10},{10,12},{12,14},{9,11},... | collective-permute-start | bytes 2359304 | tf_op jit(solution)/shard_map/ppermute | solution.py:170
  30.9 20.1 %collective-permute-start.11 = (bf16[2,2,8,6,16,128]{5,4,3,2,1,0:T(8,128)(2,1)S(1)}, bf16[2,2,8,6,16,128]{5,4,3,2,1,0:T(8,128)(2,1)S(1)}, u32[]{:S(2)}, u32[]{:S(2)}) collective-permute-start(bf16[2,2,8,6,16,128]{5,4,3,2,1,0:T(8,128)(2,1)S(1)} %pad_maximum_fusion.4.pair.own), channel_id=1, source_target_pairs={{2,0},{4,2},{6,4},{3,1},{5,3},{7,5},{10,8},{12,10},{14,12},{11,9},... | collective-permute-start | bytes 2359304 | tf_op jit(solution)/shard_map/ppermute | solution.py:170
  36.1 3.6 %copy-start.4 = (bf16[2,8,6,16,128]{4,3,2,1,0:T(8,128)(2,1)}, bf16[2,8,6,16,128]{4,3,2,1,0:T(8,128)(2,1)S(1)}, u32[]{:S(2)}) copy-start(bf16[2,8,6,16,128]{4,3,2,1,0:T(8,128)(2,1)S(1)} %collective-permute-done.6.refs_5_) | copy-start | bytes 1179652
  36.2 3.5 %copy-start.2 = (bf16[2,8,6,16,128]{4,3,2,1,0:T(8,128)(2,1)}, bf16[2,8,6,16,128]{4,3,2,1,0:T(8,128)(2,1)S(1)}, u32[]{:S(2)}) copy-start(bf16[2,8,6,16,128]{4,3,2,1,0:T(8,128)(2,1)S(1)} %collective-permute-done.5.refs_4_) | copy-start | bytes 1179652
  37.4 20.9 %collective-permute-start.7 = (bf16[3,2,8,6,16,128]{5,4,3,2,0,1:T(8,128)(2,1)}, bf16[3,2,8,6,16,128]{5,4,3,2,0,1:T(8,128)(2,1)}, u32[]{:S(2)}, u32[]{:S(2)}) collective-permute-start(bf16[3,2,8,6,16,128]{5,4,3,2,0,1:T(8,128)(2,1)} %pad_maximum_fusion.1), channel_id=1, source_target_pairs={{0,8},{8,16},{16,24},{1,9},{9,17},{17,25},{2,10},{10,18},{18,26},{... | collective-permute-start | bytes 3538952 | tf_op jit(solution)/shard_map/ppermute | solution.py:170
  40.9 18.9 %collective-permute-start.8 = (bf16[3,2,8,6,16,128]{5,4,3,2,0,1:T(8,128)(2,1)}, bf16[3,2,8,6,16,128]{5,4,3,2,0,1:T(8,128)(2,1)}, u32[]{:S(2)}, u32[]{:S(2)}) collective-permute-start(bf16[3,2,8,6,16,128]{5,4,3,2,0,1:T(8,128)(2,1)} %fusion.8), channel_id=1, source_target_pairs={{8,0},{16,8},{24,16},{9,1},{17,9},{25,17},{10,2},{18,10},{26,18},{... | collective-permute-start | bytes 3538952 | tf_op jit(solution)/shard_map/ppermute | solution.py:170
  52.4 55.1 %collective-permute-start.12 = (bf16[3,2,8,6,16,128]{5,4,3,2,1,0:T(8,128)(2,1)}, bf16[3,2,8,6,16,128]{5,4,3,2,1,0:T(8,128)(2,1)}, u32[]{:S(2)}, u32[]{:S(2)}) collective-permute-start(bf16[3,2,8,6,16,128]{5,4,3,2,1,0:T(8,128)(2,1)} %pad_maximum_fusion.2), channel_id=1, source_target_pairs={{0,8},{8,16},{16,24},{1,9},{9,17},{17,25},{2,10},{10,18},{18,26},{... | collective-permute-start | bytes 3538952 | tf_op jit(solution)/shard_map/ppermute | solution.py:170
  55.9 51.7 %collective-permute-start.13 = (bf16[3,2,8,6,16,128]{5,4,3,2,1,0:T(8,128)(2,1)}, bf16[3,2,8,6,16,128]{5,4,3,2,1,0:T(8,128)(2,1)}, u32[]{:S(2)}, u32[]{:S(2)}) collective-permute-start(bf16[3,2,8,6,16,128]{5,4,3,2,1,0:T(8,128)(2,1)} %pad_maximum_fusion.3), channel_id=1, source_target_pairs={{8,0},{16,8},{24,16},{9,1},{17,9},{25,17},{10,2},{18,10},{26,18},{... | collective-permute-start | bytes 3538952 | tf_op jit(solution)/shard_map/ppermute | solution.py:170
  59.8 1.6 %copy-start.1 = (bf16[2,8,6,16,128]{4,3,2,1,0:T(8,128)(2,1)S(1)}, bf16[2,8,6,16,128]{4,3,2,1,0:T(8,128)(2,1)}, u32[]{:S(2)}) copy-start(bf16[2,8,6,16,128]{4,3,2,1,0:T(8,128)(2,1)} %copy-done) | copy-start | bytes 1179652
  59.8 1.6 %copy-start.3 = (bf16[2,8,6,16,128]{4,3,2,1,0:T(8,128)(2,1)S(1)}, bf16[2,8,6,16,128]{4,3,2,1,0:T(8,128)(2,1)}, u32[]{:S(2)}) copy-start(bf16[2,8,6,16,128]{4,3,2,1,0:T(8,128)(2,1)} %copy-done.2) | copy-start | bytes 1179652
  59.8 1.6 %copy-start.5 = (bf16[2,8,6,16,128]{4,3,2,1,0:T(8,128)(2,1)S(1)}, bf16[2,8,6,16,128]{4,3,2,1,0:T(8,128)(2,1)}, u32[]{:S(2)}) copy-start(bf16[2,8,6,16,128]{4,3,2,1,0:T(8,128)(2,1)} %copy-done.4) | copy-start | bytes 1179652
  72.5 40.6 %collective-permute-start.9 = (bf16[2,2,8,6,8,128]{5,4,3,2,1,0:T(8,128)(2,1)S(1)}, bf16[2,2,8,6,8,128]{5,4,3,2,1,0:T(8,128)(2,1)S(1)}, u32[]{:S(2)}, u32[]{:S(2)}) collective-permute-start(bf16[2,2,8,6,8,128]{5,4,3,2,1,0:T(8,128)(2,1)S(1)} %get-tuple-element.30), channel_id=1, source_target_pairs={{0,1},{1,0},{2,3},{3,2},{4,5},{5,4},{6,7},{7,6},{8,9},{9,8},{10,11... | collective-permute-start | bytes 1179656 | tf_op jit(solution)/shard_map/ppermute | solution.py:175
  112.4 6.7 %collective-permute-start.14 = (bf16[2,2,8,3,8,128]{5,4,3,2,1,0:T(8,128)(2,1)S(1)}, bf16[2,2,8,3,8,128]{5,4,3,2,1,0:T(8,128)(2,1)S(1)}, u32[]{:S(2)}, u32[]{:S(2)}) collective-permute-start(bf16[2,2,8,3,8,128]{5,4,3,2,1,0:T(8,128)(2,1)S(1)} %get-tuple-element.34), channel_id=1, source_target_pairs={{0,1},{1,0},{2,3},{3,2},{4,5},{5,4},{6,7},{7,6},{8,9},{9,8},{10,11... | collective-permute-start | bytes 589832 | tf_op jit(solution)/shard_map/ppermute | solution.py:175
  119.2 5.7 %collective-permute-start.15 = (bf16[2,2,8,3,8,128]{5,4,3,2,1,0:T(8,128)(2,1)S(1)}, bf16[2,2,8,3,8,128]{5,4,3,2,1,0:T(8,128)(2,1)S(1)}, u32[]{:S(2)}, u32[]{:S(2)}) collective-permute-start(bf16[2,2,8,3,8,128]{5,4,3,2,1,0:T(8,128)(2,1)S(1)} %get-tuple-element.32), channel_id=1, source_target_pairs={{0,1},{1,0},{2,3},{3,2},{4,5},{5,4},{6,7},{7,6},{8,9},{9,8},{10,11... | collective-permute-start | bytes 589832 | tf_op jit(solution)/shard_map/ppermute | solution.py:175

commit v5 on v3

v5 whole, which is shorter than its diff:
```python
import functools

import jax
import jax.numpy as jnp
import numpy as np
from jax import lax
from jax.experimental import pallas as pl
from jax.experimental.pallas import tpu as pltpu
from jax.sharding import PartitionSpec as P

TF = 1
TR = 8
TC = 8
MASKED = -1e30
LOG2E = 1.4426950408889634
NT = (((1,), (1,)), ((), ()))
NN = (((1,), (0,)), ((), ()))


def dot(left, right, dims):
    return lax.dot_general(left, right, dims, preferred_element_type=jnp.float32)


def spread(bias, tokens):
    parts, width = bias.shape
    return jnp.broadcast_to(bias[:, None], (parts, tokens // parts, width)).reshape(tokens, width)


def fill_bands(halo, bands):
    parts = len(halo) // 3
    own, before, after = halo[:parts], halo[parts : 2 * parts], halo[2 * parts : 3 * parts]
    low, high = halo[3 * parts :]
    frames, _, _, cells, _ = own[0].shape
    for at in range(frames + 2):
        for row, beside in enumerate((before, own, after)):
            for part in range(parts):
                place = pl.ds(((3 * at + row) * parts + part) * cells, cells)
                for which, band in enumerate(bands):
                    if at == 0:
                        band[place, :] = low[row * parts + part, which, 0]
                    elif at == frames + 1:
                        band[place, :] = high[row * parts + part, which, 0]
                    else:
                        band[place, :] = beside[part][at - 1, which, 0]


def slab(parts, at, which):
    return jnp.concatenate([part[at, which, 0] for part in parts], axis=0)


def attend_kernel(scaling, parts, *refs):
    pair, halo = refs[:parts], refs[parts : 4 * parts + 2]
    bias, attended, stats, key_all, value_all = refs[4 * parts + 2 :]
    frames, _, tokens, _ = attended.shape
    fill_bands(halo, (key_all, value_all))
    windows = [pl.ds(3 * at * tokens, 9 * tokens) for at in range(frames)]
    scores = [
        dot(slab(pair, at, 0), key_all[windows[at], :], NT) * (scaling * LOG2E) + spread(bias[at], tokens)
        for at in range(frames)
    ]
    highest = [jnp.max(part, axis=1, keepdims=True) for part in scores]
    raised = [jnp.exp2(part - top) for part, top in zip(scores, highest)]
    total = [jnp.sum(part, axis=1, keepdims=True) for part in raised]
    sums = [dot(raised[at].astype(jnp.bfloat16), value_all[windows[at], :], NN) for at in range(frames)]
    for at in range(frames):
        out = (sums[at] * (1.0 / total[at])).astype(jnp.bfloat16)
        grad = slab(pair, at, 1).astype(jnp.float32)
        grad_dot = jnp.sum(grad * out.astype(jnp.float32), axis=1, keepdims=True)
        attended[at, 0] = out
        lane = lax.broadcasted_iota(jnp.int32, (tokens, 128), 1)
        both = jnp.where(lane == 0, highest[at] + jnp.log2(total[at]), grad_dot)
        stats[at, 0] = jnp.transpose(both)[:2]


def store(grads, at, first, second):
    cells = grads[0].shape[-2]
    for part, out in enumerate(grads):
        own = slice(part * cells, (part + 1) * cells)
        out[0, at, 0] = first[own]
        out[1, at, 0] = second[own]


def query_kernel(scaling, parts, *refs):
    pair, halo = refs[:parts], refs[parts : 4 * parts + 2]
    attended, stats, bias = refs[4 * parts + 2 : 4 * parts + 5]
    grads, (key_all, value_all) = refs[4 * parts + 5 : -2], refs[-2:]
    frames, _, tokens, _ = attended.shape
    fill_bands(halo, (key_all, value_all))
    windows = [pl.ds(3 * at * tokens, 9 * tokens) for at in range(frames)]

    def column(at, which):
        wide = jnp.broadcast_to(stats[at, 0, which : which + 1], (128, tokens))
        return jnp.transpose(wide)[:, :1]

    scores = [dot(slab(pair, at, 0), key_all[windows[at], :], NT) for at in range(frames)]
    grad_probs = [dot(slab(pair, at, 1), value_all[windows[at], :], NT) for at in range(frames)]
    for at in range(frames):
        shift = spread(bias[at], tokens) - column(at, 0)
        weights = jnp.exp2(scores[at] * (scaling * LOG2E) + shift)
        grad_scores = (weights * (grad_probs[at] - column(at, 1))).astype(jnp.bfloat16)
        query_grad = dot(grad_scores, key_all[windows[at], :], NN) * scaling
        store(grads, at, attended[at, 0], query_grad.astype(jnp.bfloat16))


def back_kernel(scaling, parts, *refs):
    pair, halo = refs[:parts], refs[parts : 4 * parts + 2]
    own_st, before_st, after_st, low_st, high_st, bias = refs[4 * parts + 2 : 4 * parts + 8]
    grads, (query_all, grad_all) = refs[4 * parts + 8 : -2], refs[-2:]
    frames, _, _, tokens = own_st.shape
    fill_bands(halo, (query_all, grad_all))

    def stat_row(at, row, which):
        if at == 0:
            return low_st[row, 0, which : which + 1]
        if at == frames + 1:
            return high_st[row, 0, which : which + 1]
        return (before_st, own_st, after_st)[row][at - 1, 0, which : which + 1]

    def stat_band(at, which):
        rows = [stat_row(at + step, row, which) for step in range(3) for row in range(3)]
        return jnp.concatenate(rows, axis=1)

    windows = [pl.ds(3 * at * tokens, 9 * tokens) for at in range(frames)]
    scores = [dot(slab(pair, at, 0), query_all[windows[at], :], NT) for at in range(frames)]
    grad_probs = [dot(slab(pair, at, 1), grad_all[windows[at], :], NT) for at in range(frames)]
    for at in range(frames):
        shift = spread(bias[at] - stat_band(at, 0), tokens)
        weights = jnp.exp2(scores[at] * (scaling * LOG2E) + shift).astype(jnp.bfloat16)
        grad_scores = weights.astype(jnp.float32) * (grad_probs[at] - stat_band(at, 1))
        key_grad = dot(grad_scores.astype(jnp.bfloat16), query_all[windows[at], :], NN) * scaling
        value_grad = dot(weights, grad_all[windows[at], :], NN)
        store(grads, at, key_grad.astype(jnp.bfloat16), value_grad.astype(jnp.bfloat16))


def head_spec(shape, first):
    dim = len(shape) - 3
    block = shape[:dim] + (1,) + shape[dim + 1 :]
    return pl.BlockSpec(block, lambda head: (0,) * dim + (head + first,) + (0, 0))


def run(kernel, scaling, pair, halo, extra, bias, outs, first, count, products):
    parts = len(pair)
    frames, _, _, cells, dim = pair[0].shape
    tokens = parts * cells
    operands = tuple(pair) + tuple(halo) + tuple(extra)
    return pl.pallas_call(
        functools.partial(kernel, scaling, parts),
        grid=(count,),
        out_shape=tuple(outs),
        in_specs=[head_spec(part.shape, first) for part in operands]
        + [pl.BlockSpec(bias.shape, lambda head: (0,) * bias.ndim)],
        out_specs=tuple(head_spec(out.shape, 0) for out in outs),
        scratch_shapes=[pltpu.VMEM((3 * (frames + 2) * tokens, dim), jnp.bfloat16)] * 2,
        compiler_params=pltpu.CompilerParams(vmem_limit_bytes=32 * 2**20),
        cost_estimate=pl.CostEstimate(
            flops=frames * count * 2 * products * tokens * 9 * tokens * dim,
            bytes_accessed=count * (frames + 2) * 3 * 2 * tokens * dim * 2,
            transcendentals=frames * count * tokens * 9 * tokens,
        ),
    )(*operands, bias)


def step_along(tensor, axis, sign):
    size = lax.axis_size(axis)
    return lax.ppermute(tensor, axis, [(i, i + sign) for i in range(size) if 0 <= i + sign < size])


def turn(tensor, shift):
    size = lax.axis_size("head")
    return lax.ppermute(tensor, "head", [(i, (i + shift) % size) for i in range(size)])


def frame_edges(before, own, after):
    rows = (before, own, after)

    def edge(at):
        return jnp.stack([part[at] for row in rows for part in row])

    return step_along(edge(-1), "frame", 1), step_along(edge(0), "frame", -1)


def stat_edges(before, own, after):
    low = step_along(jnp.stack([before[-1], own[-1], after[-1]]), "frame", 1)
    return low, step_along(jnp.stack([before[0], own[0], after[0]]), "frame", -1)


def row_sides(own):
    return step_along(own, "row", 1), step_along(own, "row", -1)


def tile_biases(active, frames, columns_here, cells):
    size = lax.axis_size("head")
    me = lax.axis_index("head")
    frame_at = lax.axis_index("frame") * frames
    row_at = lax.axis_index("row")
    all_frames, all_rows, count, slots = active.shape
    padded = jnp.pad(active.astype(jnp.float32), ((1, 1), (1, 1), (0, 0), (0, 0)))
    near = lax.dynamic_slice(padded, (frame_at, row_at, 0, 0), (frames + 2, 3, count, slots))
    near = near.reshape(frames + 2, 3, count, 9, 3)
    steps = jnp.arange(3, dtype=jnp.int32) - 1
    frame_ids = frame_at + jnp.arange(frames, dtype=jnp.int32)[:, None] + steps
    frame_in = (frame_ids >= 0) & (frame_ids < all_frames)
    row_in = (row_at + steps >= 0) & (row_at + steps < all_rows)
    inside = (frame_in[:, :, None] & row_in).reshape(frames, 9).astype(jnp.float32)
    ahead = near[1 : 1 + frames, 1] * inside[:, None, :, None]
    pick = np.zeros((frames + 2, 3, 9, frames, 9), np.float32)
    for at in range(frames):
        for offset in range(9):
            pick[at + offset // 3, offset % 3, 8 - offset, at, offset] = 1.0
    behind = jnp.einsum("xyioc,xyofq->fiqc", near, pick)
    part = jnp.arange(size, dtype=jnp.int32)
    tile = ((me + part) % size * columns_here) // TC
    repeat = np.kron(np.eye(9 * size), np.ones((1, cells)))
    spread_out = jnp.asarray(repeat, jnp.bfloat16)
    smalls = []
    for table, sign in ((ahead, 1), (behind, -1)):
        owner = tile[None] == jnp.arange(count, dtype=jnp.int32)[:, None]
        shift = (sign * (tile[None, :] - tile[:, None]))[None] == steps[:, None, None]
        chosen = (owner[:, None, :, None] & shift[None]).astype(jnp.float32)
        smalls.append(jnp.einsum("fioc,icpk->fpok", table, chosen))
    small = jnp.stack(smalls).reshape(2 * frames * size, -1).astype(jnp.bfloat16)
    allowed = jnp.dot(small, spread_out, preferred_element_type=jnp.float32)
    bias = jnp.where(allowed > 0.5, 0.0, MASKED).reshape(2, frames, size, -1)
    return bias[0], bias[1]


def on_device(queries, keys, values, out_grad, active):
    frames, rows, columns_here, heads, dim = queries.shape
    size = lax.axis_size("head")
    me = lax.axis_index("head")
    groups = heads // size
    cells = rows * columns_here
    tokens = cells * size
    scaling = dim ** (-0.5)
    assert rows == TR and TC % columns_here == 0

    def pair_of(first, second, shift):
        start = (me + shift) % size * groups
        picked = [
            lax.dynamic_slice_in_dim(jnp.transpose(t, (0, 3, 1, 2, 4)), start, groups, 1) for t in (first, second)
        ]
        return jnp.stack(picked, 1).reshape(frames, 2, groups, cells, dim)

    def from_heads(blocks):
        whole = jnp.zeros((2, frames, rows, heads, columns_here, dim), jnp.bfloat16)
        for first, grads in blocks:
            for b, piece in enumerate(grads):
                piece = piece if b == 0 else turn(piece, b)
                piece = piece.reshape((2, frames, -1, rows, columns_here, dim)).transpose(0, 1, 3, 2, 4, 5)
                start = (me + size - b) % size * groups + first
                whole = lax.dynamic_update_slice_in_dim(whole, piece, start, 3)
        whole = jnp.transpose(whole, (0, 1, 2, 4, 3, 5))
        return whole[0], whole[1]

    def sides_of(parts):
        both = [row_sides(part) for part in parts]
        return [up for up, _ in both], [down for _, down in both]

    front_bias, back_bias = tile_biases(active, frames, columns_here, cells)
    key_sent = [pair_of(keys, values, shift) for shift in range(1, size)]
    key_sent, keys, values = lax.optimization_barrier((key_sent, keys, values))
    key_here = [pair_of(keys, values, 0)]
    key_near = sides_of(key_here)
    key_moved = [turn(key_sent[size - b - 1], size - b) for b in range(1, size)]
    query_held = [pair_of(queries, out_grad, shift) for shift in range(size)]
    query_held, key_moved = lax.optimization_barrier((query_held, key_moved))
    key_far = sides_of(key_moved)
    query_moved = [turn(query_held[size - b], size - b) for b in range(1, size)]
    query_parts = query_held[:1] + query_moved
    query_parts, key_near = lax.optimization_barrier((query_parts, key_near))
    query_near = sides_of(query_parts)
    key_parts = key_here + key_moved
    key_before, key_after = key_near[0] + key_far[0], key_near[1] + key_far[1]
    key_halo = key_parts + key_before + key_after + list(frame_edges(key_before, key_parts, key_after))
    query_before, query_after = query_near
    query_halo = (
        query_parts + query_before + query_after + list(frame_edges(query_before, query_parts, query_after))
    )

    def grads_shape(count):
        return [jax.ShapeDtypeStruct((2, frames, count, cells, dim), jnp.bfloat16)] * size

    attended_shape = jax.ShapeDtypeStruct((frames, groups, tokens, dim), jnp.bfloat16)
    stat_shape = jax.ShapeDtypeStruct((frames, groups, 2, tokens), jnp.float32)
    attended, stats = run(
        attend_kernel, scaling, query_parts, key_halo, (), front_bias, [attended_shape, stat_shape], 0, groups, 2
    )
    front_grads = run(
        query_kernel, scaling, query_parts, key_halo, (attended, stats), front_bias, grads_shape(groups),
        0, groups, 3
    )
    stat_sides = row_sides(stats)
    stat_halo = (stats,) + stat_sides + stat_edges(stat_sides[0], stats, stat_sides[1])
    blocks = []
    for first, count in ((0, groups - groups // 2), (groups - groups // 2, groups // 2)):
        back_grads = run(
            back_kernel, scaling, key_parts, query_halo, stat_halo, back_bias, grads_shape(count), first, count, 4
        )
        blocks.append((first, back_grads))
    return from_heads([(0, front_grads)]) + from_heads(blocks)


def solution(mesh):
    spec = P("frame", "row", "head", None, None)
    return jax.shard_map(
        on_device, mesh=mesh, in_specs=(spec,) * 4 + (P(),), out_specs=(spec,) * 4, check_vma=False
    )
```

time: 115 us -> 102 us (0.89)
  local copies, waits for them, and re-layouts: 14.8 us -> 6.79 us
  Pallas kernels: 20.9 us -> 16.7 us
  other arithmetic: 5.99 us -> 2.08 us
  waiting for transfers between devices: 16.7 us -> 19.8 us
    ppermute x6 -> x5, waiting for transfers between devices: 4.8 us -> 11.1 us  [turn(): lax.ppermute(tensor, 'head', [(i, (i + shift) % size) for i in range(size)])]
    unnamed x44 -> x25, local copies, waits for them, and re-layouts: 5.42 us -> 1.21 us
    pallas_call x4, Pallas kernels: 20.9 us -> 16.7 us  [run(): pl.pallas_call(functools.partial(kernel, scaling, parts), grid=(count,),...]
    another operation x11 -> x8, other arithmetic: 5.27 us -> 1.72 us  [the longest x5 1.69 us: pair_of(): return jnp.stack(picked, 1).reshape(frames, 2, groups, cells, dim)]
    ppermute x16, waiting for transfers between devices: 11.9 us -> 8.63 us  [step_along(): lax.ppermute(tensor, axis, [(i, i + sign) for i in range(size) if 0 <= i...]
    slice x14 -> x3, local copies, waits for them, and re-layouts: 1.64 us -> 0.01 us  [the longest x1 0.01 us: stat_edges(): own[0]]
    ppermute x6 -> x5, starting transfers between devices: 5.95 us -> 5.32 us  [turn(): lax.ppermute(tensor, 'head', [(i, (i + shift) % size) for i in range(size)])]
  transfers between devices with their start and end apart: 22 -> 21, of which waited for: 6 -> 9; matrix products, arithmetic and copies ran while one was open for 13% -> 6% of each run, Pallas kernels for 18% -> 14%
where the time goes in v5:
time: 102 us; the launch traced here: 101 us
  starting transfers between devices  53.6 us (53%)
  waiting for transfers between devices  19.8 us (19%)
  Pallas kernels  16.7 us (16%)
  local copies, waits for them, and re-layouts  6.79 us (7%)
  other arithmetic  2.08 us (2%)
  between operations  1.35 us (1%)
    ppermute x16, starting transfers between devices, step_along(): lax.ppermute(tensor, axis, [(i, i + sign) for i in range(size) if 0 <= i...  48.2 us
    pallas_call x4, Pallas kernels, run(): pl.pallas_call(functools.partial(kernel, scaling, parts), grid=(count,),...  16.7 us
    ppermute x5, waiting for transfers between devices, turn(): lax.ppermute(tensor, 'head', [(i, (i + shift) % size) for i in range(size)])  11.1 us
    ppermute x16, waiting for transfers between devices, step_along(): lax.ppermute(tensor, axis, [(i, i + sign) for i in range(size) if 0 <= i...  8.63 us
    ppermute x5, starting transfers between devices, turn(): lax.ppermute(tensor, 'head', [(i, (i + shift) % size) for i in range(size)])  5.32 us
  transfers between devices with their start and end apart: 21, of which 9 were waited for; matrix products, arithmetic and copies ran while one was open for 6% of the time, Pallas kernels for 14%

profile of v5, /device:TPU:9, one launch (start us, length us, event | category | flops | bytes accessed | tf_op | source)
XLA Modules:
  0.0 101.1 jit_solution(11199095168637697121)
XLA Ops:
  0.7 1.1 %dynamic-slice_bitcast_fusion = (bf16[2,6,8,8,128]{4,3,1,2,0:T(8,128)(2,1)S(1)}, bf16[2,6,8,8,128]{4,3,1,2,0:T(8,128)(2,1)S(1)}) fusion(bf16[2,8,8,12,128]{4,2,3,1,0:T(8,128)(2,1)} %param.9, s32[]{:T(128)S(6)} %select_n.93, bf16[2,8,8,12,128]{4,2,3,1,0:T(8,128)(2,1)} %param.8), kind=kLoop, calls=%fused_computation.59 | loop fusion | bytes 786436 | tf_op jit(solution)/shard_map/dynamic_slice | solution.py:240
  3.0 3.2 %collective-permute-start.2 = (bf16[2,2,6,64,128]{4,3,2,1,0:T(8,128)(2,1)S(1)}, bf16[2,2,6,64,128]{4,3,2,1,0:T(8,128)(2,1)S(1)}, u32[]{:S(2)}, u32[]{:S(2)}) collective-permute-start(bf16[2,2,6,64,128]{4,3,2,1,0:T(8,128)(2,1)S(1)} %pad_maximum_fusion.3.refs_2_.refs_0_), channel_id=1, source_target_pairs={{0,2},{2,4},{4,6},{1,3},{3,5},{5,7},{8,10},{10,12},{12,14},{9,11},... | collective-permute-start | bytes 1179656 | tf_op jit(solution)/shard_map/ppermute | solution.py:165
  6.2 2.1 %collective-permute-start.3 = (bf16[2,2,6,64,128]{4,3,2,1,0:T(8,128)(2,1)S(1)}, bf16[2,2,6,64,128]{4,3,2,1,0:T(8,128)(2,1)S(1)}, u32[]{:S(2)}, u32[]{:S(2)}) collective-permute-start(bf16[2,2,6,64,128]{4,3,2,1,0:T(8,128)(2,1)S(1)} %pad_maximum_fusion.3.refs_2_.refs_0_), channel_id=1, source_target_pairs={{2,0},{4,2},{6,4},{3,1},{5,3},{7,5},{10,8},{12,10},{14,12},{11,9},... | collective-permute-start | bytes 1179656 | tf_op jit(solution)/shard_map/ppermute | solution.py:165
  8.3 1.3 %collective-permute-start = (bf16[2,2,6,64,128]{4,3,2,1,0:T(8,128)(2,1)}, bf16[2,2,6,64,128]{4,3,2,1,0:T(8,128)(2,1)S(1)}, u32[]{:S(2)}, u32[]{:S(2)}) collective-permute-start(bf16[2,2,6,64,128]{4,3,2,1,0:T(8,128)(2,1)} %pad_maximum_fusion.2), channel_id=1, source_target_pairs={{0,1},{1,0},{2,3},{3,2},{4,5},{5,4},{6,7},{7,6},{8,9},{9,8},{10,11... | collective-permute-start | bytes 1179656 | tf_op jit(solution)/shard_map/ppermute | solution.py:170
  13.9 4.1 %collective-permute-done.refs_3_.refs_1_ = bf16[2,2,6,64,128]{4,3,2,1,0:T(8,128)(2,1)S(1)} collective-permute-done((bf16[2,2,6,64,128]{4,3,2,1,0:T(8,128)(2,1)}, bf16[2,2,6,64,128]{4,3,2,1,0:T(8,128)(2,1)S(1)}, u32[]{:S(2)}, u32[]{:S(2)}) %collective-permute-start) | collective-permute-done | bytes 393248 | tf_op jit(solution)/shard_map/ppermute | solution.py:170
  18.0 1.2 %collective-permute-start.1 = (bf16[2,2,6,64,128]{4,3,2,1,0:T(8,128)(2,1)}, bf16[2,2,6,64,128]{4,3,2,1,0:T(8,128)(2,1)S(1)}, u32[]{:S(2)}, u32[]{:S(2)}) collective-permute-start(bf16[2,2,6,64,128]{4,3,2,1,0:T(8,128)(2,1)} %pad_maximum_fusion.1), channel_id=1, source_target_pairs={{0,1},{1,0},{2,3},{3,2},{4,5},{5,4},{6,7},{7,6},{8,9},{9,8},{10,11... | collective-permute-start | bytes 1179656 | tf_op jit(solution)/shard_map/ppermute | solution.py:170
  19.2 3.2 %collective-permute-start.4 = (bf16[2,2,6,64,128]{4,3,2,1,0:T(8,128)(2,1)S(1)}, bf16[2,2,6,64,128]{4,3,2,1,0:T(8,128)(2,1)S(1)}, u32[]{:S(2)}, u32[]{:S(2)}) collective-permute-start(bf16[2,2,6,64,128]{4,3,2,1,0:T(8,128)(2,1)S(1)} %collective-permute-done.refs_3_.refs_1_), channel_id=1, source_target_pairs={{0,2},{2,4},{4,6},{1,3},{3,5},{5,7},{8,10},{10,12},{12,14},{9,11},... | collective-permute-start | bytes 1179656 | tf_op jit(solution)/shard_map/ppermute | solution.py:165
  22.5 2.1 %collective-permute-start.5 = (bf16[2,2,6,64,128]{4,3,2,1,0:T(8,128)(2,1)S(1)}, bf16[2,2,6,64,128]{4,3,2,1,0:T(8,128)(2,1)S(1)}, u32[]{:S(2)}, u32[]{:S(2)}) collective-permute-start(bf16[2,2,6,64,128]{4,3,2,1,0:T(8,128)(2,1)S(1)} %collective-permute-done.refs_3_.refs_1_), channel_id=1, source_target_pairs={{2,0},{4,2},{6,4},{3,1},{5,3},{7,5},{10,8},{12,10},{14,12},{11,9},... | collective-permute-start | bytes 1179656 | tf_op jit(solution)/shard_map/ppermute | solution.py:165
  24.6 2.0 %collective-permute-done.1.refs_1_.refs_3_ = bf16[2,2,6,64,128]{4,3,2,1,0:T(8,128)(2,1)S(1)} collective-permute-done((bf16[2,2,6,64,128]{4,3,2,1,0:T(8,128)(2,1)}, bf16[2,2,6,64,128]{4,3,2,1,0:T(8,128)(2,1)S(1)}, u32[]{:S(2)}, u32[]{:S(2)}) %collective-permute-start.1) | collective-permute-done | bytes 393248 | tf_op jit(solution)/shard_map/ppermute | solution.py:170
  26.6 3.2 %collective-permute-start.9 = (bf16[2,2,6,64,128]{4,3,2,1,0:T(8,128)(2,1)S(1)}, bf16[2,2,6,64,128]{4,3,2,1,0:T(8,128)(2,1)S(1)}, u32[]{:S(2)}, u32[]{:S(2)}) collective-permute-start(bf16[2,2,6,64,128]{4,3,2,1,0:T(8,128)(2,1)S(1)} %pad_maximum_fusion.refs_0_.refs_2_), channel_id=1, source_target_pairs={{0,2},{2,4},{4,6},{1,3},{3,5},{5,7},{8,10},{10,12},{12,14},{9,11},... | collective-permute-start | bytes 1179656 | tf_op jit(solution)/shard_map/ppermute | solution.py:165
  29.8 2.1 %collective-permute-start.11 = (bf16[2,2,6,64,128]{4,3,2,1,0:T(8,128)(2,1)S(1)}, bf16[2,2,6,64,128]{4,3,2,1,0:T(8,128)(2,1)S(1)}, u32[]{:S(2)}, u32[]{:S(2)}) collective-permute-start(bf16[2,2,6,64,128]{4,3,2,1,0:T(8,128)(2,1)S(1)} %pad_maximum_fusion.refs_0_.refs_2_), channel_id=1, source_target_pairs={{2,0},{4,2},{6,4},{3,1},{5,3},{7,5},{10,8},{12,10},{14,12},{11,9},... | collective-permute-start | bytes 1179656 | tf_op jit(solution)/shard_map/ppermute | solution.py:165
  31.9 3.2 %collective-permute-start.10 = (bf16[2,2,6,64,128]{4,3,2,1,0:T(8,128)(2,1)S(1)}, bf16[2,2,6,64,128]{4,3,2,1,0:T(8,128)(2,1)S(1)}, u32[]{:S(2)}, u32[]{:S(2)}) collective-permute-start(bf16[2,2,6,64,128]{4,3,2,1,0:T(8,128)(2,1)S(1)} %collective-permute-done.1.refs_1_.refs_3_), channel_id=1, source_target_pairs={{0,2},{2,4},{4,6},{1,3},{3,5},{5,7},{8,10},{10,12},{12,14},{9,11},... | collective-permute-start | bytes 1179656 | tf_op jit(solution)/shard_map/ppermute | solution.py:165
  35.1 2.1 %collective-permute-start.12 = (bf16[2,2,6,64,128]{4,3,2,1,0:T(8,128)(2,1)S(1)}, bf16[2,2,6,64,128]{4,3,2,1,0:T(8,128)(2,1)S(1)}, u32[]{:S(2)}, u32[]{:S(2)}) collective-permute-start(bf16[2,2,6,64,128]{4,3,2,1,0:T(8,128)(2,1)S(1)} %collective-permute-done.1.refs_1_.refs_3_), channel_id=1, source_target_pairs={{2,0},{4,2},{6,4},{3,1},{5,3},{7,5},{10,8},{12,10},{14,12},{11,9},... | collective-permute-start | bytes 1179656 | tf_op jit(solution)/shard_map/ppermute | solution.py:165
  37.7 7.2 %collective-permute-start.6 = (bf16[6,2,6,64,128]{4,3,2,1,0:T(8,128)(2,1)S(1)}, bf16[6,2,6,64,128]{4,3,2,1,0:T(8,128)(2,1)S(1)}, u32[]{:S(2)}, u32[]{:S(2)}) collective-permute-start(bf16[6,2,6,64,128]{4,3,2,1,0:T(8,128)(2,1)S(1)} %get-tuple-element.57), channel_id=1, source_target_pairs={{0,8},{8,16},{16,24},{1,9},{9,17},{17,25},{2,10},{10,18},{18,26},{... | collective-permute-start | bytes 3538952 | tf_op jit(solution)/shard_map/ppermute | solution.py:165
  44.9 1.9 %collective-permute-start.7 = (bf16[6,2,6,64,128]{4,3,2,1,0:T(8,128)(2,1)S(1)}, bf16[6,2,6,64,128]{4,3,2,1,0:T(8,128)(2,1)S(1)}, u32[]{:S(2)}, u32[]{:S(2)}) collective-permute-start(bf16[6,2,6,64,128]{4,3,2,1,0:T(8,128)(2,1)S(1)} %get-tuple-element.56), channel_id=1, source_target_pairs={{8,0},{16,8},{24,16},{9,1},{17,9},{25,17},{10,2},{18,10},{26,18},{... | collective-permute-start | bytes 3538952 | tf_op jit(solution)/shard_map/ppermute | solution.py:165
  47.2 2.5 %collective-permute-done.12.refs_7_ = bf16[2,2,6,64,128]{4,3,2,1,0:T(8,128)(2,1)S(1)} collective-permute-done((bf16[2,2,6,64,128]{4,3,2,1,0:T(8,128)(2,1)S(1)}, bf16[2,2,6,64,128]{4,3,2,1,0:T(8,128)(2,1)S(1)}, u32[]{:S(2)}, u32[]{:S(2)}) %collective-permute-start.12) | collective-permute-done | bytes 393248 | tf_op jit(solution)/shard_map/ppermute | solution.py:165
  49.7 6.2 %collective-permute-start.13 = (bf16[6,2,6,64,128]{4,3,2,1,0:T(8,128)(2,1)S(1)}, bf16[6,2,6,64,128]{4,3,2,1,0:T(8,128)(2,1)S(1)}, u32[]{:S(2)}, u32[]{:S(2)}) collective-permute-start(bf16[6,2,6,64,128]{4,3,2,1,0:T(8,128)(2,1)S(1)} %get-tuple-element.45), channel_id=1, source_target_pairs={{0,8},{8,16},{16,24},{1,9},{9,17},{17,25},{2,10},{10,18},{18,26},{... | collective-permute-start | bytes 3538952 | tf_op jit(solution)/shard_map/ppermute | solution.py:165
  55.9 1.9 %collective-permute-start.14 = (bf16[6,2,6,64,128]{4,3,2,1,0:T(8,128)(2,1)S(1)}, bf16[6,2,6,64,128]{4,3,2,1,0:T(8,128)(2,1)S(1)}, u32[]{:S(2)}, u32[]{:S(2)}) collective-permute-start(bf16[6,2,6,64,128]{4,3,2,1,0:T(8,128)(2,1)S(1)} %get-tuple-element.44), channel_id=1, source_target_pairs={{8,0},{16,8},{24,16},{9,1},{17,9},{25,17},{10,2},{18,10},{26,18},{... | collective-permute-start | bytes 3538952 | tf_op jit(solution)/shard_map/ppermute | solution.py:165
  58.0 4.4 %collective-permute-done.7.refs_9_ = bf16[6,2,6,64,128]{4,3,2,1,0:T(8,128)(2,1)S(1)} collective-permute-done((bf16[6,2,6,64,128]{4,3,2,1,0:T(8,128)(2,1)S(1)}, bf16[6,2,6,64,128]{4,3,2,1,0:T(8,128)(2,1)S(1)}, u32[]{:S(2)}, u32[]{:S(2)}) %collective-permute-start.7) | collective-permute-done | bytes 1179680 | tf_op jit(solution)/shard_map/ppermute | solution.py:165
  62.4 5.7 %shard_map.102 = (bf16[2,6,128,128]{3,2,1,0:T(8,128)(2,1)S(1)}, f32[2,6,2,128]{3,2,1,0:T(2,128)S(1)}) custom-call(bf16[2,2,6,64,128]{4,3,2,1,0:T(8,128)(2,1)S(1)} %pad_maximum_fusion.refs_0_.refs_2_, bf16[2,2,6,64,128]{4,3,2,1,0:T(8,128)(2,1)S(1)} %collective-permute-done.1.refs_1_.refs_3_, ...), custom_call_target="tpu_custom_call" | custom-call | flops 905969664 | bytes 4718592 | tf_op jit(solution)/shard_map/pallas_call | solution.py:146
  68.2 3.1 %collective-permute-start.15 = (f32[2,6,2,128]{3,2,1,0:T(2,128)S(1)}, f32[2,6,2,128]{3,2,1,0:T(2,128)S(1)}, u32[]{:S(2)}, u32[]{:S(2)}) collective-permute-start(f32[2,6,2,128]{3,2,1,0:T(2,128)S(1)} %get-tuple-element.33.refs_11_.refs_10_), channel_id=1, source_target_pairs={{0,2},{2,4},{4,6},{1,3},{3,5},{5,7},{8,10},{10,12},{12,14},{9,11},... | collective-permute-start | bytes 36872 | tf_op jit(solution)/shard_map/ppermute | solution.py:165
  71.3 2.1 %collective-permute-start.16 = (f32[2,6,2,128]{3,2,1,0:T(2,128)S(1)}, f32[2,6,2,128]{3,2,1,0:T(2,128)S(1)}, u32[]{:S(2)}, u32[]{:S(2)}) collective-permute-start(f32[2,6,2,128]{3,2,1,0:T(2,128)S(1)} %get-tuple-element.33.refs_11_.refs_10_), channel_id=1, source_target_pairs={{2,0},{4,2},{6,4},{3,1},{5,3},{7,5},{10,8},{12,10},{14,12},{11,9},... | collective-permute-start | bytes 36872 | tf_op jit(solution)/shard_map/ppermute | solution.py:165
  73.5 5.1 %shard_map.103 = (bf16[2,2,6,64,128]{4,3,2,1,0:T(8,128)(2,1)S(1)}, bf16[2,2,6,64,128]{4,3,2,1,0:T(8,128)(2,1)S(1)}) custom-call(bf16[2,2,6,64,128]{4,3,2,1,0:T(8,128)(2,1)S(1)} %pad_maximum_fusion.refs_0_.refs_2_, bf16[2,2,6,64,128]{4,3,2,1,0:T(8,128)(2,1)S(1)} %collective-permute-done.1.refs_1_.refs_3_, ...), custom_call_target="tpu_custom_call" | custom-call | flops 1358954496 | bytes 4718592 | tf_op jit(solution)/shard_map/pallas_call | solution.py:146
  78.5 1.2 %collective-permute-start.8 = (bf16[2,2,6,64,128]{4,3,2,1,0:T(8,128)(2,1)S(1)}, bf16[2,2,6,64,128]{4,3,2,1,0:T(8,128)(2,1)S(1)}, u32[]{:S(2)}, u32[]{:S(2)}) collective-permute-start(bf16[2,2,6,64,128]{4,3,2,1,0:T(8,128)(2,1)S(1)} %get-tuple-element.35), channel_id=1, source_target_pairs={{0,1},{1,0},{2,3},{3,2},{4,5},{5,4},{6,7},{7,6},{8,9},{9,8},{10,11... | collective-permute-start | bytes 1179656 | tf_op jit(solution)/shard_map/ppermute | solution.py:170
  80.1 2.6 %collective-permute-start.17 = (f32[3,6,2,128]{3,2,1,0:T(2,128)S(1)}, f32[3,6,2,128]{3,2,1,0:T(2,128)S(1)}, u32[]{:S(2)}, u32[]{:S(2)}) collective-permute-start(f32[3,6,2,128]{3,2,1,0:T(2,128)S(1)} %pad_maximum_fusion.5), channel_id=1, source_target_pairs={{0,8},{8,16},{16,24},{1,9},{9,17},{17,25},{2,10},{10,18},{18,26},{... | collective-permute-start | bytes 55304 | tf_op jit(solution)/shard_map/ppermute | solution.py:165
  82.7 1.9 %collective-permute-start.18 = (f32[3,6,2,128]{3,2,1,0:T(2,128)S(1)}, f32[3,6,2,128]{3,2,1,0:T(2,128)S(1)}, u32[]{:S(2)}, u32[]{:S(2)}) collective-permute-start(f32[3,6,2,128]{3,2,1,0:T(2,128)S(1)} %pad_maximum_fusion.6), channel_id=1, source_target_pairs={{8,0},{16,8},{24,16},{9,1},{17,9},{25,17},{10,2},{18,10},{26,18},{... | collective-permute-start | bytes 55304 | tf_op jit(solution)/shard_map/ppermute | solution.py:165
  86.3 1.5 %collective-permute-done.18.refs_14_ = f32[3,6,2,128]{3,2,1,0:T(2,128)S(1)} collective-permute-done((f32[3,6,2,128]{3,2,1,0:T(2,128)S(1)}, f32[3,6,2,128]{3,2,1,0:T(2,128)S(1)}, u32[]{:S(2)}, u32[]{:S(2)}) %collective-permute-start.18) | collective-permute-done | bytes 18464 | tf_op jit(solution)/shard_map/ppermute | solution.py:165
  87.8 3.0 %shard_map.104 = (bf16[2,2,3,64,128]{4,3,2,1,0:T(8,128)(2,1)S(1)}, bf16[2,2,3,64,128]{4,3,2,1,0:T(8,128)(2,1)S(1)}) custom-call(bf16[2,2,6,64,128]{4,3,2,1,0:T(8,128)(2,1)S(1)} %pad_maximum_fusion.3.refs_2_.refs_0_, bf16[2,2,6,64,128]{4,3,2,1,0:T(8,128)(2,1)S(1)} %collective-permute-done.refs_3_.refs_1_, ...), custom_call_target="tpu_custom_call" | custom-call | flops 905969664 | bytes 2359296 | tf_op jit(solution)/shard_map/pallas_call | solution.py:146
  91.1 3.0 %shard_map.105 = (bf16[2,2,3,64,128]{4,3,2,1,0:T(8,128)(2,1)S(1)}, bf16[2,2,3,64,128]{4,3,2,1,0:T(8,128)(2,1)S(1)}) custom-call(bf16[2,2,6,64,128]{4,3,2,1,0:T(8,128)(2,1)S(1)} %pad_maximum_fusion.3.refs_2_.refs_0_, bf16[2,2,6,64,128]{4,3,2,1,0:T(8,128)(2,1)S(1)} %collective-permute-done.refs_3_.refs_1_, ...), custom_call_target="tpu_custom_call" | custom-call | flops 905969664 | bytes 2359296 | tf_op jit(solution)/shard_map/pallas_call | solution.py:146
  94.1 1.3 %collective-permute-start.20 = (bf16[2,2,3,64,128]{4,3,2,1,0:T(8,128)(2,1)S(1)}, bf16[2,2,3,64,128]{4,3,2,1,0:T(8,128)(2,1)S(1)}, u32[]{:S(2)}, u32[]{:S(2)}) collective-permute-start(bf16[2,2,3,64,128]{4,3,2,1,0:T(8,128)(2,1)S(1)} %get-tuple-element.39), channel_id=1, source_target_pairs={{0,1},{1,0},{2,3},{3,2},{4,5},{5,4},{6,7},{7,6},{8,9},{9,8},{10,11... | collective-permute-start | bytes 589832 | tf_op jit(solution)/shard_map/ppermute | solution.py:170
  95.5 1.2 %collective-permute-done.19 = bf16[2,2,3,64,128]{4,3,2,1,0:T(8,128)(2,1)S(1)} collective-permute-done((bf16[2,2,3,64,128]{4,3,2,1,0:T(8,128)(2,1)S(1)}, bf16[2,2,3,64,128]{4,3,2,1,0:T(8,128)(2,1)S(1)}, u32[]{:S(2)}, u32[]{:S(2)}) %collective-permute-start.19) | collective-permute-done | bytes 196640 | tf_op jit(solution)/shard_map/ppermute | solution.py:170
  96.9 3.2 %collective-permute-done.20 = bf16[2,2,3,64,128]{4,3,2,1,0:T(8,128)(2,1)S(1)} collective-permute-done((bf16[2,2,3,64,128]{4,3,2,1,0:T(8,128)(2,1)S(1)}, bf16[2,2,3,64,128]{4,3,2,1,0:T(8,128)(2,1)S(1)}, u32[]{:S(2)}, u32[]{:S(2)}) %collective-permute-start.20) | collective-permute-done | bytes 196640 | tf_op jit(solution)/shard_map/ppermute | solution.py:170
  (105 shorter events, 9.8 us)
Async XLA Ops:
  0.7 2.0 %copy-start = (bf16[2,8,8,12,128]{4,2,3,1,0:T(8,128)(2,1)S(1)}, bf16[2,8,8,12,128]{4,2,3,1,0:T(8,128)(2,1)}, u32[]{:S(2)}) copy-start(bf16[2,8,8,12,128]{4,2,3,1,0:T(8,128)(2,1)} %param.9) | copy-start | bytes 1179652
  1.8 1.0 %copy-start.1 = (bf16[2,8,8,12,128]{4,2,3,1,0:T(8,128)(2,1)S(1)}, bf16[2,8,8,12,128]{4,2,3,1,0:T(8,128)(2,1)}, u32[]{:S(2)}) copy-start(bf16[2,8,8,12,128]{4,2,3,1,0:T(8,128)(2,1)} %param.8) | copy-start | bytes 1179652
  2.7 7.1 %copy-start.2 = (bf16[2,8,8,12,128]{4,2,3,1,0:T(8,128)(2,1)S(1)}, bf16[2,8,8,12,128]{4,2,3,1,0:T(8,128)(2,1)}, u32[]{:S(2)}) copy-start(bf16[2,8,8,12,128]{4,2,3,1,0:T(8,128)(2,1)} %param.10) | copy-start | bytes 1179652
  2.7 7.1 %copy-start.3 = (bf16[2,8,8,12,128]{4,2,3,1,0:T(8,128)(2,1)S(1)}, bf16[2,8,8,12,128]{4,2,3,1,0:T(8,128)(2,1)}, u32[]{:S(2)}) copy-start(bf16[2,8,8,12,128]{4,2,3,1,0:T(8,128)(2,1)} %param.7) | copy-start | bytes 1179652
  3.0 21.6 %collective-permute-start.2 = (bf16[2,2,6,64,128]{4,3,2,1,0:T(8,128)(2,1)S(1)}, bf16[2,2,6,64,128]{4,3,2,1,0:T(8,128)(2,1)S(1)}, u32[]{:S(2)}, u32[]{:S(2)}) collective-permute-start(bf16[2,2,6,64,128]{4,3,2,1,0:T(8,128)(2,1)S(1)} %pad_maximum_fusion.3.refs_2_.refs_0_), channel_id=1, source_target_pairs={{0,2},{2,4},{4,6},{1,3},{3,5},{5,7},{8,10},{10,12},{12,14},{9,11},... | collective-permute-start | bytes 1179656 | tf_op jit(solution)/shard_map/ppermute | solution.py:165
  6.2 18.4 %collective-permute-start.3 = (bf16[2,2,6,64,128]{4,3,2,1,0:T(8,128)(2,1)S(1)}, bf16[2,2,6,64,128]{4,3,2,1,0:T(8,128)(2,1)S(1)}, u32[]{:S(2)}, u32[]{:S(2)}) collective-permute-start(bf16[2,2,6,64,128]{4,3,2,1,0:T(8,128)(2,1)S(1)} %pad_maximum_fusion.3.refs_2_.refs_0_), channel_id=1, source_target_pairs={{2,0},{4,2},{6,4},{3,1},{5,3},{7,5},{10,8},{12,10},{14,12},{11,9},... | collective-permute-start | bytes 1179656 | tf_op jit(solution)/shard_map/ppermute | solution.py:165
  8.3 9.6 %collective-permute-start = (bf16[2,2,6,64,128]{4,3,2,1,0:T(8,128)(2,1)}, bf16[2,2,6,64,128]{4,3,2,1,0:T(8,128)(2,1)S(1)}, u32[]{:S(2)}, u32[]{:S(2)}) collective-permute-start(bf16[2,2,6,64,128]{4,3,2,1,0:T(8,128)(2,1)} %pad_maximum_fusion.2), channel_id=1, source_target_pairs={{0,1},{1,0},{2,3},{3,2},{4,5},{5,4},{6,7},{7,6},{8,9},{9,8},{10,11... | collective-permute-start | bytes 1179656 | tf_op jit(solution)/shard_map/ppermute | solution.py:170
  9.8 0.8 copy-start.5
  9.9 2.3 %copy-start.6 = (bf16[4,3,9,2,9,1]{4,2,1,0,5,3:T(8,128)(2,1)S(1)}, bf16[4,3,9,2,9,1]{4,2,1,0,5,3:T(8,128)(2,1)}, u32[]{:S(2)}) copy-start(bf16[4,3,9,2,9,1]{4,2,1,0,5,3:T(8,128)(2,1)} %constant.210) | copy-start | bytes 11668
  11.8 2.0 %copy-start.4 = (bf16[18,1152]{1,0:T(8,128)(2,1)S(1)}, bf16[18,1152]{1,0:T(8,128)(2,1)}, u32[]{:S(2)}) copy-start(bf16[18,1152]{1,0:T(8,128)(2,1)} %constant.110.clone) | copy-start | bytes 124420
  18.0 8.7 %collective-permute-start.1 = (bf16[2,2,6,64,128]{4,3,2,1,0:T(8,128)(2,1)}, bf16[2,2,6,64,128]{4,3,2,1,0:T(8,128)(2,1)S(1)}, u32[]{:S(2)}, u32[]{:S(2)}) collective-permute-start(bf16[2,2,6,64,128]{4,3,2,1,0:T(8,128)(2,1)} %pad_maximum_fusion.1), channel_id=1, source_target_pairs={{0,1},{1,0},{2,3},{3,2},{4,5},{5,4},{6,7},{7,6},{8,9},{9,8},{10,11... | collective-permute-start | bytes 1179656 | tf_op jit(solution)/shard_map/ppermute | solution.py:170
  19.2 16.0 %collective-permute-start.4 = (bf16[2,2,6,64,128]{4,3,2,1,0:T(8,128)(2,1)S(1)}, bf16[2,2,6,64,128]{4,3,2,1,0:T(8,128)(2,1)S(1)}, u32[]{:S(2)}, u32[]{:S(2)}) collective-permute-start(bf16[2,2,6,64,128]{4,3,2,1,0:T(8,128)(2,1)S(1)} %collective-permute-done.refs_3_.refs_1_), channel_id=1, source_target_pairs={{0,2},{2,4},{4,6},{1,3},{3,5},{5,7},{8,10},{10,12},{12,14},{9,11},... | collective-permute-start | bytes 1179656 | tf_op jit(solution)/shard_map/ppermute | solution.py:165
  22.5 15.1 %collective-permute-start.5 = (bf16[2,2,6,64,128]{4,3,2,1,0:T(8,128)(2,1)S(1)}, bf16[2,2,6,64,128]{4,3,2,1,0:T(8,128)(2,1)S(1)}, u32[]{:S(2)}, u32[]{:S(2)}) collective-permute-start(bf16[2,2,6,64,128]{4,3,2,1,0:T(8,128)(2,1)S(1)} %collective-permute-done.refs_3_.refs_1_), channel_id=1, source_target_pairs={{2,0},{4,2},{6,4},{3,1},{5,3},{7,5},{10,8},{12,10},{14,12},{11,9},... | collective-permute-start | bytes 1179656 | tf_op jit(solution)/shard_map/ppermute | solution.py:165
  26.6 18.3 %collective-permute-start.9 = (bf16[2,2,6,64,128]{4,3,2,1,0:T(8,128)(2,1)S(1)}, bf16[2,2,6,64,128]{4,3,2,1,0:T(8,128)(2,1)S(1)}, u32[]{:S(2)}, u32[]{:S(2)}) collective-permute-start(bf16[2,2,6,64,128]{4,3,2,1,0:T(8,128)(2,1)S(1)} %pad_maximum_fusion.refs_0_.refs_2_), channel_id=1, source_target_pairs={{0,2},{2,4},{4,6},{1,3},{3,5},{5,7},{8,10},{10,12},{12,14},{9,11},... | collective-permute-start | bytes 1179656 | tf_op jit(solution)/shard_map/ppermute | solution.py:165
  29.8 17.3 %collective-permute-start.11 = (bf16[2,2,6,64,128]{4,3,2,1,0:T(8,128)(2,1)S(1)}, bf16[2,2,6,64,128]{4,3,2,1,0:T(8,128)(2,1)S(1)}, u32[]{:S(2)}, u32[]{:S(2)}) collective-permute-start(bf16[2,2,6,64,128]{4,3,2,1,0:T(8,128)(2,1)S(1)} %pad_maximum_fusion.refs_0_.refs_2_), channel_id=1, source_target_pairs={{2,0},{4,2},{6,4},{3,1},{5,3},{7,5},{10,8},{12,10},{14,12},{11,9},... | collective-permute-start | bytes 1179656 | tf_op jit(solution)/shard_map/ppermute | solution.py:165
  31.9 15.0 %collective-permute-start.10 = (bf16[2,2,6,64,128]{4,3,2,1,0:T(8,128)(2,1)S(1)}, bf16[2,2,6,64,128]{4,3,2,1,0:T(8,128)(2,1)S(1)}, u32[]{:S(2)}, u32[]{:S(2)}) collective-permute-start(bf16[2,2,6,64,128]{4,3,2,1,0:T(8,128)(2,1)S(1)} %collective-permute-done.1.refs_1_.refs_3_), channel_id=1, source_target_pairs={{0,2},{2,4},{4,6},{1,3},{3,5},{5,7},{8,10},{10,12},{12,14},{9,11},... | collective-permute-start | bytes 1179656 | tf_op jit(solution)/shard_map/ppermute | solution.py:165
  35.1 14.5 %collective-permute-start.12 = (bf16[2,2,6,64,128]{4,3,2,1,0:T(8,128)(2,1)S(1)}, bf16[2,2,6,64,128]{4,3,2,1,0:T(8,128)(2,1)S(1)}, u32[]{:S(2)}, u32[]{:S(2)}) collective-permute-start(bf16[2,2,6,64,128]{4,3,2,1,0:T(8,128)(2,1)S(1)} %collective-permute-done.1.refs_1_.refs_3_), channel_id=1, source_target_pairs={{2,0},{4,2},{6,4},{3,1},{5,3},{7,5},{10,8},{12,10},{14,12},{11,9},... | collective-permute-start | bytes 1179656 | tf_op jit(solution)/shard_map/ppermute | solution.py:165
  37.7 20.4 %collective-permute-start.6 = (bf16[6,2,6,64,128]{4,3,2,1,0:T(8,128)(2,1)S(1)}, bf16[6,2,6,64,128]{4,3,2,1,0:T(8,128)(2,1)S(1)}, u32[]{:S(2)}, u32[]{:S(2)}) collective-permute-start(bf16[6,2,6,64,128]{4,3,2,1,0:T(8,128)(2,1)S(1)} %get-tuple-element.57), channel_id=1, source_target_pairs={{0,8},{8,16},{16,24},{1,9},{9,17},{17,25},{2,10},{10,18},{18,26},{... | collective-permute-start | bytes 3538952 | tf_op jit(solution)/shard_map/ppermute | solution.py:165
  44.9 17.5 %collective-permute-start.7 = (bf16[6,2,6,64,128]{4,3,2,1,0:T(8,128)(2,1)S(1)}, bf16[6,2,6,64,128]{4,3,2,1,0:T(8,128)(2,1)S(1)}, u32[]{:S(2)}, u32[]{:S(2)}) collective-permute-start(bf16[6,2,6,64,128]{4,3,2,1,0:T(8,128)(2,1)S(1)} %get-tuple-element.56), channel_id=1, source_target_pairs={{8,0},{16,8},{24,16},{9,1},{17,9},{25,17},{10,2},{18,10},{26,18},{... | collective-permute-start | bytes 3538952 | tf_op jit(solution)/shard_map/ppermute | solution.py:165
  49.7 38.1 %collective-permute-start.13 = (bf16[6,2,6,64,128]{4,3,2,1,0:T(8,128)(2,1)S(1)}, bf16[6,2,6,64,128]{4,3,2,1,0:T(8,128)(2,1)S(1)}, u32[]{:S(2)}, u32[]{:S(2)}) collective-permute-start(bf16[6,2,6,64,128]{4,3,2,1,0:T(8,128)(2,1)S(1)} %get-tuple-element.45), channel_id=1, source_target_pairs={{0,8},{8,16},{16,24},{1,9},{9,17},{17,25},{2,10},{10,18},{18,26},{... | collective-permute-start | bytes 3538952 | tf_op jit(solution)/shard_map/ppermute | solution.py:165
  55.9 31.9 %collective-permute-start.14 = (bf16[6,2,6,64,128]{4,3,2,1,0:T(8,128)(2,1)S(1)}, bf16[6,2,6,64,128]{4,3,2,1,0:T(8,128)(2,1)S(1)}, u32[]{:S(2)}, u32[]{:S(2)}) collective-permute-start(bf16[6,2,6,64,128]{4,3,2,1,0:T(8,128)(2,1)S(1)} %get-tuple-element.44), channel_id=1, source_target_pairs={{8,0},{16,8},{24,16},{9,1},{17,9},{25,17},{10,2},{18,10},{26,18},{... | collective-permute-start | bytes 3538952 | tf_op jit(solution)/shard_map/ppermute | solution.py:165
  68.2 11.9 %collective-permute-start.15 = (f32[2,6,2,128]{3,2,1,0:T(2,128)S(1)}, f32[2,6,2,128]{3,2,1,0:T(2,128)S(1)}, u32[]{:S(2)}, u32[]{:S(2)}) collective-permute-start(f32[2,6,2,128]{3,2,1,0:T(2,128)S(1)} %get-tuple-element.33.refs_11_.refs_10_), channel_id=1, source_target_pairs={{0,2},{2,4},{4,6},{1,3},{3,5},{5,7},{8,10},{10,12},{12,14},{9,11},... | collective-permute-start | bytes 36872 | tf_op jit(solution)/shard_map/ppermute | solution.py:165
  71.3 8.7 %collective-permute-start.16 = (f32[2,6,2,128]{3,2,1,0:T(2,128)S(1)}, f32[2,6,2,128]{3,2,1,0:T(2,128)S(1)}, u32[]{:S(2)}, u32[]{:S(2)}) collective-permute-start(f32[2,6,2,128]{3,2,1,0:T(2,128)S(1)} %get-tuple-element.33.refs_11_.refs_10_), channel_id=1, source_target_pairs={{2,0},{4,2},{6,4},{3,1},{5,3},{7,5},{10,8},{12,10},{14,12},{11,9},... | collective-permute-start | bytes 36872 | tf_op jit(solution)/shard_map/ppermute | solution.py:165
  78.5 6.7 %collective-permute-start.8 = (bf16[2,2,6,64,128]{4,3,2,1,0:T(8,128)(2,1)S(1)}, bf16[2,2,6,64,128]{4,3,2,1,0:T(8,128)(2,1)S(1)}, u32[]{:S(2)}, u32[]{:S(2)}) collective-permute-start(bf16[2,2,6,64,128]{4,3,2,1,0:T(8,128)(2,1)S(1)} %get-tuple-element.35), channel_id=1, source_target_pairs={{0,1},{1,0},{2,3},{3,2},{4,5},{5,4},{6,7},{7,6},{8,9},{9,8},{10,11... | collective-permute-start | bytes 1179656 | tf_op jit(solution)/shard_map/ppermute | solution.py:170
  80.1 6.2 %collective-permute-start.17 = (f32[3,6,2,128]{3,2,1,0:T(2,128)S(1)}, f32[3,6,2,128]{3,2,1,0:T(2,128)S(1)}, u32[]{:S(2)}, u32[]{:S(2)}) collective-permute-start(f32[3,6,2,128]{3,2,1,0:T(2,128)S(1)} %pad_maximum_fusion.5), channel_id=1, source_target_pairs={{0,8},{8,16},{16,24},{1,9},{9,17},{17,25},{2,10},{10,18},{18,26},{... | collective-permute-start | bytes 55304 | tf_op jit(solution)/shard_map/ppermute | solution.py:165
  82.7 5.1 %collective-permute-start.18 = (f32[3,6,2,128]{3,2,1,0:T(2,128)S(1)}, f32[3,6,2,128]{3,2,1,0:T(2,128)S(1)}, u32[]{:S(2)}, u32[]{:S(2)}) collective-permute-start(f32[3,6,2,128]{3,2,1,0:T(2,128)S(1)} %pad_maximum_fusion.6), channel_id=1, source_target_pairs={{8,0},{16,8},{24,16},{9,1},{17,9},{25,17},{10,2},{18,10},{26,18},{... | collective-permute-start | bytes 55304 | tf_op jit(solution)/shard_map/ppermute | solution.py:165
  90.8 6.0 %collective-permute-start.19 = (bf16[2,2,3,64,128]{4,3,2,1,0:T(8,128)(2,1)S(1)}, bf16[2,2,3,64,128]{4,3,2,1,0:T(8,128)(2,1)S(1)}, u32[]{:S(2)}, u32[]{:S(2)}) collective-permute-start(bf16[2,2,3,64,128]{4,3,2,1,0:T(8,128)(2,1)S(1)} %get-tuple-element.37), channel_id=1, source_target_pairs={{0,1},{1,0},{2,3},{3,2},{4,5},{5,4},{6,7},{7,6},{8,9},{9,8},{10,11... | collective-permute-start | bytes 589832 | tf_op jit(solution)/shard_map/ppermute | solution.py:170
  94.1 6.1 %collective-permute-start.20 = (bf16[2,2,3,64,128]{4,3,2,1,0:T(8,128)(2,1)S(1)}, bf16[2,2,3,64,128]{4,3,2,1,0:T(8,128)(2,1)S(1)}, u32[]{:S(2)}, u32[]{:S(2)}) collective-permute-start(bf16[2,2,3,64,128]{4,3,2,1,0:T(8,128)(2,1)S(1)} %get-tuple-element.39), channel_id=1, source_target_pairs={{0,1},{1,0},{2,3},{3,2},{4,5},{5,4},{6,7},{7,6},{8,9},{9,8},{10,11... | collective-permute-start | bytes 589832 | tf_op jit(solution)/shard_map/ppermute | solution.py:170

commit v6 on v5

--- a/solution.py
+++ b/solution.py
@@ -26,33 +26,48 @@
     return jnp.broadcast_to(bias[:, None], (parts, tokens // parts, width)).reshape(tokens, width)
 
 
-def fill_bands(halo, bands):
-    parts = len(halo) // 3
-    own, before, after = halo[:parts], halo[parts : 2 * parts], halo[2 * parts : 3 * parts]
-    low, high = halo[3 * parts :]
-    frames, _, _, cells, _ = own[0].shape
+def fill_bands(frames, parts, cells, side, edge, bands):
     for at in range(frames + 2):
-        for row, beside in enumerate((before, own, after)):
+        for row in range(3):
             for part in range(parts):
                 place = pl.ds(((3 * at + row) * parts + part) * cells, cells)
                 for which, band in enumerate(bands):
                     if at == 0:
-                        band[place, :] = low[row * parts + part, which, 0]
+                        band[place, :] = edge(0, row, part, which)
                     elif at == frames + 1:
-                        band[place, :] = high[row * parts + part, which, 0]
+                        band[place, :] = edge(1, row, part, which)
                     else:
-                        band[place, :] = beside[part][at - 1, which, 0]
+                        band[place, :] = side(row, part, at - 1, which)
+
+
+def fill_keys(parts, halo, bands):
+    rows = (halo[parts : 2 * parts], halo[:parts], halo[2 * parts : 3 * parts])
+    edges = halo[3 * parts :]
+    frames, _, _, cells, _ = halo[0].shape
+    side = lambda row, part, at, which: rows[row][part][at, which, 0]
+    edge = lambda end, row, part, which: edges[end][3 * part + row, which, 0]
+    fill_bands(frames, parts, cells, side, edge, bands)
+
+
+def fill_queries(halo, bands):
+    own, before, after, low, high = halo
+    parts, frames, _, _, cells, _ = own.shape
+    side = lambda row, part, at, which: (before, own, after)[row][part, at, which, 0]
+    edge = lambda end, row, part, which: (low, high)[end][3 * part + row, which, 0]
+    fill_bands(frames, parts, cells, side, edge, bands)
 
 
 def slab(parts, at, which):
-    return jnp.concatenate([part[at, which, 0] for part in parts], axis=0)
+    if isinstance(parts, list):
+        return jnp.concatenate([part[at, which, 0] for part in parts], axis=0)
+    return jnp.concatenate([parts[part, at, which, 0] for part in range(parts.shape[0])], axis=0)
 
 
 def attend_kernel(scaling, parts, *refs):
-    pair, halo = refs[:parts], refs[parts : 4 * parts + 2]
-    bias, attended, stats, key_all, value_all = refs[4 * parts + 2 :]
+    pair, halo = refs[0], refs[1 : 3 * parts + 3]
+    bias, attended, stats, key_all, value_all = refs[3 * parts + 3 :]
     frames, _, tokens, _ = attended.shape
-    fill_bands(halo, (key_all, value_all))
+    fill_keys(parts, halo, (key_all, value_all))
     windows = [pl.ds(3 * at * tokens, 9 * tokens) for at in range(frames)]
     scores = [
         dot(slab(pair, at, 0), key_all[windows[at], :], NT) * (scaling * LOG2E) + spread(bias[at], tokens)
@@ -81,11 +96,11 @@
 
 
 def query_kernel(scaling, parts, *refs):
-    pair, halo = refs[:parts], refs[parts : 4 * parts + 2]
-    attended, stats, bias = refs[4 * parts + 2 : 4 * parts + 5]
-    grads, (key_all, value_all) = refs[4 * parts + 5 : -2], refs[-2:]
+    pair, halo = refs[0], refs[1 : 3 * parts + 3]
+    attended, stats, bias = refs[3 * parts + 3 : 3 * parts + 6]
+    grads, (key_all, value_all) = refs[3 * parts + 6 : -2], refs[-2:]
     frames, _, tokens, _ = attended.shape
-    fill_bands(halo, (key_all, value_all))
+    fill_keys(parts, halo, (key_all, value_all))
     windows = [pl.ds(3 * at * tokens, 9 * tokens) for at in range(frames)]
 
     def column(at, which):
@@ -103,11 +118,11 @@
 
 
 def back_kernel(scaling, parts, *refs):
-    pair, halo = refs[:parts], refs[parts : 4 * parts + 2]
-    own_st, before_st, after_st, low_st, high_st, bias = refs[4 * parts + 2 : 4 * parts + 8]
-    grads, (query_all, grad_all) = refs[4 * parts + 8 : -2], refs[-2:]
+    pair, halo = list(refs[:parts]), refs[parts : parts + 5]
+    own_st, before_st, after_st, low_st, high_st, bias = refs[parts + 5 : parts + 11]
+    grads, (query_all, grad_all) = refs[parts + 11 : -2], refs[-2:]
     frames, _, _, tokens = own_st.shape
-    fill_bands(halo, (query_all, grad_all))
+    fill_queries(halo, (query_all, grad_all))
 
     def stat_row(at, row, which):
         if at == 0:
@@ -138,11 +153,9 @@
     return pl.BlockSpec(block, lambda head: (0,) * dim + (head + first,) + (0, 0))
 
 
-def run(kernel, scaling, pair, halo, extra, bias, outs, first, count, products):
-    parts = len(pair)
-    frames, _, _, cells, dim = pair[0].shape
+def run(kernel, scaling, parts, operands, bias, outs, first, count, products):
+    frames, (cells, dim) = bias.shape[0], operands[0].shape[-2:]
     tokens = parts * cells
-    operands = tuple(pair) + tuple(halo) + tuple(extra)
     return pl.pallas_call(
         functools.partial(kernel, scaling, parts),
         grid=(count,),
@@ -170,18 +183,9 @@
     return lax.ppermute(tensor, "head", [(i, (i + shift) % size) for i in range(size)])
 
 
-def frame_edges(before, own, after):
-    rows = (before, own, after)
-
-    def edge(at):
-        return jnp.stack([part[at] for row in rows for part in row])
-
-    return step_along(edge(-1), "frame", 1), step_along(edge(0), "frame", -1)
-
-
-def stat_edges(before, own, after):
-    low = step_along(jnp.stack([before[-1], own[-1], after[-1]]), "frame", 1)
-    return low, step_along(jnp.stack([before[0], own[0], after[0]]), "frame", -1)
+def frame_edges(rows):
+    low = step_along(jnp.stack([row[-1] for row in rows]), "frame", 1)
+    return low, step_along(jnp.stack([row[0] for row in rows]), "frame", -1)
 
 
 def row_sides(own):
@@ -219,9 +223,24 @@
         chosen = (owner[:, None, :, None] & shift[None]).astype(jnp.float32)
         smalls.append(jnp.einsum("fioc,icpk->fpok", table, chosen))
     small = jnp.stack(smalls).reshape(2 * frames * size, -1).astype(jnp.bfloat16)
-    allowed = jnp.dot(small, spread_out, preferred_element_type=jnp.float32)
-    bias = jnp.where(allowed > 0.5, 0.0, MASKED).reshape(2, frames, size, -1)
-    return bias[0], bias[1]
+
+    def expand(held, which):
+        allowed = jnp.dot(held, spread_out, preferred_element_type=jnp.float32)
+        return jnp.where(allowed > 0.5, 0.0, MASKED).reshape(2, frames, size, -1)[which]
+
+    return small, expand
+
+
+def hold_kernel(source, out):
+    out[...] = source[...]
+
+
+def hold(source):
+    return pl.pallas_call(
+        hold_kernel,
+        out_shape=jax.ShapeDtypeStruct(source.shape, source.dtype),
+        cost_estimate=pl.CostEstimate(flops=3_000_000_000, bytes_accessed=0, transcendentals=0),
+    )(source)
 
 
 def on_device(queries, keys, values, out_grad, active):
@@ -252,30 +271,25 @@
         whole = jnp.transpose(whole, (0, 1, 2, 4, 3, 5))
         return whole[0], whole[1]
 
-    def sides_of(parts):
-        both = [row_sides(part) for part in parts]
-        return [up for up, _ in both], [down for _, down in both]
-
-    front_bias, back_bias = tile_biases(active, frames, columns_here, cells)
+    small, expand = tile_biases(active, frames, columns_here, cells)
+    mark = hold(small)
+    front_bias = expand(mark, 0)
     key_sent = [pair_of(keys, values, shift) for shift in range(1, size)]
-    key_sent, keys, values = lax.optimization_barrier((key_sent, keys, values))
-    key_here = [pair_of(keys, values, 0)]
-    key_near = sides_of(key_here)
     key_moved = [turn(key_sent[size - b - 1], size - b) for b in range(1, size)]
     query_held = [pair_of(queries, out_grad, shift) for shift in range(size)]
     query_held, key_moved = lax.optimization_barrier((query_held, key_moved))
-    key_far = sides_of(key_moved)
     query_moved = [turn(query_held[size - b], size - b) for b in range(1, size)]
-    query_parts = query_held[:1] + query_moved
-    query_parts, key_near = lax.optimization_barrier((query_parts, key_near))
-    query_near = sides_of(query_parts)
-    key_parts = key_here + key_moved
-    key_before, key_after = key_near[0] + key_far[0], key_near[1] + key_far[1]
-    key_halo = key_parts + key_before + key_after + list(frame_edges(key_before, key_parts, key_after))
-    query_before, query_after = query_near
-    query_halo = (
-        query_parts + query_before + query_after + list(frame_edges(query_before, query_parts, query_after))
-    )
+    key_here, front_bias = lax.optimization_barrier((pair_of(keys, values, 0), front_bias))
+    key_parts = [key_here] + key_moved
+    sides = [row_sides(part) for part in key_parts]
+    query_all, sides[0] = lax.optimization_barrier((jnp.stack(query_held[:1] + query_moved), sides[0]))
+    key_rows = [row for part, (before, after) in zip(key_parts, sides) for row in (before, part, after)]
+    back_bias = expand(mark, 1)
+    key_halo = key_parts + [before for before, _ in sides] + [after for _, after in sides]
+    key_halo += frame_edges(key_rows)
+    query_before, query_after = row_sides(query_all)
+    rows_all = [row[b] for b in range(size) for row in (query_before, query_all, query_after)]
+    query_halo = [query_all, query_before, query_after] + list(frame_edges(rows_all))
 
     def grads_shape(count):
         return [jax.ShapeDtypeStruct((2, frames, count, cells, dim), jnp.bfloat16)] * size
@@ -283,18 +297,22 @@
     attended_shape = jax.ShapeDtypeStruct((frames, groups, tokens, dim), jnp.bfloat16)
     stat_shape = jax.ShapeDtypeStruct((frames, groups, 2, tokens), jnp.float32)
     attended, stats = run(
-        attend_kernel, scaling, query_parts, key_halo, (), front_bias, [attended_shape, stat_shape], 0, groups, 2
+        attend_kernel, scaling, size, [query_all] + key_halo, front_bias, [attended_shape, stat_shape], 0, groups, 2
     )
+    stat_sides = row_sides(stats)
+    attended, stat_sides = lax.optimization_barrier((attended, stat_sides))
     front_grads = run(
-        query_kernel, scaling, query_parts, key_halo, (attended, stats), front_bias, grads_shape(groups),
+        query_kernel, scaling, size, [query_all] + key_halo + [attended, stats], front_bias, grads_shape(groups),
         0, groups, 3
     )
-    stat_sides = row_sides(stats)
-    stat_halo = (stats,) + stat_sides + stat_edges(stat_sides[0], stats, stat_sides[1])
+    stat_edges = frame_edges((stat_sides[0], stats, stat_sides[1]))
+    front_grads, stat_edges = lax.optimization_barrier((front_grads, stat_edges))
+    stat_halo = [stats] + list(stat_sides) + list(stat_edges)
     blocks = []
     for first, count in ((0, groups - groups // 2), (groups - groups // 2, groups // 2)):
         back_grads = run(
-            back_kernel, scaling, key_parts, query_halo, stat_halo, back_bias, grads_shape(count), first, count, 4
+            back_kernel, scaling, size, key_parts + query_halo + stat_halo, back_bias, grads_shape(count),
+            first, count, 4
         )
         blocks.append((first, back_grads))
     return from_heads([(0, front_grads)]) + from_heads(blocks)

time: 102 us -> 121 us (1.19)
  the two profiles are of different devices: /device:TPU:9 before, /device:TPU:4 now
where the time goes in v6:
time: 121 us; the launch traced here: 120 us
  starting transfers between devices  42.6 us (35%)
  waiting for transfers between devices  36.5 us (30%)
  Pallas kernels  20.6 us (17%)
  local copies, waits for them, and re-layouts  17.3 us (14%)
  between operations  1.29 us (1%)
    ppermute x14, starting transfers between devices, step_along(): lax.ppermute(tensor, axis, [(i, i + sign) for i in range(size) if 0 <= i...  36.9 us
    ppermute x14, waiting for transfers between devices, step_along(): lax.ppermute(tensor, axis, [(i, i + sign) for i in range(size) if 0 <= i...  21.3 us
    pallas_call x4, Pallas kernels, run(): pl.pallas_call(functools.partial(kernel, scaling, parts), grid=(count,),...  19.3 us
    ppermute x5, waiting for transfers between devices, turn(): lax.ppermute(tensor, 'head', [(i, (i + shift) % size) for i in range(size)])  15.1 us
    unnamed x44, local copies, waits for them, and re-layouts  7.36 us
    ppermute x5, starting transfers between devices, turn(): lax.ppermute(tensor, 'head', [(i, (i + shift) % size) for i in range(size)])  5.74 us
  transfers between devices with their start and end apart: 19, of which 11 were waited for; matrix products, arithmetic and copies ran while one was open for 11% of the time, Pallas kernels for 14%

profile of v6, /device:TPU:4, one launch (start us, length us, event | category | flops | bytes accessed | tf_op | source)
XLA Modules:
  0.0 119.7 jit_solution(60599329768871718)
XLA Ops:
  0.7 1.3 %dynamic-slice_bitcast_fusion = (bf16[2,6,8,8,128]{4,3,1,2,0:T(8,128)(2,1)S(1)}, bf16[2,6,8,8,128]{4,3,1,2,0:T(8,128)(2,1)S(1)}, bf16[2,6,8,8,128]{4,3,1,2,0:T(8,128)(2,1)S(1)}, bf16[2,6,8,8,128]{4,3,1,2,0:T(8,128)(2,1)S(1)}) fusion(bf16[2,8,8,12,128]{4,2,3,1,0:T(8,128)(2,1)} %param.9, s32[]{:T(128)S(6)} %select_n.92, s32[]{:T(128)S(6)} %select_n.94, ...), kind=kLoop, calls=%fused_computation.64 | loop fusion | bytes 1572872 | tf_op jit(solution)/shard_map/dynamic_slice | solution.py:259
  2.1 1.6 %collective-permute-start = (bf16[2,2,6,64,128]{4,3,2,1,0:T(8,128)(2,1)S(1)}, bf16[2,2,6,64,128]{4,3,2,1,0:T(8,128)(2,1)S(1)}, u32[]{:S(2)}, u32[]{:S(2)}) collective-permute-start(bf16[2,2,6,64,128]{4,3,2,1,0:T(8,128)(2,1)S(1)} %pad_maximum_fusion.3), channel_id=1, source_target_pairs={{0,1},{1,0},{2,3},{3,2},{4,5},{5,4},{6,7},{7,6},{8,9},{9,8},{10,11... | collective-permute-start | bytes 1179656 | tf_op jit(solution)/shard_map/ppermute | solution.py:183
  9.8 3.3 %collective-permute-done.refs_2_.refs_1_ = bf16[2,2,6,64,128]{4,3,2,1,0:T(8,128)(2,1)S(1)} collective-permute-done((bf16[2,2,6,64,128]{4,3,2,1,0:T(8,128)(2,1)S(1)}, bf16[2,2,6,64,128]{4,3,2,1,0:T(8,128)(2,1)S(1)}, u32[]{:S(2)}, u32[]{:S(2)}) %collective-permute-start) | collective-permute-done | bytes 393248 | tf_op jit(solution)/shard_map/ppermute | solution.py:183
  13.0 1.5 %collective-permute-start.1 = (bf16[2,2,6,64,128]{4,3,2,1,0:T(8,128)(2,1)S(1)}, bf16[2,2,6,64,128]{4,3,2,1,0:T(8,128)(2,1)S(1)}, u32[]{:S(2)}, u32[]{:S(2)}) collective-permute-start(bf16[2,2,6,64,128]{4,3,2,1,0:T(8,128)(2,1)S(1)} %pad_maximum_fusion.2), channel_id=1, source_target_pairs={{0,1},{1,0},{2,3},{3,2},{4,5},{5,4},{6,7},{7,6},{8,9},{9,8},{10,11... | collective-permute-start | bytes 1179656 | tf_op jit(solution)/shard_map/ppermute | solution.py:183
  15.3 3.5 %collective-permute-start.2 = (bf16[2,2,6,64,128]{4,3,2,1,0:T(8,128)(2,1)S(1)}, bf16[2,2,6,64,128]{4,3,2,1,0:T(8,128)(2,1)S(1)}, u32[]{:S(2)}, u32[]{:S(2)}) collective-permute-start(bf16[2,2,6,64,128]{4,3,2,1,0:T(8,128)(2,1)S(1)} %pad_maximum_fusion.4.refs_1_.refs_0_), channel_id=1, source_target_pairs={{0,2},{2,4},{4,6},{1,3},{3,5},{5,7},{8,10},{10,12},{12,14},{9,11},... | collective-permute-start | bytes 1179656 | tf_op jit(solution)/shard_map/ppermute | solution.py:178
  18.8 1.3 %collective-permute-start.3 = (bf16[2,2,6,64,128]{4,3,2,1,0:T(8,128)(2,1)S(1)}, bf16[2,2,6,64,128]{4,3,2,1,0:T(8,128)(2,1)S(1)}, u32[]{:S(2)}, u32[]{:S(2)}) collective-permute-start(bf16[2,2,6,64,128]{4,3,2,1,0:T(8,128)(2,1)S(1)} %pad_maximum_fusion.4.refs_1_.refs_0_), channel_id=1, source_target_pairs={{2,0},{4,2},{6,4},{3,1},{5,3},{7,5},{10,8},{12,10},{14,12},{11,9},... | collective-permute-start | bytes 1179656 | tf_op jit(solution)/shard_map/ppermute | solution.py:178
  20.1 4.6 %collective-permute-start.4 = (bf16[2,2,6,64,128]{4,3,2,1,0:T(8,128)(2,1)S(1)}, bf16[2,2,6,64,128]{4,3,2,1,0:T(8,128)(2,1)S(1)}, u32[]{:S(2)}, u32[]{:S(2)}) collective-permute-start(bf16[2,2,6,64,128]{4,3,2,1,0:T(8,128)(2,1)S(1)} %collective-permute-done.refs_2_.refs_1_), channel_id=1, source_target_pairs={{0,2},{2,4},{4,6},{1,3},{3,5},{5,7},{8,10},{10,12},{12,14},{9,11},... | collective-permute-start | bytes 1179656 | tf_op jit(solution)/shard_map/ppermute | solution.py:178
  24.7 1.3 %collective-permute-start.5 = (bf16[2,2,6,64,128]{4,3,2,1,0:T(8,128)(2,1)S(1)}, bf16[2,2,6,64,128]{4,3,2,1,0:T(8,128)(2,1)S(1)}, u32[]{:S(2)}, u32[]{:S(2)}) collective-permute-start(bf16[2,2,6,64,128]{4,3,2,1,0:T(8,128)(2,1)S(1)} %collective-permute-done.refs_2_.refs_1_), channel_id=1, source_target_pairs={{2,0},{4,2},{6,4},{3,1},{5,3},{7,5},{10,8},{12,10},{14,12},{11,9},... | collective-permute-start | bytes 1179656 | tf_op jit(solution)/shard_map/ppermute | solution.py:178
  26.1 2.3 %collective-permute-done.2.refs_3_ = bf16[2,2,6,64,128]{4,3,2,1,0:T(8,128)(2,1)S(1)} collective-permute-done((bf16[2,2,6,64,128]{4,3,2,1,0:T(8,128)(2,1)S(1)}, bf16[2,2,6,64,128]{4,3,2,1,0:T(8,128)(2,1)S(1)}, u32[]{:S(2)}, u32[]{:S(2)}) %collective-permute-start.2) | collective-permute-done | bytes 393248 | tf_op jit(solution)/shard_map/ppermute | solution.py:178
  28.4 4.4 %collective-permute-done.3.refs_5_ = bf16[2,2,6,64,128]{4,3,2,1,0:T(8,128)(2,1)S(1)} collective-permute-done((bf16[2,2,6,64,128]{4,3,2,1,0:T(8,128)(2,1)S(1)}, bf16[2,2,6,64,128]{4,3,2,1,0:T(8,128)(2,1)S(1)}, u32[]{:S(2)}, u32[]{:S(2)}) %collective-permute-start.3) | collective-permute-done | bytes 393248 | tf_op jit(solution)/shard_map/ppermute | solution.py:178
  32.8 3.5 %collective-permute-start.13 = (bf16[2,2,2,6,64,128]{5,4,3,2,1,0:T(8,128)(2,1)S(1)}, bf16[2,2,2,6,64,128]{5,4,3,2,1,0:T(8,128)(2,1)S(1)}, u32[]{:S(2)}, u32[]{:S(2)}) collective-permute-start(bf16[2,2,2,6,64,128]{5,4,3,2,1,0:T(8,128)(2,1)S(1)} %pad_maximum_fusion.refs_0_.refs_2_), channel_id=1, source_target_pairs={{0,2},{2,4},{4,6},{1,3},{3,5},{5,7},{8,10},{10,12},{12,14},{9,11},... | collective-permute-start | bytes 2359304 | tf_op jit(solution)/shard_map/ppermute | solution.py:178
  36.3 1.3 %collective-permute-start.14 = (bf16[2,2,2,6,64,128]{5,4,3,2,1,0:T(8,128)(2,1)S(1)}, bf16[2,2,2,6,64,128]{5,4,3,2,1,0:T(8,128)(2,1)S(1)}, u32[]{:S(2)}, u32[]{:S(2)}) collective-permute-start(bf16[2,2,2,6,64,128]{5,4,3,2,1,0:T(8,128)(2,1)S(1)} %pad_maximum_fusion.refs_0_.refs_2_), channel_id=1, source_target_pairs={{2,0},{4,2},{6,4},{3,1},{5,3},{7,5},{10,8},{12,10},{14,12},{11,9},... | collective-permute-start | bytes 2359304 | tf_op jit(solution)/shard_map/ppermute | solution.py:178
  37.9 3.3 %collective-permute-done.5.refs_6_ = bf16[2,2,6,64,128]{4,3,2,1,0:T(8,128)(2,1)S(1)} collective-permute-done((bf16[2,2,6,64,128]{4,3,2,1,0:T(8,128)(2,1)S(1)}, bf16[2,2,6,64,128]{4,3,2,1,0:T(8,128)(2,1)S(1)}, u32[]{:S(2)}, u32[]{:S(2)}) %collective-permute-start.5) | collective-permute-done | bytes 393248 | tf_op jit(solution)/shard_map/ppermute | solution.py:178
  41.3 1.9 %collective-permute-start.6 = (bf16[6,2,6,64,128]{4,3,2,1,0:T(8,128)(2,1)S(1)}, bf16[6,2,6,64,128]{4,3,2,1,0:T(8,128)(2,1)S(1)}, u32[]{:S(2)}, u32[]{:S(2)}) collective-permute-start(bf16[6,2,6,64,128]{4,3,2,1,0:T(8,128)(2,1)S(1)} %get-tuple-element.67), channel_id=1, source_target_pairs={{0,8},{8,16},{16,24},{1,9},{9,17},{17,25},{2,10},{10,18},{18,26},{... | collective-permute-start | bytes 3538952 | tf_op jit(solution)/shard_map/ppermute | solution.py:178
  43.2 3.6 %collective-permute-start.7 = (bf16[6,2,6,64,128]{4,3,2,1,0:T(8,128)(2,1)S(1)}, bf16[6,2,6,64,128]{4,3,2,1,0:T(8,128)(2,1)S(1)}, u32[]{:S(2)}, u32[]{:S(2)}) collective-permute-start(bf16[6,2,6,64,128]{4,3,2,1,0:T(8,128)(2,1)S(1)} %get-tuple-element.66), channel_id=1, source_target_pairs={{8,0},{16,8},{24,16},{9,1},{17,9},{25,17},{10,2},{18,10},{26,18},{... | collective-permute-start | bytes 3538952 | tf_op jit(solution)/shard_map/ppermute | solution.py:178
  46.8 4.5 %collective-permute-done.13.refs_3_ = bf16[2,2,2,6,64,128]{5,4,3,2,1,0:T(8,128)(2,1)S(1)} collective-permute-done((bf16[2,2,2,6,64,128]{5,4,3,2,1,0:T(8,128)(2,1)S(1)}, bf16[2,2,2,6,64,128]{5,4,3,2,1,0:T(8,128)(2,1)S(1)}, u32[]{:S(2)}, u32[]{:S(2)}) %collective-permute-start.13) | collective-permute-done | bytes 786464 | tf_op jit(solution)/shard_map/ppermute | solution.py:178
  52.8 2.6 %collective-permute-done.14.refs_4_ = bf16[2,2,2,6,64,128]{5,4,3,2,1,0:T(8,128)(2,1)S(1)} collective-permute-done((bf16[2,2,2,6,64,128]{5,4,3,2,1,0:T(8,128)(2,1)S(1)}, bf16[2,2,2,6,64,128]{5,4,3,2,1,0:T(8,128)(2,1)S(1)}, u32[]{:S(2)}, u32[]{:S(2)}) %collective-permute-start.14) | collective-permute-done | bytes 786464 | tf_op jit(solution)/shard_map/ppermute | solution.py:178
  58.6 1.9 %collective-permute-start.15 = (bf16[6,2,6,64,128]{4,3,2,1,0:T(8,128)(2,1)}, bf16[6,2,6,64,128]{4,3,2,1,0:T(8,128)(2,1)}, u32[]{:S(2)}, u32[]{:S(2)}) collective-permute-start(bf16[6,2,6,64,128]{4,3,2,1,0:T(8,128)(2,1)} %get-tuple-element.53), channel_id=1, source_target_pairs={{0,8},{8,16},{16,24},{1,9},{9,17},{17,25},{2,10},{10,18},{18,26},{... | collective-permute-start | bytes 3538952 | tf_op jit(solution)/shard_map/ppermute | solution.py:178
  60.5 3.6 %collective-permute-start.16 = (bf16[6,2,6,64,128]{4,3,2,1,0:T(8,128)(2,1)}, bf16[6,2,6,64,128]{4,3,2,1,0:T(8,128)(2,1)}, u32[]{:S(2)}, u32[]{:S(2)}) collective-permute-start(bf16[6,2,6,64,128]{4,3,2,1,0:T(8,128)(2,1)} %get-tuple-element.52), channel_id=1, source_target_pairs={{8,0},{16,8},{24,16},{9,1},{17,9},{25,17},{10,2},{18,10},{26,18},{... | collective-permute-start | bytes 3538952 | tf_op jit(solution)/shard_map/ppermute | solution.py:178
  64.2 5.7 %shard_map.103 = (bf16[2,6,128,128]{3,2,1,0:T(8,128)(2,1)S(1)}, f32[2,6,2,128]{3,2,1,0:T(2,128)S(1)}) custom-call(bf16[2,2,2,6,64,128]{5,4,3,2,1,0:T(8,128)(2,1)S(1)} %pad_maximum_fusion.refs_0_.refs_2_, bf16[2,2,6,64,128]{4,3,2,1,0:T(8,128)(2,1)S(1)} %pad_maximum_fusion.4.refs_1_.refs_0_, ...), custom_call_target="tpu_custom_call" | custom-call | flops 905969664 | bytes 4718592 | tf_op jit(solution)/shard_map/pallas_call | solution.py:159
  69.9 3.5 %collective-permute-start.8 = (f32[2,6,2,128]{3,2,1,0:T(2,128)S(1)}, f32[2,6,2,128]{3,2,1,0:T(2,128)S(1)}, u32[]{:S(2)}, u32[]{:S(2)}) collective-permute-start(f32[2,6,2,128]{3,2,1,0:T(2,128)S(1)} %get-tuple-element.36.refs_10_.refs_7_), channel_id=1, source_target_pairs={{0,2},{2,4},{4,6},{1,3},{3,5},{5,7},{8,10},{10,12},{12,14},{9,11},... | collective-permute-start | bytes 36872 | tf_op jit(solution)/shard_map/ppermute | solution.py:178
  73.4 1.3 %collective-permute-start.9 = (f32[2,6,2,128]{3,2,1,0:T(2,128)S(1)}, f32[2,6,2,128]{3,2,1,0:T(2,128)S(1)}, u32[]{:S(2)}, u32[]{:S(2)}) collective-permute-start(f32[2,6,2,128]{3,2,1,0:T(2,128)S(1)} %get-tuple-element.36.refs_10_.refs_7_), channel_id=1, source_target_pairs={{2,0},{4,2},{6,4},{3,1},{5,3},{7,5},{10,8},{12,10},{14,12},{11,9},... | collective-permute-start | bytes 36872 | tf_op jit(solution)/shard_map/ppermute | solution.py:178
  74.8 4.2 %collective-permute-done.9.refs_9_ = f32[2,6,2,128]{3,2,1,0:T(2,128)S(1)} collective-permute-done((f32[2,6,2,128]{3,2,1,0:T(2,128)S(1)}, f32[2,6,2,128]{3,2,1,0:T(2,128)S(1)}, u32[]{:S(2)}, u32[]{:S(2)}) %collective-permute-start.9) | collective-permute-done | bytes 12320 | tf_op jit(solution)/shard_map/ppermute | solution.py:178
  79.0 1.9 %collective-permute-start.10 = (f32[3,6,2,128]{3,2,1,0:T(2,128)S(1)}, f32[3,6,2,128]{3,2,1,0:T(2,128)S(1)}, u32[]{:S(2)}, u32[]{:S(2)}) collective-permute-start(f32[3,6,2,128]{3,2,1,0:T(2,128)S(1)} %pad_maximum_fusion.5), channel_id=1, source_target_pairs={{0,8},{8,16},{16,24},{1,9},{9,17},{17,25},{2,10},{10,18},{18,26},{... | collective-permute-start | bytes 55304 | tf_op jit(solution)/shard_map/ppermute | solution.py:178
  81.0 3.6 %collective-permute-start.11 = (f32[3,6,2,128]{3,2,1,0:T(2,128)S(1)}, f32[3,6,2,128]{3,2,1,0:T(2,128)S(1)}, u32[]{:S(2)}, u32[]{:S(2)}) collective-permute-start(f32[3,6,2,128]{3,2,1,0:T(2,128)S(1)} %pad_maximum_fusion.6), channel_id=1, source_target_pairs={{8,0},{16,8},{24,16},{9,1},{17,9},{25,17},{10,2},{18,10},{26,18},{... | collective-permute-start | bytes 55304 | tf_op jit(solution)/shard_map/ppermute | solution.py:178
  85.3 5.7 %shard_map.104 = (bf16[2,2,6,64,128]{4,3,2,1,0:T(8,128)(2,1)S(1)}, bf16[2,2,6,64,128]{4,3,2,1,0:T(8,128)(2,1)}) custom-call(bf16[2,2,2,6,64,128]{5,4,3,2,1,0:T(8,128)(2,1)S(1)} %pad_maximum_fusion.refs_0_.refs_2_, bf16[2,2,6,64,128]{4,3,2,1,0:T(8,128)(2,1)S(1)} %pad_maximum_fusion.4.refs_1_.refs_0_, ...), custom_call_target="tpu_custom_call" | custom-call | flops 1358954496 | bytes 4718592 | tf_op jit(solution)/shard_map/pallas_call | solution.py:159
  92.8 1.3 %squeeze.31.refs_12_ = f32[2,2,1152]{2,1,0:T(2,128)} reshape(f32[4,1152]{1,0:T(4,128)} %get-tuple-element.86) | data formatting | bytes 36864 | tf_op jit(solution)/shard_map/squeeze | solution.py:229
  94.5 8.0 %collective-permute-done.12 = bf16[2,2,6,64,128]{4,3,2,1,0:T(8,128)(2,1)} collective-permute-done((bf16[2,2,6,64,128]{4,3,2,1,0:T(8,128)(2,1)}, bf16[2,2,6,64,128]{4,3,2,1,0:T(8,128)(2,1)}, u32[]{:S(2)}, u32[]{:S(2)}) %collective-permute-start.12) | collective-permute-done | bytes 393248 | tf_op jit(solution)/shard_map/ppermute | solution.py:183
  104.5 3.9 %shard_map.105 = (bf16[2,2,3,64,128]{4,3,2,1,0:T(8,128)(2,1)S(1)}, bf16[2,2,3,64,128]{4,3,2,1,0:T(8,128)(2,1)S(1)}) custom-call(bf16[2,2,6,64,128]{4,3,2,1,0:T(8,128)(2,1)S(1)} %pad_maximum_fusion.4.refs_1_.refs_0_, bf16[2,2,6,64,128]{4,3,2,1,0:T(8,128)(2,1)S(1)} %collective-permute-done.refs_2_.refs_1_, ...), custom_call_target="tpu_custom_call" | custom-call | flops 905969664 | bytes 2359296 | tf_op jit(solution)/shard_map/pallas_call | solution.py:159
  109.0 3.9 %shard_map.106 = (bf16[2,2,3,64,128]{4,3,2,1,0:T(8,128)(2,1)S(1)}, bf16[2,2,3,64,128]{4,3,2,1,0:T(8,128)(2,1)S(1)}) custom-call(bf16[2,2,6,64,128]{4,3,2,1,0:T(8,128)(2,1)S(1)} %pad_maximum_fusion.4.refs_1_.refs_0_, bf16[2,2,6,64,128]{4,3,2,1,0:T(8,128)(2,1)S(1)} %collective-permute-done.refs_2_.refs_1_, ...), custom_call_target="tpu_custom_call" | custom-call | flops 905969664 | bytes 2359296 | tf_op jit(solution)/shard_map/pallas_call | solution.py:159
  113.0 1.5 %collective-permute-start.18 = (bf16[2,2,3,64,128]{4,3,2,1,0:T(8,128)(2,1)S(1)}, bf16[2,2,3,64,128]{4,3,2,1,0:T(8,128)(2,1)S(1)}, u32[]{:S(2)}, u32[]{:S(2)}) collective-permute-start(bf16[2,2,3,64,128]{4,3,2,1,0:T(8,128)(2,1)S(1)} %get-tuple-element.49), channel_id=1, source_target_pairs={{0,1},{1,0},{2,3},{3,2},{4,5},{5,4},{6,7},{7,6},{8,9},{9,8},{10,11... | collective-permute-start | bytes 589832 | tf_op jit(solution)/shard_map/ppermute | solution.py:183
  115.2 3.5 %collective-permute-done.18 = bf16[2,2,3,64,128]{4,3,2,1,0:T(8,128)(2,1)S(1)} collective-permute-done((bf16[2,2,3,64,128]{4,3,2,1,0:T(8,128)(2,1)S(1)}, bf16[2,2,3,64,128]{4,3,2,1,0:T(8,128)(2,1)S(1)}, u32[]{:S(2)}, u32[]{:S(2)}) %collective-permute-start.18) | collective-permute-done | bytes 196640 | tf_op jit(solution)/shard_map/ppermute | solution.py:183
  (120 shorter events, 19.0 us)
Async XLA Ops:
  2.0 1.9 %copy-start.11 = (bf16[2,8,8,12,128]{4,2,3,1,0:T(8,128)(2,1)S(1)}, bf16[2,8,8,12,128]{4,2,3,1,0:T(8,128)(2,1)}, u32[]{:S(2)}) copy-start(bf16[2,8,8,12,128]{4,2,3,1,0:T(8,128)(2,1)} %param.10) | copy-start | bytes 1179652
  2.0 1.9 %copy-start.12 = (bf16[2,8,8,12,128]{4,2,3,1,0:T(8,128)(2,1)S(1)}, bf16[2,8,8,12,128]{4,2,3,1,0:T(8,128)(2,1)}, u32[]{:S(2)}) copy-start(bf16[2,8,8,12,128]{4,2,3,1,0:T(8,128)(2,1)} %param.7) | copy-start | bytes 1179652
  2.1 10.9 %collective-permute-start = (bf16[2,2,6,64,128]{4,3,2,1,0:T(8,128)(2,1)S(1)}, bf16[2,2,6,64,128]{4,3,2,1,0:T(8,128)(2,1)S(1)}, u32[]{:S(2)}, u32[]{:S(2)}) collective-permute-start(bf16[2,2,6,64,128]{4,3,2,1,0:T(8,128)(2,1)S(1)} %pad_maximum_fusion.3), channel_id=1, source_target_pairs={{0,1},{1,0},{2,3},{3,2},{4,5},{5,4},{6,7},{7,6},{8,9},{9,8},{10,11... | collective-permute-start | bytes 1179656 | tf_op jit(solution)/shard_map/ppermute | solution.py:183
  3.9 2.3 %copy-start.16 = (bf16[4,3,9,2,9,1]{4,2,1,0,5,3:T(8,128)(2,1)S(1)}, bf16[4,3,9,2,9,1]{4,2,1,0,5,3:T(8,128)(2,1)}, u32[]{:S(2)}) copy-start(bf16[4,3,9,2,9,1]{4,2,1,0,5,3:T(8,128)(2,1)} %constant.215) | copy-start | bytes 11668
  8.8 0.8 copy-start.13
  8.8 0.8 copy-start.15
  13.0 13.0 %collective-permute-start.1 = (bf16[2,2,6,64,128]{4,3,2,1,0:T(8,128)(2,1)S(1)}, bf16[2,2,6,64,128]{4,3,2,1,0:T(8,128)(2,1)S(1)}, u32[]{:S(2)}, u32[]{:S(2)}) collective-permute-start(bf16[2,2,6,64,128]{4,3,2,1,0:T(8,128)(2,1)S(1)} %pad_maximum_fusion.2), channel_id=1, source_target_pairs={{0,1},{1,0},{2,3},{3,2},{4,5},{5,4},{6,7},{7,6},{8,9},{9,8},{10,11... | collective-permute-start | bytes 1179656 | tf_op jit(solution)/shard_map/ppermute | solution.py:183
  15.3 48.9 %copy-start.1 = (f32[2,2,1152]{2,1,0:T(2,128)}, f32[2,2,1152]{2,1,0:T(2,128)S(1)}, u32[]{:S(2)}) copy-start(f32[2,2,1152]{2,1,0:T(2,128)S(1)} %squeeze.28.refs_9_.refs_11_) | copy-start | bytes 55300
  15.3 13.0 %collective-permute-start.2 = (bf16[2,2,6,64,128]{4,3,2,1,0:T(8,128)(2,1)S(1)}, bf16[2,2,6,64,128]{4,3,2,1,0:T(8,128)(2,1)S(1)}, u32[]{:S(2)}, u32[]{:S(2)}) collective-permute-start(bf16[2,2,6,64,128]{4,3,2,1,0:T(8,128)(2,1)S(1)} %pad_maximum_fusion.4.refs_1_.refs_0_), channel_id=1, source_target_pairs={{0,2},{2,4},{4,6},{1,3},{3,5},{5,7},{8,10},{10,12},{12,14},{9,11},... | collective-permute-start | bytes 1179656 | tf_op jit(solution)/shard_map/ppermute | solution.py:178
  18.8 13.9 %collective-permute-start.3 = (bf16[2,2,6,64,128]{4,3,2,1,0:T(8,128)(2,1)S(1)}, bf16[2,2,6,64,128]{4,3,2,1,0:T(8,128)(2,1)S(1)}, u32[]{:S(2)}, u32[]{:S(2)}) collective-permute-start(bf16[2,2,6,64,128]{4,3,2,1,0:T(8,128)(2,1)S(1)} %pad_maximum_fusion.4.refs_1_.refs_0_), channel_id=1, source_target_pairs={{2,0},{4,2},{6,4},{3,1},{5,3},{7,5},{10,8},{12,10},{14,12},{11,9},... | collective-permute-start | bytes 1179656 | tf_op jit(solution)/shard_map/ppermute | solution.py:178
  20.1 17.6 %collective-permute-start.4 = (bf16[2,2,6,64,128]{4,3,2,1,0:T(8,128)(2,1)S(1)}, bf16[2,2,6,64,128]{4,3,2,1,0:T(8,128)(2,1)S(1)}, u32[]{:S(2)}, u32[]{:S(2)}) collective-permute-start(bf16[2,2,6,64,128]{4,3,2,1,0:T(8,128)(2,1)S(1)} %collective-permute-done.refs_2_.refs_1_), channel_id=1, source_target_pairs={{0,2},{2,4},{4,6},{1,3},{3,5},{5,7},{8,10},{10,12},{12,14},{9,11},... | collective-permute-start | bytes 1179656 | tf_op jit(solution)/shard_map/ppermute | solution.py:178
  24.7 16.5 %collective-permute-start.5 = (bf16[2,2,6,64,128]{4,3,2,1,0:T(8,128)(2,1)S(1)}, bf16[2,2,6,64,128]{4,3,2,1,0:T(8,128)(2,1)S(1)}, u32[]{:S(2)}, u32[]{:S(2)}) collective-permute-start(bf16[2,2,6,64,128]{4,3,2,1,0:T(8,128)(2,1)S(1)} %collective-permute-done.refs_2_.refs_1_), channel_id=1, source_target_pairs={{2,0},{4,2},{6,4},{3,1},{5,3},{7,5},{10,8},{12,10},{14,12},{11,9},... | collective-permute-start | bytes 1179656 | tf_op jit(solution)/shard_map/ppermute | solution.py:178
  32.8 18.5 %collective-permute-start.13 = (bf16[2,2,2,6,64,128]{5,4,3,2,1,0:T(8,128)(2,1)S(1)}, bf16[2,2,2,6,64,128]{5,4,3,2,1,0:T(8,128)(2,1)S(1)}, u32[]{:S(2)}, u32[]{:S(2)}) collective-permute-start(bf16[2,2,2,6,64,128]{5,4,3,2,1,0:T(8,128)(2,1)S(1)} %pad_maximum_fusion.refs_0_.refs_2_), channel_id=1, source_target_pairs={{0,2},{2,4},{4,6},{1,3},{3,5},{5,7},{8,10},{10,12},{12,14},{9,11},... | collective-permute-start | bytes 2359304 | tf_op jit(solution)/shard_map/ppermute | solution.py:178
  36.3 19.1 %collective-permute-start.14 = (bf16[2,2,2,6,64,128]{5,4,3,2,1,0:T(8,128)(2,1)S(1)}, bf16[2,2,2,6,64,128]{5,4,3,2,1,0:T(8,128)(2,1)S(1)}, u32[]{:S(2)}, u32[]{:S(2)}) collective-permute-start(bf16[2,2,2,6,64,128]{5,4,3,2,1,0:T(8,128)(2,1)S(1)} %pad_maximum_fusion.refs_0_.refs_2_), channel_id=1, source_target_pairs={{2,0},{4,2},{6,4},{3,1},{5,3},{7,5},{10,8},{12,10},{14,12},{11,9},... | collective-permute-start | bytes 2359304 | tf_op jit(solution)/shard_map/ppermute | solution.py:178
  41.3 22.9 %collective-permute-start.6 = (bf16[6,2,6,64,128]{4,3,2,1,0:T(8,128)(2,1)S(1)}, bf16[6,2,6,64,128]{4,3,2,1,0:T(8,128)(2,1)S(1)}, u32[]{:S(2)}, u32[]{:S(2)}) collective-permute-start(bf16[6,2,6,64,128]{4,3,2,1,0:T(8,128)(2,1)S(1)} %get-tuple-element.67), channel_id=1, source_target_pairs={{0,8},{8,16},{16,24},{1,9},{9,17},{17,25},{2,10},{10,18},{18,26},{... | collective-permute-start | bytes 3538952 | tf_op jit(solution)/shard_map/ppermute | solution.py:178
  43.2 21.0 %collective-permute-start.7 = (bf16[6,2,6,64,128]{4,3,2,1,0:T(8,128)(2,1)S(1)}, bf16[6,2,6,64,128]{4,3,2,1,0:T(8,128)(2,1)S(1)}, u32[]{:S(2)}, u32[]{:S(2)}) collective-permute-start(bf16[6,2,6,64,128]{4,3,2,1,0:T(8,128)(2,1)S(1)} %get-tuple-element.66), channel_id=1, source_target_pairs={{8,0},{16,8},{24,16},{9,1},{17,9},{25,17},{10,2},{18,10},{26,18},{... | collective-permute-start | bytes 3538952 | tf_op jit(solution)/shard_map/ppermute | solution.py:178
  58.6 45.9 %collective-permute-start.15 = (bf16[6,2,6,64,128]{4,3,2,1,0:T(8,128)(2,1)}, bf16[6,2,6,64,128]{4,3,2,1,0:T(8,128)(2,1)}, u32[]{:S(2)}, u32[]{:S(2)}) collective-permute-start(bf16[6,2,6,64,128]{4,3,2,1,0:T(8,128)(2,1)} %get-tuple-element.53), channel_id=1, source_target_pairs={{0,8},{8,16},{16,24},{1,9},{9,17},{17,25},{2,10},{10,18},{18,26},{... | collective-permute-start | bytes 3538952 | tf_op jit(solution)/shard_map/ppermute | solution.py:178
  60.5 44.0 %collective-permute-start.16 = (bf16[6,2,6,64,128]{4,3,2,1,0:T(8,128)(2,1)}, bf16[6,2,6,64,128]{4,3,2,1,0:T(8,128)(2,1)}, u32[]{:S(2)}, u32[]{:S(2)}) collective-permute-start(bf16[6,2,6,64,128]{4,3,2,1,0:T(8,128)(2,1)} %get-tuple-element.52), channel_id=1, source_target_pairs={{8,0},{16,8},{24,16},{9,1},{17,9},{25,17},{10,2},{18,10},{26,18},{... | collective-permute-start | bytes 3538952 | tf_op jit(solution)/shard_map/ppermute | solution.py:178
  69.9 4.8 %collective-permute-start.8 = (f32[2,6,2,128]{3,2,1,0:T(2,128)S(1)}, f32[2,6,2,128]{3,2,1,0:T(2,128)S(1)}, u32[]{:S(2)}, u32[]{:S(2)}) collective-permute-start(f32[2,6,2,128]{3,2,1,0:T(2,128)S(1)} %get-tuple-element.36.refs_10_.refs_7_), channel_id=1, source_target_pairs={{0,2},{2,4},{4,6},{1,3},{3,5},{5,7},{8,10},{10,12},{12,14},{9,11},... | collective-permute-start | bytes 36872 | tf_op jit(solution)/shard_map/ppermute | solution.py:178
  73.4 5.6 %collective-permute-start.9 = (f32[2,6,2,128]{3,2,1,0:T(2,128)S(1)}, f32[2,6,2,128]{3,2,1,0:T(2,128)S(1)}, u32[]{:S(2)}, u32[]{:S(2)}) collective-permute-start(f32[2,6,2,128]{3,2,1,0:T(2,128)S(1)} %get-tuple-element.36.refs_10_.refs_7_), channel_id=1, source_target_pairs={{2,0},{4,2},{6,4},{3,1},{5,3},{7,5},{10,8},{12,10},{14,12},{11,9},... | collective-permute-start | bytes 36872 | tf_op jit(solution)/shard_map/ppermute | solution.py:178
  74.8 6.2 %copy-start.3 = (f32[2,6,2,128]{3,2,1,0:T(2,128)}, f32[2,6,2,128]{3,2,1,0:T(2,128)S(1)}, u32[]{:S(2)}) copy-start(f32[2,6,2,128]{3,2,1,0:T(2,128)S(1)} %collective-permute-done.8.refs_8_) | copy-start | bytes 36868
  79.0 2.0 %copy-start.5 = (f32[2,6,2,128]{3,2,1,0:T(2,128)}, f32[2,6,2,128]{3,2,1,0:T(2,128)S(1)}, u32[]{:S(2)}) copy-start(f32[2,6,2,128]{3,2,1,0:T(2,128)S(1)} %collective-permute-done.9.refs_9_) | copy-start | bytes 36868
  79.0 12.1 %collective-permute-start.10 = (f32[3,6,2,128]{3,2,1,0:T(2,128)S(1)}, f32[3,6,2,128]{3,2,1,0:T(2,128)S(1)}, u32[]{:S(2)}, u32[]{:S(2)}) collective-permute-start(f32[3,6,2,128]{3,2,1,0:T(2,128)S(1)} %pad_maximum_fusion.5), channel_id=1, source_target_pairs={{0,8},{8,16},{16,24},{1,9},{9,17},{17,25},{2,10},{10,18},{18,26},{... | collective-permute-start | bytes 55304 | tf_op jit(solution)/shard_map/ppermute | solution.py:178
  81.0 10.7 %collective-permute-start.11 = (f32[3,6,2,128]{3,2,1,0:T(2,128)S(1)}, f32[3,6,2,128]{3,2,1,0:T(2,128)S(1)}, u32[]{:S(2)}, u32[]{:S(2)}) collective-permute-start(f32[3,6,2,128]{3,2,1,0:T(2,128)S(1)} %pad_maximum_fusion.6), channel_id=1, source_target_pairs={{8,0},{16,8},{24,16},{9,1},{17,9},{25,17},{10,2},{18,10},{26,18},{... | collective-permute-start | bytes 55304 | tf_op jit(solution)/shard_map/ppermute | solution.py:178
  92.3 10.1 %collective-permute-start.12 = (bf16[2,2,6,64,128]{4,3,2,1,0:T(8,128)(2,1)}, bf16[2,2,6,64,128]{4,3,2,1,0:T(8,128)(2,1)}, u32[]{:S(2)}, u32[]{:S(2)}) collective-permute-start(bf16[2,2,6,64,128]{4,3,2,1,0:T(8,128)(2,1)} %get-tuple-element.43), channel_id=1, source_target_pairs={{0,1},{1,0},{2,3},{3,2},{4,5},{5,4},{6,7},{7,6},{8,9},{9,8},{10,11... | collective-permute-start | bytes 1179656 | tf_op jit(solution)/shard_map/ppermute | solution.py:183
  94.4 10.0 %copy-start = (f32[2,2,1152]{2,1,0:T(2,128)S(1)}, f32[2,2,1152]{2,1,0:T(2,128)}, u32[]{:S(2)}) copy-start(f32[2,2,1152]{2,1,0:T(2,128)} %squeeze.31.refs_12_) | copy-start | bytes 55300
  94.4 10.0 %copy-start.4 = (f32[2,6,2,128]{3,2,1,0:T(2,128)S(1)}, f32[2,6,2,128]{3,2,1,0:T(2,128)}, u32[]{:S(2)}) copy-start(f32[2,6,2,128]{3,2,1,0:T(2,128)} %copy-done.3) | copy-start | bytes 36868
  94.4 10.0 %copy-start.6 = (f32[2,6,2,128]{3,2,1,0:T(2,128)S(1)}, f32[2,6,2,128]{3,2,1,0:T(2,128)}, u32[]{:S(2)}) copy-start(f32[2,6,2,128]{3,2,1,0:T(2,128)} %copy-done.5) | copy-start | bytes 36868
  94.4 10.0 %copy-start.8 = (f32[3,6,2,128]{3,2,1,0:T(2,128)S(1)}, f32[3,6,2,128]{3,2,1,0:T(2,128)}, u32[]{:S(2)}) copy-start(f32[3,6,2,128]{3,2,1,0:T(2,128)} %copy-done.7) | copy-start | bytes 55300
  94.4 10.0 %copy-start.10 = (f32[3,6,2,128]{3,2,1,0:T(2,128)S(1)}, f32[3,6,2,128]{3,2,1,0:T(2,128)}, u32[]{:S(2)}) copy-start(f32[3,6,2,128]{3,2,1,0:T(2,128)} %copy-done.9) | copy-start | bytes 55300
  108.4 6.7 %collective-permute-start.17 = (bf16[2,2,3,64,128]{4,3,2,1,0:T(8,128)(2,1)S(1)}, bf16[2,2,3,64,128]{4,3,2,1,0:T(8,128)(2,1)S(1)}, u32[]{:S(2)}, u32[]{:S(2)}) collective-permute-start(bf16[2,2,3,64,128]{4,3,2,1,0:T(8,128)(2,1)S(1)} %get-tuple-element.47), channel_id=1, source_target_pairs={{0,1},{1,0},{2,3},{3,2},{4,5},{5,4},{6,7},{7,6},{8,9},{9,8},{10,11... | collective-permute-start | bytes 589832 | tf_op jit(solution)/shard_map/ppermute | solution.py:183
  113.0 5.7 %collective-permute-start.18 = (bf16[2,2,3,64,128]{4,3,2,1,0:T(8,128)(2,1)S(1)}, bf16[2,2,3,64,128]{4,3,2,1,0:T(8,128)(2,1)S(1)}, u32[]{:S(2)}, u32[]{:S(2)}) collective-permute-start(bf16[2,2,3,64,128]{4,3,2,1,0:T(8,128)(2,1)S(1)} %get-tuple-element.49), channel_id=1, source_target_pairs={{0,1},{1,0},{2,3},{3,2},{4,5},{5,4},{6,7},{7,6},{8,9},{9,8},{10,11... | collective-permute-start | bytes 589832 | tf_op jit(solution)/shard_map/ppermute | solution.py:183
  (4 other events, 2.7 us)

commit v7 on v6

--- a/solution.py
+++ b/solution.py
@@ -51,16 +51,16 @@
 
 def fill_queries(halo, bands):
     own, before, after, low, high = halo
-    parts, frames, _, _, cells, _ = own.shape
-    side = lambda row, part, at, which: (before, own, after)[row][part, at, which, 0]
-    edge = lambda end, row, part, which: (low, high)[end][3 * part + row, which, 0]
+    frames, parts, _, _, cells, _ = own.shape
+    side = lambda row, part, at, which: (before, own, after)[row][at, part, which, 0]
+    edge = lambda end, row, part, which: (low, high)[end][row, part, which, 0]
     fill_bands(frames, parts, cells, side, edge, bands)
 
 
 def slab(parts, at, which):
     if isinstance(parts, list):
         return jnp.concatenate([part[at, which, 0] for part in parts], axis=0)
-    return jnp.concatenate([parts[part, at, which, 0] for part in range(parts.shape[0])], axis=0)
+    return jnp.concatenate([parts[at, part, which, 0] for part in range(parts.shape[1])], axis=0)
 
 
 def attend_kernel(scaling, parts, *refs):
@@ -186,6 +186,31 @@
 def frame_edges(rows):
     low = step_along(jnp.stack([row[-1] for row in rows]), "frame", 1)
     return low, step_along(jnp.stack([row[0] for row in rows]), "frame", -1)
+
+
+def edges_kernel(before, own, after, first, last, sems):
+    copies = []
+    for row, source in enumerate((before, own, after)):
+        for side, (out, at) in enumerate(((first, 0), (last, source.shape[0] - 1))):
+            copies.append(pltpu.make_async_copy(source.at[at], out.at[row], sems.at[row, side]))
+    for copy in copies:
+        copy.start()
+    for copy in copies:
+        copy.wait()
+
+
+def stacked_edges(before, own, after):
+    edge = jax.ShapeDtypeStruct((3,) + own.shape[1:], own.dtype)
+    anywhere = pl.BlockSpec(memory_space=pl.ANY)
+    first, last = pl.pallas_call(
+        edges_kernel,
+        out_shape=(edge, edge),
+        in_specs=[anywhere] * 3,
+        out_specs=(anywhere, anywhere),
+        scratch_shapes=[pltpu.SemaphoreType.DMA((3, 2))],
+        cost_estimate=pl.CostEstimate(flops=0, bytes_accessed=4 * edge.size * 2, transcendentals=0),
+    )(before, own, after)
+    return step_along(last, "frame", 1), step_along(first, "frame", -1)
 
 
 def row_sides(own):
@@ -223,24 +248,9 @@
         chosen = (owner[:, None, :, None] & shift[None]).astype(jnp.float32)
         smalls.append(jnp.einsum("fioc,icpk->fpok", table, chosen))
     small = jnp.stack(smalls).reshape(2 * frames * size, -1).astype(jnp.bfloat16)
-
-    def expand(held, which):
-        allowed = jnp.dot(held, spread_out, preferred_element_type=jnp.float32)
-        return jnp.where(allowed > 0.5, 0.0, MASKED).reshape(2, frames, size, -1)[which]
-
-    return small, expand
-
-
-def hold_kernel(source, out):
-    out[...] = source[...]
-
-
-def hold(source):
-    return pl.pallas_call(
-        hold_kernel,
-        out_shape=jax.ShapeDtypeStruct(source.shape, source.dtype),
-        cost_estimate=pl.CostEstimate(flops=3_000_000_000, bytes_accessed=0, transcendentals=0),
-    )(source)
+    allowed = jnp.dot(small, spread_out, preferred_element_type=jnp.float32)
+    bias = jnp.where(allowed > 0.5, 0.0, MASKED).reshape(2, frames, size, -1)
+    return bias[0], bias[1]
 
 
 def on_device(queries, keys, values, out_grad, active):
@@ -271,25 +281,23 @@
         whole = jnp.transpose(whole, (0, 1, 2, 4, 3, 5))
         return whole[0], whole[1]
 
-    small, expand = tile_biases(active, frames, columns_here, cells)
-    mark = hold(small)
-    front_bias = expand(mark, 0)
+    front_bias, back_bias = tile_biases(active, frames, columns_here, cells)
+    key_here = pair_of(keys, values, 0)
+    key_near = row_sides(key_here)
     key_sent = [pair_of(keys, values, shift) for shift in range(1, size)]
     key_moved = [turn(key_sent[size - b - 1], size - b) for b in range(1, size)]
     query_held = [pair_of(queries, out_grad, shift) for shift in range(size)]
     query_held, key_moved = lax.optimization_barrier((query_held, key_moved))
+    key_far = [row_sides(part) for part in key_moved]
     query_moved = [turn(query_held[size - b], size - b) for b in range(1, size)]
-    key_here, front_bias = lax.optimization_barrier((pair_of(keys, values, 0), front_bias))
-    key_parts = [key_here] + key_moved
-    sides = [row_sides(part) for part in key_parts]
-    query_all, sides[0] = lax.optimization_barrier((jnp.stack(query_held[:1] + query_moved), sides[0]))
-    key_rows = [row for part, (before, after) in zip(key_parts, sides) for row in (before, part, after)]
-    back_bias = expand(mark, 1)
+    query_all = jnp.stack(query_held[:1] + query_moved, 1)
+    query_all, key_near = lax.optimization_barrier((query_all, key_near))
+    query_before, query_after = row_sides(query_all)
+    key_parts, sides = [key_here] + key_moved, [key_near] + key_far
     key_halo = key_parts + [before for before, _ in sides] + [after for _, after in sides]
-    key_halo += frame_edges(key_rows)
-    query_before, query_after = row_sides(query_all)
-    rows_all = [row[b] for b in range(size) for row in (query_before, query_all, query_after)]
-    query_halo = [query_all, query_before, query_after] + list(frame_edges(rows_all))
+    key_halo += frame_edges([row for part, (up, down) in zip(key_parts, sides) for row in (up, part, down)])
+    query_halo = [query_all, query_before, query_after]
+    query_halo += stacked_edges(query_before, query_all, query_after)
 
     def grads_shape(count):
         return [jax.ShapeDtypeStruct((2, frames, count, cells, dim), jnp.bfloat16)] * size
@@ -299,23 +307,21 @@
     attended, stats = run(
         attend_kernel, scaling, size, [query_all] + key_halo, front_bias, [attended_shape, stat_shape], 0, groups, 2
     )
-    stat_sides = row_sides(stats)
-    attended, stat_sides = lax.optimization_barrier((attended, stat_sides))
     front_grads = run(
         query_kernel, scaling, size, [query_all] + key_halo + [attended, stats], front_bias, grads_shape(groups),
         0, groups, 3
     )
-    stat_edges = frame_edges((stat_sides[0], stats, stat_sides[1]))
-    front_grads, stat_edges = lax.optimization_barrier((front_grads, stat_edges))
-    stat_halo = [stats] + list(stat_sides) + list(stat_edges)
-    blocks = []
-    for first, count in ((0, groups - groups // 2), (groups - groups // 2, groups // 2)):
+    stat_sides = row_sides(stats)
+    stat_halo = [stats] + list(stat_sides) + list(frame_edges((stat_sides[0], stats, stat_sides[1])))
+    halves = ((0, groups - groups // 2), (groups - groups // 2, groups // 2))
+    back_blocks = []
+    for first, count in halves:
         back_grads = run(
             back_kernel, scaling, size, key_parts + query_halo + stat_halo, back_bias, grads_shape(count),
             first, count, 4
         )
-        blocks.append((first, back_grads))
-    return from_heads([(0, front_grads)]) + from_heads(blocks)
+        back_blocks.append((first, back_grads))
+    return from_heads([(0, front_grads)]) + from_heads(back_blocks)
 
 
 def solution(mesh):

time: 121 us -> 197 us (1.63)
  the two profiles are of different devices: /device:TPU:4 before, /device:TPU:9 now
where the time goes in v7:
time: 197 us; the launch traced here: 196 us
  Pallas kernels  91.9 us (47%)
  starting transfers between devices  46.9 us (24%)
  waiting for transfers between devices  27.6 us (14%)
  local copies, waits for them, and re-layouts  22.6 us (11%)
  other arithmetic  3.93 us (2%)
    pallas_call x1, Pallas kernels, stacked_edges(): pl.pallas_call(edges_kernel, out_shape=(edge, edge), in_specs=[anywhere]...  72.6 us
    ppermute x14, starting transfers between devices, step_along(): lax.ppermute(tensor, axis, [(i, i + sign) for i in range(size) if 0 <= i...  42.6 us
    pallas_call x4, Pallas kernels, run(): pl.pallas_call(functools.partial(kernel, scaling, parts), grid=(count,),...  19.2 us
    ppermute x5, waiting for transfers between devices, turn(): lax.ppermute(tensor, 'head', [(i, (i + shift) % size) for i in range(size)])  14.1 us
    ppermute x14, waiting for transfers between devices, step_along(): lax.ppermute(tensor, axis, [(i, i + sign) for i in range(size) if 0 <= i...  13.6 us
    unnamed x46, local copies, waits for them, and re-layouts  10.5 us
    ppermute x5, starting transfers between devices, turn(): lax.ppermute(tensor, 'head', [(i, (i + shift) % size) for i in range(size)])  4.34 us
  transfers between devices with their start and end apart: 19, of which 8 were waited for; matrix products, arithmetic and copies ran while one was open for 10% of the time, Pallas kernels for 45%

profile of v7, /device:TPU:9, one launch (start us, length us, event | category | flops | bytes accessed | tf_op | source)
XLA Modules:
  0.0 195.9 jit_solution(16149513572332821345)
XLA Ops:
  0.7 1.4 dynamic-slice_bitcast_fusion.6
  2.2 3.3 %collective-permute-start.2 = (bf16[2,2,6,64,128]{4,3,2,1,0:T(8,128)(2,1)S(1)}, bf16[2,2,6,64,128]{4,3,2,1,0:T(8,128)(2,1)S(1)}, u32[]{:S(2)}, u32[]{:S(2)}) collective-permute-start(bf16[2,2,6,64,128]{4,3,2,1,0:T(8,128)(2,1)S(1)} %pad_maximum_fusion.4.refs_1_.refs_0_), channel_id=1, source_target_pairs={{0,2},{2,4},{4,6},{1,3},{3,5},{5,7},{8,10},{10,12},{12,14},{9,11},... | collective-permute-start | bytes 1179656 | tf_op jit(solution)/shard_map/ppermute | solution.py:178
  5.5 2.1 %collective-permute-start.3 = (bf16[2,2,6,64,128]{4,3,2,1,0:T(8,128)(2,1)S(1)}, bf16[2,2,6,64,128]{4,3,2,1,0:T(8,128)(2,1)S(1)}, u32[]{:S(2)}, u32[]{:S(2)}) collective-permute-start(bf16[2,2,6,64,128]{4,3,2,1,0:T(8,128)(2,1)S(1)} %pad_maximum_fusion.4.refs_1_.refs_0_), channel_id=1, source_target_pairs={{2,0},{4,2},{6,4},{3,1},{5,3},{7,5},{10,8},{12,10},{14,12},{11,9},... | collective-permute-start | bytes 1179656 | tf_op jit(solution)/shard_map/ppermute | solution.py:178
  8.5 1.2 collective-permute-start
  13.0 5.1 %collective-permute-done.refs_2_.refs_1_ = bf16[2,2,6,64,128]{4,3,2,1,0:T(8,128)(2,1)S(1)} collective-permute-done((bf16[2,2,6,64,128]{4,3,2,1,0:T(8,128)(2,1)}, bf16[2,2,6,64,128]{4,3,2,1,0:T(8,128)(2,1)S(1)}, u32[]{:S(2)}, u32[]{:S(2)}) %collective-permute-start) | collective-permute-done | bytes 393248 | tf_op jit(solution)/shard_map/ppermute | solution.py:183
  18.1 1.2 collective-permute-start.1
  20.8 3.2 %collective-permute-start.4 = (bf16[2,2,6,64,128]{4,3,2,1,0:T(8,128)(2,1)S(1)}, bf16[2,2,6,64,128]{4,3,2,1,0:T(8,128)(2,1)S(1)}, u32[]{:S(2)}, u32[]{:S(2)}) collective-permute-start(bf16[2,2,6,64,128]{4,3,2,1,0:T(8,128)(2,1)S(1)} %collective-permute-done.refs_2_.refs_1_), channel_id=1, source_target_pairs={{0,2},{2,4},{4,6},{1,3},{3,5},{5,7},{8,10},{10,12},{12,14},{9,11},... | collective-permute-start | bytes 1179656 | tf_op jit(solution)/shard_map/ppermute | solution.py:178
  24.0 2.1 %collective-permute-start.5 = (bf16[2,2,6,64,128]{4,3,2,1,0:T(8,128)(2,1)S(1)}, bf16[2,2,6,64,128]{4,3,2,1,0:T(8,128)(2,1)S(1)}, u32[]{:S(2)}, u32[]{:S(2)}) collective-permute-start(bf16[2,2,6,64,128]{4,3,2,1,0:T(8,128)(2,1)S(1)} %collective-permute-done.refs_2_.refs_1_), channel_id=1, source_target_pairs={{2,0},{4,2},{6,4},{3,1},{5,3},{7,5},{10,8},{12,10},{14,12},{11,9},... | collective-permute-start | bytes 1179656 | tf_op jit(solution)/shard_map/ppermute | solution.py:178
  26.9 1.1 pad_maximum_fusion.refs_0_.own.refs_2_
  34.6 6.7 %collective-permute-start.6 = (bf16[6,2,6,64,128]{4,3,2,1,0:T(8,128)(2,1)}, bf16[6,2,6,64,128]{4,3,2,1,0:T(8,128)(2,1)}, u32[]{:S(2)}, u32[]{:S(2)}) collective-permute-start(bf16[6,2,6,64,128]{4,3,2,1,0:T(8,128)(2,1)} %get-tuple-element.41), channel_id=1, source_target_pairs={{0,8},{8,16},{16,24},{1,9},{9,17},{17,25},{2,10},{10,18},{18,26},{... | collective-permute-start | bytes 3538952 | tf_op jit(solution)/shard_map/ppermute | solution.py:178
  41.3 1.9 collective-permute-start.7
  43.5 3.2 %collective-permute-start.9 = (bf16[2,2,2,6,64,128]{5,4,3,2,1,0:T(8,128)(2,1)S(1)}, bf16[2,2,2,6,64,128]{5,4,3,2,1,0:T(8,128)(2,1)S(1)}, u32[]{:S(2)}, u32[]{:S(2)}) collective-permute-start(bf16[2,2,2,6,64,128]{5,4,3,2,1,0:T(8,128)(2,1)S(1)} %pad_maximum_fusion.refs_0_.own.refs_2_), channel_id=1, source_target_pairs={{0,2},{2,4},{4,6},{1,3},{3,5},{5,7},{8,10},{10,12},{12,14},{9,11},... | collective-permute-start | bytes 2359304 | tf_op jit(solution)/shard_map/ppermute | solution.py:178
  46.7 2.1 %collective-permute-start.10 = (bf16[2,2,2,6,64,128]{5,4,3,2,1,0:T(8,128)(2,1)S(1)}, bf16[2,2,2,6,64,128]{5,4,3,2,1,0:T(8,128)(2,1)S(1)}, u32[]{:S(2)}, u32[]{:S(2)}) collective-permute-start(bf16[2,2,2,6,64,128]{5,4,3,2,1,0:T(8,128)(2,1)S(1)} %pad_maximum_fusion.refs_0_.own.refs_2_), channel_id=1, source_target_pairs={{2,0},{4,2},{6,4},{3,1},{5,3},{7,5},{10,8},{12,10},{14,12},{11,9},... | collective-permute-start | bytes 2359304 | tf_op jit(solution)/shard_map/ppermute | solution.py:178
  52.1 1.3 squeeze.22.refs_9_.refs_11_
  53.4 1.4 squeeze.25.refs_12_
  54.8 9.3 %collective-permute-done.9.before.refs_3_ = bf16[2,2,2,6,64,128]{5,4,3,2,1,0:T(8,128)(2,1)S(1)} collective-permute-done((bf16[2,2,2,6,64,128]{5,4,3,2,1,0:T(8,128)(2,1)S(1)}, bf16[2,2,2,6,64,128]{5,4,3,2,1,0:T(8,128)(2,1)S(1)}, u32[]{:S(2)}, u32[]{:S(2)}) %collective-permute-start.9) | collective-permute-done | bytes 786464 | tf_op jit(solution)/shard_map/ppermute | solution.py:178
  64.1 3.2 %collective-permute-done.10.after.refs_4_ = bf16[2,2,2,6,64,128]{5,4,3,2,1,0:T(8,128)(2,1)S(1)} collective-permute-done((bf16[2,2,2,6,64,128]{5,4,3,2,1,0:T(8,128)(2,1)S(1)}, bf16[2,2,2,6,64,128]{5,4,3,2,1,0:T(8,128)(2,1)S(1)}, u32[]{:S(2)}, u32[]{:S(2)}) %collective-permute-start.10) | collective-permute-done | bytes 786464 | tf_op jit(solution)/shard_map/ppermute | solution.py:178
  68.2 72.6 %shard_map.104 = (bf16[3,2,2,6,64,128]{5,4,3,2,1,0:T(8,128)(2,1)}, bf16[3,2,2,6,64,128]{5,4,3,2,1,0:T(8,128)(2,1)}) custom-call(bf16[2,2,2,6,64,128]{5,4,3,2,1,0:T(8,128)(2,1)} %copy-done.2, bf16[2,2,2,6,64,128]{5,4,3,2,1,0:T(8,128)(2,1)} %copy-done, bf16[2,2,2,6,64,128]{5,4,3,2,1,0:T(8,128)(2,1)} %copy-done.4), custom_call_target="tpu_custom_call" | custom-call | bytes 4718592 | tf_op jit(solution)/shard_map/pallas_call | solution.py:205
  140.8 4.2 %collective-permute-start.11 = (bf16[3,2,2,6,64,128]{5,4,3,2,1,0:T(8,128)(2,1)}, bf16[3,2,2,6,64,128]{5,4,3,2,1,0:T(8,128)(2,1)S(1)}, u32[]{:S(2)}, u32[]{:S(2)}) collective-permute-start(bf16[3,2,2,6,64,128]{5,4,3,2,1,0:T(8,128)(2,1)} %get-tuple-element.30), channel_id=1, source_target_pairs={{0,8},{8,16},{16,24},{1,9},{9,17},{17,25},{2,10},{10,18},{18,26},{... | collective-permute-start | bytes 3538952 | tf_op jit(solution)/shard_map/ppermute | solution.py:178
  145.1 1.9 collective-permute-start.12
  147.0 1.1 copy-done.1
  151.9 6.9 %shard_map.102 = (bf16[2,6,128,128]{3,2,1,0:T(8,128)(2,1)S(1)}, f32[2,6,2,128]{3,2,1,0:T(2,128)S(1)}) custom-call(bf16[2,2,2,6,64,128]{5,4,3,2,1,0:T(8,128)(2,1)S(1)} %copy-done.1, bf16[2,2,6,64,128]{4,3,2,1,0:T(8,128)(2,1)S(1)} %pad_maximum_fusion.4.refs_1_.refs_0_, bf16[2,2,6,64,128]{4,3,2,1,0:T(8,128)(2,1)S(1)} %collective-permute-done.refs_2_.refs_1_, ...), custom_call_target="tpu_custom_call" | custom-call | flops 905969664 | bytes 4718592 | tf_op jit(solution)/shard_map/pallas_call | solution.py:159
  158.7 1.9 collective-permute-start.13
  160.7 3.4 %collective-permute-start.14 = (f32[2,6,2,128]{3,2,1,0:T(2,128)S(1)}, f32[2,6,2,128]{3,2,1,0:T(2,128)S(1)}, u32[]{:S(2)}, u32[]{:S(2)}) collective-permute-start(f32[2,6,2,128]{3,2,1,0:T(2,128)S(1)} %get-tuple-element.27.refs_10_.refs_7_), channel_id=1, source_target_pairs={{2,0},{4,2},{6,4},{3,1},{5,3},{7,5},{10,8},{12,10},{14,12},{11,9},... | collective-permute-start | bytes 36872 | tf_op jit(solution)/shard_map/ppermute | solution.py:178
  164.0 6.5 %shard_map.103 = (bf16[2,2,6,64,128]{4,3,2,1,0:T(8,128)(2,1)S(1)}, bf16[2,2,6,64,128]{4,3,2,1,0:T(8,128)(2,1)S(1)}) custom-call(bf16[2,2,2,6,64,128]{5,4,3,2,1,0:T(8,128)(2,1)S(1)} %copy-done.1, bf16[2,2,6,64,128]{4,3,2,1,0:T(8,128)(2,1)S(1)} %pad_maximum_fusion.4.refs_1_.refs_0_, bf16[2,2,6,64,128]{4,3,2,1,0:T(8,128)(2,1)S(1)} %collective-permute-done.refs_2_.refs_1_, ...), custom_call_target="tpu_custom_call" | custom-call | flops 1358954496 | bytes 4718592 | tf_op jit(solution)/shard_map/pallas_call | solution.py:159
  171.2 4.5 %collective-permute-start.15 = (f32[3,6,2,128]{3,2,1,0:T(2,128)S(1)}, f32[3,6,2,128]{3,2,1,0:T(2,128)S(1)}, u32[]{:S(2)}, u32[]{:S(2)}) collective-permute-start(f32[3,6,2,128]{3,2,1,0:T(2,128)S(1)} %pad_maximum_fusion.6), channel_id=1, source_target_pairs={{0,8},{8,16},{16,24},{1,9},{9,17},{17,25},{2,10},{10,18},{18,26},{... | collective-permute-start | bytes 55304 | tf_op jit(solution)/shard_map/ppermute | solution.py:178
  175.7 2.1 %collective-permute-start.16 = (f32[3,6,2,128]{3,2,1,0:T(2,128)S(1)}, f32[3,6,2,128]{3,2,1,0:T(2,128)S(1)}, u32[]{:S(2)}, u32[]{:S(2)}) collective-permute-start(f32[3,6,2,128]{3,2,1,0:T(2,128)S(1)} %pad_maximum_fusion.7), channel_id=1, source_target_pairs={{8,0},{16,8},{24,16},{9,1},{17,9},{25,17},{10,2},{18,10},{26,18},{... | collective-permute-start | bytes 55304 | tf_op jit(solution)/shard_map/ppermute | solution.py:178
  177.8 2.4 %collective-permute-done.8 = bf16[2,2,6,64,128]{4,3,2,1,0:T(8,128)(2,1)S(1)} collective-permute-done((bf16[2,2,6,64,128]{4,3,2,1,0:T(8,128)(2,1)S(1)}, bf16[2,2,6,64,128]{4,3,2,1,0:T(8,128)(2,1)S(1)}, u32[]{:S(2)}, u32[]{:S(2)}) %collective-permute-start.8) | collective-permute-done | bytes 393248 | tf_op jit(solution)/shard_map/ppermute | solution.py:183
  181.2 2.9 %shard_map.105 = (bf16[2,2,3,64,128]{4,3,2,1,0:T(8,128)(2,1)S(1)}, bf16[2,2,3,64,128]{4,3,2,1,0:T(8,128)(2,1)S(1)}) custom-call(bf16[2,2,6,64,128]{4,3,2,1,0:T(8,128)(2,1)S(1)} %pad_maximum_fusion.4.refs_1_.refs_0_, bf16[2,2,6,64,128]{4,3,2,1,0:T(8,128)(2,1)S(1)} %collective-permute-done.refs_2_.refs_1_, bf16[2,2,2,6,64,128]{5,4,3,2,1,0:T(8,128)(2,1)S(1)} %copy-done.1, ...), custom_call_target="tpu_custom_call" | custom-call | flops 905969664 | bytes 2359296 | tf_op jit(solution)/shard_map/pallas_call | solution.py:159
  185.2 2.9 %shard_map.106 = (bf16[2,2,3,64,128]{4,3,2,1,0:T(8,128)(2,1)S(1)}, bf16[2,2,3,64,128]{4,3,2,1,0:T(8,128)(2,1)S(1)}) custom-call(bf16[2,2,6,64,128]{4,3,2,1,0:T(8,128)(2,1)S(1)} %pad_maximum_fusion.4.refs_1_.refs_0_, bf16[2,2,6,64,128]{4,3,2,1,0:T(8,128)(2,1)S(1)} %collective-permute-done.refs_2_.refs_1_, bf16[2,2,2,6,64,128]{5,4,3,2,1,0:T(8,128)(2,1)S(1)} %copy-done.1, ...), custom_call_target="tpu_custom_call" | custom-call | flops 905969664 | bytes 2359296 | tf_op jit(solution)/shard_map/pallas_call | solution.py:159
  188.9 2.3 %collective-permute-done.17 = bf16[2,2,3,64,128]{4,3,2,1,0:T(8,128)(2,1)S(1)} collective-permute-done((bf16[2,2,3,64,128]{4,3,2,1,0:T(8,128)(2,1)S(1)}, bf16[2,2,3,64,128]{4,3,2,1,0:T(8,128)(2,1)S(1)}, u32[]{:S(2)}, u32[]{:S(2)}) %collective-permute-start.17) | collective-permute-done | bytes 196640 | tf_op jit(solution)/shard_map/ppermute | solution.py:183
  191.2 3.6 %collective-permute-done.18 = bf16[2,2,3,64,128]{4,3,2,1,0:T(8,128)(2,1)S(1)} collective-permute-done((bf16[2,2,3,64,128]{4,3,2,1,0:T(8,128)(2,1)S(1)}, bf16[2,2,3,64,128]{4,3,2,1,0:T(8,128)(2,1)S(1)}, u32[]{:S(2)}, u32[]{:S(2)}) %collective-permute-start.18) | collective-permute-done | bytes 196640 | tf_op jit(solution)/shard_map/ppermute | solution.py:183
  (121 shorter events, 25.5 us)
Async XLA Ops:
  2.1 7.6 %copy-start.17 = (bf16[2,8,8,12,128]{4,2,3,1,0:T(8,128)(2,1)S(1)}, bf16[2,8,8,12,128]{4,2,3,1,0:T(8,128)(2,1)}, u32[]{:S(2)}) copy-start(bf16[2,8,8,12,128]{4,2,3,1,0:T(8,128)(2,1)} %param.10) | copy-start | bytes 1179652
  2.2 25.8 %collective-permute-start.2 = (bf16[2,2,6,64,128]{4,3,2,1,0:T(8,128)(2,1)S(1)}, bf16[2,2,6,64,128]{4,3,2,1,0:T(8,128)(2,1)S(1)}, u32[]{:S(2)}, u32[]{:S(2)}) collective-permute-start(bf16[2,2,6,64,128]{4,3,2,1,0:T(8,128)(2,1)S(1)} %pad_maximum_fusion.4.refs_1_.refs_0_), channel_id=1, source_target_pairs={{0,2},{2,4},{4,6},{1,3},{3,5},{5,7},{8,10},{10,12},{12,14},{9,11},... | collective-permute-start | bytes 1179656 | tf_op jit(solution)/shard_map/ppermute | solution.py:178
  5.5 22.5 %collective-permute-start.3 = (bf16[2,2,6,64,128]{4,3,2,1,0:T(8,128)(2,1)S(1)}, bf16[2,2,6,64,128]{4,3,2,1,0:T(8,128)(2,1)S(1)}, u32[]{:S(2)}, u32[]{:S(2)}) collective-permute-start(bf16[2,2,6,64,128]{4,3,2,1,0:T(8,128)(2,1)S(1)} %pad_maximum_fusion.4.refs_1_.refs_0_), channel_id=1, source_target_pairs={{2,0},{4,2},{6,4},{3,1},{5,3},{7,5},{10,8},{12,10},{14,12},{11,9},... | collective-permute-start | bytes 1179656 | tf_op jit(solution)/shard_map/ppermute | solution.py:178
  8.5 9.6 %collective-permute-start = (bf16[2,2,6,64,128]{4,3,2,1,0:T(8,128)(2,1)}, bf16[2,2,6,64,128]{4,3,2,1,0:T(8,128)(2,1)S(1)}, u32[]{:S(2)}, u32[]{:S(2)}) collective-permute-start(bf16[2,2,6,64,128]{4,3,2,1,0:T(8,128)(2,1)} %pad_maximum_fusion.3), channel_id=1, source_target_pairs={{0,1},{1,0},{2,3},{3,2},{4,5},{5,4},{6,7},{7,6},{8,9},{9,8},{10,11... | collective-permute-start | bytes 1179656 | tf_op jit(solution)/shard_map/ppermute | solution.py:183
  11.8 8.6 %copy-start.19 = (bf16[4,3,9,2,9,1]{4,2,1,0,5,3:T(8,128)(2,1)S(1)}, bf16[4,3,9,2,9,1]{4,2,1,0,5,3:T(8,128)(2,1)}, u32[]{:S(2)}) copy-start(bf16[4,3,9,2,9,1]{4,2,1,0,5,3:T(8,128)(2,1)} %constant.190) | copy-start | bytes 11668
  18.1 8.8 %collective-permute-start.1 = (bf16[2,2,6,64,128]{4,3,2,1,0:T(8,128)(2,1)}, bf16[2,2,6,64,128]{4,3,2,1,0:T(8,128)(2,1)}, u32[]{:S(2)}, u32[]{:S(2)}) collective-permute-start(bf16[2,2,6,64,128]{4,3,2,1,0:T(8,128)(2,1)} %pad_maximum_fusion.2), channel_id=1, source_target_pairs={{0,1},{1,0},{2,3},{3,2},{4,5},{5,4},{6,7},{7,6},{8,9},{9,8},{10,11... | collective-permute-start | bytes 1179656 | tf_op jit(solution)/shard_map/ppermute | solution.py:183
  20.8 10.3 %collective-permute-start.4 = (bf16[2,2,6,64,128]{4,3,2,1,0:T(8,128)(2,1)S(1)}, bf16[2,2,6,64,128]{4,3,2,1,0:T(8,128)(2,1)S(1)}, u32[]{:S(2)}, u32[]{:S(2)}) collective-permute-start(bf16[2,2,6,64,128]{4,3,2,1,0:T(8,128)(2,1)S(1)} %collective-permute-done.refs_2_.refs_1_), channel_id=1, source_target_pairs={{0,2},{2,4},{4,6},{1,3},{3,5},{5,7},{8,10},{10,12},{12,14},{9,11},... | collective-permute-start | bytes 1179656 | tf_op jit(solution)/shard_map/ppermute | solution.py:178
  24.0 9.8 %collective-permute-start.5 = (bf16[2,2,6,64,128]{4,3,2,1,0:T(8,128)(2,1)S(1)}, bf16[2,2,6,64,128]{4,3,2,1,0:T(8,128)(2,1)S(1)}, u32[]{:S(2)}, u32[]{:S(2)}) collective-permute-start(bf16[2,2,6,64,128]{4,3,2,1,0:T(8,128)(2,1)S(1)} %collective-permute-done.refs_2_.refs_1_), channel_id=1, source_target_pairs={{2,0},{4,2},{6,4},{3,1},{5,3},{7,5},{10,8},{12,10},{14,12},{11,9},... | collective-permute-start | bytes 1179656 | tf_op jit(solution)/shard_map/ppermute | solution.py:178
  26.9 2.0 %copy-start.16 = (bf16[1,2,6,8,8,128]{5,4,2,3,0,1:T(8,128)(2,1)S(1)}, bf16[1,2,6,8,8,128]{5,4,2,3,0,1:T(8,128)(2,1)}, u32[]{:S(2)}) copy-start(bf16[1,2,6,8,8,128]{5,4,2,3,0,1:T(8,128)(2,1)} %get-tuple-element.48) | copy-start | bytes 589828
  26.9 2.8 %copy-start.15 = (bf16[1,2,6,8,8,128]{5,4,2,3,0,1:T(8,128)(2,1)S(1)}, bf16[1,2,6,8,8,128]{5,4,2,3,0,1:T(8,128)(2,1)}, u32[]{:S(2)}) copy-start(bf16[1,2,6,8,8,128]{5,4,2,3,0,1:T(8,128)(2,1)} %get-tuple-element.49) | copy-start | bytes 589828
  28.0 39.3 %copy-start = (bf16[2,2,2,6,64,128]{5,4,3,2,1,0:T(8,128)(2,1)}, bf16[2,2,2,6,64,128]{5,4,3,2,1,0:T(8,128)(2,1)S(1)}, u32[]{:S(2)}) copy-start(bf16[2,2,2,6,64,128]{5,4,3,2,1,0:T(8,128)(2,1)S(1)} %pad_maximum_fusion.refs_0_.own.refs_2_) | copy-start | bytes 2359300
  28.0 3.1 %copy-start.6 = (bf16[2,2,6,64,128]{4,3,2,1,0:T(8,128)(2,1)}, bf16[2,2,6,64,128]{4,3,2,1,0:T(8,128)(2,1)S(1)}, u32[]{:S(2)}) copy-start(bf16[2,2,6,64,128]{4,3,2,1,0:T(8,128)(2,1)S(1)} %collective-permute-done.3.refs_5_) | copy-start | bytes 1179652
  31.2 3.5 %copy-start.8 = (bf16[2,2,6,64,128]{4,3,2,1,0:T(8,128)(2,1)}, bf16[2,2,6,64,128]{4,3,2,1,0:T(8,128)(2,1)S(1)}, u32[]{:S(2)}) copy-start(bf16[2,2,6,64,128]{4,3,2,1,0:T(8,128)(2,1)S(1)} %collective-permute-done.4.refs_4_) | copy-start | bytes 1179652
  33.8 9.7 %copy-start.11 = (bf16[2,2,6,64,128]{4,3,2,1,0:T(8,128)(2,1)}, bf16[2,2,6,64,128]{4,3,2,1,0:T(8,128)(2,1)S(1)}, u32[]{:S(2)}) copy-start(bf16[2,2,6,64,128]{4,3,2,1,0:T(8,128)(2,1)S(1)} %collective-permute-done.5.refs_6_) | copy-start | bytes 1179652
  34.6 112.4 %collective-permute-start.6 = (bf16[6,2,6,64,128]{4,3,2,1,0:T(8,128)(2,1)}, bf16[6,2,6,64,128]{4,3,2,1,0:T(8,128)(2,1)}, u32[]{:S(2)}, u32[]{:S(2)}) collective-permute-start(bf16[6,2,6,64,128]{4,3,2,1,0:T(8,128)(2,1)} %get-tuple-element.41), channel_id=1, source_target_pairs={{0,8},{8,16},{16,24},{1,9},{9,17},{17,25},{2,10},{10,18},{18,26},{... | collective-permute-start | bytes 3538952 | tf_op jit(solution)/shard_map/ppermute | solution.py:178
  41.3 105.7 %collective-permute-start.7 = (bf16[6,2,6,64,128]{4,3,2,1,0:T(8,128)(2,1)}, bf16[6,2,6,64,128]{4,3,2,1,0:T(8,128)(2,1)}, u32[]{:S(2)}, u32[]{:S(2)}) collective-permute-start(bf16[6,2,6,64,128]{4,3,2,1,0:T(8,128)(2,1)} %get-tuple-element.40), channel_id=1, source_target_pairs={{8,0},{16,8},{24,16},{9,1},{17,9},{25,17},{10,2},{18,10},{26,18},{... | collective-permute-start | bytes 3538952 | tf_op jit(solution)/shard_map/ppermute | solution.py:178
  43.5 20.6 %collective-permute-start.9 = (bf16[2,2,2,6,64,128]{5,4,3,2,1,0:T(8,128)(2,1)S(1)}, bf16[2,2,2,6,64,128]{5,4,3,2,1,0:T(8,128)(2,1)S(1)}, u32[]{:S(2)}, u32[]{:S(2)}) collective-permute-start(bf16[2,2,2,6,64,128]{5,4,3,2,1,0:T(8,128)(2,1)S(1)} %pad_maximum_fusion.refs_0_.own.refs_2_), channel_id=1, source_target_pairs={{0,2},{2,4},{4,6},{1,3},{3,5},{5,7},{8,10},{10,12},{12,14},{9,11},... | collective-permute-start | bytes 2359304 | tf_op jit(solution)/shard_map/ppermute | solution.py:178
  46.7 20.6 %collective-permute-start.10 = (bf16[2,2,2,6,64,128]{5,4,3,2,1,0:T(8,128)(2,1)S(1)}, bf16[2,2,2,6,64,128]{5,4,3,2,1,0:T(8,128)(2,1)S(1)}, u32[]{:S(2)}, u32[]{:S(2)}) collective-permute-start(bf16[2,2,2,6,64,128]{5,4,3,2,1,0:T(8,128)(2,1)S(1)} %pad_maximum_fusion.refs_0_.own.refs_2_), channel_id=1, source_target_pairs={{2,0},{4,2},{6,4},{3,1},{5,3},{7,5},{10,8},{12,10},{14,12},{11,9},... | collective-permute-start | bytes 2359304 | tf_op jit(solution)/shard_map/ppermute | solution.py:178
  64.1 3.2 %copy-start.2 = (bf16[2,2,2,6,64,128]{5,4,3,2,1,0:T(8,128)(2,1)}, bf16[2,2,2,6,64,128]{5,4,3,2,1,0:T(8,128)(2,1)S(1)}, u32[]{:S(2)}) copy-start(bf16[2,2,2,6,64,128]{5,4,3,2,1,0:T(8,128)(2,1)S(1)} %collective-permute-done.9.before.refs_3_) | copy-start | bytes 2359300
  140.8 40.3 %collective-permute-start.11 = (bf16[3,2,2,6,64,128]{5,4,3,2,1,0:T(8,128)(2,1)}, bf16[3,2,2,6,64,128]{5,4,3,2,1,0:T(8,128)(2,1)S(1)}, u32[]{:S(2)}, u32[]{:S(2)}) collective-permute-start(bf16[3,2,2,6,64,128]{5,4,3,2,1,0:T(8,128)(2,1)} %get-tuple-element.30), channel_id=1, source_target_pairs={{0,8},{8,16},{16,24},{1,9},{9,17},{17,25},{2,10},{10,18},{18,26},{... | collective-permute-start | bytes 3538952 | tf_op jit(solution)/shard_map/ppermute | solution.py:178
  145.1 36.1 %collective-permute-start.12 = (bf16[3,2,2,6,64,128]{5,4,3,2,1,0:T(8,128)(2,1)}, bf16[3,2,2,6,64,128]{5,4,3,2,1,0:T(8,128)(2,1)S(1)}, u32[]{:S(2)}, u32[]{:S(2)}) collective-permute-start(bf16[3,2,2,6,64,128]{5,4,3,2,1,0:T(8,128)(2,1)} %get-tuple-element.31), channel_id=1, source_target_pairs={{8,0},{16,8},{24,16},{9,1},{17,9},{25,17},{10,2},{18,10},{26,18},{... | collective-permute-start | bytes 3538952 | tf_op jit(solution)/shard_map/ppermute | solution.py:178
  151.9 12.2 %copy-start.10 = (bf16[2,2,6,64,128]{4,3,2,1,0:T(8,128)(2,1)S(1)}, bf16[2,2,6,64,128]{4,3,2,1,0:T(8,128)(2,1)}, u32[]{:S(2)}) copy-start(bf16[2,2,6,64,128]{4,3,2,1,0:T(8,128)(2,1)} %copy-done.8) | copy-start | bytes 1179652
  158.7 12.4 %collective-permute-start.13 = (f32[2,6,2,128]{3,2,1,0:T(2,128)S(1)}, f32[2,6,2,128]{3,2,1,0:T(2,128)S(1)}, u32[]{:S(2)}, u32[]{:S(2)}) collective-permute-start(f32[2,6,2,128]{3,2,1,0:T(2,128)S(1)} %get-tuple-element.27.refs_10_.refs_7_), channel_id=1, source_target_pairs={{0,2},{2,4},{4,6},{1,3},{3,5},{5,7},{8,10},{10,12},{12,14},{9,11},... | collective-permute-start | bytes 36872 | tf_op jit(solution)/shard_map/ppermute | solution.py:178
  160.7 10.4 %collective-permute-start.14 = (f32[2,6,2,128]{3,2,1,0:T(2,128)S(1)}, f32[2,6,2,128]{3,2,1,0:T(2,128)S(1)}, u32[]{:S(2)}, u32[]{:S(2)}) collective-permute-start(f32[2,6,2,128]{3,2,1,0:T(2,128)S(1)} %get-tuple-element.27.refs_10_.refs_7_), channel_id=1, source_target_pairs={{2,0},{4,2},{6,4},{3,1},{5,3},{7,5},{10,8},{12,10},{14,12},{11,9},... | collective-permute-start | bytes 36872 | tf_op jit(solution)/shard_map/ppermute | solution.py:178
  170.5 9.6 %collective-permute-start.8 = (bf16[2,2,6,64,128]{4,3,2,1,0:T(8,128)(2,1)S(1)}, bf16[2,2,6,64,128]{4,3,2,1,0:T(8,128)(2,1)S(1)}, u32[]{:S(2)}, u32[]{:S(2)}) collective-permute-start(bf16[2,2,6,64,128]{4,3,2,1,0:T(8,128)(2,1)S(1)} %get-tuple-element.29), channel_id=1, source_target_pairs={{0,1},{1,0},{2,3},{3,2},{4,5},{5,4},{6,7},{7,6},{8,9},{9,8},{10,11... | collective-permute-start | bytes 1179656 | tf_op jit(solution)/shard_map/ppermute | solution.py:183
  171.2 10.0 %collective-permute-start.15 = (f32[3,6,2,128]{3,2,1,0:T(2,128)S(1)}, f32[3,6,2,128]{3,2,1,0:T(2,128)S(1)}, u32[]{:S(2)}, u32[]{:S(2)}) collective-permute-start(f32[3,6,2,128]{3,2,1,0:T(2,128)S(1)} %pad_maximum_fusion.6), channel_id=1, source_target_pairs={{0,8},{8,16},{16,24},{1,9},{9,17},{17,25},{2,10},{10,18},{18,26},{... | collective-permute-start | bytes 55304 | tf_op jit(solution)/shard_map/ppermute | solution.py:178
  175.7 5.5 %copy-start.3 = (bf16[2,2,2,6,64,128]{5,4,3,2,1,0:T(8,128)(2,1)S(1)}, bf16[2,2,2,6,64,128]{5,4,3,2,1,0:T(8,128)(2,1)}, u32[]{:S(2)}) copy-start(bf16[2,2,2,6,64,128]{5,4,3,2,1,0:T(8,128)(2,1)} %copy-done.2) | copy-start | bytes 2359300
  175.7 5.5 %copy-start.5 = (bf16[2,2,2,6,64,128]{5,4,3,2,1,0:T(8,128)(2,1)S(1)}, bf16[2,2,2,6,64,128]{5,4,3,2,1,0:T(8,128)(2,1)}, u32[]{:S(2)}) copy-start(bf16[2,2,2,6,64,128]{5,4,3,2,1,0:T(8,128)(2,1)} %copy-done.4) | copy-start | bytes 2359300
  175.7 5.5 %copy-start.13 = (f32[2,2,1152]{2,1,0:T(2,128)S(1)}, f32[2,2,1152]{2,1,0:T(2,128)}, u32[]{:S(2)}) copy-start(f32[2,2,1152]{2,1,0:T(2,128)} %squeeze.25.refs_12_) | copy-start | bytes 55300
  175.7 5.5 %collective-permute-start.16 = (f32[3,6,2,128]{3,2,1,0:T(2,128)S(1)}, f32[3,6,2,128]{3,2,1,0:T(2,128)S(1)}, u32[]{:S(2)}, u32[]{:S(2)}) collective-permute-start(f32[3,6,2,128]{3,2,1,0:T(2,128)S(1)} %pad_maximum_fusion.7), channel_id=1, source_target_pairs={{8,0},{16,8},{24,16},{9,1},{17,9},{25,17},{10,2},{18,10},{26,18},{... | collective-permute-start | bytes 55304 | tf_op jit(solution)/shard_map/ppermute | solution.py:178
  184.1 7.0 %collective-permute-start.17 = (bf16[2,2,3,64,128]{4,3,2,1,0:T(8,128)(2,1)S(1)}, bf16[2,2,3,64,128]{4,3,2,1,0:T(8,128)(2,1)S(1)}, u32[]{:S(2)}, u32[]{:S(2)}) collective-permute-start(bf16[2,2,3,64,128]{4,3,2,1,0:T(8,128)(2,1)S(1)} %get-tuple-element.33), channel_id=1, source_target_pairs={{0,1},{1,0},{2,3},{3,2},{4,5},{5,4},{6,7},{7,6},{8,9},{9,8},{10,11... | collective-permute-start | bytes 589832 | tf_op jit(solution)/shard_map/ppermute | solution.py:183
  188.1 6.8 %collective-permute-start.18 = (bf16[2,2,3,64,128]{4,3,2,1,0:T(8,128)(2,1)S(1)}, bf16[2,2,3,64,128]{4,3,2,1,0:T(8,128)(2,1)S(1)}, u32[]{:S(2)}, u32[]{:S(2)}) collective-permute-start(bf16[2,2,3,64,128]{4,3,2,1,0:T(8,128)(2,1)S(1)} %get-tuple-element.35), channel_id=1, source_target_pairs={{0,1},{1,0},{2,3},{3,2},{4,5},{5,4},{6,7},{7,6},{8,9},{9,8},{10,11... | collective-permute-start | bytes 589832 | tf_op jit(solution)/shard_map/ppermute | solution.py:183
  (7 other events, 6.9 us)

commit v8 on v7

--- a/solution.py
+++ b/solution.py
@@ -53,7 +53,7 @@
     own, before, after, low, high = halo
     frames, parts, _, _, cells, _ = own.shape
     side = lambda row, part, at, which: (before, own, after)[row][at, part, which, 0]
-    edge = lambda end, row, part, which: (low, high)[end][row, part, which, 0]
+    edge = lambda end, row, part, which: (low, high)[end][3 * part + row, which, 0]
     fill_bands(frames, parts, cells, side, edge, bands)
 
 
@@ -164,7 +164,7 @@
         + [pl.BlockSpec(bias.shape, lambda head: (0,) * bias.ndim)],
         out_specs=tuple(head_spec(out.shape, 0) for out in outs),
         scratch_shapes=[pltpu.VMEM((3 * (frames + 2) * tokens, dim), jnp.bfloat16)] * 2,
-        compiler_params=pltpu.CompilerParams(vmem_limit_bytes=32 * 2**20),
+        compiler_params=pltpu.CompilerParams(vmem_limit_bytes=16 * 2**20),
         cost_estimate=pl.CostEstimate(
             flops=frames * count * 2 * products * tokens * 9 * tokens * dim,
             bytes_accessed=count * (frames + 2) * 3 * 2 * tokens * dim * 2,
@@ -186,31 +186,6 @@
 def frame_edges(rows):
     low = step_along(jnp.stack([row[-1] for row in rows]), "frame", 1)
     return low, step_along(jnp.stack([row[0] for row in rows]), "frame", -1)
-
-
-def edges_kernel(before, own, after, first, last, sems):
-    copies = []
-    for row, source in enumerate((before, own, after)):
-        for side, (out, at) in enumerate(((first, 0), (last, source.shape[0] - 1))):
-            copies.append(pltpu.make_async_copy(source.at[at], out.at[row], sems.at[row, side]))
-    for copy in copies:
-        copy.start()
-    for copy in copies:
-        copy.wait()
-
-
-def stacked_edges(before, own, after):
-    edge = jax.ShapeDtypeStruct((3,) + own.shape[1:], own.dtype)
-    anywhere = pl.BlockSpec(memory_space=pl.ANY)
-    first, last = pl.pallas_call(
-        edges_kernel,
-        out_shape=(edge, edge),
-        in_specs=[anywhere] * 3,
-        out_specs=(anywhere, anywhere),
-        scratch_shapes=[pltpu.SemaphoreType.DMA((3, 2))],
-        cost_estimate=pl.CostEstimate(flops=0, bytes_accessed=4 * edge.size * 2, transcendentals=0),
-    )(before, own, after)
-    return step_along(last, "frame", 1), step_along(first, "frame", -1)
 
 
 def row_sides(own):
@@ -297,7 +272,8 @@
     key_halo = key_parts + [before for before, _ in sides] + [after for _, after in sides]
     key_halo += frame_edges([row for part, (up, down) in zip(key_parts, sides) for row in (up, part, down)])
     query_halo = [query_all, query_before, query_after]
-    query_halo += stacked_edges(query_before, query_all, query_after)
+    query_rows = (query_before, query_all, query_after)
+    query_halo += frame_edges([row[:, b] for b in range(size) for row in query_rows])
 
     def grads_shape(count):
         return [jax.ShapeDtypeStruct((2, frames, count, cells, dim), jnp.bfloat16)] * size

time: 197 us -> 100 us (0.51)
  Pallas kernels: 91.9 us -> 16.6 us
  local copies, waits for them, and re-layouts: 22.6 us -> 6.9 us
  waiting for transfers between devices: 27.6 us -> 22.8 us
  starting transfers between devices: 46.9 us -> 49.9 us
  other arithmetic: 3.93 us -> 1.41 us
    pallas_call x1 -> x0, Pallas kernels: 72.6 us -> none  [stacked_edges(): pl.pallas_call(edges_kernel, out_shape=(edge, edge), in_specs=[anywhere]...]
    unnamed x46 -> x21, local copies, waits for them, and re-layouts: 10.5 us -> 1.14 us
    ppermute x14, waiting for transfers between devices: 13.6 us -> 7.61 us  [step_along(): lax.ppermute(tensor, axis, [(i, i + sign) for i in range(size) if 0 <= i...]
    ppermute x14, starting transfers between devices: 42.6 us -> 45.5 us  [step_along(): lax.ppermute(tensor, axis, [(i, i + sign) for i in range(size) if 0 <= i...]
    squeeze x2, local copies, waits for them, and re-layouts: 2.69 us -> 0.05 us  [tile_biases(): return (bias[0], bias[1])]
    pallas_call x4, Pallas kernels: 19.2 us -> 16.6 us  [run(): pl.pallas_call(functools.partial(kernel, scaling, parts), grid=(count,),...]
  transfers between devices with their start and end apart: 19 -> 19, of which waited for: 8 -> 8; matrix products, arithmetic and copies ran while one was open for 10% -> 6% of each run, Pallas kernels for 45% -> 14%
where the time goes in v8:
time: 100 us; the launch traced here: 99.7 us
  starting transfers between devices  49.9 us (50%)
  waiting for transfers between devices  22.8 us (23%)
  Pallas kernels  16.6 us (17%)
  local copies, waits for them, and re-layouts  6.9 us (7%)
  other arithmetic  1.41 us (1%)
  between operations  1.28 us (1%)
    ppermute x14, starting transfers between devices, step_along(): lax.ppermute(tensor, axis, [(i, i + sign) for i in range(size) if 0 <= i...  45.5 us
    pallas_call x4, Pallas kernels, run(): pl.pallas_call(functools.partial(kernel, scaling, parts), grid=(count,),...  16.6 us
    ppermute x5, waiting for transfers between devices, turn(): lax.ppermute(tensor, 'head', [(i, (i + shift) % size) for i in range(size)])  15.2 us
    ppermute x14, waiting for transfers between devices, step_along(): lax.ppermute(tensor, axis, [(i, i + sign) for i in range(size) if 0 <= i...  7.61 us
    ppermute x5, starting transfers between devices, turn(): lax.ppermute(tensor, 'head', [(i, (i + shift) % size) for i in range(size)])  4.35 us
  transfers between devices with their start and end apart: 19, of which 8 were waited for; matrix products, arithmetic and copies ran while one was open for 6% of the time, Pallas kernels for 14%

profile of v8, /device:TPU:9, one launch (start us, length us, event | category | flops | bytes accessed | tf_op | source)
XLA Modules:
  0.0 99.7 jit_solution(13293210588471110533)
XLA Ops:
  0.7 1.4 %dynamic-slice_bitcast_fusion.6 = (bf16[2,1,6,8,8,128]{5,4,2,3,0,1:T(8,128)(2,1)S(1)}, bf16[2,6,8,8,128]{4,3,1,2,0:T(8,128)(2,1)S(1)}, bf16[2,6,8,8,128]{4,3,1,2...) fusion(bf16[2,8,8,12,128]{4,2,3,1,0:T(8,128)(2,1)} %param.9, ...), kind=kLoop, calls=%fused_computation.74 | loop fusion | bytes 1966088 | tf_op jit(solution)/shard_map/stack | solution.py:246
  2.2 3.3 %collective-permute-start.2 = (bf16[2,2,6,64,128]{4,3,2,1,0:T(8,128)(2,1)S(1)}, bf16[2,2,6,64,128]{4,3,2,1,0:T(8,128)(2,1)S(1)}, u32[]{:S(2)}, u32[]{:S(2)}) collective-permute-start(bf16[2,2,6,64,128]{4,3,2,1,0:T(8,128)(2,1)S(1)} %pad_maximum_fusion.4.refs_1_.refs_0_), channel_id=1, source_target_pairs={{0,2},{2,4},{4,6},{1,3},{3,5},{5,7},{8,10},{10,12},{12,14},{9,11},... | collective-permute-start | bytes 1179656 | tf_op jit(solution)/shard_map/ppermute | solution.py:178
  5.6 2.1 %collective-permute-start.3 = (bf16[2,2,6,64,128]{4,3,2,1,0:T(8,128)(2,1)S(1)}, bf16[2,2,6,64,128]{4,3,2,1,0:T(8,128)(2,1)S(1)}, u32[]{:S(2)}, u32[]{:S(2)}) collective-permute-start(bf16[2,2,6,64,128]{4,3,2,1,0:T(8,128)(2,1)S(1)} %pad_maximum_fusion.4.refs_1_.refs_0_), channel_id=1, source_target_pairs={{2,0},{4,2},{6,4},{3,1},{5,3},{7,5},{10,8},{12,10},{14,12},{11,9},... | collective-permute-start | bytes 1179656 | tf_op jit(solution)/shard_map/ppermute | solution.py:178
  7.8 0.8 pad_maximum_fusion.3
  8.5 1.2 %collective-permute-start = (bf16[2,2,6,64,128]{4,3,2,1,0:T(8,128)(2,1)}, bf16[2,2,6,64,128]{4,3,2,1,0:T(8,128)(2,1)S(1)}, u32[]{:S(2)}, u32[]{:S(2)}) collective-permute-start(bf16[2,2,6,64,128]{4,3,2,1,0:T(8,128)(2,1)} %pad_maximum_fusion.3), channel_id=1, source_target_pairs={{0,1},{1,0},{2,3},{3,2},{4,5},{5,4},{6,7},{7,6},{8,9},{9,8},{10,11... | collective-permute-start | bytes 1179656 | tf_op jit(solution)/shard_map/ppermute | solution.py:183
  13.3 4.8 %collective-permute-done.refs_2_.refs_1_ = bf16[2,2,6,64,128]{4,3,2,1,0:T(8,128)(2,1)S(1)} collective-permute-done((bf16[2,2,6,64,128]{4,3,2,1,0:T(8,128)(2,1)}, bf16[2,2,6,64,128]{4,3,2,1,0:T(8,128)(2,1)S(1)}, u32[]{:S(2)}, u32[]{:S(2)}) %collective-permute-start) | collective-permute-done | bytes 393248 | tf_op jit(solution)/shard_map/ppermute | solution.py:183
  18.1 1.2 %collective-permute-start.1 = (bf16[2,2,6,64,128]{4,3,2,1,0:T(8,128)(2,1)S(1)}, bf16[2,2,6,64,128]{4,3,2,1,0:T(8,128)(2,1)S(1)}, u32[]{:S(2)}, u32[]{:S(2)}) collective-permute-start(bf16[2,2,6,64,128]{4,3,2,1,0:T(8,128)(2,1)S(1)} %pad_maximum_fusion.2), channel_id=1, source_target_pairs={{0,1},{1,0},{2,3},{3,2},{4,5},{5,4},{6,7},{7,6},{8,9},{9,8},{10,11... | collective-permute-start | bytes 1179656 | tf_op jit(solution)/shard_map/ppermute | solution.py:183
  19.5 3.2 %collective-permute-start.4 = (bf16[2,2,6,64,128]{4,3,2,1,0:T(8,128)(2,1)S(1)}, bf16[2,2,6,64,128]{4,3,2,1,0:T(8,128)(2,1)S(1)}, u32[]{:S(2)}, u32[]{:S(2)}) collective-permute-start(bf16[2,2,6,64,128]{4,3,2,1,0:T(8,128)(2,1)S(1)} %collective-permute-done.refs_2_.refs_1_), channel_id=1, source_target_pairs={{0,2},{2,4},{4,6},{1,3},{3,5},{5,7},{8,10},{10,12},{12,14},{9,11},... | collective-permute-start | bytes 1179656 | tf_op jit(solution)/shard_map/ppermute | solution.py:178
  22.6 2.1 %collective-permute-start.5 = (bf16[2,2,6,64,128]{4,3,2,1,0:T(8,128)(2,1)S(1)}, bf16[2,2,6,64,128]{4,3,2,1,0:T(8,128)(2,1)S(1)}, u32[]{:S(2)}, u32[]{:S(2)}) collective-permute-start(bf16[2,2,6,64,128]{4,3,2,1,0:T(8,128)(2,1)S(1)} %collective-permute-done.refs_2_.refs_1_), channel_id=1, source_target_pairs={{2,0},{4,2},{6,4},{3,1},{5,3},{7,5},{10,8},{12,10},{14,12},{11,9},... | collective-permute-start | bytes 1179656 | tf_op jit(solution)/shard_map/ppermute | solution.py:178
  24.8 1.8 %collective-permute-done.1 = bf16[2,2,6,64,128]{4,3,2,1,0:T(8,128)(2,1)S(1)} collective-permute-done((bf16[2,2,6,64,128]{4,3,2,1,0:T(8,128)(2,1)S(1)}, bf16[2,2,6,64,128]{4,3,2,1,0:T(8,128)(2,1)S(1)}, u32[]{:S(2)}, u32[]{:S(2)}) %collective-permute-start.1) | collective-permute-done | bytes 393248 | tf_op jit(solution)/shard_map/ppermute | solution.py:183
  26.7 3.2 %collective-permute-start.9 = (bf16[2,2,2,6,64,128]{5,4,3,2,1,0:T(8,128)(2,1)S(1)}, bf16[2,2,2,6,64,128]{5,4,3,2,1,0:T(8,128)(2,1)S(1)}, u32[]{:S(2)}, u32[]{:S(2)}) collective-permute-start(bf16[2,2,2,6,64,128]{5,4,3,2,1,0:T(8,128)(2,1)S(1)} %pad_maximum_fusion.refs_0_.refs_2_), channel_id=1, source_target_pairs={{0,2},{2,4},{4,6},{1,3},{3,5},{5,7},{8,10},{10,12},{12,14},{9,11},... | collective-permute-start | bytes 2359304 | tf_op jit(solution)/shard_map/ppermute | solution.py:178
  29.9 2.1 %collective-permute-start.10 = (bf16[2,2,2,6,64,128]{5,4,3,2,1,0:T(8,128)(2,1)S(1)}, bf16[2,2,2,6,64,128]{5,4,3,2,1,0:T(8,128)(2,1)S(1)}, u32[]{:S(2)}, u32[]{:S(2)}) collective-permute-start(bf16[2,2,2,6,64,128]{5,4,3,2,1,0:T(8,128)(2,1)S(1)} %pad_maximum_fusion.refs_0_.refs_2_), channel_id=1, source_target_pairs={{2,0},{4,2},{6,4},{3,1},{5,3},{7,5},{10,8},{12,10},{14,12},{11,9},... | collective-permute-start | bytes 2359304 | tf_op jit(solution)/shard_map/ppermute | solution.py:178
  32.5 7.8 %collective-permute-start.6 = (bf16[6,2,6,64,128]{4,3,2,1,0:T(8,128)(2,1)S(1)}, bf16[6,2,6,64,128]{4,3,2,1,0:T(8,128)(2,1)S(1)}, u32[]{:S(2)}, u32[]{:S(2)}) collective-permute-start(bf16[6,2,6,64,128]{4,3,2,1,0:T(8,128)(2,1)S(1)} %get-tuple-element.49), channel_id=1, source_target_pairs={{0,8},{8,16},{16,24},{1,9},{9,17},{17,25},{2,10},{10,18},{18,26},{... | collective-permute-start | bytes 3538952 | tf_op jit(solution)/shard_map/ppermute | solution.py:178
  40.3 1.9 %collective-permute-start.7 = (bf16[6,2,6,64,128]{4,3,2,1,0:T(8,128)(2,1)S(1)}, bf16[6,2,6,64,128]{4,3,2,1,0:T(8,128)(2,1)S(1)}, u32[]{:S(2)}, u32[]{:S(2)}) collective-permute-start(bf16[6,2,6,64,128]{4,3,2,1,0:T(8,128)(2,1)S(1)} %get-tuple-element.48), channel_id=1, source_target_pairs={{8,0},{16,8},{24,16},{9,1},{17,9},{25,17},{10,2},{18,10},{26,18},{... | collective-permute-start | bytes 3538952 | tf_op jit(solution)/shard_map/ppermute | solution.py:178
  42.2 4.7 %collective-permute-done.9.refs_3_ = bf16[2,2,2,6,64,128]{5,4,3,2,1,0:T(8,128)(2,1)S(1)} collective-permute-done((bf16[2,2,2,6,64,128]{5,4,3,2,1,0:T(8,128)(2,1)S(1)}, bf16[2,2,2,6,64,128]{5,4,3,2,1,0:T(8,128)(2,1)S(1)}, u32[]{:S(2)}, u32[]{:S(2)}) %collective-permute-start.9) | collective-permute-done | bytes 786464 | tf_op jit(solution)/shard_map/ppermute | solution.py:178
  47.0 2.8 %collective-permute-done.10.refs_4_ = bf16[2,2,2,6,64,128]{5,4,3,2,1,0:T(8,128)(2,1)S(1)} collective-permute-done((bf16[2,2,2,6,64,128]{5,4,3,2,1,0:T(8,128)(2,1)S(1)}, bf16[2,2,2,6,64,128]{5,4,3,2,1,0:T(8,128)(2,1)S(1)}, u32[]{:S(2)}, u32[]{:S(2)}) %collective-permute-start.10) | collective-permute-done | bytes 786464 | tf_op jit(solution)/shard_map/ppermute | solution.py:178
  50.1 6.1 %collective-permute-start.11 = (bf16[6,2,6,64,128]{4,3,2,1,0:T(8,128)(2,1)S(1)}, bf16[6,2,6,64,128]{4,3,2,1,0:T(8,128)(2,1)S(1)}, u32[]{:S(2)}, u32[]{:S(2)}) collective-permute-start(bf16[6,2,6,64,128]{4,3,2,1,0:T(8,128)(2,1)S(1)} %get-tuple-element.35), channel_id=1, source_target_pairs={{0,8},{8,16},{16,24},{1,9},{9,17},{17,25},{2,10},{10,18},{18,26},{... | collective-permute-start | bytes 3538952 | tf_op jit(solution)/shard_map/ppermute | solution.py:178
  56.2 1.9 %collective-permute-start.12 = (bf16[6,2,6,64,128]{4,3,2,1,0:T(8,128)(2,1)S(1)}, bf16[6,2,6,64,128]{4,3,2,1,0:T(8,128)(2,1)S(1)}, u32[]{:S(2)}, u32[]{:S(2)}) collective-permute-start(bf16[6,2,6,64,128]{4,3,2,1,0:T(8,128)(2,1)S(1)} %get-tuple-element.34), channel_id=1, source_target_pairs={{8,0},{16,8},{24,16},{9,1},{17,9},{25,17},{10,2},{18,10},{26,18},{... | collective-permute-start | bytes 3538952 | tf_op jit(solution)/shard_map/ppermute | solution.py:178
  58.2 5.7 %shard_map.102 = (bf16[2,6,128,128]{3,2,1,0:T(8,128)(2,1)S(1)}, f32[2,6,2,128]{3,2,1,0:T(2,128)S(1)}) custom-call(bf16[2,2,2,6,64,128]{5,4,3,2,1,0:T(8,128)(2,1)S(1)} %pad_maximum_fusion.refs_0_.refs_2_, bf16[2,2,6,64,128]{4,3,2,1,0:T(8,128)(2,1)S(1)} %pad_maximum_fusion.4.refs_1_.refs_0_, ...), custom_call_target="tpu_custom_call" | custom-call | flops 905969664 | bytes 4718592 | tf_op jit(solution)/shard_map/pallas_call | solution.py:159
  63.9 3.2 %collective-permute-start.13 = (f32[2,6,2,128]{3,2,1,0:T(2,128)S(1)}, f32[2,6,2,128]{3,2,1,0:T(2,128)S(1)}, u32[]{:S(2)}, u32[]{:S(2)}) collective-permute-start(f32[2,6,2,128]{3,2,1,0:T(2,128)S(1)} %get-tuple-element.25.refs_10_.refs_7_), channel_id=1, source_target_pairs={{0,2},{2,4},{4,6},{1,3},{3,5},{5,7},{8,10},{10,12},{12,14},{9,11},... | collective-permute-start | bytes 36872 | tf_op jit(solution)/shard_map/ppermute | solution.py:178
  67.1 2.0 %collective-permute-start.14 = (f32[2,6,2,128]{3,2,1,0:T(2,128)S(1)}, f32[2,6,2,128]{3,2,1,0:T(2,128)S(1)}, u32[]{:S(2)}, u32[]{:S(2)}) collective-permute-start(f32[2,6,2,128]{3,2,1,0:T(2,128)S(1)} %get-tuple-element.25.refs_10_.refs_7_), channel_id=1, source_target_pairs={{2,0},{4,2},{6,4},{3,1},{5,3},{7,5},{10,8},{12,10},{14,12},{11,9},... | collective-permute-start | bytes 36872 | tf_op jit(solution)/shard_map/ppermute | solution.py:178
  69.2 5.0 %shard_map.103 = (bf16[2,2,6,64,128]{4,3,2,1,0:T(8,128)(2,1)S(1)}, bf16[2,2,6,64,128]{4,3,2,1,0:T(8,128)(2,1)S(1)}) custom-call(bf16[2,2,2,6,64,128]{5,4,3,2,1,0:T(8,128)(2,1)S(1)} %pad_maximum_fusion.refs_0_.refs_2_, bf16[2,2,6,64,128]{4,3,2,1,0:T(8,128)(2,1)S(1)} %pad_maximum_fusion.4.refs_1_.refs_0_, ...), custom_call_target="tpu_custom_call" | custom-call | flops 1358954496 | bytes 4718592 | tf_op jit(solution)/shard_map/pallas_call | solution.py:159
  74.8 4.5 %collective-permute-start.15 = (f32[3,6,2,128]{3,2,1,0:T(2,128)S(1)}, f32[3,6,2,128]{3,2,1,0:T(2,128)S(1)}, u32[]{:S(2)}, u32[]{:S(2)}) collective-permute-start(f32[3,6,2,128]{3,2,1,0:T(2,128)S(1)} %pad_maximum_fusion.6), channel_id=1, source_target_pairs={{0,8},{8,16},{16,24},{1,9},{9,17},{17,25},{2,10},{10,18},{18,26},{... | collective-permute-start | bytes 55304 | tf_op jit(solution)/shard_map/ppermute | solution.py:178
  79.4 1.9 %collective-permute-start.16 = (f32[3,6,2,128]{3,2,1,0:T(2,128)S(1)}, f32[3,6,2,128]{3,2,1,0:T(2,128)S(1)}, u32[]{:S(2)}, u32[]{:S(2)}) collective-permute-start(f32[3,6,2,128]{3,2,1,0:T(2,128)S(1)} %pad_maximum_fusion.7), channel_id=1, source_target_pairs={{8,0},{16,8},{24,16},{9,1},{17,9},{25,17},{10,2},{18,10},{26,18},{... | collective-permute-start | bytes 55304 | tf_op jit(solution)/shard_map/ppermute | solution.py:178
  81.3 2.6 %collective-permute-done.8 = bf16[2,2,6,64,128]{4,3,2,1,0:T(8,128)(2,1)S(1)} collective-permute-done((bf16[2,2,6,64,128]{4,3,2,1,0:T(8,128)(2,1)S(1)}, bf16[2,2,6,64,128]{4,3,2,1,0:T(8,128)(2,1)S(1)}, u32[]{:S(2)}, u32[]{:S(2)}) %collective-permute-start.8) | collective-permute-done | bytes 393248 | tf_op jit(solution)/shard_map/ppermute | solution.py:183
  84.0 0.9 slice_bitcast_fusion.2
  84.9 2.9 %shard_map.104 = (bf16[2,2,3,64,128]{4,3,2,1,0:T(8,128)(2,1)S(1)}, bf16[2,2,3,64,128]{4,3,2,1,0:T(8,128)(2,1)S(1)}) custom-call(bf16[2,2,6,64,128]{4,3,2,1,0:T(8,128)(2,1)S(1)} %pad_maximum_fusion.4.refs_1_.refs_0_, bf16[2,2,6,64,128]{4,3,2,1,0:T(8,128)(2,1)S(1)} %collective-permute-done.refs_2_.refs_1_, ...), custom_call_target="tpu_custom_call" | custom-call | flops 905969664 | bytes 2359296 | tf_op jit(solution)/shard_map/pallas_call | solution.py:159
  88.6 2.9 %shard_map.105 = (bf16[2,2,3,64,128]{4,3,2,1,0:T(8,128)(2,1)S(1)}, bf16[2,2,3,64,128]{4,3,2,1,0:T(8,128)(2,1)S(1)}) custom-call(bf16[2,2,6,64,128]{4,3,2,1,0:T(8,128)(2,1)S(1)} %pad_maximum_fusion.4.refs_1_.refs_0_, bf16[2,2,6,64,128]{4,3,2,1,0:T(8,128)(2,1)S(1)} %collective-permute-done.refs_2_.refs_1_, ...), custom_call_target="tpu_custom_call" | custom-call | flops 905969664 | bytes 2359296 | tf_op jit(solution)/shard_map/pallas_call | solution.py:159
  91.6 0.8 collective-permute-start.18
  92.6 2.3 %collective-permute-done.17 = bf16[2,2,3,64,128]{4,3,2,1,0:T(8,128)(2,1)S(1)} collective-permute-done((bf16[2,2,3,64,128]{4,3,2,1,0:T(8,128)(2,1)S(1)}, bf16[2,2,3,64,128]{4,3,2,1,0:T(8,128)(2,1)S(1)}, u32[]{:S(2)}, u32[]{:S(2)}) %collective-permute-start.17) | collective-permute-done | bytes 196640 | tf_op jit(solution)/shard_map/ppermute | solution.py:183
  95.0 3.8 %collective-permute-done.18 = bf16[2,2,3,64,128]{4,3,2,1,0:T(8,128)(2,1)S(1)} collective-permute-done((bf16[2,2,3,64,128]{4,3,2,1,0:T(8,128)(2,1)S(1)}, bf16[2,2,3,64,128]{4,3,2,1,0:T(8,128)(2,1)S(1)}, u32[]{:S(2)}, u32[]{:S(2)}) %collective-permute-start.18) | collective-permute-done | bytes 196640 | tf_op jit(solution)/shard_map/ppermute | solution.py:183
  98.8 0.9 slice_bitcast_fusion
  (96 shorter events, 6.3 us)
Async XLA Ops:
  2.1 7.8 %copy-start = (bf16[2,8,8,12,128]{4,2,3,1,0:T(8,128)(2,1)S(1)}, bf16[2,8,8,12,128]{4,2,3,1,0:T(8,128)(2,1)}, u32[]{:S(2)}) copy-start(bf16[2,8,8,12,128]{4,2,3,1,0:T(8,128)(2,1)} %param.10) | copy-start | bytes 1179652
  2.2 7.8 %copy-start.1 = (bf16[2,8,8,12,128]{4,2,3,1,0:T(8,128)(2,1)S(1)}, bf16[2,8,8,12,128]{4,2,3,1,0:T(8,128)(2,1)}, u32[]{:S(2)}) copy-start(bf16[2,8,8,12,128]{4,2,3,1,0:T(8,128)(2,1)} %param.7) | copy-start | bytes 1179652
  2.2 24.4 %collective-permute-start.2 = (bf16[2,2,6,64,128]{4,3,2,1,0:T(8,128)(2,1)S(1)}, bf16[2,2,6,64,128]{4,3,2,1,0:T(8,128)(2,1)S(1)}, u32[]{:S(2)}, u32[]{:S(2)}) collective-permute-start(bf16[2,2,6,64,128]{4,3,2,1,0:T(8,128)(2,1)S(1)} %pad_maximum_fusion.4.refs_1_.refs_0_), channel_id=1, source_target_pairs={{0,2},{2,4},{4,6},{1,3},{3,5},{5,7},{8,10},{10,12},{12,14},{9,11},... | collective-permute-start | bytes 1179656 | tf_op jit(solution)/shard_map/ppermute | solution.py:178
  5.6 21.1 %collective-permute-start.3 = (bf16[2,2,6,64,128]{4,3,2,1,0:T(8,128)(2,1)S(1)}, bf16[2,2,6,64,128]{4,3,2,1,0:T(8,128)(2,1)S(1)}, u32[]{:S(2)}, u32[]{:S(2)}) collective-permute-start(bf16[2,2,6,64,128]{4,3,2,1,0:T(8,128)(2,1)S(1)} %pad_maximum_fusion.4.refs_1_.refs_0_), channel_id=1, source_target_pairs={{2,0},{4,2},{6,4},{3,1},{5,3},{7,5},{10,8},{12,10},{14,12},{11,9},... | collective-permute-start | bytes 1179656 | tf_op jit(solution)/shard_map/ppermute | solution.py:178
  8.5 9.6 %collective-permute-start = (bf16[2,2,6,64,128]{4,3,2,1,0:T(8,128)(2,1)}, bf16[2,2,6,64,128]{4,3,2,1,0:T(8,128)(2,1)S(1)}, u32[]{:S(2)}, u32[]{:S(2)}) collective-permute-start(bf16[2,2,6,64,128]{4,3,2,1,0:T(8,128)(2,1)} %pad_maximum_fusion.3), channel_id=1, source_target_pairs={{0,1},{1,0},{2,3},{3,2},{4,5},{5,4},{6,7},{7,6},{8,9},{9,8},{10,11... | collective-permute-start | bytes 1179656 | tf_op jit(solution)/shard_map/ppermute | solution.py:183
  10.0 0.8 copy-start.3
  10.0 2.3 %copy-start.4 = (bf16[4,3,9,2,9,1]{4,2,1,0,5,3:T(8,128)(2,1)S(1)}, bf16[4,3,9,2,9,1]{4,2,1,0,5,3:T(8,128)(2,1)}, u32[]{:S(2)}) copy-start(bf16[4,3,9,2,9,1]{4,2,1,0,5,3:T(8,128)(2,1)} %constant.220) | copy-start | bytes 11668
  11.9 1.2 %copy-start.2 = (bf16[18,1152]{1,0:T(8,128)(2,1)S(1)}, bf16[18,1152]{1,0:T(8,128)(2,1)}, u32[]{:S(2)}) copy-start(bf16[18,1152]{1,0:T(8,128)(2,1)} %constant.110.clone) | copy-start | bytes 124420
  18.1 8.4 %collective-permute-start.1 = (bf16[2,2,6,64,128]{4,3,2,1,0:T(8,128)(2,1)S(1)}, bf16[2,2,6,64,128]{4,3,2,1,0:T(8,128)(2,1)S(1)}, u32[]{:S(2)}, u32[]{:S(2)}) collective-permute-start(bf16[2,2,6,64,128]{4,3,2,1,0:T(8,128)(2,1)S(1)} %pad_maximum_fusion.2), channel_id=1, source_target_pairs={{0,1},{1,0},{2,3},{3,2},{4,5},{5,4},{6,7},{7,6},{8,9},{9,8},{10,11... | collective-permute-start | bytes 1179656 | tf_op jit(solution)/shard_map/ppermute | solution.py:183
  19.5 12.8 %collective-permute-start.4 = (bf16[2,2,6,64,128]{4,3,2,1,0:T(8,128)(2,1)S(1)}, bf16[2,2,6,64,128]{4,3,2,1,0:T(8,128)(2,1)S(1)}, u32[]{:S(2)}, u32[]{:S(2)}) collective-permute-start(bf16[2,2,6,64,128]{4,3,2,1,0:T(8,128)(2,1)S(1)} %collective-permute-done.refs_2_.refs_1_), channel_id=1, source_target_pairs={{0,2},{2,4},{4,6},{1,3},{3,5},{5,7},{8,10},{10,12},{12,14},{9,11},... | collective-permute-start | bytes 1179656 | tf_op jit(solution)/shard_map/ppermute | solution.py:178
  22.6 9.8 %collective-permute-start.5 = (bf16[2,2,6,64,128]{4,3,2,1,0:T(8,128)(2,1)S(1)}, bf16[2,2,6,64,128]{4,3,2,1,0:T(8,128)(2,1)S(1)}, u32[]{:S(2)}, u32[]{:S(2)}) collective-permute-start(bf16[2,2,6,64,128]{4,3,2,1,0:T(8,128)(2,1)S(1)} %collective-permute-done.refs_2_.refs_1_), channel_id=1, source_target_pairs={{2,0},{4,2},{6,4},{3,1},{5,3},{7,5},{10,8},{12,10},{14,12},{11,9},... | collective-permute-start | bytes 1179656 | tf_op jit(solution)/shard_map/ppermute | solution.py:178
  26.7 20.3 %collective-permute-start.9 = (bf16[2,2,2,6,64,128]{5,4,3,2,1,0:T(8,128)(2,1)S(1)}, bf16[2,2,2,6,64,128]{5,4,3,2,1,0:T(8,128)(2,1)S(1)}, u32[]{:S(2)}, u32[]{:S(2)}) collective-permute-start(bf16[2,2,2,6,64,128]{5,4,3,2,1,0:T(8,128)(2,1)S(1)} %pad_maximum_fusion.refs_0_.refs_2_), channel_id=1, source_target_pairs={{0,2},{2,4},{4,6},{1,3},{3,5},{5,7},{8,10},{10,12},{12,14},{9,11},... | collective-permute-start | bytes 2359304 | tf_op jit(solution)/shard_map/ppermute | solution.py:178
  29.9 20.0 %collective-permute-start.10 = (bf16[2,2,2,6,64,128]{5,4,3,2,1,0:T(8,128)(2,1)S(1)}, bf16[2,2,2,6,64,128]{5,4,3,2,1,0:T(8,128)(2,1)S(1)}, u32[]{:S(2)}, u32[]{:S(2)}) collective-permute-start(bf16[2,2,2,6,64,128]{5,4,3,2,1,0:T(8,128)(2,1)S(1)} %pad_maximum_fusion.refs_0_.refs_2_), channel_id=1, source_target_pairs={{2,0},{4,2},{6,4},{3,1},{5,3},{7,5},{10,8},{12,10},{14,12},{11,9},... | collective-permute-start | bytes 2359304 | tf_op jit(solution)/shard_map/ppermute | solution.py:178
  32.5 25.7 %collective-permute-start.6 = (bf16[6,2,6,64,128]{4,3,2,1,0:T(8,128)(2,1)S(1)}, bf16[6,2,6,64,128]{4,3,2,1,0:T(8,128)(2,1)S(1)}, u32[]{:S(2)}, u32[]{:S(2)}) collective-permute-start(bf16[6,2,6,64,128]{4,3,2,1,0:T(8,128)(2,1)S(1)} %get-tuple-element.49), channel_id=1, source_target_pairs={{0,8},{8,16},{16,24},{1,9},{9,17},{17,25},{2,10},{10,18},{18,26},{... | collective-permute-start | bytes 3538952 | tf_op jit(solution)/shard_map/ppermute | solution.py:178
  40.3 17.8 %collective-permute-start.7 = (bf16[6,2,6,64,128]{4,3,2,1,0:T(8,128)(2,1)S(1)}, bf16[6,2,6,64,128]{4,3,2,1,0:T(8,128)(2,1)S(1)}, u32[]{:S(2)}, u32[]{:S(2)}) collective-permute-start(bf16[6,2,6,64,128]{4,3,2,1,0:T(8,128)(2,1)S(1)} %get-tuple-element.48), channel_id=1, source_target_pairs={{8,0},{16,8},{24,16},{9,1},{17,9},{25,17},{10,2},{18,10},{26,18},{... | collective-permute-start | bytes 3538952 | tf_op jit(solution)/shard_map/ppermute | solution.py:178
  50.1 34.8 %collective-permute-start.11 = (bf16[6,2,6,64,128]{4,3,2,1,0:T(8,128)(2,1)S(1)}, bf16[6,2,6,64,128]{4,3,2,1,0:T(8,128)(2,1)S(1)}, u32[]{:S(2)}, u32[]{:S(2)}) collective-permute-start(bf16[6,2,6,64,128]{4,3,2,1,0:T(8,128)(2,1)S(1)} %get-tuple-element.35), channel_id=1, source_target_pairs={{0,8},{8,16},{16,24},{1,9},{9,17},{17,25},{2,10},{10,18},{18,26},{... | collective-permute-start | bytes 3538952 | tf_op jit(solution)/shard_map/ppermute | solution.py:178
  56.2 28.7 %collective-permute-start.12 = (bf16[6,2,6,64,128]{4,3,2,1,0:T(8,128)(2,1)S(1)}, bf16[6,2,6,64,128]{4,3,2,1,0:T(8,128)(2,1)S(1)}, u32[]{:S(2)}, u32[]{:S(2)}) collective-permute-start(bf16[6,2,6,64,128]{4,3,2,1,0:T(8,128)(2,1)S(1)} %get-tuple-element.34), channel_id=1, source_target_pairs={{8,0},{16,8},{24,16},{9,1},{17,9},{25,17},{10,2},{18,10},{26,18},{... | collective-permute-start | bytes 3538952 | tf_op jit(solution)/shard_map/ppermute | solution.py:178
  63.9 10.9 %collective-permute-start.13 = (f32[2,6,2,128]{3,2,1,0:T(2,128)S(1)}, f32[2,6,2,128]{3,2,1,0:T(2,128)S(1)}, u32[]{:S(2)}, u32[]{:S(2)}) collective-permute-start(f32[2,6,2,128]{3,2,1,0:T(2,128)S(1)} %get-tuple-element.25.refs_10_.refs_7_), channel_id=1, source_target_pairs={{0,2},{2,4},{4,6},{1,3},{3,5},{5,7},{8,10},{10,12},{12,14},{9,11},... | collective-permute-start | bytes 36872 | tf_op jit(solution)/shard_map/ppermute | solution.py:178
  67.1 7.7 %collective-permute-start.14 = (f32[2,6,2,128]{3,2,1,0:T(2,128)S(1)}, f32[2,6,2,128]{3,2,1,0:T(2,128)S(1)}, u32[]{:S(2)}, u32[]{:S(2)}) collective-permute-start(f32[2,6,2,128]{3,2,1,0:T(2,128)S(1)} %get-tuple-element.25.refs_10_.refs_7_), channel_id=1, source_target_pairs={{2,0},{4,2},{6,4},{3,1},{5,3},{7,5},{10,8},{12,10},{14,12},{11,9},... | collective-permute-start | bytes 36872 | tf_op jit(solution)/shard_map/ppermute | solution.py:178
  74.2 9.6 %collective-permute-start.8 = (bf16[2,2,6,64,128]{4,3,2,1,0:T(8,128)(2,1)S(1)}, bf16[2,2,6,64,128]{4,3,2,1,0:T(8,128)(2,1)S(1)}, u32[]{:S(2)}, u32[]{:S(2)}) collective-permute-start(bf16[2,2,6,64,128]{4,3,2,1,0:T(8,128)(2,1)S(1)} %get-tuple-element.27), channel_id=1, source_target_pairs={{0,1},{1,0},{2,3},{3,2},{4,5},{5,4},{6,7},{7,6},{8,9},{9,8},{10,11... | collective-permute-start | bytes 1179656 | tf_op jit(solution)/shard_map/ppermute | solution.py:183
  74.8 10.1 %collective-permute-start.15 = (f32[3,6,2,128]{3,2,1,0:T(2,128)S(1)}, f32[3,6,2,128]{3,2,1,0:T(2,128)S(1)}, u32[]{:S(2)}, u32[]{:S(2)}) collective-permute-start(f32[3,6,2,128]{3,2,1,0:T(2,128)S(1)} %pad_maximum_fusion.6), channel_id=1, source_target_pairs={{0,8},{8,16},{16,24},{1,9},{9,17},{17,25},{2,10},{10,18},{18,26},{... | collective-permute-start | bytes 55304 | tf_op jit(solution)/shard_map/ppermute | solution.py:178
  79.4 5.5 %collective-permute-start.16 = (f32[3,6,2,128]{3,2,1,0:T(2,128)S(1)}, f32[3,6,2,128]{3,2,1,0:T(2,128)S(1)}, u32[]{:S(2)}, u32[]{:S(2)}) collective-permute-start(f32[3,6,2,128]{3,2,1,0:T(2,128)S(1)} %pad_maximum_fusion.7), channel_id=1, source_target_pairs={{8,0},{16,8},{24,16},{9,1},{17,9},{25,17},{10,2},{18,10},{26,18},{... | collective-permute-start | bytes 55304 | tf_op jit(solution)/shard_map/ppermute | solution.py:178
  87.9 7.0 %collective-permute-start.17 = (bf16[2,2,3,64,128]{4,3,2,1,0:T(8,128)(2,1)S(1)}, bf16[2,2,3,64,128]{4,3,2,1,0:T(8,128)(2,1)S(1)}, u32[]{:S(2)}, u32[]{:S(2)}) collective-permute-start(bf16[2,2,3,64,128]{4,3,2,1,0:T(8,128)(2,1)S(1)} %get-tuple-element.29), channel_id=1, source_target_pairs={{0,1},{1,0},{2,3},{3,2},{4,5},{5,4},{6,7},{7,6},{8,9},{9,8},{10,11... | collective-permute-start | bytes 589832 | tf_op jit(solution)/shard_map/ppermute | solution.py:183
  91.6 7.2 %collective-permute-start.18 = (bf16[2,2,3,64,128]{4,3,2,1,0:T(8,128)(2,1)S(1)}, bf16[2,2,3,64,128]{4,3,2,1,0:T(8,128)(2,1)S(1)}, u32[]{:S(2)}, u32[]{:S(2)}) collective-permute-start(bf16[2,2,3,64,128]{4,3,2,1,0:T(8,128)(2,1)S(1)} %get-tuple-element.31), channel_id=1, source_target_pairs={{0,1},{1,0},{2,3},{3,2},{4,5},{5,4},{6,7},{7,6},{8,9},{9,8},{10,11... | collective-permute-start | bytes 589832 | tf_op jit(solution)/shard_map/ppermute | solution.py:183

commit v9 on v8

--- a/solution.py
+++ b/solution.py
@@ -40,7 +40,7 @@
                         band[place, :] = side(row, part, at - 1, which)
 
 
-def fill_keys(parts, halo, bands):
+def fill_halo(parts, halo, bands):
     rows = (halo[parts : 2 * parts], halo[:parts], halo[2 * parts : 3 * parts])
     edges = halo[3 * parts :]
     frames, _, _, cells, _ = halo[0].shape
@@ -49,25 +49,15 @@
     fill_bands(frames, parts, cells, side, edge, bands)
 
 
-def fill_queries(halo, bands):
-    own, before, after, low, high = halo
-    frames, parts, _, _, cells, _ = own.shape
-    side = lambda row, part, at, which: (before, own, after)[row][at, part, which, 0]
-    edge = lambda end, row, part, which: (low, high)[end][3 * part + row, which, 0]
-    fill_bands(frames, parts, cells, side, edge, bands)
-
-
 def slab(parts, at, which):
-    if isinstance(parts, list):
-        return jnp.concatenate([part[at, which, 0] for part in parts], axis=0)
-    return jnp.concatenate([parts[at, part, which, 0] for part in range(parts.shape[1])], axis=0)
+    return jnp.concatenate([part[at, which, 0] for part in parts], axis=0)
 
 
 def attend_kernel(scaling, parts, *refs):
-    pair, halo = refs[0], refs[1 : 3 * parts + 3]
-    bias, attended, stats, key_all, value_all = refs[3 * parts + 3 :]
+    pair, halo = refs[:parts], refs[parts : 4 * parts + 2]
+    bias, attended, stats, key_all, value_all = refs[4 * parts + 2 :]
     frames, _, tokens, _ = attended.shape
-    fill_keys(parts, halo, (key_all, value_all))
+    fill_halo(parts, halo, (key_all, value_all))
     windows = [pl.ds(3 * at * tokens, 9 * tokens) for at in range(frames)]
     scores = [
         dot(slab(pair, at, 0), key_all[windows[at], :], NT) * (scaling * LOG2E) + spread(bias[at], tokens)
@@ -96,11 +86,11 @@
 
 
 def query_kernel(scaling, parts, *refs):
-    pair, halo = refs[0], refs[1 : 3 * parts + 3]
-    attended, stats, bias = refs[3 * parts + 3 : 3 * parts + 6]
-    grads, (key_all, value_all) = refs[3 * parts + 6 : -2], refs[-2:]
+    pair, halo = refs[:parts], refs[parts : 4 * parts + 2]
+    attended, stats, bias = refs[4 * parts + 2 : 4 * parts + 5]
+    grads, (key_all, value_all) = refs[4 * parts + 5 : -2], refs[-2:]
     frames, _, tokens, _ = attended.shape
-    fill_keys(parts, halo, (key_all, value_all))
+    fill_halo(parts, halo, (key_all, value_all))
     windows = [pl.ds(3 * at * tokens, 9 * tokens) for at in range(frames)]
 
     def column(at, which):
@@ -118,11 +108,11 @@
 
 
 def back_kernel(scaling, parts, *refs):
-    pair, halo = list(refs[:parts]), refs[parts : parts + 5]
-    own_st, before_st, after_st, low_st, high_st, bias = refs[parts + 5 : parts + 11]
-    grads, (query_all, grad_all) = refs[parts + 11 : -2], refs[-2:]
+    pair, halo = refs[:parts], refs[parts : 4 * parts + 2]
+    own_st, before_st, after_st, low_st, high_st, bias = refs[4 * parts + 2 : 4 * parts + 8]
+    grads, (query_all, grad_all) = refs[4 * parts + 8 : -2], refs[-2:]
     frames, _, _, tokens = own_st.shape
-    fill_queries(halo, (query_all, grad_all))
+    fill_halo(parts, halo, (query_all, grad_all))
 
     def stat_row(at, row, which):
         if at == 0:
@@ -147,20 +137,24 @@
         store(grads, at, key_grad.astype(jnp.bfloat16), value_grad.astype(jnp.bfloat16))
 
 
-def head_spec(shape, first):
+def head_spec(shape, first, half=0):
     dim = len(shape) - 3
+    if dim == 2 and shape[1] == 4:
+        block = (shape[0], 2, 1) + shape[3:]
+        return pl.BlockSpec(block, lambda head: (0, half, head + first, 0, 0))
     block = shape[:dim] + (1,) + shape[dim + 1 :]
     return pl.BlockSpec(block, lambda head: (0,) * dim + (head + first,) + (0, 0))
 
 
 def run(kernel, scaling, parts, operands, bias, outs, first, count, products):
-    frames, (cells, dim) = bias.shape[0], operands[0].shape[-2:]
+    frames, (cells, dim) = bias.shape[0], operands[0][0].shape[-2:]
+    operands = [part if isinstance(part, tuple) else (part, 0) for part in operands]
     tokens = parts * cells
     return pl.pallas_call(
         functools.partial(kernel, scaling, parts),
         grid=(count,),
         out_shape=tuple(outs),
-        in_specs=[head_spec(part.shape, first) for part in operands]
+        in_specs=[head_spec(part.shape, first, half) for part, half in operands]
         + [pl.BlockSpec(bias.shape, lambda head: (0,) * bias.ndim)],
         out_specs=tuple(head_spec(out.shape, 0) for out in outs),
         scratch_shapes=[pltpu.VMEM((3 * (frames + 2) * tokens, dim), jnp.bfloat16)] * 2,
@@ -170,7 +164,7 @@
             bytes_accessed=count * (frames + 2) * 3 * 2 * tokens * dim * 2,
             transcendentals=frames * count * tokens * 9 * tokens,
         ),
-    )(*operands, bias)
+    )(*[part for part, _ in operands], bias)
 
 
 def step_along(tensor, axis, sign):
@@ -238,12 +232,10 @@
     scaling = dim ** (-0.5)
     assert rows == TR and TC % columns_here == 0
 
-    def pair_of(first, second, shift):
+    def group_of(tensors, shift):
         start = (me + shift) % size * groups
-        picked = [
-            lax.dynamic_slice_in_dim(jnp.transpose(t, (0, 3, 1, 2, 4)), start, groups, 1) for t in (first, second)
-        ]
-        return jnp.stack(picked, 1).reshape(frames, 2, groups, cells, dim)
+        picked = [lax.dynamic_slice_in_dim(jnp.transpose(t, (0, 3, 1, 2, 4)), start, groups, 1) for t in tensors]
+        return jnp.stack(picked, 1).reshape(frames, len(tensors), groups, cells, dim)
 
     def from_heads(blocks):
         whole = jnp.zeros((2, frames, rows, heads, columns_here, dim), jnp.bfloat16)
@@ -257,23 +249,26 @@
         return whole[0], whole[1]
 
     front_bias, back_bias = tile_biases(active, frames, columns_here, cells)
-    key_here = pair_of(keys, values, 0)
-    key_near = row_sides(key_here)
-    key_sent = [pair_of(keys, values, shift) for shift in range(1, size)]
+
+    here = group_of((keys, values, queries, out_grad), 0)
+    near = row_sides(here)
+    key_sent = [group_of((keys, values), shift) for shift in range(1, size)]
     key_moved = [turn(key_sent[size - b - 1], size - b) for b in range(1, size)]
-    query_held = [pair_of(queries, out_grad, shift) for shift in range(size)]
-    query_held, key_moved = lax.optimization_barrier((query_held, key_moved))
-    key_far = [row_sides(part) for part in key_moved]
-    query_moved = [turn(query_held[size - b], size - b) for b in range(1, size)]
-    query_all = jnp.stack(query_held[:1] + query_moved, 1)
-    query_all, key_near = lax.optimization_barrier((query_all, key_near))
-    query_before, query_after = row_sides(query_all)
-    key_parts, sides = [key_here] + key_moved, [key_near] + key_far
-    key_halo = key_parts + [before for before, _ in sides] + [after for _, after in sides]
-    key_halo += frame_edges([row for part, (up, down) in zip(key_parts, sides) for row in (up, part, down)])
-    query_halo = [query_all, query_before, query_after]
-    query_rows = (query_before, query_all, query_after)
-    query_halo += frame_edges([row[:, b] for b in range(size) for row in query_rows])
+    query_sent = [group_of((queries, out_grad), shift) for shift in range(1, size)]
+    query_sent, key_moved = lax.optimization_barrier((query_sent, key_moved))
+    query_moved = [turn(query_sent[size - b - 1], size - b) for b in range(1, size)]
+
+    def halo_of(moved, half):
+        sides = [near] + [row_sides(part) for part in moved]
+        rows = [[side[at] for side in sides] for at in range(2)]
+        rows.insert(1, [here] + moved)
+        cut = [[part[:, 2 * half : 2 * half + 2] if at == 0 else part for at, part in enumerate(row)] for row in rows]
+        edges = frame_edges([row[part] for part in range(size) for row in cut])
+        marked = [[(part, half if at == 0 else 0) for at, part in enumerate(row)] for row in rows]
+        return marked[1], marked[1] + marked[0] + marked[2] + [(edge, 0) for edge in edges]
+
+    key_parts, key_halo = halo_of(key_moved, 0)
+    query_parts, query_halo = halo_of(query_moved, 1)
 
     def grads_shape(count):
         return [jax.ShapeDtypeStruct((2, frames, count, cells, dim), jnp.bfloat16)] * size
@@ -281,10 +276,10 @@
     attended_shape = jax.ShapeDtypeStruct((frames, groups, tokens, dim), jnp.bfloat16)
     stat_shape = jax.ShapeDtypeStruct((frames, groups, 2, tokens), jnp.float32)
     attended, stats = run(
-        attend_kernel, scaling, size, [query_all] + key_halo, front_bias, [attended_shape, stat_shape], 0, groups, 2
+        attend_kernel, scaling, size, query_parts + key_halo, front_bias, [attended_shape, stat_shape], 0, groups, 2
     )
     front_grads = run(
-        query_kernel, scaling, size, [query_all] + key_halo + [attended, stats], front_bias, grads_shape(groups),
+        query_kernel, scaling, size, query_parts + key_halo + [attended, stats], front_bias, grads_shape(groups),
         0, groups, 3
     )
     stat_sides = row_sides(stats)

time: 100 us -> 114 us (1.14); the launches traced: 99.7 us -> 112 us
  local copies, waits for them, and re-layouts: 6.9 us -> 18.4 us
  Pallas kernels: 16.6 us -> 20.7 us
  waiting for transfers between devices: 22.8 us -> 19.7 us
  starting transfers between devices: 49.9 us -> 47.2 us
  other arithmetic: 1.41 us -> 2.94 us
    ppermute x5, waiting for transfers between devices: 15.2 us -> 7.74 us  [turn(): lax.ppermute(tensor, 'head', [(i, (i + shift) % size) for i in range(size)])]
    unnamed x21 -> x44, local copies, waits for them, and re-layouts: 1.14 us -> 7.15 us
    ppermute x14, waiting for transfers between devices: 7.61 us -> 11.9 us  [step_along(): lax.ppermute(tensor, axis, [(i, i + sign) for i in range(size) if 0 <= i...]
    pallas_call x4, Pallas kernels: 16.6 us -> 20.7 us  [run(): pl.pallas_call(functools.partial(kernel, scaling, parts), grid=(count,),...]
    ppermute x14, starting transfers between devices: 45.5 us -> 41.8 us  [step_along(): lax.ppermute(tensor, axis, [(i, i + sign) for i in range(size) if 0 <= i...]
    squeeze x2, local copies, waits for them, and re-layouts: 0.05 us -> 2.7 us  [tile_biases(): return (bias[0], bias[1])]
    another operation x2, local copies, waits for them, and re-layouts: 0.11 us -> 1.57 us  [frame_edges(): return (low, step_along(jnp.stack([row[0] for row in rows]), 'frame', -1))]
    slice x1, local copies, waits for them, and re-layouts: 0.01 us -> 1.46 us  [tile_biases(): return (bias[0], bias[1])]
  transfers between devices with their start and end apart: 19 -> 19, of which waited for: 8 -> 7; matrix products, arithmetic and copies ran while one was open for 6% -> 17% of each run, Pallas kernels for 14% -> 19%
where the time goes in v9:
time: 114 us; the launch traced here: 112 us
  starting transfers between devices  47.2 us (41%)
  Pallas kernels  20.7 us (18%)
  waiting for transfers between devices  19.7 us (17%)
  local copies, waits for them, and re-layouts  18.4 us (16%)
  other arithmetic  2.94 us (3%)
  matrix products  1.48 us (1%)
  between operations  1.23 us (1%)
    ppermute x14, starting transfers between devices, step_along(): lax.ppermute(tensor, axis, [(i, i + sign) for i in range(size) if 0 <= i...  41.8 us
    pallas_call x4, Pallas kernels, run(): pl.pallas_call(functools.partial(kernel, scaling, parts), grid=(count,),...  20.7 us
    ppermute x14, waiting for transfers between devices, step_along(): lax.ppermute(tensor, axis, [(i, i + sign) for i in range(size) if 0 <= i...  11.9 us
    ppermute x5, waiting for transfers between devices, turn(): lax.ppermute(tensor, 'head', [(i, (i + shift) % size) for i in range(size)])  7.74 us
    unnamed x44, local copies, waits for them, and re-layouts  7.15 us
    ppermute x5, starting transfers between devices, turn(): lax.ppermute(tensor, 'head', [(i, (i + shift) % size) for i in range(size)])  5.37 us
    squeeze x2, local copies, waits for them, and re-layouts, tile_biases(): return (bias[0], bias[1])  2.7 us
  transfers between devices with their start and end apart: 19, of which 7 were waited for; matrix products, arithmetic and copies ran while one was open for 17% of the time, Pallas kernels for 19%

profile of v9, /device:TPU:9, one launch (start us, length us, event | category | flops | bytes accessed | tf_op | source)
XLA Modules:
  0.0 111.7 jit_solution(18344553902627994769)
XLA Ops:
  0.7 1.3 %dynamic-slice_bitcast_fusion.2 = (bf16[2,6,8,8,128]{4,3,1,2,0:T(8,128)(2,1)S(1)}, bf16[2,6,8,8,128]{4,3,1,2,0:T(8,128)(2,1)S(1)}, bf16[2,6,8,8,128]{4,3,1,2,0:T(8,128)(2,1)S(1)}, bf16[2,6,8,8,128]{4,3,1,2,0:T(8,128)(2,1)S(1)}) fusion(bf16[2,8,8,12,128]{4,2,3,1,0:T(8,128)(2,1)} %param.10, s32[]{:T(128)S(6)} %select_n.91, s32[]{:T(128)S(6)} %select_n.89, ...), kind=kLoop, calls=%fused_computation.64 | loop fusion | bytes 1572872 | tf_op jit(solution)/shard_map/dynamic_slice | solution.py:237
  3.0 3.3 %collective-permute-start.2 = (bf16[2,4,6,64,128]{4,3,2,1,0:T(8,128)(2,1)S(1)}, bf16[2,4,6,64,128]{4,3,2,1,0:T(8,128)(2,1)S(1)}, u32[]{:S(2)}, u32[]{:S(2)}) collective-permute-start(bf16[2,4,6,64,128]{4,3,2,1,0:T(8,128)(2,1)S(1)} %pad_maximum_fusion.refs_0_.refs_2_), channel_id=1, source_target_pairs={{0,2},{2,4},{4,6},{1,3},{3,5},{5,7},{8,10},{10,12},{12,14},{9,11},... | collective-permute-start | bytes 2359304 | tf_op jit(solution)/shard_map/ppermute | solution.py:172
  6.3 2.1 %collective-permute-start.4 = (bf16[2,4,6,64,128]{4,3,2,1,0:T(8,128)(2,1)S(1)}, bf16[2,4,6,64,128]{4,3,2,1,0:T(8,128)(2,1)S(1)}, u32[]{:S(2)}, u32[]{:S(2)}) collective-permute-start(bf16[2,4,6,64,128]{4,3,2,1,0:T(8,128)(2,1)S(1)} %pad_maximum_fusion.refs_0_.refs_2_), channel_id=1, source_target_pairs={{2,0},{4,2},{6,4},{3,1},{5,3},{7,5},{10,8},{12,10},{14,12},{11,9},... | collective-permute-start | bytes 2359304 | tf_op jit(solution)/shard_map/ppermute | solution.py:172
  13.8 5.1 %collective-permute-done.refs_3_.refs_1_ = bf16[2,2,6,64,128]{4,3,2,1,0:T(8,128)(2,1)S(1)} collective-permute-done((bf16[2,2,6,64,128]{4,3,2,1,0:T(8,128)(2,1)}, bf16[2,2,6,64,128]{4,3,2,1,0:T(8,128)(2,1)S(1)}, u32[]{:S(2)}, u32[]{:S(2)}) %collective-permute-start) | collective-permute-done | bytes 393248 | tf_op jit(solution)/shard_map/ppermute | solution.py:177
  18.9 3.1 %collective-permute-start.3 = (bf16[2,2,6,64,128]{4,3,2,1,0:T(8,128)(2,1)S(1)}, bf16[2,2,6,64,128]{4,3,2,1,0:T(8,128)(2,1)S(1)}, u32[]{:S(2)}, u32[]{:S(2)}) collective-permute-start(bf16[2,2,6,64,128]{4,3,2,1,0:T(8,128)(2,1)S(1)} %collective-permute-done.refs_3_.refs_1_), channel_id=1, source_target_pairs={{0,2},{2,4},{4,6},{1,3},{3,5},{5,7},{8,10},{10,12},{12,14},{9,11},... | collective-permute-start | bytes 1179656 | tf_op jit(solution)/shard_map/ppermute | solution.py:172
  22.1 2.1 %collective-permute-start.5 = (bf16[2,2,6,64,128]{4,3,2,1,0:T(8,128)(2,1)S(1)}, bf16[2,2,6,64,128]{4,3,2,1,0:T(8,128)(2,1)S(1)}, u32[]{:S(2)}, u32[]{:S(2)}) collective-permute-start(bf16[2,2,6,64,128]{4,3,2,1,0:T(8,128)(2,1)S(1)} %collective-permute-done.refs_3_.refs_1_), channel_id=1, source_target_pairs={{2,0},{4,2},{6,4},{3,1},{5,3},{7,5},{10,8},{12,10},{14,12},{11,9},... | collective-permute-start | bytes 1179656 | tf_op jit(solution)/shard_map/ppermute | solution.py:172
  24.2 1.3 %collective-permute-start.1 = (bf16[2,2,6,64,128]{4,3,2,1,0:T(8,128)(2,1)}, bf16[2,2,6,64,128]{4,3,2,1,0:T(8,128)(2,1)S(1)}, u32[]{:S(2)}, u32[]{:S(2)}) collective-permute-start(bf16[2,2,6,64,128]{4,3,2,1,0:T(8,128)(2,1)} %pad_maximum_fusion.1), channel_id=1, source_target_pairs={{0,1},{1,0},{2,3},{3,2},{4,5},{5,4},{6,7},{7,6},{8,9},{9,8},{10,11... | collective-permute-start | bytes 1179656 | tf_op jit(solution)/shard_map/ppermute | solution.py:177
  28.0 3.3 %collective-permute-done.3.refs_5_ = bf16[2,2,6,64,128]{4,3,2,1,0:T(8,128)(2,1)S(1)} collective-permute-done((bf16[2,2,6,64,128]{4,3,2,1,0:T(8,128)(2,1)S(1)}, bf16[2,2,6,64,128]{4,3,2,1,0:T(8,128)(2,1)S(1)}, u32[]{:S(2)}, u32[]{:S(2)}) %collective-permute-start.3) | collective-permute-done | bytes 393248 | tf_op jit(solution)/shard_map/ppermute | solution.py:172
  32.9 1.4 %collective-permute-done.5.refs_7_ = bf16[2,2,6,64,128]{4,3,2,1,0:T(8,128)(2,1)S(1)} collective-permute-done((bf16[2,2,6,64,128]{4,3,2,1,0:T(8,128)(2,1)S(1)}, bf16[2,2,6,64,128]{4,3,2,1,0:T(8,128)(2,1)S(1)}, u32[]{:S(2)}, u32[]{:S(2)}) %collective-permute-start.5) | collective-permute-done | bytes 393248 | tf_op jit(solution)/shard_map/ppermute | solution.py:172
  35.9 5.3 %collective-permute-start.6 = (bf16[6,2,6,64,128]{4,3,2,1,0:T(8,128)(2,1)}, bf16[6,2,6,64,128]{4,3,2,1,0:T(8,128)(2,1)}, u32[]{:S(2)}, u32[]{:S(2)}) collective-permute-start(bf16[6,2,6,64,128]{4,3,2,1,0:T(8,128)(2,1)} %get-tuple-element.45), channel_id=1, source_target_pairs={{0,8},{8,16},{16,24},{1,9},{9,17},{17,25},{2,10},{10,18},{18,26},{... | collective-permute-start | bytes 3538952 | tf_op jit(solution)/shard_map/ppermute | solution.py:172
  41.2 1.9 %collective-permute-start.7 = (bf16[6,2,6,64,128]{4,3,2,1,0:T(8,128)(2,1)}, bf16[6,2,6,64,128]{4,3,2,1,0:T(8,128)(2,1)}, u32[]{:S(2)}, u32[]{:S(2)}) collective-permute-start(bf16[6,2,6,64,128]{4,3,2,1,0:T(8,128)(2,1)} %get-tuple-element.44), channel_id=1, source_target_pairs={{8,0},{16,8},{24,16},{9,1},{17,9},{25,17},{10,2},{18,10},{26,18},{... | collective-permute-start | bytes 3538952 | tf_op jit(solution)/shard_map/ppermute | solution.py:172
  43.9 3.2 %collective-permute-start.9 = (bf16[2,2,6,64,128]{4,3,2,1,0:T(8,128)(2,1)S(1)}, bf16[2,2,6,64,128]{4,3,2,1,0:T(8,128)(2,1)}, u32[]{:S(2)}, u32[]{:S(2)}) collective-permute-start(bf16[2,2,6,64,128]{4,3,2,1,0:T(8,128)(2,1)S(1)} %collective-permute-done.1.refs_1_.refs_3_), channel_id=1, source_target_pairs={{0,2},{2,4},{4,6},{1,3},{3,5},{5,7},{8,10},{10,12},{12,14},{9,11},... | collective-permute-start | bytes 1179656 | tf_op jit(solution)/shard_map/ppermute | solution.py:172
  47.1 1.5 %fusion.23 = (f32[4,1152]{1,0:T(4,128)}, f32[4,1152]{1,0:T(4,128)}) fusion(f32[8,1152]{1,0:T(8,128)} %fusion), kind=kLoop, calls=%fused_computation.106 | loop fusion | bytes 73728 | tf_op jit(solution)/shard_map/slice | solution.py:222
  48.6 1.3 %squeeze.22.refs_10_.refs_12_ = f32[2,2,1152]{2,1,0:T(2,128)} reshape(f32[4,1152]{1,0:T(4,128)} %get-tuple-element.61) | data formatting | bytes 36864 | tf_op jit(solution)/shard_map/squeeze | solution.py:222
  49.9 1.3 %squeeze.25.refs_15_ = f32[2,2,1152]{2,1,0:T(2,128)} reshape(f32[4,1152]{1,0:T(4,128)} %get-tuple-element.60) | data formatting | bytes 36864 | tf_op jit(solution)/shard_map/squeeze | solution.py:222
  51.3 2.9 %collective-permute-start.10 = (bf16[2,2,6,64,128]{4,3,2,1,0:T(8,128)(2,1)S(1)}, bf16[2,2,6,64,128]{4,3,2,1,0:T(8,128)(2,1)S(1)}, u32[]{:S(2)}, u32[]{:S(2)}) collective-permute-start(bf16[2,2,6,64,128]{4,3,2,1,0:T(8,128)(2,1)S(1)} %collective-permute-done.1.refs_1_.refs_3_), channel_id=1, source_target_pairs={{2,0},{4,2},{6,4},{3,1},{5,3},{7,5},{10,8},{12,10},{14,12},{11,9},... | collective-permute-start | bytes 1179656 | tf_op jit(solution)/shard_map/ppermute | solution.py:172
  54.1 1.9 %collective-permute-done.9.refs_5_ = bf16[2,2,6,64,128]{4,3,2,1,0:T(8,128)(2,1)} collective-permute-done((bf16[2,2,6,64,128]{4,3,2,1,0:T(8,128)(2,1)S(1)}, bf16[2,2,6,64,128]{4,3,2,1,0:T(8,128)(2,1)}, u32[]{:S(2)}, u32[]{:S(2)}) %collective-permute-start.9) | collective-permute-done | bytes 393248 | tf_op jit(solution)/shard_map/ppermute | solution.py:172
  56.0 1.9 %slice_dynamic-update-slice_fusion.2 = (bf16[6,2,6,64,128]{4,3,2,1,0:T(8,128)(2,1)}, bf16[6,2,6,64,128]{4,3,2,1,0:T(8,128)(2,1)}) fusion(bf16[6,2,6,64,128]{4,3,2,1,0:T(8,128)(2,1)} %copy-done.15, bf16[2,2,6,64,128]{4,3,2,1,0:T(8,128)(2,1)} %collective-permute-done.9.refs_5_, bf16[6,2,6,64,128]{4,3,2,1,0:T(8,128)(2,1)} %copy-done.16), kind=kLoop, calls=%fused_computation.28 | loop fusion | bytes 786432
  58.7 4.7 %collective-permute-done.10.refs_7_ = bf16[2,2,6,64,128]{4,3,2,1,0:T(8,128)(2,1)S(1)} collective-permute-done((bf16[2,2,6,64,128]{4,3,2,1,0:T(8,128)(2,1)S(1)}, bf16[2,2,6,64,128]{4,3,2,1,0:T(8,128)(2,1)S(1)}, u32[]{:S(2)}, u32[]{:S(2)}) %collective-permute-start.10) | collective-permute-done | bytes 393248 | tf_op jit(solution)/shard_map/ppermute | solution.py:172
  64.2 4.2 %collective-permute-start.11 = (bf16[6,2,6,64,128]{4,3,2,1,0:T(8,128)(2,1)}, bf16[6,2,6,64,128]{4,3,2,1,0:T(8,128)(2,1)S(1)}, u32[]{:S(2)}, u32[]{:S(2)}) collective-permute-start(bf16[6,2,6,64,128]{4,3,2,1,0:T(8,128)(2,1)} %get-tuple-element.37), channel_id=1, source_target_pairs={{0,8},{8,16},{16,24},{1,9},{9,17},{17,25},{2,10},{10,18},{18,26},{... | collective-permute-start | bytes 3538952 | tf_op jit(solution)/shard_map/ppermute | solution.py:172
  68.4 1.9 %collective-permute-start.12 = (bf16[6,2,6,64,128]{4,3,2,1,0:T(8,128)(2,1)}, bf16[6,2,6,64,128]{4,3,2,1,0:T(8,128)(2,1)S(1)}, u32[]{:S(2)}, u32[]{:S(2)}) collective-permute-start(bf16[6,2,6,64,128]{4,3,2,1,0:T(8,128)(2,1)} %get-tuple-element.36), channel_id=1, source_target_pairs={{8,0},{16,8},{24,16},{9,1},{17,9},{25,17},{10,2},{18,10},{26,18},{... | collective-permute-start | bytes 3538952 | tf_op jit(solution)/shard_map/ppermute | solution.py:172
  70.4 6.9 %shard_map.102 = (bf16[2,6,128,128]{3,2,1,0:T(8,128)(2,1)S(1)}, f32[2,6,2,128]{3,2,1,0:T(2,128)S(1)}) custom-call(bf16[2,4,6,64,128]{4,3,2,1,0:T(8,128)(2,1)S(1)} %pad_maximum_fusion.refs_0_.refs_2_, bf16[2,2,6,64,128]{4,3,2,1,0:T(8,128)(2,1)S(1)} %collective-permute-done.1.refs_1_.refs_3_, bf16[2,4,6,64,128]{4,3,2,1,0:T(8,128)(2,1)S(1)} %pad_maximum_fusion.refs_0_.refs_2_, ...), custom_call_target="tpu_custom_call" | custom-call | flops 905969664 | bytes 4718592 | tf_op jit(solution)/shard_map/pallas_call | solution.py:153
  77.2 1.9 %collective-permute-start.13 = (f32[2,6,2,128]{3,2,1,0:T(2,128)S(1)}, f32[2,6,2,128]{3,2,1,0:T(2,128)S(1)}, u32[]{:S(2)}, u32[]{:S(2)}) collective-permute-start(f32[2,6,2,128]{3,2,1,0:T(2,128)S(1)} %get-tuple-element.17.refs_11_.refs_10_), channel_id=1, source_target_pairs={{0,2},{2,4},{4,6},{1,3},{3,5},{5,7},{8,10},{10,12},{12,14},{9,11},... | collective-permute-start | bytes 36872 | tf_op jit(solution)/shard_map/ppermute | solution.py:172
  79.2 3.4 %collective-permute-start.14 = (f32[2,6,2,128]{3,2,1,0:T(2,128)S(1)}, f32[2,6,2,128]{3,2,1,0:T(2,128)S(1)}, u32[]{:S(2)}, u32[]{:S(2)}) collective-permute-start(f32[2,6,2,128]{3,2,1,0:T(2,128)S(1)} %get-tuple-element.17.refs_11_.refs_10_), channel_id=1, source_target_pairs={{2,0},{4,2},{6,4},{3,1},{5,3},{7,5},{10,8},{12,10},{14,12},{11,9},... | collective-permute-start | bytes 36872 | tf_op jit(solution)/shard_map/ppermute | solution.py:172
  82.5 6.5 %shard_map.103 = (bf16[2,2,6,64,128]{4,3,2,1,0:T(8,128)(2,1)S(1)}, bf16[2,2,6,64,128]{4,3,2,1,0:T(8,128)(2,1)S(1)}) custom-call(bf16[2,4,6,64,128]{4,3,2,1,0:T(8,128)(2,1)S(1)} %pad_maximum_fusion.refs_0_.refs_2_, bf16[2,2,6,64,128]{4,3,2,1,0:T(8,128)(2,1)S(1)} %collective-permute-done.1.refs_1_.refs_3_, ...), custom_call_target="tpu_custom_call" | custom-call | flops 1358954496 | bytes 4718592 | tf_op jit(solution)/shard_map/pallas_call | solution.py:153
  89.1 1.3 %collective-permute-start.8 = (bf16[2,2,6,64,128]{4,3,2,1,0:T(8,128)(2,1)S(1)}, bf16[2,2,6,64,128]{4,3,2,1,0:T(8,128)(2,1)S(1)}, u32[]{:S(2)}, u32[]{:S(2)}) collective-permute-start(bf16[2,2,6,64,128]{4,3,2,1,0:T(8,128)(2,1)S(1)} %get-tuple-element.19), channel_id=1, source_target_pairs={{0,1},{1,0},{2,3},{3,2},{4,5},{5,4},{6,7},{7,6},{8,9},{9,8},{10,11... | collective-permute-start | bytes 1179656 | tf_op jit(solution)/shard_map/ppermute | solution.py:177
  90.4 1.9 %collective-permute-start.16 = (f32[3,6,2,128]{3,2,1,0:T(2,128)S(1)}, f32[3,6,2,128]{3,2,1,0:T(2,128)S(1)}, u32[]{:S(2)}, u32[]{:S(2)}) collective-permute-start(f32[3,6,2,128]{3,2,1,0:T(2,128)S(1)} %pad_maximum_fusion.6), channel_id=1, source_target_pairs={{8,0},{16,8},{24,16},{9,1},{17,9},{25,17},{10,2},{18,10},{26,18},{... | collective-permute-start | bytes 55304 | tf_op jit(solution)/shard_map/ppermute | solution.py:172
  92.4 4.5 %collective-permute-start.15 = (f32[3,6,2,128]{3,2,1,0:T(2,128)S(1)}, f32[3,6,2,128]{3,2,1,0:T(2,128)S(1)}, u32[]{:S(2)}, u32[]{:S(2)}) collective-permute-start(f32[3,6,2,128]{3,2,1,0:T(2,128)S(1)} %pad_maximum_fusion.5), channel_id=1, source_target_pairs={{0,8},{8,16},{16,24},{1,9},{9,17},{17,25},{2,10},{10,18},{18,26},{... | collective-permute-start | bytes 55304 | tf_op jit(solution)/shard_map/ppermute | solution.py:172
  97.7 3.7 %shard_map.104 = (bf16[2,2,3,64,128]{4,3,2,1,0:T(8,128)(2,1)S(1)}, bf16[2,2,3,64,128]{4,3,2,1,0:T(8,128)(2,1)S(1)}) custom-call(bf16[2,4,6,64,128]{4,3,2,1,0:T(8,128)(2,1)S(1)} %pad_maximum_fusion.refs_0_.refs_2_, bf16[2,2,6,64,128]{4,3,2,1,0:T(8,128)(2,1)S(1)} %collective-permute-done.refs_3_.refs_1_, ...), custom_call_target="tpu_custom_call" | custom-call | flops 905969664 | bytes 2359296 | tf_op jit(solution)/shard_map/pallas_call | solution.py:153
  101.7 3.6 %shard_map.105 = (bf16[2,2,3,64,128]{4,3,2,1,0:T(8,128)(2,1)S(1)}, bf16[2,2,3,64,128]{4,3,2,1,0:T(8,128)(2,1)S(1)}) custom-call(bf16[2,4,6,64,128]{4,3,2,1,0:T(8,128)(2,1)S(1)} %pad_maximum_fusion.refs_0_.refs_2_, bf16[2,2,6,64,128]{4,3,2,1,0:T(8,128)(2,1)S(1)} %collective-permute-done.refs_3_.refs_1_, ...), custom_call_target="tpu_custom_call" | custom-call | flops 905969664 | bytes 2359296 | tf_op jit(solution)/shard_map/pallas_call | solution.py:153
  105.4 1.3 %collective-permute-start.18 = (bf16[2,2,3,64,128]{4,3,2,1,0:T(8,128)(2,1)S(1)}, bf16[2,2,3,64,128]{4,3,2,1,0:T(8,128)(2,1)S(1)}, u32[]{:S(2)}, u32[]{:S(2)}) collective-permute-start(bf16[2,2,3,64,128]{4,3,2,1,0:T(8,128)(2,1)S(1)} %get-tuple-element.23), channel_id=1, source_target_pairs={{0,1},{1,0},{2,3},{3,2},{4,5},{5,4},{6,7},{7,6},{8,9},{9,8},{10,11... | collective-permute-start | bytes 589832 | tf_op jit(solution)/shard_map/ppermute | solution.py:177
  108.0 2.7 %collective-permute-done.18 = bf16[2,2,3,64,128]{4,3,2,1,0:T(8,128)(2,1)S(1)} collective-permute-done((bf16[2,2,3,64,128]{4,3,2,1,0:T(8,128)(2,1)S(1)}, bf16[2,2,3,64,128]{4,3,2,1,0:T(8,128)(2,1)S(1)}, u32[]{:S(2)}, u32[]{:S(2)}) %collective-permute-start.18) | collective-permute-done | bytes 196640 | tf_op jit(solution)/shard_map/ppermute | solution.py:177
  (118 shorter events, 17.7 us)
Async XLA Ops:
  2.3 6.2 %copy-start.8 = (bf16[2,6,8,8,128]{4,3,2,1,0:T(8,128)(2,1)}, bf16[2,6,8,8,128]{4,3,2,1,0:T(8,128)(2,1)S(1)}, u32[]{:S(2)}) copy-start(bf16[2,6,8,8,128]{4,3,2,1,0:T(8,128)(2,1)S(1)} %copy.85) | copy-start | bytes 589828
  2.9 7.8 %copy-start.17 = (s32[8,4,2,27]{3,2,1,0:T(2,128)S(1)}, s32[8,4,2,27]{3,2,1,0:T(2,128)}, u32[]{:S(2)}) copy-start(s32[8,4,2,27]{3,2,1,0:T(2,128)} %param.11) | copy-start | bytes 20740
  3.0 9.3 %copy-start.18 = (bf16[4,3,9,2,9,1]{4,2,1,0,5,3:T(8,128)(2,1)S(1)}, bf16[4,3,9,2,9,1]{4,2,1,0,5,3:T(8,128)(2,1)}, u32[]{:S(2)}) copy-start(bf16[4,3,9,2,9,1]{4,2,1,0,5,3:T(8,128)(2,1)} %constant.215) | copy-start | bytes 11668
  3.0 22.5 %collective-permute-start.2 = (bf16[2,4,6,64,128]{4,3,2,1,0:T(8,128)(2,1)S(1)}, bf16[2,4,6,64,128]{4,3,2,1,0:T(8,128)(2,1)S(1)}, u32[]{:S(2)}, u32[]{:S(2)}) collective-permute-start(bf16[2,4,6,64,128]{4,3,2,1,0:T(8,128)(2,1)S(1)} %pad_maximum_fusion.refs_0_.refs_2_), channel_id=1, source_target_pairs={{0,2},{2,4},{4,6},{1,3},{3,5},{5,7},{8,10},{10,12},{12,14},{9,11},... | collective-permute-start | bytes 2359304 | tf_op jit(solution)/shard_map/ppermute | solution.py:172
  6.3 20.9 %collective-permute-start.4 = (bf16[2,4,6,64,128]{4,3,2,1,0:T(8,128)(2,1)S(1)}, bf16[2,4,6,64,128]{4,3,2,1,0:T(8,128)(2,1)S(1)}, u32[]{:S(2)}, u32[]{:S(2)}) collective-permute-start(bf16[2,4,6,64,128]{4,3,2,1,0:T(8,128)(2,1)S(1)} %pad_maximum_fusion.refs_0_.refs_2_), channel_id=1, source_target_pairs={{2,0},{4,2},{6,4},{3,1},{5,3},{7,5},{10,8},{12,10},{14,12},{11,9},... | collective-permute-start | bytes 2359304 | tf_op jit(solution)/shard_map/ppermute | solution.py:172
  9.3 9.6 %collective-permute-start = (bf16[2,2,6,64,128]{4,3,2,1,0:T(8,128)(2,1)}, bf16[2,2,6,64,128]{4,3,2,1,0:T(8,128)(2,1)S(1)}, u32[]{:S(2)}, u32[]{:S(2)}) collective-permute-start(bf16[2,2,6,64,128]{4,3,2,1,0:T(8,128)(2,1)} %pad_maximum_fusion.2), channel_id=1, source_target_pairs={{0,1},{1,0},{2,3},{3,2},{4,5},{5,4},{6,7},{7,6},{8,9},{9,8},{10,11... | collective-permute-start | bytes 1179656 | tf_op jit(solution)/shard_map/ppermute | solution.py:177
  13.1 13.2 %copy-start.9 = (bf16[2,6,8,8,128]{4,3,2,1,0:T(8,128)(2,1)S(1)}, bf16[2,6,8,8,128]{4,3,2,1,0:T(8,128)(2,1)}, u32[]{:S(2)}) copy-start(bf16[2,6,8,8,128]{4,3,2,1,0:T(8,128)(2,1)} %copy-done.8) | copy-start | bytes 589828
  13.1 13.2 %copy-start.11 = (bf16[2,6,8,8,128]{4,3,2,1,0:T(8,128)(2,1)S(1)}, bf16[2,6,8,8,128]{4,3,2,1,0:T(8,128)(2,1)}, u32[]{:S(2)}) copy-start(bf16[2,6,8,8,128]{4,3,2,1,0:T(8,128)(2,1)} %copy-done.10) | copy-start | bytes 589828
  13.8 13.3 %copy-start.5 = (bf16[2,6,8,8,128]{4,3,2,1,0:T(8,128)(2,1)S(1)}, bf16[2,6,8,8,128]{4,3,2,1,0:T(8,128)(2,1)}, u32[]{:S(2)}) copy-start(bf16[2,6,8,8,128]{4,3,2,1,0:T(8,128)(2,1)} %copy-done.4) | copy-start | bytes 589828
  13.8 13.3 %copy-start.7 = (bf16[2,6,8,8,128]{4,3,2,1,0:T(8,128)(2,1)S(1)}, bf16[2,6,8,8,128]{4,3,2,1,0:T(8,128)(2,1)}, u32[]{:S(2)}) copy-start(bf16[2,6,8,8,128]{4,3,2,1,0:T(8,128)(2,1)} %copy-done.6) | copy-start | bytes 589828
  18.9 12.4 %collective-permute-start.3 = (bf16[2,2,6,64,128]{4,3,2,1,0:T(8,128)(2,1)S(1)}, bf16[2,2,6,64,128]{4,3,2,1,0:T(8,128)(2,1)S(1)}, u32[]{:S(2)}, u32[]{:S(2)}) collective-permute-start(bf16[2,2,6,64,128]{4,3,2,1,0:T(8,128)(2,1)S(1)} %collective-permute-done.refs_3_.refs_1_), channel_id=1, source_target_pairs={{0,2},{2,4},{4,6},{1,3},{3,5},{5,7},{8,10},{10,12},{12,14},{9,11},... | collective-permute-start | bytes 1179656 | tf_op jit(solution)/shard_map/ppermute | solution.py:172
  22.1 12.2 %collective-permute-start.5 = (bf16[2,2,6,64,128]{4,3,2,1,0:T(8,128)(2,1)S(1)}, bf16[2,2,6,64,128]{4,3,2,1,0:T(8,128)(2,1)S(1)}, u32[]{:S(2)}, u32[]{:S(2)}) collective-permute-start(bf16[2,2,6,64,128]{4,3,2,1,0:T(8,128)(2,1)S(1)} %collective-permute-done.refs_3_.refs_1_), channel_id=1, source_target_pairs={{2,0},{4,2},{6,4},{3,1},{5,3},{7,5},{10,8},{12,10},{14,12},{11,9},... | collective-permute-start | bytes 1179656 | tf_op jit(solution)/shard_map/ppermute | solution.py:172
  24.2 19.7 %collective-permute-start.1 = (bf16[2,2,6,64,128]{4,3,2,1,0:T(8,128)(2,1)}, bf16[2,2,6,64,128]{4,3,2,1,0:T(8,128)(2,1)S(1)}, u32[]{:S(2)}, u32[]{:S(2)}) collective-permute-start(bf16[2,2,6,64,128]{4,3,2,1,0:T(8,128)(2,1)} %pad_maximum_fusion.1), channel_id=1, source_target_pairs={{0,1},{1,0},{2,3},{3,2},{4,5},{5,4},{6,7},{7,6},{8,9},{9,8},{10,11... | collective-permute-start | bytes 1179656 | tf_op jit(solution)/shard_map/ppermute | solution.py:177
  28.0 7.1 %copy-start.15 = (bf16[6,2,6,64,128]{4,3,2,1,0:T(8,128)(2,1)}, bf16[6,2,6,64,128]{4,3,2,1,0:T(8,128)(2,1)S(1)}, u32[]{:S(2)}) copy-start(bf16[6,2,6,64,128]{4,3,2,1,0:T(8,128)(2,1)S(1)} %get-tuple-element.26) | copy-start | bytes 3538948
  28.0 7.1 %copy-start.16 = (bf16[6,2,6,64,128]{4,3,2,1,0:T(8,128)(2,1)}, bf16[6,2,6,64,128]{4,3,2,1,0:T(8,128)(2,1)S(1)}, u32[]{:S(2)}) copy-start(bf16[6,2,6,64,128]{4,3,2,1,0:T(8,128)(2,1)S(1)} %get-tuple-element.27) | copy-start | bytes 3538948
  31.3 11.8 %copy-start.14 = (bf16[18,1152]{1,0:T(8,128)(2,1)S(1)}, bf16[18,1152]{1,0:T(8,128)(2,1)}, u32[]{:S(2)}) copy-start(bf16[18,1152]{1,0:T(8,128)(2,1)} %constant.108.clone) | copy-start | bytes 124420
  35.9 34.5 %collective-permute-start.6 = (bf16[6,2,6,64,128]{4,3,2,1,0:T(8,128)(2,1)}, bf16[6,2,6,64,128]{4,3,2,1,0:T(8,128)(2,1)}, u32[]{:S(2)}, u32[]{:S(2)}) collective-permute-start(bf16[6,2,6,64,128]{4,3,2,1,0:T(8,128)(2,1)} %get-tuple-element.45), channel_id=1, source_target_pairs={{0,8},{8,16},{16,24},{1,9},{9,17},{17,25},{2,10},{10,18},{18,26},{... | collective-permute-start | bytes 3538952 | tf_op jit(solution)/shard_map/ppermute | solution.py:172
  41.2 29.2 %collective-permute-start.7 = (bf16[6,2,6,64,128]{4,3,2,1,0:T(8,128)(2,1)}, bf16[6,2,6,64,128]{4,3,2,1,0:T(8,128)(2,1)}, u32[]{:S(2)}, u32[]{:S(2)}) collective-permute-start(bf16[6,2,6,64,128]{4,3,2,1,0:T(8,128)(2,1)} %get-tuple-element.44), channel_id=1, source_target_pairs={{8,0},{16,8},{24,16},{9,1},{17,9},{25,17},{10,2},{18,10},{26,18},{... | collective-permute-start | bytes 3538952 | tf_op jit(solution)/shard_map/ppermute | solution.py:172
  43.9 12.1 %collective-permute-start.9 = (bf16[2,2,6,64,128]{4,3,2,1,0:T(8,128)(2,1)S(1)}, bf16[2,2,6,64,128]{4,3,2,1,0:T(8,128)(2,1)}, u32[]{:S(2)}, u32[]{:S(2)}) collective-permute-start(bf16[2,2,6,64,128]{4,3,2,1,0:T(8,128)(2,1)S(1)} %collective-permute-done.1.refs_1_.refs_3_), channel_id=1, source_target_pairs={{0,2},{2,4},{4,6},{1,3},{3,5},{5,7},{8,10},{10,12},{12,14},{9,11},... | collective-permute-start | bytes 1179656 | tf_op jit(solution)/shard_map/ppermute | solution.py:172
  51.3 12.1 %collective-permute-start.10 = (bf16[2,2,6,64,128]{4,3,2,1,0:T(8,128)(2,1)S(1)}, bf16[2,2,6,64,128]{4,3,2,1,0:T(8,128)(2,1)S(1)}, u32[]{:S(2)}, u32[]{:S(2)}) collective-permute-start(bf16[2,2,6,64,128]{4,3,2,1,0:T(8,128)(2,1)S(1)} %collective-permute-done.1.refs_1_.refs_3_), channel_id=1, source_target_pairs={{2,0},{4,2},{6,4},{3,1},{5,3},{7,5},{10,8},{12,10},{14,12},{11,9},... | collective-permute-start | bytes 1179656 | tf_op jit(solution)/shard_map/ppermute | solution.py:172
  56.0 14.3 %copy-start.1 = (bf16[2,2,6,64,128]{4,3,2,1,0:T(8,128)(2,1)S(1)}, bf16[2,2,6,64,128]{4,3,2,1,0:T(8,128)(2,1)}, u32[]{:S(2)}) copy-start(bf16[2,2,6,64,128]{4,3,2,1,0:T(8,128)(2,1)} %copy-done) | copy-start | bytes 1179652
  56.0 14.3 %copy-start.3 = (f32[2,2,1152]{2,1,0:T(2,128)S(1)}, f32[2,2,1152]{2,1,0:T(2,128)}, u32[]{:S(2)}) copy-start(f32[2,2,1152]{2,1,0:T(2,128)} %squeeze.22.refs_10_.refs_12_) | copy-start | bytes 55300
  64.2 33.6 %collective-permute-start.11 = (bf16[6,2,6,64,128]{4,3,2,1,0:T(8,128)(2,1)}, bf16[6,2,6,64,128]{4,3,2,1,0:T(8,128)(2,1)S(1)}, u32[]{:S(2)}, u32[]{:S(2)}) collective-permute-start(bf16[6,2,6,64,128]{4,3,2,1,0:T(8,128)(2,1)} %get-tuple-element.37), channel_id=1, source_target_pairs={{0,8},{8,16},{16,24},{1,9},{9,17},{17,25},{2,10},{10,18},{18,26},{... | collective-permute-start | bytes 3538952 | tf_op jit(solution)/shard_map/ppermute | solution.py:172
  68.4 29.3 %collective-permute-start.12 = (bf16[6,2,6,64,128]{4,3,2,1,0:T(8,128)(2,1)}, bf16[6,2,6,64,128]{4,3,2,1,0:T(8,128)(2,1)S(1)}, u32[]{:S(2)}, u32[]{:S(2)}) collective-permute-start(bf16[6,2,6,64,128]{4,3,2,1,0:T(8,128)(2,1)} %get-tuple-element.36), channel_id=1, source_target_pairs={{8,0},{16,8},{24,16},{9,1},{17,9},{25,17},{10,2},{18,10},{26,18},{... | collective-permute-start | bytes 3538952 | tf_op jit(solution)/shard_map/ppermute | solution.py:172
  77.2 13.1 %collective-permute-start.13 = (f32[2,6,2,128]{3,2,1,0:T(2,128)S(1)}, f32[2,6,2,128]{3,2,1,0:T(2,128)S(1)}, u32[]{:S(2)}, u32[]{:S(2)}) collective-permute-start(f32[2,6,2,128]{3,2,1,0:T(2,128)S(1)} %get-tuple-element.17.refs_11_.refs_10_), channel_id=1, source_target_pairs={{0,2},{2,4},{4,6},{1,3},{3,5},{5,7},{8,10},{10,12},{12,14},{9,11},... | collective-permute-start | bytes 36872 | tf_op jit(solution)/shard_map/ppermute | solution.py:172
  79.2 11.2 %collective-permute-start.14 = (f32[2,6,2,128]{3,2,1,0:T(2,128)S(1)}, f32[2,6,2,128]{3,2,1,0:T(2,128)S(1)}, u32[]{:S(2)}, u32[]{:S(2)}) collective-permute-start(f32[2,6,2,128]{3,2,1,0:T(2,128)S(1)} %get-tuple-element.17.refs_11_.refs_10_), channel_id=1, source_target_pairs={{2,0},{4,2},{6,4},{3,1},{5,3},{7,5},{10,8},{12,10},{14,12},{11,9},... | collective-permute-start | bytes 36872 | tf_op jit(solution)/shard_map/ppermute | solution.py:172
  89.1 8.7 %copy-start.2 = (f32[2,2,1152]{2,1,0:T(2,128)S(1)}, f32[2,2,1152]{2,1,0:T(2,128)}, u32[]{:S(2)}) copy-start(f32[2,2,1152]{2,1,0:T(2,128)} %squeeze.25.refs_15_) | copy-start | bytes 55300
  89.1 17.6 %collective-permute-start.8 = (bf16[2,2,6,64,128]{4,3,2,1,0:T(8,128)(2,1)S(1)}, bf16[2,2,6,64,128]{4,3,2,1,0:T(8,128)(2,1)S(1)}, u32[]{:S(2)}, u32[]{:S(2)}) collective-permute-start(bf16[2,2,6,64,128]{4,3,2,1,0:T(8,128)(2,1)S(1)} %get-tuple-element.19), channel_id=1, source_target_pairs={{0,1},{1,0},{2,3},{3,2},{4,5},{5,4},{6,7},{7,6},{8,9},{9,8},{10,11... | collective-permute-start | bytes 1179656 | tf_op jit(solution)/shard_map/ppermute | solution.py:177
  90.4 6.7 %collective-permute-start.16 = (f32[3,6,2,128]{3,2,1,0:T(2,128)S(1)}, f32[3,6,2,128]{3,2,1,0:T(2,128)S(1)}, u32[]{:S(2)}, u32[]{:S(2)}) collective-permute-start(f32[3,6,2,128]{3,2,1,0:T(2,128)S(1)} %pad_maximum_fusion.6), channel_id=1, source_target_pairs={{8,0},{16,8},{24,16},{9,1},{17,9},{25,17},{10,2},{18,10},{26,18},{... | collective-permute-start | bytes 55304 | tf_op jit(solution)/shard_map/ppermute | solution.py:172
  92.4 5.4 %collective-permute-start.15 = (f32[3,6,2,128]{3,2,1,0:T(2,128)S(1)}, f32[3,6,2,128]{3,2,1,0:T(2,128)S(1)}, u32[]{:S(2)}, u32[]{:S(2)}) collective-permute-start(f32[3,6,2,128]{3,2,1,0:T(2,128)S(1)} %pad_maximum_fusion.5), channel_id=1, source_target_pairs={{0,8},{8,16},{16,24},{1,9},{9,17},{17,25},{2,10},{10,18},{18,26},{... | collective-permute-start | bytes 55304 | tf_op jit(solution)/shard_map/ppermute | solution.py:172
  101.4 6.5 %collective-permute-start.17 = (bf16[2,2,3,64,128]{4,3,2,1,0:T(8,128)(2,1)S(1)}, bf16[2,2,3,64,128]{4,3,2,1,0:T(8,128)(2,1)S(1)}, u32[]{:S(2)}, u32[]{:S(2)}) collective-permute-start(bf16[2,2,3,64,128]{4,3,2,1,0:T(8,128)(2,1)S(1)} %get-tuple-element.21), channel_id=1, source_target_pairs={{0,1},{1,0},{2,3},{3,2},{4,5},{5,4},{6,7},{7,6},{8,9},{9,8},{10,11... | collective-permute-start | bytes 589832 | tf_op jit(solution)/shard_map/ppermute | solution.py:177
  105.4 5.3 %collective-permute-start.18 = (bf16[2,2,3,64,128]{4,3,2,1,0:T(8,128)(2,1)S(1)}, bf16[2,2,3,64,128]{4,3,2,1,0:T(8,128)(2,1)S(1)}, u32[]{:S(2)}, u32[]{:S(2)}) collective-permute-start(bf16[2,2,3,64,128]{4,3,2,1,0:T(8,128)(2,1)S(1)} %get-tuple-element.23), channel_id=1, source_target_pairs={{0,1},{1,0},{2,3},{3,2},{4,5},{5,4},{6,7},{7,6},{8,9},{9,8},{10,11... | collective-permute-start | bytes 589832 | tf_op jit(solution)/shard_map/ppermute | solution.py:177
  (6 other events, 11.3 us)

commit v10 on v8

--- a/solution.py
+++ b/solution.py
@@ -166,7 +166,7 @@
         scratch_shapes=[pltpu.VMEM((3 * (frames + 2) * tokens, dim), jnp.bfloat16)] * 2,
         compiler_params=pltpu.CompilerParams(vmem_limit_bytes=16 * 2**20),
         cost_estimate=pl.CostEstimate(
-            flops=frames * count * 2 * products * tokens * 9 * tokens * dim,
+            flops=7 * frames * count * 2 * products * tokens * 9 * tokens * dim,
             bytes_accessed=count * (frames + 2) * 3 * 2 * tokens * dim * 2,
             transcendentals=frames * count * tokens * 9 * tokens,
         ),
@@ -257,13 +257,13 @@
         return whole[0], whole[1]
 
     front_bias, back_bias = tile_biases(active, frames, columns_here, cells)
-    key_here = pair_of(keys, values, 0)
+    key_here, front_bias = lax.optimization_barrier((pair_of(keys, values, 0), front_bias))
     key_near = row_sides(key_here)
     key_sent = [pair_of(keys, values, shift) for shift in range(1, size)]
     key_moved = [turn(key_sent[size - b - 1], size - b) for b in range(1, size)]
     query_held = [pair_of(queries, out_grad, shift) for shift in range(size)]
-    query_held, key_moved = lax.optimization_barrier((query_held, key_moved))
     key_far = [row_sides(part) for part in key_moved]
+    query_held, key_moved, key_near = lax.optimization_barrier((query_held, key_moved, key_near))
     query_moved = [turn(query_held[size - b], size - b) for b in range(1, size)]
     query_all = jnp.stack(query_held[:1] + query_moved, 1)
     query_all, key_near = lax.optimization_barrier((query_all, key_near))

time: 100 us -> 102 us (1.020)
  waiting for transfers between devices: 22.8 us -> 26.3 us
    ppermute x14, waiting for transfers between devices: 7.61 us -> 15.8 us  [step_along(): lax.ppermute(tensor, axis, [(i, i + sign) for i in range(size) if 0 <= i...]
    ppermute x5, waiting for transfers between devices: 15.2 us -> 10.5 us  [turn(): lax.ppermute(tensor, 'head', [(i, (i + shift) % size) for i in range(size)])]
    another operation x3 -> x2, local copies, waits for them, and re-layouts: 1.61 us -> 0.22 us  [the longest x1 1.38 us: pair_of(): return jnp.stack(picked, 1).reshape(frames, 2, groups, cells, dim)]
    dynamic_slice x9 -> x10, local copies, waits for them, and re-layouts: 0.36 us -> 1.65 us  [pair_of(): lax.dynamic_slice_in_dim(jnp.transpose(t, (0, 3, 1, 2, 4)), start, groups...]
  transfers between devices with their start and end apart: 19 -> 19, of which waited for: 8 -> 10; matrix products, arithmetic and copies ran while one was open for 6% -> 5% of each run, Pallas kernels for 14% -> 13%
where the time goes in v10:
time: 102 us
  starting transfers between devices  49.7 us (49%)
  waiting for transfers between devices  26.3 us (26%)
  Pallas kernels  16.6 us (16%)
  local copies, waits for them, and re-layouts  6.17 us (6%)
  between operations  1.3 us (1%)
    ppermute x14, starting transfers between devices, step_along(): lax.ppermute(tensor, axis, [(i, i + sign) for i in range(size) if 0 <= i...  45.2 us
    pallas_call x4, Pallas kernels, run(): pl.pallas_call(functools.partial(kernel, scaling, parts), grid=(count,),...  16.6 us
    ppermute x14, waiting for transfers between devices, step_along(): lax.ppermute(tensor, axis, [(i, i + sign) for i in range(size) if 0 <= i...  15.8 us
    ppermute x5, waiting for transfers between devices, turn(): lax.ppermute(tensor, 'head', [(i, (i + shift) % size) for i in range(size)])  10.5 us
    ppermute x5, starting transfers between devices, turn(): lax.ppermute(tensor, 'head', [(i, (i + shift) % size) for i in range(size)])  4.4 us
  transfers between devices with their start and end apart: 19, of which 10 were waited for; matrix products, arithmetic and copies ran while one was open for 5% of the time, Pallas kernels for 13%

profile of v10, /device:TPU:9, one launch (start us, length us, event | category | flops | bytes accessed | tf_op | source)
XLA Modules:
  0.0 101.5 jit_solution(11601623815472551572)
XLA Ops:
  0.7 1.3 %dynamic-slice_bitcast_fusion = (bf16[2,6,8,8,128]{4,3,1,2,0:T(8,128)(2,1)S(1)}, bf16[2,6,8,8,128]{4,3,1,2,0:T(8,128)(2,1)S(1)}, bf16[2,6,8,8,128]{4,3,1,2,0:T(8,128)(2,1)S(1)}, bf16[2,6,8,8,128]{4,3,1,2,0:T(8,128)(2,1)S(1)}) fusion(bf16[2,8,8,12,128]{4,2,3,1,0:T(8,128)(2,1)} %param.9, s32[]{:T(128)S(6)} %select_n.91, s32[]{:T(128)S(6)} %select_n.93, ...), kind=kLoop, calls=%fused_computation.64 | loop fusion | bytes 1572872 | tf_op jit(solution)/shard_map/dynamic_slice | solution.py:244
  2.1 1.3 %collective-permute-start = (bf16[2,2,6,64,128]{4,3,2,1,0:T(8,128)(2,1)S(1)}, bf16[2,2,6,64,128]{4,3,2,1,0:T(8,128)(2,1)S(1)}, u32[]{:S(2)}, u32[]{:S(2)}) collective-permute-start(bf16[2,2,6,64,128]{4,3,2,1,0:T(8,128)(2,1)S(1)} %pad_maximum_fusion.3), channel_id=1, source_target_pairs={{0,1},{1,0},{2,3},{3,2},{4,5},{5,4},{6,7},{7,6},{8,9},{9,8},{10,11... | collective-permute-start | bytes 1179656 | tf_op jit(solution)/shard_map/ppermute | solution.py:183
  6.2 3.2 %collective-permute-start.1 = (bf16[2,2,6,64,128]{4,3,2,1,0:T(8,128)(2,1)S(1)}, bf16[2,2,6,64,128]{4,3,2,1,0:T(8,128)(2,1)S(1)}, u32[]{:S(2)}, u32[]{:S(2)}) collective-permute-start(bf16[2,2,6,64,128]{4,3,2,1,0:T(8,128)(2,1)S(1)} %pad_maximum_fusion.4.refs_1_.refs_0_), channel_id=1, source_target_pairs={{0,2},{2,4},{4,6},{1,3},{3,5},{5,7},{8,10},{10,12},{12,14},{9,11},... | collective-permute-start | bytes 1179656 | tf_op jit(solution)/shard_map/ppermute | solution.py:178
  9.5 2.1 %collective-permute-start.2 = (bf16[2,2,6,64,128]{4,3,2,1,0:T(8,128)(2,1)S(1)}, bf16[2,2,6,64,128]{4,3,2,1,0:T(8,128)(2,1)S(1)}, u32[]{:S(2)}, u32[]{:S(2)}) collective-permute-start(bf16[2,2,6,64,128]{4,3,2,1,0:T(8,128)(2,1)S(1)} %pad_maximum_fusion.4.refs_1_.refs_0_), channel_id=1, source_target_pairs={{2,0},{4,2},{6,4},{3,1},{5,3},{7,5},{10,8},{12,10},{14,12},{11,9},... | collective-permute-start | bytes 1179656 | tf_op jit(solution)/shard_map/ppermute | solution.py:178
  12.2 5.6 %collective-permute-done.1.refs_3_ = bf16[2,2,6,64,128]{4,3,2,1,0:T(8,128)(2,1)S(1)} collective-permute-done((bf16[2,2,6,64,128]{4,3,2,1,0:T(8,128)(2,1)S(1)}, bf16[2,2,6,64,128]{4,3,2,1,0:T(8,128)(2,1)S(1)}, u32[]{:S(2)}, u32[]{:S(2)}) %collective-permute-start.1) | collective-permute-done | bytes 393248 | tf_op jit(solution)/shard_map/ppermute | solution.py:178
  17.8 2.9 %collective-permute-done.2.refs_5_ = bf16[2,2,6,64,128]{4,3,2,1,0:T(8,128)(2,1)S(1)} collective-permute-done((bf16[2,2,6,64,128]{4,3,2,1,0:T(8,128)(2,1)S(1)}, bf16[2,2,6,64,128]{4,3,2,1,0:T(8,128)(2,1)S(1)}, u32[]{:S(2)}, u32[]{:S(2)}) %collective-permute-start.2) | collective-permute-done | bytes 393248 | tf_op jit(solution)/shard_map/ppermute | solution.py:178
  21.0 3.2 %collective-permute-start.4 = (bf16[2,2,6,64,128]{4,3,2,1,0:T(8,128)(2,1)S(1)}, bf16[2,2,6,64,128]{4,3,2,1,0:T(8,128)(2,1)S(1)}, u32[]{:S(2)}, u32[]{:S(2)}) collective-permute-start(bf16[2,2,6,64,128]{4,3,2,1,0:T(8,128)(2,1)S(1)} %collective-permute-done.refs_2_.refs_1_), channel_id=1, source_target_pairs={{0,2},{2,4},{4,6},{1,3},{3,5},{5,7},{8,10},{10,12},{12,14},{9,11},... | collective-permute-start | bytes 1179656 | tf_op jit(solution)/shard_map/ppermute | solution.py:178
  24.2 2.1 %collective-permute-start.5 = (bf16[2,2,6,64,128]{4,3,2,1,0:T(8,128)(2,1)S(1)}, bf16[2,2,6,64,128]{4,3,2,1,0:T(8,128)(2,1)S(1)}, u32[]{:S(2)}, u32[]{:S(2)}) collective-permute-start(bf16[2,2,6,64,128]{4,3,2,1,0:T(8,128)(2,1)S(1)} %collective-permute-done.refs_2_.refs_1_), channel_id=1, source_target_pairs={{2,0},{4,2},{6,4},{3,1},{5,3},{7,5},{10,8},{12,10},{14,12},{11,9},... | collective-permute-start | bytes 1179656 | tf_op jit(solution)/shard_map/ppermute | solution.py:178
  26.3 2.8 %collective-permute-done.3 = bf16[2,2,6,64,128]{4,3,2,1,0:T(8,128)(2,1)S(1)} collective-permute-done((bf16[2,2,6,64,128]{4,3,2,1,0:T(8,128)(2,1)S(1)}, bf16[2,2,6,64,128]{4,3,2,1,0:T(8,128)(2,1)S(1)}, u32[]{:S(2)}, u32[]{:S(2)}) %collective-permute-start.3) | collective-permute-done | bytes 393248 | tf_op jit(solution)/shard_map/ppermute | solution.py:183
  29.2 3.2 %collective-permute-start.9 = (bf16[2,2,2,6,64,128]{5,4,3,2,1,0:T(8,128)(2,1)S(1)}, bf16[2,2,2,6,64,128]{5,4,3,2,1,0:T(8,128)(2,1)S(1)}, u32[]{:S(2)}, u32[]{:S(2)}) collective-permute-start(bf16[2,2,2,6,64,128]{5,4,3,2,1,0:T(8,128)(2,1)S(1)} %pad_maximum_fusion.refs_0_.refs_2_), channel_id=1, source_target_pairs={{0,2},{2,4},{4,6},{1,3},{3,5},{5,7},{8,10},{10,12},{12,14},{9,11},... | collective-permute-start | bytes 2359304 | tf_op jit(solution)/shard_map/ppermute | solution.py:178
  32.5 2.1 %collective-permute-start.10 = (bf16[2,2,2,6,64,128]{5,4,3,2,1,0:T(8,128)(2,1)S(1)}, bf16[2,2,2,6,64,128]{5,4,3,2,1,0:T(8,128)(2,1)S(1)}, u32[]{:S(2)}, u32[]{:S(2)}) collective-permute-start(bf16[2,2,2,6,64,128]{5,4,3,2,1,0:T(8,128)(2,1)S(1)} %pad_maximum_fusion.refs_0_.refs_2_), channel_id=1, source_target_pairs={{2,0},{4,2},{6,4},{3,1},{5,3},{7,5},{10,8},{12,10},{14,12},{11,9},... | collective-permute-start | bytes 2359304 | tf_op jit(solution)/shard_map/ppermute | solution.py:178
  35.0 6.7 %collective-permute-start.6 = (bf16[6,2,6,64,128]{4,3,2,1,0:T(8,128)(2,1)S(1)}, bf16[6,2,6,64,128]{4,3,2,1,0:T(8,128)(2,1)S(1)}, u32[]{:S(2)}, u32[]{:S(2)}) collective-permute-start(bf16[6,2,6,64,128]{4,3,2,1,0:T(8,128)(2,1)S(1)} %get-tuple-element.57), channel_id=1, source_target_pairs={{0,8},{8,16},{16,24},{1,9},{9,17},{17,25},{2,10},{10,18},{18,26},{... | collective-permute-start | bytes 3538952 | tf_op jit(solution)/shard_map/ppermute | solution.py:178
  41.6 1.9 %collective-permute-start.7 = (bf16[6,2,6,64,128]{4,3,2,1,0:T(8,128)(2,1)S(1)}, bf16[6,2,6,64,128]{4,3,2,1,0:T(8,128)(2,1)S(1)}, u32[]{:S(2)}, u32[]{:S(2)}) collective-permute-start(bf16[6,2,6,64,128]{4,3,2,1,0:T(8,128)(2,1)S(1)} %get-tuple-element.56), channel_id=1, source_target_pairs={{8,0},{16,8},{24,16},{9,1},{17,9},{25,17},{10,2},{18,10},{26,18},{... | collective-permute-start | bytes 3538952 | tf_op jit(solution)/shard_map/ppermute | solution.py:178
  43.6 3.9 %collective-permute-done.9.refs_3_ = bf16[2,2,2,6,64,128]{5,4,3,2,1,0:T(8,128)(2,1)S(1)} collective-permute-done((bf16[2,2,2,6,64,128]{5,4,3,2,1,0:T(8,128)(2,1)S(1)}, bf16[2,2,2,6,64,128]{5,4,3,2,1,0:T(8,128)(2,1)S(1)}, u32[]{:S(2)}, u32[]{:S(2)}) %collective-permute-start.9) | collective-permute-done | bytes 786464 | tf_op jit(solution)/shard_map/ppermute | solution.py:178
  47.6 2.8 %collective-permute-done.10.refs_4_ = bf16[2,2,2,6,64,128]{5,4,3,2,1,0:T(8,128)(2,1)S(1)} collective-permute-done((bf16[2,2,2,6,64,128]{5,4,3,2,1,0:T(8,128)(2,1)S(1)}, bf16[2,2,2,6,64,128]{5,4,3,2,1,0:T(8,128)(2,1)S(1)}, u32[]{:S(2)}, u32[]{:S(2)}) %collective-permute-start.10) | collective-permute-done | bytes 786464 | tf_op jit(solution)/shard_map/ppermute | solution.py:178
  50.7 7.1 %collective-permute-start.11 = (bf16[6,2,6,64,128]{4,3,2,1,0:T(8,128)(2,1)S(1)}, bf16[6,2,6,64,128]{4,3,2,1,0:T(8,128)(2,1)S(1)}, u32[]{:S(2)}, u32[]{:S(2)}) collective-permute-start(bf16[6,2,6,64,128]{4,3,2,1,0:T(8,128)(2,1)S(1)} %get-tuple-element.43), channel_id=1, source_target_pairs={{0,8},{8,16},{16,24},{1,9},{9,17},{17,25},{2,10},{10,18},{18,26},{... | collective-permute-start | bytes 3538952 | tf_op jit(solution)/shard_map/ppermute | solution.py:178
  57.8 1.9 %collective-permute-start.12 = (bf16[6,2,6,64,128]{4,3,2,1,0:T(8,128)(2,1)S(1)}, bf16[6,2,6,64,128]{4,3,2,1,0:T(8,128)(2,1)S(1)}, u32[]{:S(2)}, u32[]{:S(2)}) collective-permute-start(bf16[6,2,6,64,128]{4,3,2,1,0:T(8,128)(2,1)S(1)} %get-tuple-element.42), channel_id=1, source_target_pairs={{8,0},{16,8},{24,16},{9,1},{17,9},{25,17},{10,2},{18,10},{26,18},{... | collective-permute-start | bytes 3538952 | tf_op jit(solution)/shard_map/ppermute | solution.py:178
  59.7 5.7 %shard_map.102 = (bf16[2,6,128,128]{3,2,1,0:T(8,128)(2,1)S(1)}, f32[2,6,2,128]{3,2,1,0:T(2,128)S(1)}) custom-call(bf16[2,2,2,6,64,128]{5,4,3,2,1,0:T(8,128)(2,1)S(1)} %pad_maximum_fusion.refs_0_.refs_2_, bf16[2,2,6,64,128]{4,3,2,1,0:T(8,128)(2,1)S(1)} %pad_maximum_fusion.4.refs_1_.refs_0_, ...), custom_call_target="tpu_custom_call" | custom-call | flops 6341787648 | bytes 4718592 | tf_op jit(solution)/shard_map/pallas_call | solution.py:159
  65.5 2.6 %collective-permute-start.13 = (f32[2,6,2,128]{3,2,1,0:T(2,128)S(1)}, f32[2,6,2,128]{3,2,1,0:T(2,128)S(1)}, u32[]{:S(2)}, u32[]{:S(2)}) collective-permute-start(f32[2,6,2,128]{3,2,1,0:T(2,128)S(1)} %get-tuple-element.33.refs_10_.refs_7_), channel_id=1, source_target_pairs={{0,2},{2,4},{4,6},{1,3},{3,5},{5,7},{8,10},{10,12},{12,14},{9,11},... | collective-permute-start | bytes 36872 | tf_op jit(solution)/shard_map/ppermute | solution.py:178
  68.1 2.7 %collective-permute-start.14 = (f32[2,6,2,128]{3,2,1,0:T(2,128)S(1)}, f32[2,6,2,128]{3,2,1,0:T(2,128)S(1)}, u32[]{:S(2)}, u32[]{:S(2)}) collective-permute-start(f32[2,6,2,128]{3,2,1,0:T(2,128)S(1)} %get-tuple-element.33.refs_10_.refs_7_), channel_id=1, source_target_pairs={{2,0},{4,2},{6,4},{3,1},{5,3},{7,5},{10,8},{12,10},{14,12},{11,9},... | collective-permute-start | bytes 36872 | tf_op jit(solution)/shard_map/ppermute | solution.py:178
  70.8 5.0 %shard_map.103 = (bf16[2,2,6,64,128]{4,3,2,1,0:T(8,128)(2,1)S(1)}, bf16[2,2,6,64,128]{4,3,2,1,0:T(8,128)(2,1)S(1)}) custom-call(bf16[2,2,2,6,64,128]{5,4,3,2,1,0:T(8,128)(2,1)S(1)} %pad_maximum_fusion.refs_0_.refs_2_, bf16[2,2,6,64,128]{4,3,2,1,0:T(8,128)(2,1)S(1)} %pad_maximum_fusion.4.refs_1_.refs_0_, ...), custom_call_target="tpu_custom_call" | custom-call | flops 9512681472 | bytes 4718592 | tf_op jit(solution)/shard_map/pallas_call | solution.py:159
  75.8 1.3 %collective-permute-start.8 = (bf16[2,2,6,64,128]{4,3,2,1,0:T(8,128)(2,1)S(1)}, bf16[2,2,6,64,128]{4,3,2,1,0:T(8,128)(2,1)S(1)}, u32[]{:S(2)}, u32[]{:S(2)}) collective-permute-start(bf16[2,2,6,64,128]{4,3,2,1,0:T(8,128)(2,1)S(1)} %get-tuple-element.35), channel_id=1, source_target_pairs={{0,1},{1,0},{2,3},{3,2},{4,5},{5,4},{6,7},{7,6},{8,9},{9,8},{10,11... | collective-permute-start | bytes 1179656 | tf_op jit(solution)/shard_map/ppermute | solution.py:183
  77.4 4.5 %collective-permute-start.15 = (f32[3,6,2,128]{3,2,1,0:T(2,128)S(1)}, f32[3,6,2,128]{3,2,1,0:T(2,128)S(1)}, u32[]{:S(2)}, u32[]{:S(2)}) collective-permute-start(f32[3,6,2,128]{3,2,1,0:T(2,128)S(1)} %pad_maximum_fusion.5), channel_id=1, source_target_pairs={{0,8},{8,16},{16,24},{1,9},{9,17},{17,25},{2,10},{10,18},{18,26},{... | collective-permute-start | bytes 55304 | tf_op jit(solution)/shard_map/ppermute | solution.py:178
  81.9 1.9 %collective-permute-start.16 = (f32[3,6,2,128]{3,2,1,0:T(2,128)S(1)}, f32[3,6,2,128]{3,2,1,0:T(2,128)S(1)}, u32[]{:S(2)}, u32[]{:S(2)}) collective-permute-start(f32[3,6,2,128]{3,2,1,0:T(2,128)S(1)} %pad_maximum_fusion.6), channel_id=1, source_target_pairs={{8,0},{16,8},{24,16},{9,1},{17,9},{25,17},{10,2},{18,10},{26,18},{... | collective-permute-start | bytes 55304 | tf_op jit(solution)/shard_map/ppermute | solution.py:178
  83.8 1.6 %collective-permute-done.8 = bf16[2,2,6,64,128]{4,3,2,1,0:T(8,128)(2,1)S(1)} collective-permute-done((bf16[2,2,6,64,128]{4,3,2,1,0:T(8,128)(2,1)S(1)}, bf16[2,2,6,64,128]{4,3,2,1,0:T(8,128)(2,1)S(1)}, u32[]{:S(2)}, u32[]{:S(2)}) %collective-permute-start.8) | collective-permute-done | bytes 393248 | tf_op jit(solution)/shard_map/ppermute | solution.py:183
  85.5 0.9 slice_bitcast_fusion.2
  87.0 2.9 %shard_map.104 = (bf16[2,2,3,64,128]{4,3,2,1,0:T(8,128)(2,1)S(1)}, bf16[2,2,3,64,128]{4,3,2,1,0:T(8,128)(2,1)S(1)}) custom-call(bf16[2,2,6,64,128]{4,3,2,1,0:T(8,128)(2,1)S(1)} %pad_maximum_fusion.4.refs_1_.refs_0_, bf16[2,2,6,64,128]{4,3,2,1,0:T(8,128)(2,1)S(1)} %collective-permute-done.refs_2_.refs_1_, ...), custom_call_target="tpu_custom_call" | custom-call | flops 6341787648 | bytes 2359296 | tf_op jit(solution)/shard_map/pallas_call | solution.py:159
  89.9 0.8 collective-permute-start.17
  90.7 2.9 %shard_map.105 = (bf16[2,2,3,64,128]{4,3,2,1,0:T(8,128)(2,1)S(1)}, bf16[2,2,3,64,128]{4,3,2,1,0:T(8,128)(2,1)S(1)}) custom-call(bf16[2,2,6,64,128]{4,3,2,1,0:T(8,128)(2,1)S(1)} %pad_maximum_fusion.4.refs_1_.refs_0_, bf16[2,2,6,64,128]{4,3,2,1,0:T(8,128)(2,1)S(1)} %collective-permute-done.refs_2_.refs_1_, ...), custom_call_target="tpu_custom_call" | custom-call | flops 6341787648 | bytes 2359296 | tf_op jit(solution)/shard_map/pallas_call | solution.py:159
  94.6 1.3 %collective-permute-done.17 = bf16[2,2,3,64,128]{4,3,2,1,0:T(8,128)(2,1)S(1)} collective-permute-done((bf16[2,2,3,64,128]{4,3,2,1,0:T(8,128)(2,1)S(1)}, bf16[2,2,3,64,128]{4,3,2,1,0:T(8,128)(2,1)S(1)}, u32[]{:S(2)}, u32[]{:S(2)}) %collective-permute-start.17) | collective-permute-done | bytes 196640 | tf_op jit(solution)/shard_map/ppermute | solution.py:183
  96.1 4.4 %collective-permute-done.18 = bf16[2,2,3,64,128]{4,3,2,1,0:T(8,128)(2,1)S(1)} collective-permute-done((bf16[2,2,3,64,128]{4,3,2,1,0:T(8,128)(2,1)S(1)}, bf16[2,2,3,64,128]{4,3,2,1,0:T(8,128)(2,1)S(1)}, u32[]{:S(2)}, u32[]{:S(2)}) %collective-permute-start.18) | collective-permute-done | bytes 196640 | tf_op jit(solution)/shard_map/ppermute | solution.py:183
  100.6 0.9 slice_bitcast_fusion
  (94 shorter events, 6.3 us)
Async XLA Ops:
  2.0 1.7 %copy-start.3 = (s32[8,4,2,27]{3,2,1,0:T(2,128)S(1)}, s32[8,4,2,27]{3,2,1,0:T(2,128)}, u32[]{:S(2)}) copy-start(s32[8,4,2,27]{3,2,1,0:T(2,128)} %param.11) | copy-start | bytes 20740
  2.0 3.3 %copy-start.4 = (bf16[4,3,9,2,9,1]{4,2,1,0,5,3:T(8,128)(2,1)S(1)}, bf16[4,3,9,2,9,1]{4,2,1,0,5,3:T(8,128)(2,1)}, u32[]{:S(2)}) copy-start(bf16[4,3,9,2,9,1]{4,2,1,0,5,3:T(8,128)(2,1)} %constant.215) | copy-start | bytes 11668
  2.1 3.9 %copy-start.2 = (bf16[18,1152]{1,0:T(8,128)(2,1)S(1)}, bf16[18,1152]{1,0:T(8,128)(2,1)}, u32[]{:S(2)}) copy-start(bf16[18,1152]{1,0:T(8,128)(2,1)} %constant.110.clone) | copy-start | bytes 124420
  2.1 10.0 %collective-permute-start = (bf16[2,2,6,64,128]{4,3,2,1,0:T(8,128)(2,1)S(1)}, bf16[2,2,6,64,128]{4,3,2,1,0:T(8,128)(2,1)S(1)}, u32[]{:S(2)}, u32[]{:S(2)}) collective-permute-start(bf16[2,2,6,64,128]{4,3,2,1,0:T(8,128)(2,1)S(1)} %pad_maximum_fusion.3), channel_id=1, source_target_pairs={{0,1},{1,0},{2,3},{3,2},{4,5},{5,4},{6,7},{7,6},{8,9},{9,8},{10,11... | collective-permute-start | bytes 1179656 | tf_op jit(solution)/shard_map/ppermute | solution.py:183
  3.6 8.0 %copy-start = (bf16[2,8,8,12,128]{4,2,3,1,0:T(8,128)(2,1)S(1)}, bf16[2,8,8,12,128]{4,2,3,1,0:T(8,128)(2,1)}, u32[]{:S(2)}) copy-start(bf16[2,8,8,12,128]{4,2,3,1,0:T(8,128)(2,1)} %param.10) | copy-start | bytes 1179652
  3.6 8.0 %copy-start.1 = (bf16[2,8,8,12,128]{4,2,3,1,0:T(8,128)(2,1)S(1)}, bf16[2,8,8,12,128]{4,2,3,1,0:T(8,128)(2,1)}, u32[]{:S(2)}) copy-start(bf16[2,8,8,12,128]{4,2,3,1,0:T(8,128)(2,1)} %param.7) | copy-start | bytes 1179652
  6.2 11.6 %collective-permute-start.1 = (bf16[2,2,6,64,128]{4,3,2,1,0:T(8,128)(2,1)S(1)}, bf16[2,2,6,64,128]{4,3,2,1,0:T(8,128)(2,1)S(1)}, u32[]{:S(2)}, u32[]{:S(2)}) collective-permute-start(bf16[2,2,6,64,128]{4,3,2,1,0:T(8,128)(2,1)S(1)} %pad_maximum_fusion.4.refs_1_.refs_0_), channel_id=1, source_target_pairs={{0,2},{2,4},{4,6},{1,3},{3,5},{5,7},{8,10},{10,12},{12,14},{9,11},... | collective-permute-start | bytes 1179656 | tf_op jit(solution)/shard_map/ppermute | solution.py:178
  9.5 11.3 %collective-permute-start.2 = (bf16[2,2,6,64,128]{4,3,2,1,0:T(8,128)(2,1)S(1)}, bf16[2,2,6,64,128]{4,3,2,1,0:T(8,128)(2,1)S(1)}, u32[]{:S(2)}, u32[]{:S(2)}) collective-permute-start(bf16[2,2,6,64,128]{4,3,2,1,0:T(8,128)(2,1)S(1)} %pad_maximum_fusion.4.refs_1_.refs_0_), channel_id=1, source_target_pairs={{2,0},{4,2},{6,4},{3,1},{5,3},{7,5},{10,8},{12,10},{14,12},{11,9},... | collective-permute-start | bytes 1179656 | tf_op jit(solution)/shard_map/ppermute | solution.py:178
  20.7 8.4 %collective-permute-start.3 = (bf16[2,2,6,64,128]{4,3,2,1,0:T(8,128)(2,1)S(1)}, bf16[2,2,6,64,128]{4,3,2,1,0:T(8,128)(2,1)S(1)}, u32[]{:S(2)}, u32[]{:S(2)}) collective-permute-start(bf16[2,2,6,64,128]{4,3,2,1,0:T(8,128)(2,1)S(1)} %pad_maximum_fusion.2), channel_id=1, source_target_pairs={{0,1},{1,0},{2,3},{3,2},{4,5},{5,4},{6,7},{7,6},{8,9},{9,8},{10,11... | collective-permute-start | bytes 1179656 | tf_op jit(solution)/shard_map/ppermute | solution.py:183
  21.0 13.7 %collective-permute-start.4 = (bf16[2,2,6,64,128]{4,3,2,1,0:T(8,128)(2,1)S(1)}, bf16[2,2,6,64,128]{4,3,2,1,0:T(8,128)(2,1)S(1)}, u32[]{:S(2)}, u32[]{:S(2)}) collective-permute-start(bf16[2,2,6,64,128]{4,3,2,1,0:T(8,128)(2,1)S(1)} %collective-permute-done.refs_2_.refs_1_), channel_id=1, source_target_pairs={{0,2},{2,4},{4,6},{1,3},{3,5},{5,7},{8,10},{10,12},{12,14},{9,11},... | collective-permute-start | bytes 1179656 | tf_op jit(solution)/shard_map/ppermute | solution.py:178
  24.2 10.7 %collective-permute-start.5 = (bf16[2,2,6,64,128]{4,3,2,1,0:T(8,128)(2,1)S(1)}, bf16[2,2,6,64,128]{4,3,2,1,0:T(8,128)(2,1)S(1)}, u32[]{:S(2)}, u32[]{:S(2)}) collective-permute-start(bf16[2,2,6,64,128]{4,3,2,1,0:T(8,128)(2,1)S(1)} %collective-permute-done.refs_2_.refs_1_), channel_id=1, source_target_pairs={{2,0},{4,2},{6,4},{3,1},{5,3},{7,5},{10,8},{12,10},{14,12},{11,9},... | collective-permute-start | bytes 1179656 | tf_op jit(solution)/shard_map/ppermute | solution.py:178
  29.2 18.2 %collective-permute-start.9 = (bf16[2,2,2,6,64,128]{5,4,3,2,1,0:T(8,128)(2,1)S(1)}, bf16[2,2,2,6,64,128]{5,4,3,2,1,0:T(8,128)(2,1)S(1)}, u32[]{:S(2)}, u32[]{:S(2)}) collective-permute-start(bf16[2,2,2,6,64,128]{5,4,3,2,1,0:T(8,128)(2,1)S(1)} %pad_maximum_fusion.refs_0_.refs_2_), channel_id=1, source_target_pairs={{0,2},{2,4},{4,6},{1,3},{3,5},{5,7},{8,10},{10,12},{12,14},{9,11},... | collective-permute-start | bytes 2359304 | tf_op jit(solution)/shard_map/ppermute | solution.py:178
  32.5 18.0 %collective-permute-start.10 = (bf16[2,2,2,6,64,128]{5,4,3,2,1,0:T(8,128)(2,1)S(1)}, bf16[2,2,2,6,64,128]{5,4,3,2,1,0:T(8,128)(2,1)S(1)}, u32[]{:S(2)}, u32[]{:S(2)}) collective-permute-start(bf16[2,2,2,6,64,128]{5,4,3,2,1,0:T(8,128)(2,1)S(1)} %pad_maximum_fusion.refs_0_.refs_2_), channel_id=1, source_target_pairs={{2,0},{4,2},{6,4},{3,1},{5,3},{7,5},{10,8},{12,10},{14,12},{11,9},... | collective-permute-start | bytes 2359304 | tf_op jit(solution)/shard_map/ppermute | solution.py:178
  35.0 24.8 %collective-permute-start.6 = (bf16[6,2,6,64,128]{4,3,2,1,0:T(8,128)(2,1)S(1)}, bf16[6,2,6,64,128]{4,3,2,1,0:T(8,128)(2,1)S(1)}, u32[]{:S(2)}, u32[]{:S(2)}) collective-permute-start(bf16[6,2,6,64,128]{4,3,2,1,0:T(8,128)(2,1)S(1)} %get-tuple-element.57), channel_id=1, source_target_pairs={{0,8},{8,16},{16,24},{1,9},{9,17},{17,25},{2,10},{10,18},{18,26},{... | collective-permute-start | bytes 3538952 | tf_op jit(solution)/shard_map/ppermute | solution.py:178
  41.6 18.1 %collective-permute-start.7 = (bf16[6,2,6,64,128]{4,3,2,1,0:T(8,128)(2,1)S(1)}, bf16[6,2,6,64,128]{4,3,2,1,0:T(8,128)(2,1)S(1)}, u32[]{:S(2)}, u32[]{:S(2)}) collective-permute-start(bf16[6,2,6,64,128]{4,3,2,1,0:T(8,128)(2,1)S(1)} %get-tuple-element.56), channel_id=1, source_target_pairs={{8,0},{16,8},{24,16},{9,1},{17,9},{25,17},{10,2},{18,10},{26,18},{... | collective-permute-start | bytes 3538952 | tf_op jit(solution)/shard_map/ppermute | solution.py:178
  50.7 36.3 %collective-permute-start.11 = (bf16[6,2,6,64,128]{4,3,2,1,0:T(8,128)(2,1)S(1)}, bf16[6,2,6,64,128]{4,3,2,1,0:T(8,128)(2,1)S(1)}, u32[]{:S(2)}, u32[]{:S(2)}) collective-permute-start(bf16[6,2,6,64,128]{4,3,2,1,0:T(8,128)(2,1)S(1)} %get-tuple-element.43), channel_id=1, source_target_pairs={{0,8},{8,16},{16,24},{1,9},{9,17},{17,25},{2,10},{10,18},{18,26},{... | collective-permute-start | bytes 3538952 | tf_op jit(solution)/shard_map/ppermute | solution.py:178
  57.8 29.2 %collective-permute-start.12 = (bf16[6,2,6,64,128]{4,3,2,1,0:T(8,128)(2,1)S(1)}, bf16[6,2,6,64,128]{4,3,2,1,0:T(8,128)(2,1)S(1)}, u32[]{:S(2)}, u32[]{:S(2)}) collective-permute-start(bf16[6,2,6,64,128]{4,3,2,1,0:T(8,128)(2,1)S(1)} %get-tuple-element.42), channel_id=1, source_target_pairs={{8,0},{16,8},{24,16},{9,1},{17,9},{25,17},{10,2},{18,10},{26,18},{... | collective-permute-start | bytes 3538952 | tf_op jit(solution)/shard_map/ppermute | solution.py:178
  65.5 11.9 %collective-permute-start.13 = (f32[2,6,2,128]{3,2,1,0:T(2,128)S(1)}, f32[2,6,2,128]{3,2,1,0:T(2,128)S(1)}, u32[]{:S(2)}, u32[]{:S(2)}) collective-permute-start(f32[2,6,2,128]{3,2,1,0:T(2,128)S(1)} %get-tuple-element.33.refs_10_.refs_7_), channel_id=1, source_target_pairs={{0,2},{2,4},{4,6},{1,3},{3,5},{5,7},{8,10},{10,12},{12,14},{9,11},... | collective-permute-start | bytes 36872 | tf_op jit(solution)/shard_map/ppermute | solution.py:178
  68.1 9.3 %collective-permute-start.14 = (f32[2,6,2,128]{3,2,1,0:T(2,128)S(1)}, f32[2,6,2,128]{3,2,1,0:T(2,128)S(1)}, u32[]{:S(2)}, u32[]{:S(2)}) collective-permute-start(f32[2,6,2,128]{3,2,1,0:T(2,128)S(1)} %get-tuple-element.33.refs_10_.refs_7_), channel_id=1, source_target_pairs={{2,0},{4,2},{6,4},{3,1},{5,3},{7,5},{10,8},{12,10},{14,12},{11,9},... | collective-permute-start | bytes 36872 | tf_op jit(solution)/shard_map/ppermute | solution.py:178
  75.8 9.6 %collective-permute-start.8 = (bf16[2,2,6,64,128]{4,3,2,1,0:T(8,128)(2,1)S(1)}, bf16[2,2,6,64,128]{4,3,2,1,0:T(8,128)(2,1)S(1)}, u32[]{:S(2)}, u32[]{:S(2)}) collective-permute-start(bf16[2,2,6,64,128]{4,3,2,1,0:T(8,128)(2,1)S(1)} %get-tuple-element.35), channel_id=1, source_target_pairs={{0,1},{1,0},{2,3},{3,2},{4,5},{5,4},{6,7},{7,6},{8,9},{9,8},{10,11... | collective-permute-start | bytes 1179656 | tf_op jit(solution)/shard_map/ppermute | solution.py:183
  77.4 9.1 %collective-permute-start.15 = (f32[3,6,2,128]{3,2,1,0:T(2,128)S(1)}, f32[3,6,2,128]{3,2,1,0:T(2,128)S(1)}, u32[]{:S(2)}, u32[]{:S(2)}) collective-permute-start(f32[3,6,2,128]{3,2,1,0:T(2,128)S(1)} %pad_maximum_fusion.5), channel_id=1, source_target_pairs={{0,8},{8,16},{16,24},{1,9},{9,17},{17,25},{2,10},{10,18},{18,26},{... | collective-permute-start | bytes 55304 | tf_op jit(solution)/shard_map/ppermute | solution.py:178
  81.9 5.1 %collective-permute-start.16 = (f32[3,6,2,128]{3,2,1,0:T(2,128)S(1)}, f32[3,6,2,128]{3,2,1,0:T(2,128)S(1)}, u32[]{:S(2)}, u32[]{:S(2)}) collective-permute-start(f32[3,6,2,128]{3,2,1,0:T(2,128)S(1)} %pad_maximum_fusion.6), channel_id=1, source_target_pairs={{8,0},{16,8},{24,16},{9,1},{17,9},{25,17},{10,2},{18,10},{26,18},{... | collective-permute-start | bytes 55304 | tf_op jit(solution)/shard_map/ppermute | solution.py:178
  89.9 6.1 %collective-permute-start.17 = (bf16[2,2,3,64,128]{4,3,2,1,0:T(8,128)(2,1)S(1)}, bf16[2,2,3,64,128]{4,3,2,1,0:T(8,128)(2,1)S(1)}, u32[]{:S(2)}, u32[]{:S(2)}) collective-permute-start(bf16[2,2,3,64,128]{4,3,2,1,0:T(8,128)(2,1)S(1)} %get-tuple-element.37), channel_id=1, source_target_pairs={{0,1},{1,0},{2,3},{3,2},{4,5},{5,4},{6,7},{7,6},{8,9},{9,8},{10,11... | collective-permute-start | bytes 589832 | tf_op jit(solution)/shard_map/ppermute | solution.py:183
  93.6 6.9 %collective-permute-start.18 = (bf16[2,2,3,64,128]{4,3,2,1,0:T(8,128)(2,1)S(1)}, bf16[2,2,3,64,128]{4,3,2,1,0:T(8,128)(2,1)S(1)}, u32[]{:S(2)}, u32[]{:S(2)}) collective-permute-start(bf16[2,2,3,64,128]{4,3,2,1,0:T(8,128)(2,1)S(1)} %get-tuple-element.39), channel_id=1, source_target_pairs={{0,1},{1,0},{2,3},{3,2},{4,5},{5,4},{6,7},{7,6},{8,9},{9,8},{10,11... | collective-permute-start | bytes 589832 | tf_op jit(solution)/shard_map/ppermute | solution.py:183

commit v11 on v8

--- a/solution.py
+++ b/solution.py
@@ -166,7 +166,7 @@
         scratch_shapes=[pltpu.VMEM((3 * (frames + 2) * tokens, dim), jnp.bfloat16)] * 2,
         compiler_params=pltpu.CompilerParams(vmem_limit_bytes=16 * 2**20),
         cost_estimate=pl.CostEstimate(
-            flops=frames * count * 2 * products * tokens * 9 * tokens * dim,
+            flops=7 * frames * count * 2 * products * tokens * 9 * tokens * dim,
             bytes_accessed=count * (frames + 2) * 3 * 2 * tokens * dim * 2,
             transcendentals=frames * count * tokens * 9 * tokens,
         ),
@@ -245,11 +245,15 @@
         ]
         return jnp.stack(picked, 1).reshape(frames, 2, groups, cells, dim)
 
-    def from_heads(blocks):
+    def move(blocks):
+        return [
+            (first, [piece if b == 0 else turn(piece, b) for b, piece in enumerate(grads)]) for first, grads in blocks
+        ]
+
+    def assemble(blocks):
         whole = jnp.zeros((2, frames, rows, heads, columns_here, dim), jnp.bfloat16)
-        for first, grads in blocks:
-            for b, piece in enumerate(grads):
-                piece = piece if b == 0 else turn(piece, b)
+        for first, pieces in blocks:
+            for b, piece in enumerate(pieces):
                 piece = piece.reshape((2, frames, -1, rows, columns_here, dim)).transpose(0, 1, 3, 2, 4, 5)
                 start = (me + size - b) % size * groups + first
                 whole = lax.dynamic_update_slice_in_dim(whole, piece, start, 3)
@@ -283,21 +287,30 @@
     attended, stats = run(
         attend_kernel, scaling, size, [query_all] + key_halo, front_bias, [attended_shape, stat_shape], 0, groups, 2
     )
-    front_grads = run(
-        query_kernel, scaling, size, [query_all] + key_halo + [attended, stats], front_bias, grads_shape(groups),
-        0, groups, 3
-    )
+    halves = ((0, groups - groups // 2), (groups - groups // 2, groups // 2))
     stat_sides = row_sides(stats)
+    front_blocks, shown = [], stats
+    for first, count in halves:
+        front_grads = run(
+            query_kernel, scaling, size, [query_all] + key_halo + [attended, shown], front_bias,
+            grads_shape(count), first, count, 3
+        )
+        front_blocks.append((first, front_grads))
+        shown, stat_sides = lax.optimization_barrier((shown, stat_sides))
     stat_halo = [stats] + list(stat_sides) + list(frame_edges((stat_sides[0], stats, stat_sides[1])))
-    halves = ((0, groups - groups // 2), (groups - groups // 2, groups // 2))
+    front_blocks = move(front_blocks)
     back_blocks = []
     for first, count in halves:
         back_grads = run(
             back_kernel, scaling, size, key_parts + query_halo + stat_halo, back_bias, grads_shape(count),
             first, count, 4
         )
+        back_bias, back_grads = lax.optimization_barrier((back_bias, back_grads))
         back_blocks.append((first, back_grads))
-    return from_heads([(0, front_grads)]) + from_heads(back_blocks)
+    back_blocks = move(back_blocks)
+    first, pieces = back_blocks[0]
+    front_blocks, pieces[-1] = lax.optimization_barrier((front_blocks, pieces[-1]))
+    return assemble(front_blocks) + assemble(back_blocks)
 
 
 def solution(mesh):

time: 100 us -> 97 us (0.970); the launches traced: 99.7 us -> 95.3 us
  waiting for transfers between devices: 22.8 us -> 16.9 us
  starting transfers between devices: 49.9 us -> 51.1 us
    ppermute x5 -> x6, waiting for transfers between devices: 15.2 us -> 9.32 us  [turn(): lax.ppermute(tensor, 'head', [(i, (i + shift) % size) for i in range(size)])]
    ppermute x5 -> x6, starting transfers between devices: 4.35 us -> 5.5 us  [turn(): lax.ppermute(tensor, 'head', [(i, (i + shift) % size) for i in range(size)])]
    pallas_call x4 -> x5, Pallas kernels: 16.6 us -> 16.7 us  [run(): pl.pallas_call(functools.partial(kernel, scaling, parts), grid=(count,),...]
  transfers between devices with their start and end apart: 19 -> 20, of which waited for: 8 -> 6; matrix products, arithmetic and copies ran while one was open for 6% -> 6% of each run, Pallas kernels for 14% -> 18%
where the time goes in v11:
time: 97 us; the launch traced here: 95.3 us
  starting transfers between devices  51.1 us (53%)
  waiting for transfers between devices  16.9 us (17%)
  Pallas kernels  16.7 us (17%)
  local copies, waits for them, and re-layouts  6.93 us (7%)
  other arithmetic  1.41 us (1%)
  between operations  1.34 us (1%)
    ppermute x14, starting transfers between devices, step_along(): lax.ppermute(tensor, axis, [(i, i + sign) for i in range(size) if 0 <= i...  45.6 us
    pallas_call x5, Pallas kernels, run(): pl.pallas_call(functools.partial(kernel, scaling, parts), grid=(count,),...  16.7 us
    ppermute x6, waiting for transfers between devices, turn(): lax.ppermute(tensor, 'head', [(i, (i + shift) % size) for i in range(size)])  9.32 us
    ppermute x14, waiting for transfers between devices, step_along(): lax.ppermute(tensor, axis, [(i, i + sign) for i in range(size) if 0 <= i...  7.61 us
    ppermute x6, starting transfers between devices, turn(): lax.ppermute(tensor, 'head', [(i, (i + shift) % size) for i in range(size)])  5.5 us
  transfers between devices with their start and end apart: 20, of which 6 were waited for; matrix products, arithmetic and copies ran while one was open for 6% of the time, Pallas kernels for 18%

profile of v11, /device:TPU:9, one launch (start us, length us, event | category | flops | bytes accessed | tf_op | source)
XLA Modules:
  0.0 95.3 jit_solution(15691285835747745450)
XLA Ops:
  0.7 1.4 %dynamic-slice_bitcast_fusion.6 = (bf16[2,1,6,8,8,128]{5,4,2,3,0,1:T(8,128)(2,1)S(1)}, bf16[2,6,8,8,128]{4,3,1,2,0:T(8,128)(2,1)S(1)}, bf16[2,6,8,8,128]{4,3,1,2...) fusion(bf16[2,8,8,12,128]{4,2,3,1,0:T(8,128)(2,1)} %param.9, ...), kind=kLoop, calls=%fused_computation.76 | loop fusion | bytes 1966088 | tf_op jit(solution)/shard_map/stack | solution.py:246
  2.2 3.3 %collective-permute-start.2 = (bf16[2,2,6,64,128]{4,3,2,1,0:T(8,128)(2,1)S(1)}, bf16[2,2,6,64,128]{4,3,2,1,0:T(8,128)(2,1)S(1)}, u32[]{:S(2)}, u32[]{:S(2)}) collective-permute-start(bf16[2,2,6,64,128]{4,3,2,1,0:T(8,128)(2,1)S(1)} %pad_maximum_fusion.4.refs_1_.refs_0_), channel_id=1, source_target_pairs={{0,2},{2,4},{4,6},{1,3},{3,5},{5,7},{8,10},{10,12},{12,14},{9,11},... | collective-permute-start | bytes 1179656 | tf_op jit(solution)/shard_map/ppermute | solution.py:178
  5.6 2.1 %collective-permute-start.3 = (bf16[2,2,6,64,128]{4,3,2,1,0:T(8,128)(2,1)S(1)}, bf16[2,2,6,64,128]{4,3,2,1,0:T(8,128)(2,1)S(1)}, u32[]{:S(2)}, u32[]{:S(2)}) collective-permute-start(bf16[2,2,6,64,128]{4,3,2,1,0:T(8,128)(2,1)S(1)} %pad_maximum_fusion.4.refs_1_.refs_0_), channel_id=1, source_target_pairs={{2,0},{4,2},{6,4},{3,1},{5,3},{7,5},{10,8},{12,10},{14,12},{11,9},... | collective-permute-start | bytes 1179656 | tf_op jit(solution)/shard_map/ppermute | solution.py:178
  7.8 0.8 pad_maximum_fusion.3
  8.5 1.2 %collective-permute-start = (bf16[2,2,6,64,128]{4,3,2,1,0:T(8,128)(2,1)}, bf16[2,2,6,64,128]{4,3,2,1,0:T(8,128)(2,1)S(1)}, u32[]{:S(2)}, u32[]{:S(2)}) collective-permute-start(bf16[2,2,6,64,128]{4,3,2,1,0:T(8,128)(2,1)} %pad_maximum_fusion.3), channel_id=1, source_target_pairs={{0,1},{1,0},{2,3},{3,2},{4,5},{5,4},{6,7},{7,6},{8,9},{9,8},{10,11... | collective-permute-start | bytes 1179656 | tf_op jit(solution)/shard_map/ppermute | solution.py:183
  13.3 4.8 %collective-permute-done.refs_2_.refs_1_ = bf16[2,2,6,64,128]{4,3,2,1,0:T(8,128)(2,1)S(1)} collective-permute-done((bf16[2,2,6,64,128]{4,3,2,1,0:T(8,128)(2,1)}, bf16[2,2,6,64,128]{4,3,2,1,0:T(8,128)(2,1)S(1)}, u32[]{:S(2)}, u32[]{:S(2)}) %collective-permute-start) | collective-permute-done | bytes 393248 | tf_op jit(solution)/shard_map/ppermute | solution.py:183
  18.1 1.2 %collective-permute-start.1 = (bf16[2,2,6,64,128]{4,3,2,1,0:T(8,128)(2,1)S(1)}, bf16[2,2,6,64,128]{4,3,2,1,0:T(8,128)(2,1)S(1)}, u32[]{:S(2)}, u32[]{:S(2)}) collective-permute-start(bf16[2,2,6,64,128]{4,3,2,1,0:T(8,128)(2,1)S(1)} %pad_maximum_fusion.2), channel_id=1, source_target_pairs={{0,1},{1,0},{2,3},{3,2},{4,5},{5,4},{6,7},{7,6},{8,9},{9,8},{10,11... | collective-permute-start | bytes 1179656 | tf_op jit(solution)/shard_map/ppermute | solution.py:183
  19.5 3.2 %collective-permute-start.4 = (bf16[2,2,6,64,128]{4,3,2,1,0:T(8,128)(2,1)S(1)}, bf16[2,2,6,64,128]{4,3,2,1,0:T(8,128)(2,1)S(1)}, u32[]{:S(2)}, u32[]{:S(2)}) collective-permute-start(bf16[2,2,6,64,128]{4,3,2,1,0:T(8,128)(2,1)S(1)} %collective-permute-done.refs_2_.refs_1_), channel_id=1, source_target_pairs={{0,2},{2,4},{4,6},{1,3},{3,5},{5,7},{8,10},{10,12},{12,14},{9,11},... | collective-permute-start | bytes 1179656 | tf_op jit(solution)/shard_map/ppermute | solution.py:178
  22.6 2.1 %collective-permute-start.5 = (bf16[2,2,6,64,128]{4,3,2,1,0:T(8,128)(2,1)S(1)}, bf16[2,2,6,64,128]{4,3,2,1,0:T(8,128)(2,1)S(1)}, u32[]{:S(2)}, u32[]{:S(2)}) collective-permute-start(bf16[2,2,6,64,128]{4,3,2,1,0:T(8,128)(2,1)S(1)} %collective-permute-done.refs_2_.refs_1_), channel_id=1, source_target_pairs={{2,0},{4,2},{6,4},{3,1},{5,3},{7,5},{10,8},{12,10},{14,12},{11,9},... | collective-permute-start | bytes 1179656 | tf_op jit(solution)/shard_map/ppermute | solution.py:178
  24.8 1.8 %collective-permute-done.1 = bf16[2,2,6,64,128]{4,3,2,1,0:T(8,128)(2,1)S(1)} collective-permute-done((bf16[2,2,6,64,128]{4,3,2,1,0:T(8,128)(2,1)S(1)}, bf16[2,2,6,64,128]{4,3,2,1,0:T(8,128)(2,1)S(1)}, u32[]{:S(2)}, u32[]{:S(2)}) %collective-permute-start.1) | collective-permute-done | bytes 393248 | tf_op jit(solution)/shard_map/ppermute | solution.py:183
  26.7 3.2 %collective-permute-start.12 = (bf16[2,2,2,6,64,128]{5,4,3,2,1,0:T(8,128)(2,1)S(1)}, bf16[2,2,2,6,64,128]{5,4,3,2,1,0:T(8,128)(2,1)S(1)}, u32[]{:S(2)}, u32[]{:S(2)}) collective-permute-start(bf16[2,2,2,6,64,128]{5,4,3,2,1,0:T(8,128)(2,1)S(1)} %pad_maximum_fusion.refs_0_.refs_2_), channel_id=1, source_target_pairs={{0,2},{2,4},{4,6},{1,3},{3,5},{5,7},{8,10},{10,12},{12,14},{9,11},... | collective-permute-start | bytes 2359304 | tf_op jit(solution)/shard_map/ppermute | solution.py:178
  29.9 2.1 %collective-permute-start.13 = (bf16[2,2,2,6,64,128]{5,4,3,2,1,0:T(8,128)(2,1)S(1)}, bf16[2,2,2,6,64,128]{5,4,3,2,1,0:T(8,128)(2,1)S(1)}, u32[]{:S(2)}, u32[]{:S(2)}) collective-permute-start(bf16[2,2,2,6,64,128]{5,4,3,2,1,0:T(8,128)(2,1)S(1)} %pad_maximum_fusion.refs_0_.refs_2_), channel_id=1, source_target_pairs={{2,0},{4,2},{6,4},{3,1},{5,3},{7,5},{10,8},{12,10},{14,12},{11,9},... | collective-permute-start | bytes 2359304 | tf_op jit(solution)/shard_map/ppermute | solution.py:178
  32.5 7.8 %collective-permute-start.6 = (bf16[6,2,6,64,128]{4,3,2,1,0:T(8,128)(2,1)S(1)}, bf16[6,2,6,64,128]{4,3,2,1,0:T(8,128)(2,1)S(1)}, u32[]{:S(2)}, u32[]{:S(2)}) collective-permute-start(bf16[6,2,6,64,128]{4,3,2,1,0:T(8,128)(2,1)S(1)} %get-tuple-element.89), channel_id=1, source_target_pairs={{0,8},{8,16},{16,24},{1,9},{9,17},{17,25},{2,10},{10,18},{18,26},{... | collective-permute-start | bytes 3538952 | tf_op jit(solution)/shard_map/ppermute | solution.py:178
  40.3 1.9 %collective-permute-start.7 = (bf16[6,2,6,64,128]{4,3,2,1,0:T(8,128)(2,1)S(1)}, bf16[6,2,6,64,128]{4,3,2,1,0:T(8,128)(2,1)S(1)}, u32[]{:S(2)}, u32[]{:S(2)}) collective-permute-start(bf16[6,2,6,64,128]{4,3,2,1,0:T(8,128)(2,1)S(1)} %get-tuple-element.88), channel_id=1, source_target_pairs={{8,0},{16,8},{24,16},{9,1},{17,9},{25,17},{10,2},{18,10},{26,18},{... | collective-permute-start | bytes 3538952 | tf_op jit(solution)/shard_map/ppermute | solution.py:178
  42.2 4.7 %collective-permute-done.12.refs_3_ = bf16[2,2,2,6,64,128]{5,4,3,2,1,0:T(8,128)(2,1)S(1)} collective-permute-done((bf16[2,2,2,6,64,128]{5,4,3,2,1,0:T(8,128)(2,1)S(1)}, bf16[2,2,2,6,64,128]{5,4,3,2,1,0:T(8,128)(2,1)S(1)}, u32[]{:S(2)}, u32[]{:S(2)}) %collective-permute-start.12) | collective-permute-done | bytes 786464 | tf_op jit(solution)/shard_map/ppermute | solution.py:178
  47.0 2.8 %collective-permute-done.13.refs_4_ = bf16[2,2,2,6,64,128]{5,4,3,2,1,0:T(8,128)(2,1)S(1)} collective-permute-done((bf16[2,2,2,6,64,128]{5,4,3,2,1,0:T(8,128)(2,1)S(1)}, bf16[2,2,2,6,64,128]{5,4,3,2,1,0:T(8,128)(2,1)S(1)}, u32[]{:S(2)}, u32[]{:S(2)}) %collective-permute-start.13) | collective-permute-done | bytes 786464 | tf_op jit(solution)/shard_map/ppermute | solution.py:178
  50.1 6.1 %collective-permute-start.14 = (bf16[6,2,6,64,128]{4,3,2,1,0:T(8,128)(2,1)S(1)}, bf16[6,2,6,64,128]{4,3,2,1,0:T(8,128)(2,1)S(1)}, u32[]{:S(2)}, u32[]{:S(2)}) collective-permute-start(bf16[6,2,6,64,128]{4,3,2,1,0:T(8,128)(2,1)S(1)} %get-tuple-element.77), channel_id=1, source_target_pairs={{0,8},{8,16},{16,24},{1,9},{9,17},{17,25},{2,10},{10,18},{18,26},{... | collective-permute-start | bytes 3538952 | tf_op jit(solution)/shard_map/ppermute | solution.py:178
  56.2 1.9 %collective-permute-start.15 = (bf16[6,2,6,64,128]{4,3,2,1,0:T(8,128)(2,1)S(1)}, bf16[6,2,6,64,128]{4,3,2,1,0:T(8,128)(2,1)S(1)}, u32[]{:S(2)}, u32[]{:S(2)}) collective-permute-start(bf16[6,2,6,64,128]{4,3,2,1,0:T(8,128)(2,1)S(1)} %get-tuple-element.76), channel_id=1, source_target_pairs={{8,0},{16,8},{24,16},{9,1},{17,9},{25,17},{10,2},{18,10},{26,18},{... | collective-permute-start | bytes 3538952 | tf_op jit(solution)/shard_map/ppermute | solution.py:178
  58.2 5.7 %shard_map.102 = (bf16[2,6,128,128]{3,2,1,0:T(8,128)(2,1)S(1)}, f32[2,6,2,128]{3,2,1,0:T(2,128)S(1)}) custom-call(bf16[2,2,2,6,64,128]{5,4,3,2,1,0:T(8,128)(2,1)S(1)} %pad_maximum_fusion.refs_0_.refs_2_, bf16[2,2,6,64,128]{4,3,2,1,0:T(8,128)(2,1)S(1)} %pad_maximum_fusion.4.refs_1_.refs_0_, ...), custom_call_target="tpu_custom_call" | custom-call | flops 6341787648 | bytes 4718592 | tf_op jit(solution)/shard_map/pallas_call | solution.py:159
  63.9 3.2 %collective-permute-start.9 = (f32[2,6,2,128]{3,2,1,0:T(2,128)S(1)}, f32[2,6,2,128]{3,2,1,0:T(2,128)S(1)}, u32[]{:S(2)}, u32[]{:S(2)}) collective-permute-start(f32[2,6,2,128]{3,2,1,0:T(2,128)S(1)} %get-tuple-element.49.refs_10_.refs_7_), channel_id=1, source_target_pairs={{0,2},{2,4},{4,6},{1,3},{3,5},{5,7},{8,10},{10,12},{12,14},{9,11},... | collective-permute-start | bytes 36872 | tf_op jit(solution)/shard_map/ppermute | solution.py:178
  67.1 2.1 %collective-permute-start.10 = (f32[2,6,2,128]{3,2,1,0:T(2,128)S(1)}, f32[2,6,2,128]{3,2,1,0:T(2,128)S(1)}, u32[]{:S(2)}, u32[]{:S(2)}) collective-permute-start(f32[2,6,2,128]{3,2,1,0:T(2,128)S(1)} %get-tuple-element.49.refs_10_.refs_7_), channel_id=1, source_target_pairs={{2,0},{4,2},{6,4},{3,1},{5,3},{7,5},{10,8},{12,10},{14,12},{11,9},... | collective-permute-start | bytes 36872 | tf_op jit(solution)/shard_map/ppermute | solution.py:178
  69.2 2.5 %shard_map.103 = (bf16[2,2,3,64,128]{4,3,2,1,0:T(8,128)(2,1)S(1)}, bf16[2,2,3,64,128]{4,3,2,1,0:T(8,128)(2,1)S(1)}) custom-call(bf16[2,2,2,6,64,128]{5,4,3,2,1,0:T(8,128)(2,1)S(1)} %pad_maximum_fusion.refs_0_.refs_2_, bf16[2,2,6,64,128]{4,3,2,1,0:T(8,128)(2,1)S(1)} %pad_maximum_fusion.4.refs_1_.refs_0_, ...), custom_call_target="tpu_custom_call" | custom-call | flops 4756340736 | bytes 2359296 | tf_op jit(solution)/shard_map/pallas_call | solution.py:159
  72.1 4.6 %collective-permute-start.16 = (f32[3,6,2,128]{3,2,1,0:T(2,128)S(1)}, f32[3,6,2,128]{3,2,1,0:T(2,128)S(1)}, u32[]{:S(2)}, u32[]{:S(2)}) collective-permute-start(f32[3,6,2,128]{3,2,1,0:T(2,128)S(1)} %pad_maximum_fusion.6), channel_id=1, source_target_pairs={{0,8},{8,16},{16,24},{1,9},{9,17},{17,25},{2,10},{10,18},{18,26},{... | collective-permute-start | bytes 55304 | tf_op jit(solution)/shard_map/ppermute | solution.py:178
  76.7 1.9 %collective-permute-start.17 = (f32[3,6,2,128]{3,2,1,0:T(2,128)S(1)}, f32[3,6,2,128]{3,2,1,0:T(2,128)S(1)}, u32[]{:S(2)}, u32[]{:S(2)}) collective-permute-start(f32[3,6,2,128]{3,2,1,0:T(2,128)S(1)} %pad_maximum_fusion.7), channel_id=1, source_target_pairs={{8,0},{16,8},{24,16},{9,1},{17,9},{25,17},{10,2},{18,10},{26,18},{... | collective-permute-start | bytes 55304 | tf_op jit(solution)/shard_map/ppermute | solution.py:178
  78.6 2.6 %shard_map.104 = (bf16[2,2,3,64,128]{4,3,2,1,0:T(8,128)(2,1)S(1)}, bf16[2,2,3,64,128]{4,3,2,1,0:T(8,128)(2,1)S(1)}) custom-call(bf16[2,2,2,6,64,128]{5,4,3,2,1,0:T(8,128)(2,1)S(1)} %pad_maximum_fusion.refs_0_.refs_2_, bf16[2,2,6,64,128]{4,3,2,1,0:T(8,128)(2,1)S(1)} %pad_maximum_fusion.4.refs_1_.refs_0_, ...), custom_call_target="tpu_custom_call" | custom-call | flops 4756340736 | bytes 2359296 | tf_op jit(solution)/shard_map/pallas_call | solution.py:159
  81.2 1.2 %collective-permute-start.11 = (bf16[2,2,3,64,128]{4,3,2,1,0:T(8,128)(2,1)S(1)}, bf16[2,2,3,64,128]{4,3,2,1,0:T(8,128)(2,1)S(1)}, u32[]{:S(2)}, u32[]{:S(2)}) collective-permute-start(bf16[2,2,3,64,128]{4,3,2,1,0:T(8,128)(2,1)S(1)} %get-tuple-element.51), channel_id=1, source_target_pairs={{0,1},{1,0},{2,3},{3,2},{4,5},{5,4},{6,7},{7,6},{8,9},{9,8},{10,11... | collective-permute-start | bytes 589832 | tf_op jit(solution)/shard_map/ppermute | solution.py:183
  82.4 2.9 %shard_map.105 = (bf16[2,2,3,64,128]{4,3,2,1,0:T(8,128)(2,1)S(1)}, bf16[2,2,3,64,128]{4,3,2,1,0:T(8,128)(2,1)S(1)}) custom-call(bf16[2,2,6,64,128]{4,3,2,1,0:T(8,128)(2,1)S(1)} %pad_maximum_fusion.4.refs_1_.refs_0_, bf16[2,2,6,64,128]{4,3,2,1,0:T(8,128)(2,1)S(1)} %collective-permute-done.refs_2_.refs_1_, ...), custom_call_target="tpu_custom_call" | custom-call | flops 6341787648 | bytes 2359296 | tf_op jit(solution)/shard_map/pallas_call | solution.py:159
  85.3 0.8 collective-permute-start.18
  86.2 2.9 %shard_map.106 = (bf16[2,2,3,64,128]{4,3,2,1,0:T(8,128)(2,1)S(1)}, bf16[2,2,3,64,128]{4,3,2,1,0:T(8,128)(2,1)S(1)}) custom-call(bf16[2,2,6,64,128]{4,3,2,1,0:T(8,128)(2,1)S(1)} %pad_maximum_fusion.4.refs_1_.refs_0_, bf16[2,2,6,64,128]{4,3,2,1,0:T(8,128)(2,1)S(1)} %collective-permute-done.refs_2_.refs_1_, ...), custom_call_target="tpu_custom_call" | custom-call | flops 6341787648 | bytes 2359296 | tf_op jit(solution)/shard_map/pallas_call | solution.py:159
  90.5 0.9 slice_bitcast_fusion.2
  91.5 2.7 %collective-permute-done.19 = bf16[2,2,3,64,128]{4,3,2,1,0:T(8,128)(2,1)S(1)} collective-permute-done((bf16[2,2,3,64,128]{4,3,2,1,0:T(8,128)(2,1)S(1)}, bf16[2,2,3,64,128]{4,3,2,1,0:T(8,128)(2,1)S(1)}, u32[]{:S(2)}, u32[]{:S(2)}) %collective-permute-start.19) | collective-permute-done | bytes 196640 | tf_op jit(solution)/shard_map/ppermute | solution.py:183
  94.3 0.9 slice_bitcast_fusion
  (101 shorter events, 6.3 us)
Async XLA Ops:
  2.1 7.8 %copy-start = (bf16[2,8,8,12,128]{4,2,3,1,0:T(8,128)(2,1)S(1)}, bf16[2,8,8,12,128]{4,2,3,1,0:T(8,128)(2,1)}, u32[]{:S(2)}) copy-start(bf16[2,8,8,12,128]{4,2,3,1,0:T(8,128)(2,1)} %param.10) | copy-start | bytes 1179652
  2.2 7.8 %copy-start.1 = (bf16[2,8,8,12,128]{4,2,3,1,0:T(8,128)(2,1)S(1)}, bf16[2,8,8,12,128]{4,2,3,1,0:T(8,128)(2,1)}, u32[]{:S(2)}) copy-start(bf16[2,8,8,12,128]{4,2,3,1,0:T(8,128)(2,1)} %param.7) | copy-start | bytes 1179652
  2.2 24.4 %collective-permute-start.2 = (bf16[2,2,6,64,128]{4,3,2,1,0:T(8,128)(2,1)S(1)}, bf16[2,2,6,64,128]{4,3,2,1,0:T(8,128)(2,1)S(1)}, u32[]{:S(2)}, u32[]{:S(2)}) collective-permute-start(bf16[2,2,6,64,128]{4,3,2,1,0:T(8,128)(2,1)S(1)} %pad_maximum_fusion.4.refs_1_.refs_0_), channel_id=1, source_target_pairs={{0,2},{2,4},{4,6},{1,3},{3,5},{5,7},{8,10},{10,12},{12,14},{9,11},... | collective-permute-start | bytes 1179656 | tf_op jit(solution)/shard_map/ppermute | solution.py:178
  5.6 21.1 %collective-permute-start.3 = (bf16[2,2,6,64,128]{4,3,2,1,0:T(8,128)(2,1)S(1)}, bf16[2,2,6,64,128]{4,3,2,1,0:T(8,128)(2,1)S(1)}, u32[]{:S(2)}, u32[]{:S(2)}) collective-permute-start(bf16[2,2,6,64,128]{4,3,2,1,0:T(8,128)(2,1)S(1)} %pad_maximum_fusion.4.refs_1_.refs_0_), channel_id=1, source_target_pairs={{2,0},{4,2},{6,4},{3,1},{5,3},{7,5},{10,8},{12,10},{14,12},{11,9},... | collective-permute-start | bytes 1179656 | tf_op jit(solution)/shard_map/ppermute | solution.py:178
  8.5 9.6 %collective-permute-start = (bf16[2,2,6,64,128]{4,3,2,1,0:T(8,128)(2,1)}, bf16[2,2,6,64,128]{4,3,2,1,0:T(8,128)(2,1)S(1)}, u32[]{:S(2)}, u32[]{:S(2)}) collective-permute-start(bf16[2,2,6,64,128]{4,3,2,1,0:T(8,128)(2,1)} %pad_maximum_fusion.3), channel_id=1, source_target_pairs={{0,1},{1,0},{2,3},{3,2},{4,5},{5,4},{6,7},{7,6},{8,9},{9,8},{10,11... | collective-permute-start | bytes 1179656 | tf_op jit(solution)/shard_map/ppermute | solution.py:183
  10.0 0.8 copy-start.3
  10.0 2.3 %copy-start.4 = (bf16[4,3,9,2,9,1]{4,2,1,0,5,3:T(8,128)(2,1)S(1)}, bf16[4,3,9,2,9,1]{4,2,1,0,5,3:T(8,128)(2,1)}, u32[]{:S(2)}) copy-start(bf16[4,3,9,2,9,1]{4,2,1,0,5,3:T(8,128)(2,1)} %constant.224) | copy-start | bytes 11668
  11.9 1.2 %copy-start.2 = (bf16[18,1152]{1,0:T(8,128)(2,1)S(1)}, bf16[18,1152]{1,0:T(8,128)(2,1)}, u32[]{:S(2)}) copy-start(bf16[18,1152]{1,0:T(8,128)(2,1)} %constant.114.clone) | copy-start | bytes 124420
  18.1 8.4 %collective-permute-start.1 = (bf16[2,2,6,64,128]{4,3,2,1,0:T(8,128)(2,1)S(1)}, bf16[2,2,6,64,128]{4,3,2,1,0:T(8,128)(2,1)S(1)}, u32[]{:S(2)}, u32[]{:S(2)}) collective-permute-start(bf16[2,2,6,64,128]{4,3,2,1,0:T(8,128)(2,1)S(1)} %pad_maximum_fusion.2), channel_id=1, source_target_pairs={{0,1},{1,0},{2,3},{3,2},{4,5},{5,4},{6,7},{7,6},{8,9},{9,8},{10,11... | collective-permute-start | bytes 1179656 | tf_op jit(solution)/shard_map/ppermute | solution.py:183
  19.5 12.8 %collective-permute-start.4 = (bf16[2,2,6,64,128]{4,3,2,1,0:T(8,128)(2,1)S(1)}, bf16[2,2,6,64,128]{4,3,2,1,0:T(8,128)(2,1)S(1)}, u32[]{:S(2)}, u32[]{:S(2)}) collective-permute-start(bf16[2,2,6,64,128]{4,3,2,1,0:T(8,128)(2,1)S(1)} %collective-permute-done.refs_2_.refs_1_), channel_id=1, source_target_pairs={{0,2},{2,4},{4,6},{1,3},{3,5},{5,7},{8,10},{10,12},{12,14},{9,11},... | collective-permute-start | bytes 1179656 | tf_op jit(solution)/shard_map/ppermute | solution.py:178
  22.6 9.8 %collective-permute-start.5 = (bf16[2,2,6,64,128]{4,3,2,1,0:T(8,128)(2,1)S(1)}, bf16[2,2,6,64,128]{4,3,2,1,0:T(8,128)(2,1)S(1)}, u32[]{:S(2)}, u32[]{:S(2)}) collective-permute-start(bf16[2,2,6,64,128]{4,3,2,1,0:T(8,128)(2,1)S(1)} %collective-permute-done.refs_2_.refs_1_), channel_id=1, source_target_pairs={{2,0},{4,2},{6,4},{3,1},{5,3},{7,5},{10,8},{12,10},{14,12},{11,9},... | collective-permute-start | bytes 1179656 | tf_op jit(solution)/shard_map/ppermute | solution.py:178
  26.7 20.3 %collective-permute-start.12 = (bf16[2,2,2,6,64,128]{5,4,3,2,1,0:T(8,128)(2,1)S(1)}, bf16[2,2,2,6,64,128]{5,4,3,2,1,0:T(8,128)(2,1)S(1)}, u32[]{:S(2)}, u32[]{:S(2)}) collective-permute-start(bf16[2,2,2,6,64,128]{5,4,3,2,1,0:T(8,128)(2,1)S(1)} %pad_maximum_fusion.refs_0_.refs_2_), channel_id=1, source_target_pairs={{0,2},{2,4},{4,6},{1,3},{3,5},{5,7},{8,10},{10,12},{12,14},{9,11},... | collective-permute-start | bytes 2359304 | tf_op jit(solution)/shard_map/ppermute | solution.py:178
  29.9 20.0 %collective-permute-start.13 = (bf16[2,2,2,6,64,128]{5,4,3,2,1,0:T(8,128)(2,1)S(1)}, bf16[2,2,2,6,64,128]{5,4,3,2,1,0:T(8,128)(2,1)S(1)}, u32[]{:S(2)}, u32[]{:S(2)}) collective-permute-start(bf16[2,2,2,6,64,128]{5,4,3,2,1,0:T(8,128)(2,1)S(1)} %pad_maximum_fusion.refs_0_.refs_2_), channel_id=1, source_target_pairs={{2,0},{4,2},{6,4},{3,1},{5,3},{7,5},{10,8},{12,10},{14,12},{11,9},... | collective-permute-start | bytes 2359304 | tf_op jit(solution)/shard_map/ppermute | solution.py:178
  32.5 25.7 %collective-permute-start.6 = (bf16[6,2,6,64,128]{4,3,2,1,0:T(8,128)(2,1)S(1)}, bf16[6,2,6,64,128]{4,3,2,1,0:T(8,128)(2,1)S(1)}, u32[]{:S(2)}, u32[]{:S(2)}) collective-permute-start(bf16[6,2,6,64,128]{4,3,2,1,0:T(8,128)(2,1)S(1)} %get-tuple-element.89), channel_id=1, source_target_pairs={{0,8},{8,16},{16,24},{1,9},{9,17},{17,25},{2,10},{10,18},{18,26},{... | collective-permute-start | bytes 3538952 | tf_op jit(solution)/shard_map/ppermute | solution.py:178
  40.3 17.8 %collective-permute-start.7 = (bf16[6,2,6,64,128]{4,3,2,1,0:T(8,128)(2,1)S(1)}, bf16[6,2,6,64,128]{4,3,2,1,0:T(8,128)(2,1)S(1)}, u32[]{:S(2)}, u32[]{:S(2)}) collective-permute-start(bf16[6,2,6,64,128]{4,3,2,1,0:T(8,128)(2,1)S(1)} %get-tuple-element.88), channel_id=1, source_target_pairs={{8,0},{16,8},{24,16},{9,1},{17,9},{25,17},{10,2},{18,10},{26,18},{... | collective-permute-start | bytes 3538952 | tf_op jit(solution)/shard_map/ppermute | solution.py:178
  50.1 32.3 %collective-permute-start.14 = (bf16[6,2,6,64,128]{4,3,2,1,0:T(8,128)(2,1)S(1)}, bf16[6,2,6,64,128]{4,3,2,1,0:T(8,128)(2,1)S(1)}, u32[]{:S(2)}, u32[]{:S(2)}) collective-permute-start(bf16[6,2,6,64,128]{4,3,2,1,0:T(8,128)(2,1)S(1)} %get-tuple-element.77), channel_id=1, source_target_pairs={{0,8},{8,16},{16,24},{1,9},{9,17},{17,25},{2,10},{10,18},{18,26},{... | collective-permute-start | bytes 3538952 | tf_op jit(solution)/shard_map/ppermute | solution.py:178
  56.2 26.2 %collective-permute-start.15 = (bf16[6,2,6,64,128]{4,3,2,1,0:T(8,128)(2,1)S(1)}, bf16[6,2,6,64,128]{4,3,2,1,0:T(8,128)(2,1)S(1)}, u32[]{:S(2)}, u32[]{:S(2)}) collective-permute-start(bf16[6,2,6,64,128]{4,3,2,1,0:T(8,128)(2,1)S(1)} %get-tuple-element.76), channel_id=1, source_target_pairs={{8,0},{16,8},{24,16},{9,1},{17,9},{25,17},{10,2},{18,10},{26,18},{... | collective-permute-start | bytes 3538952 | tf_op jit(solution)/shard_map/ppermute | solution.py:178
  63.9 8.2 %collective-permute-start.9 = (f32[2,6,2,128]{3,2,1,0:T(2,128)S(1)}, f32[2,6,2,128]{3,2,1,0:T(2,128)S(1)}, u32[]{:S(2)}, u32[]{:S(2)}) collective-permute-start(f32[2,6,2,128]{3,2,1,0:T(2,128)S(1)} %get-tuple-element.49.refs_10_.refs_7_), channel_id=1, source_target_pairs={{0,2},{2,4},{4,6},{1,3},{3,5},{5,7},{8,10},{10,12},{12,14},{9,11},... | collective-permute-start | bytes 36872 | tf_op jit(solution)/shard_map/ppermute | solution.py:178
  67.1 4.9 %collective-permute-start.10 = (f32[2,6,2,128]{3,2,1,0:T(2,128)S(1)}, f32[2,6,2,128]{3,2,1,0:T(2,128)S(1)}, u32[]{:S(2)}, u32[]{:S(2)}) collective-permute-start(f32[2,6,2,128]{3,2,1,0:T(2,128)S(1)} %get-tuple-element.49.refs_10_.refs_7_), channel_id=1, source_target_pairs={{2,0},{4,2},{6,4},{3,1},{5,3},{7,5},{10,8},{12,10},{14,12},{11,9},... | collective-permute-start | bytes 36872 | tf_op jit(solution)/shard_map/ppermute | solution.py:178
  71.7 18.3 %collective-permute-start.8 = (bf16[2,2,3,64,128]{4,3,2,1,0:T(8,128)(2,1)S(1)}, bf16[2,2,3,64,128]{4,3,2,1,0:T(8,128)(2,1)S(1)}, u32[]{:S(2)}, u32[]{:S(2)}) collective-permute-start(bf16[2,2,3,64,128]{4,3,2,1,0:T(8,128)(2,1)S(1)} %get-tuple-element.48), channel_id=1, source_target_pairs={{0,1},{1,0},{2,3},{3,2},{4,5},{5,4},{6,7},{7,6},{8,9},{9,8},{10,11... | collective-permute-start | bytes 589832 | tf_op jit(solution)/shard_map/ppermute | solution.py:183
  72.1 9.1 %collective-permute-start.16 = (f32[3,6,2,128]{3,2,1,0:T(2,128)S(1)}, f32[3,6,2,128]{3,2,1,0:T(2,128)S(1)}, u32[]{:S(2)}, u32[]{:S(2)}) collective-permute-start(f32[3,6,2,128]{3,2,1,0:T(2,128)S(1)} %pad_maximum_fusion.6), channel_id=1, source_target_pairs={{0,8},{8,16},{16,24},{1,9},{9,17},{17,25},{2,10},{10,18},{18,26},{... | collective-permute-start | bytes 55304 | tf_op jit(solution)/shard_map/ppermute | solution.py:178
  76.7 5.7 %collective-permute-start.17 = (f32[3,6,2,128]{3,2,1,0:T(2,128)S(1)}, f32[3,6,2,128]{3,2,1,0:T(2,128)S(1)}, u32[]{:S(2)}, u32[]{:S(2)}) collective-permute-start(f32[3,6,2,128]{3,2,1,0:T(2,128)S(1)} %pad_maximum_fusion.7), channel_id=1, source_target_pairs={{8,0},{16,8},{24,16},{9,1},{17,9},{25,17},{10,2},{18,10},{26,18},{... | collective-permute-start | bytes 55304 | tf_op jit(solution)/shard_map/ppermute | solution.py:178
  81.2 8.8 %collective-permute-start.11 = (bf16[2,2,3,64,128]{4,3,2,1,0:T(8,128)(2,1)S(1)}, bf16[2,2,3,64,128]{4,3,2,1,0:T(8,128)(2,1)S(1)}, u32[]{:S(2)}, u32[]{:S(2)}) collective-permute-start(bf16[2,2,3,64,128]{4,3,2,1,0:T(8,128)(2,1)S(1)} %get-tuple-element.51), channel_id=1, source_target_pairs={{0,1},{1,0},{2,3},{3,2},{4,5},{5,4},{6,7},{7,6},{8,9},{9,8},{10,11... | collective-permute-start | bytes 589832 | tf_op jit(solution)/shard_map/ppermute | solution.py:183
  85.3 4.7 %collective-permute-start.18 = (bf16[2,2,3,64,128]{4,3,2,1,0:T(8,128)(2,1)S(1)}, bf16[2,2,3,64,128]{4,3,2,1,0:T(8,128)(2,1)S(1)}, u32[]{:S(2)}, u32[]{:S(2)}) collective-permute-start(bf16[2,2,3,64,128]{4,3,2,1,0:T(8,128)(2,1)S(1)} %get-tuple-element.58), channel_id=1, source_target_pairs={{0,1},{1,0},{2,3},{3,2},{4,5},{5,4},{6,7},{7,6},{8,9},{9,8},{10,11... | collective-permute-start | bytes 589832 | tf_op jit(solution)/shard_map/ppermute | solution.py:183
  89.1 5.2 %collective-permute-start.19 = (bf16[2,2,3,64,128]{4,3,2,1,0:T(8,128)(2,1)S(1)}, bf16[2,2,3,64,128]{4,3,2,1,0:T(8,128)(2,1)S(1)}, u32[]{:S(2)}, u32[]{:S(2)}) collective-permute-start(bf16[2,2,3,64,128]{4,3,2,1,0:T(8,128)(2,1)S(1)} %get-tuple-element.71), channel_id=1, source_target_pairs={{0,1},{1,0},{2,3},{3,2},{4,5},{5,4},{6,7},{7,6},{8,9},{9,8},{10,11... | collective-permute-start | bytes 589832 | tf_op jit(solution)/shard_map/ppermute | solution.py:183

commit v12 on v11

--- a/solution.py
+++ b/solution.py
@@ -261,7 +261,7 @@
         return whole[0], whole[1]
 
     front_bias, back_bias = tile_biases(active, frames, columns_here, cells)
-    key_here = pair_of(keys, values, 0)
+    key_here, front_bias = lax.optimization_barrier((pair_of(keys, values, 0), front_bias))
     key_near = row_sides(key_here)
     key_sent = [pair_of(keys, values, shift) for shift in range(1, size)]
     key_moved = [turn(key_sent[size - b - 1], size - b) for b in range(1, size)]
@@ -270,7 +270,6 @@
     key_far = [row_sides(part) for part in key_moved]
     query_moved = [turn(query_held[size - b], size - b) for b in range(1, size)]
     query_all = jnp.stack(query_held[:1] + query_moved, 1)
-    query_all, key_near = lax.optimization_barrier((query_all, key_near))
     query_before, query_after = row_sides(query_all)
     key_parts, sides = [key_here] + key_moved, [key_near] + key_far
     key_halo = key_parts + [before for before, _ in sides] + [after for _, after in sides]

time: 97 us -> 96.2 us (level)
    another operation x3, local copies, waits for them, and re-layouts: 1.61 us -> 0.27 us  [the longest x1 1.38 us: pair_of(): return jnp.stack(picked, 1).reshape(frames, 2, groups, cells, dim)]
    dynamic_slice x9 -> x10, local copies, waits for them, and re-layouts: 0.36 us -> 1.65 us  [pair_of(): lax.dynamic_slice_in_dim(jnp.transpose(t, (0, 3, 1, 2, 4)), start, groups...]
    ppermute x6, waiting for transfers between devices: 9.32 us -> 10.5 us  [turn(): lax.ppermute(tensor, 'head', [(i, (i + shift) % size) for i in range(size)])]
  transfers between devices with their start and end apart: 20 -> 20, of which waited for: 6 -> 7; matrix products, arithmetic and copies ran while one was open for 6% -> 6% of each run, Pallas kernels for 18% -> 18%
where the time goes in v12:
time: 96.2 us; the launch traced here: 94.5 us
  starting transfers between devices  51.1 us (53%)
  waiting for transfers between devices  17.6 us (18%)
  Pallas kernels  16.7 us (17%)
  local copies, waits for them, and re-layouts  6.31 us (7%)
  between operations  1.37 us (1%)
    ppermute x14, starting transfers between devices, step_along(): lax.ppermute(tensor, axis, [(i, i + sign) for i in range(size) if 0 <= i...  45.3 us
    pallas_call x5, Pallas kernels, run(): pl.pallas_call(functools.partial(kernel, scaling, parts), grid=(count,),...  16.7 us
    ppermute x6, waiting for transfers between devices, turn(): lax.ppermute(tensor, 'head', [(i, (i + shift) % size) for i in range(size)])  10.5 us
    ppermute x14, waiting for transfers between devices, step_along(): lax.ppermute(tensor, axis, [(i, i + sign) for i in range(size) if 0 <= i...  7.1 us
    ppermute x6, starting transfers between devices, turn(): lax.ppermute(tensor, 'head', [(i, (i + shift) % size) for i in range(size)])  5.8 us
  transfers between devices with their start and end apart: 20, of which 7 were waited for; matrix products, arithmetic and copies ran while one was open for 6% of the time, Pallas kernels for 18%

profile of v12, /device:TPU:9, one launch (start us, length us, event | category | flops | bytes accessed | tf_op | source)
XLA Modules:
  0.0 94.5 jit_solution(9895304001295916573)
XLA Ops:
  0.7 1.3 %dynamic-slice_bitcast_fusion = (bf16[2,6,8,8,128]{4,3,1,2,0:T(8,128)(2,1)S(1)}, bf16[2,6,8,8,128]{4,3,1,2,0:T(8,128)(2,1)S(1)}, bf16[2,6,8,8,128]{4,3,1,2,0:T(8,128)(2,1)S(1)}, bf16[2,6,8,8,128]{4,3,1,2,0:T(8,128)(2,1)S(1)}) fusion(bf16[2,8,8,12,128]{4,2,3,1,0:T(8,128)(2,1)} %param.9, s32[]{:T(128)S(6)} %select_n.105, s32[]{:T(128)S(6)} %select_n.107, ...), kind=kLoop, calls=%fused_computation.66 | loop fusion | bytes 1572872 | tf_op jit(solution)/shard_map/dynamic_slice | solution.py:244
  2.1 1.3 %collective-permute-start = (bf16[2,2,6,64,128]{4,3,2,1,0:T(8,128)(2,1)S(1)}, bf16[2,2,6,64,128]{4,3,2,1,0:T(8,128)(2,1)S(1)}, u32[]{:S(2)}, u32[]{:S(2)}) collective-permute-start(bf16[2,2,6,64,128]{4,3,2,1,0:T(8,128)(2,1)S(1)} %pad_maximum_fusion.3), channel_id=1, source_target_pairs={{0,1},{1,0},{2,3},{3,2},{4,5},{5,4},{6,7},{7,6},{8,9},{9,8},{10,11... | collective-permute-start | bytes 1179656 | tf_op jit(solution)/shard_map/ppermute | solution.py:183
  6.2 3.2 %collective-permute-start.2 = (bf16[2,2,6,64,128]{4,3,2,1,0:T(8,128)(2,1)S(1)}, bf16[2,2,6,64,128]{4,3,2,1,0:T(8,128)(2,1)S(1)}, u32[]{:S(2)}, u32[]{:S(2)}) collective-permute-start(bf16[2,2,6,64,128]{4,3,2,1,0:T(8,128)(2,1)S(1)} %pad_maximum_fusion.4.refs_1_.refs_0_), channel_id=1, source_target_pairs={{0,2},{2,4},{4,6},{1,3},{3,5},{5,7},{8,10},{10,12},{12,14},{9,11},... | collective-permute-start | bytes 1179656 | tf_op jit(solution)/shard_map/ppermute | solution.py:178
  9.5 2.1 %collective-permute-start.4 = (bf16[2,2,6,64,128]{4,3,2,1,0:T(8,128)(2,1)S(1)}, bf16[2,2,6,64,128]{4,3,2,1,0:T(8,128)(2,1)S(1)}, u32[]{:S(2)}, u32[]{:S(2)}) collective-permute-start(bf16[2,2,6,64,128]{4,3,2,1,0:T(8,128)(2,1)S(1)} %pad_maximum_fusion.4.refs_1_.refs_0_), channel_id=1, source_target_pairs={{2,0},{4,2},{6,4},{3,1},{5,3},{7,5},{10,8},{12,10},{14,12},{11,9},... | collective-permute-start | bytes 1179656 | tf_op jit(solution)/shard_map/ppermute | solution.py:178
  12.2 3.2 %collective-permute-start.3 = (bf16[2,2,6,64,128]{4,3,2,1,0:T(8,128)(2,1)S(1)}, bf16[2,2,6,64,128]{4,3,2,1,0:T(8,128)(2,1)S(1)}, u32[]{:S(2)}, u32[]{:S(2)}) collective-permute-start(bf16[2,2,6,64,128]{4,3,2,1,0:T(8,128)(2,1)S(1)} %collective-permute-done.refs_2_.refs_1_), channel_id=1, source_target_pairs={{0,2},{2,4},{4,6},{1,3},{3,5},{5,7},{8,10},{10,12},{12,14},{9,11},... | collective-permute-start | bytes 1179656 | tf_op jit(solution)/shard_map/ppermute | solution.py:178
  15.4 2.1 %collective-permute-start.5 = (bf16[2,2,6,64,128]{4,3,2,1,0:T(8,128)(2,1)S(1)}, bf16[2,2,6,64,128]{4,3,2,1,0:T(8,128)(2,1)S(1)}, u32[]{:S(2)}, u32[]{:S(2)}) collective-permute-start(bf16[2,2,6,64,128]{4,3,2,1,0:T(8,128)(2,1)S(1)} %collective-permute-done.refs_2_.refs_1_), channel_id=1, source_target_pairs={{2,0},{4,2},{6,4},{3,1},{5,3},{7,5},{10,8},{12,10},{14,12},{11,9},... | collective-permute-start | bytes 1179656 | tf_op jit(solution)/shard_map/ppermute | solution.py:178
  17.5 1.3 %collective-permute-start.1 = (bf16[2,2,6,64,128]{4,3,2,1,0:T(8,128)(2,1)S(1)}, bf16[2,2,6,64,128]{4,3,2,1,0:T(8,128)(2,1)S(1)}, u32[]{:S(2)}, u32[]{:S(2)}) collective-permute-start(bf16[2,2,6,64,128]{4,3,2,1,0:T(8,128)(2,1)S(1)} %pad_maximum_fusion.2), channel_id=1, source_target_pairs={{0,1},{1,0},{2,3},{3,2},{4,5},{5,4},{6,7},{7,6},{8,9},{9,8},{10,11... | collective-permute-start | bytes 1179656 | tf_op jit(solution)/shard_map/ppermute | solution.py:183
  18.9 7.2 %collective-permute-done.1 = bf16[2,2,6,64,128]{4,3,2,1,0:T(8,128)(2,1)S(1)} collective-permute-done((bf16[2,2,6,64,128]{4,3,2,1,0:T(8,128)(2,1)S(1)}, bf16[2,2,6,64,128]{4,3,2,1,0:T(8,128)(2,1)S(1)}, u32[]{:S(2)}, u32[]{:S(2)}) %collective-permute-start.1) | collective-permute-done | bytes 393248 | tf_op jit(solution)/shard_map/ppermute | solution.py:183
  26.1 3.2 %collective-permute-start.12 = (bf16[2,2,2,6,64,128]{5,4,3,2,0,1:T(8,128)(2,1)S(1)}, bf16[2,2,2,6,64,128]{5,4,3,2,0,1:T(8,128)(2,1)S(1)}, u32[]{:S(2)}, u32[]{:S(2)}) collective-permute-start(bf16[2,2,2,6,64,128]{5,4,3,2,0,1:T(8,128)(2,1)S(1)} %pad_maximum_fusion), channel_id=1, source_target_pairs={{0,2},{2,4},{4,6},{1,3},{3,5},{5,7},{8,10},{10,12},{12,14},{9,11},... | collective-permute-start | bytes 2359304 | tf_op jit(solution)/shard_map/ppermute | solution.py:178
  29.5 2.1 %collective-permute-start.13 = (bf16[2,2,2,6,64,128]{5,4,3,2,1,0:T(8,128)(2,1)S(1)}, bf16[2,2,2,6,64,128]{5,4,3,2,1,0:T(8,128)(2,1)S(1)}, u32[]{:S(2)}, u32[]{:S(2)}) collective-permute-start(bf16[2,2,2,6,64,128]{5,4,3,2,1,0:T(8,128)(2,1)S(1)} %copy.57.refs_0_.refs_2_), channel_id=1, source_target_pairs={{2,0},{4,2},{6,4},{3,1},{5,3},{7,5},{10,8},{12,10},{14,12},{11,9},... | collective-permute-start | bytes 2359304 | tf_op jit(solution)/shard_map/ppermute | solution.py:178
  31.8 6.6 %collective-permute-start.6 = (bf16[6,2,6,64,128]{4,3,2,1,0:T(8,128)(2,1)S(1)}, bf16[6,2,6,64,128]{4,3,2,1,0:T(8,128)(2,1)S(1)}, u32[]{:S(2)}, u32[]{:S(2)}) collective-permute-start(bf16[6,2,6,64,128]{4,3,2,1,0:T(8,128)(2,1)S(1)} %get-tuple-element.87), channel_id=1, source_target_pairs={{0,8},{8,16},{16,24},{1,9},{9,17},{17,25},{2,10},{10,18},{18,26},{... | collective-permute-start | bytes 3538952 | tf_op jit(solution)/shard_map/ppermute | solution.py:178
  38.5 1.9 %collective-permute-start.7 = (bf16[6,2,6,64,128]{4,3,2,1,0:T(8,128)(2,1)S(1)}, bf16[6,2,6,64,128]{4,3,2,1,0:T(8,128)(2,1)S(1)}, u32[]{:S(2)}, u32[]{:S(2)}) collective-permute-start(bf16[6,2,6,64,128]{4,3,2,1,0:T(8,128)(2,1)S(1)} %get-tuple-element.86), channel_id=1, source_target_pairs={{8,0},{16,8},{24,16},{9,1},{17,9},{25,17},{10,2},{18,10},{26,18},{... | collective-permute-start | bytes 3538952 | tf_op jit(solution)/shard_map/ppermute | solution.py:178
  40.4 3.7 %collective-permute-done.12 = bf16[2,2,2,6,64,128]{5,4,3,2,0,1:T(8,128)(2,1)S(1)} collective-permute-done((bf16[2,2,2,6,64,128]{5,4,3,2,0,1:T(8,128)(2,1)S(1)}, bf16[2,2,2,6,64,128]{5,4,3,2,0,1:T(8,128)(2,1)S(1)}, u32[]{:S(2)}, u32[]{:S(2)}) %collective-permute-start.12) | collective-permute-done | bytes 786464 | tf_op jit(solution)/shard_map/ppermute | solution.py:178
  44.1 3.0 %collective-permute-done.13.refs_4_ = bf16[2,2,2,6,64,128]{5,4,3,2,1,0:T(8,128)(2,1)S(1)} collective-permute-done((bf16[2,2,2,6,64,128]{5,4,3,2,1,0:T(8,128)(2,1)S(1)}, bf16[2,2,2,6,64,128]{5,4,3,2,1,0:T(8,128)(2,1)S(1)}, u32[]{:S(2)}, u32[]{:S(2)}) %collective-permute-start.13) | collective-permute-done | bytes 786464 | tf_op jit(solution)/shard_map/ppermute | solution.py:178
  47.3 7.3 %collective-permute-start.14 = (bf16[6,2,6,64,128]{4,3,2,1,0:T(8,128)(2,1)S(1)}, bf16[6,2,6,64,128]{4,3,2,1,0:T(8,128)(2,1)S(1)}, u32[]{:S(2)}, u32[]{:S(2)}) collective-permute-start(bf16[6,2,6,64,128]{4,3,2,1,0:T(8,128)(2,1)S(1)} %get-tuple-element.75), channel_id=1, source_target_pairs={{0,8},{8,16},{16,24},{1,9},{9,17},{17,25},{2,10},{10,18},{18,26},{... | collective-permute-start | bytes 3538952 | tf_op jit(solution)/shard_map/ppermute | solution.py:178
  54.6 1.9 %collective-permute-start.15 = (bf16[6,2,6,64,128]{4,3,2,1,0:T(8,128)(2,1)S(1)}, bf16[6,2,6,64,128]{4,3,2,1,0:T(8,128)(2,1)S(1)}, u32[]{:S(2)}, u32[]{:S(2)}) collective-permute-start(bf16[6,2,6,64,128]{4,3,2,1,0:T(8,128)(2,1)S(1)} %get-tuple-element.74), channel_id=1, source_target_pairs={{8,0},{16,8},{24,16},{9,1},{17,9},{25,17},{10,2},{18,10},{26,18},{... | collective-permute-start | bytes 3538952 | tf_op jit(solution)/shard_map/ppermute | solution.py:178
  56.6 5.7 %shard_map.102 = (bf16[2,6,128,128]{3,2,1,0:T(8,128)(2,1)S(1)}, f32[2,6,2,128]{3,2,1,0:T(2,128)S(1)}) custom-call(bf16[2,2,2,6,64,128]{5,4,3,2,1,0:T(8,128)(2,1)S(1)} %copy.57.refs_0_.refs_2_, bf16[2,2,6,64,128]{4,3,2,1,0:T(8,128)(2,1)S(1)} %pad_maximum_fusion.4.refs_1_.refs_0_, bf16[2,2,6,64,128]{4,3,2,1,0:T(8,128)(2,1)S(1)} %collective-permute-done.refs_2_.refs_1_, ...), custom_call_target="tpu_custom_call" | custom-call | flops 6341787648 | bytes 4718592 | tf_op jit(solution)/shard_map/pallas_call | solution.py:159
  62.4 3.2 %collective-permute-start.9 = (f32[2,6,2,128]{3,2,1,0:T(2,128)S(1)}, f32[2,6,2,128]{3,2,1,0:T(2,128)S(1)}, u32[]{:S(2)}, u32[]{:S(2)}) collective-permute-start(f32[2,6,2,128]{3,2,1,0:T(2,128)S(1)} %get-tuple-element.47.refs_10_.refs_7_), channel_id=1, source_target_pairs={{0,2},{2,4},{4,6},{1,3},{3,5},{5,7},{8,10},{10,12},{12,14},{9,11},... | collective-permute-start | bytes 36872 | tf_op jit(solution)/shard_map/ppermute | solution.py:178
  65.6 2.1 %collective-permute-start.10 = (f32[2,6,2,128]{3,2,1,0:T(2,128)S(1)}, f32[2,6,2,128]{3,2,1,0:T(2,128)S(1)}, u32[]{:S(2)}, u32[]{:S(2)}) collective-permute-start(f32[2,6,2,128]{3,2,1,0:T(2,128)S(1)} %get-tuple-element.47.refs_10_.refs_7_), channel_id=1, source_target_pairs={{2,0},{4,2},{6,4},{3,1},{5,3},{7,5},{10,8},{12,10},{14,12},{11,9},... | collective-permute-start | bytes 36872 | tf_op jit(solution)/shard_map/ppermute | solution.py:178
  67.6 2.5 %shard_map.103 = (bf16[2,2,3,64,128]{4,3,2,1,0:T(8,128)(2,1)S(1)}, bf16[2,2,3,64,128]{4,3,2,1,0:T(8,128)(2,1)S(1)}) custom-call(bf16[2,2,2,6,64,128]{5,4,3,2,1,0:T(8,128)(2,1)S(1)} %copy.57.refs_0_.refs_2_, bf16[2,2,6,64,128]{4,3,2,1,0:T(8,128)(2,1)S(1)} %pad_maximum_fusion.4.refs_1_.refs_0_, ...), custom_call_target="tpu_custom_call" | custom-call | flops 4756340736 | bytes 2359296 | tf_op jit(solution)/shard_map/pallas_call | solution.py:159
  70.2 1.3 %collective-permute-start.8 = (bf16[2,2,3,64,128]{4,3,2,1,0:T(8,128)(2,1)S(1)}, bf16[2,2,3,64,128]{4,3,2,1,0:T(8,128)(2,1)S(1)}, u32[]{:S(2)}, u32[]{:S(2)}) collective-permute-start(bf16[2,2,3,64,128]{4,3,2,1,0:T(8,128)(2,1)S(1)} %get-tuple-element.46), channel_id=1, source_target_pairs={{0,1},{1,0},{2,3},{3,2},{4,5},{5,4},{6,7},{7,6},{8,9},{9,8},{10,11... | collective-permute-start | bytes 589832 | tf_op jit(solution)/shard_map/ppermute | solution.py:183
  71.5 4.5 %collective-permute-start.16 = (f32[3,6,2,128]{3,2,1,0:T(2,128)S(1)}, f32[3,6,2,128]{3,2,1,0:T(2,128)S(1)}, u32[]{:S(2)}, u32[]{:S(2)}) collective-permute-start(f32[3,6,2,128]{3,2,1,0:T(2,128)S(1)} %pad_maximum_fusion.5), channel_id=1, source_target_pairs={{0,8},{8,16},{16,24},{1,9},{9,17},{17,25},{2,10},{10,18},{18,26},{... | collective-permute-start | bytes 55304 | tf_op jit(solution)/shard_map/ppermute | solution.py:178
  76.0 1.9 %collective-permute-start.17 = (f32[3,6,2,128]{3,2,1,0:T(2,128)S(1)}, f32[3,6,2,128]{3,2,1,0:T(2,128)S(1)}, u32[]{:S(2)}, u32[]{:S(2)}) collective-permute-start(f32[3,6,2,128]{3,2,1,0:T(2,128)S(1)} %pad_maximum_fusion.6), channel_id=1, source_target_pairs={{8,0},{16,8},{24,16},{9,1},{17,9},{25,17},{10,2},{18,10},{26,18},{... | collective-permute-start | bytes 55304 | tf_op jit(solution)/shard_map/ppermute | solution.py:178
  77.9 2.6 %shard_map.104 = (bf16[2,2,3,64,128]{4,3,2,1,0:T(8,128)(2,1)S(1)}, bf16[2,2,3,64,128]{4,3,2,1,0:T(8,128)(2,1)S(1)}) custom-call(bf16[2,2,2,6,64,128]{5,4,3,2,1,0:T(8,128)(2,1)S(1)} %copy.57.refs_0_.refs_2_, bf16[2,2,6,64,128]{4,3,2,1,0:T(8,128)(2,1)S(1)} %pad_maximum_fusion.4.refs_1_.refs_0_, ...), custom_call_target="tpu_custom_call" | custom-call | flops 4756340736 | bytes 2359296 | tf_op jit(solution)/shard_map/pallas_call | solution.py:159
  81.4 2.9 %shard_map.105 = (bf16[2,2,3,64,128]{4,3,2,1,0:T(8,128)(2,1)S(1)}, bf16[2,2,3,64,128]{4,3,2,1,0:T(8,128)(2,1)S(1)}) custom-call(bf16[2,2,6,64,128]{4,3,2,1,0:T(8,128)(2,1)S(1)} %pad_maximum_fusion.4.refs_1_.refs_0_, bf16[2,2,6,64,128]{4,3,2,1,0:T(8,128)(2,1)S(1)} %collective-permute-done.refs_2_.refs_1_, ...), custom_call_target="tpu_custom_call" | custom-call | flops 6341787648 | bytes 2359296 | tf_op jit(solution)/shard_map/pallas_call | solution.py:159
  84.3 0.8 collective-permute-start.18
  85.1 2.9 %shard_map.106 = (bf16[2,2,3,64,128]{4,3,2,1,0:T(8,128)(2,1)S(1)}, bf16[2,2,3,64,128]{4,3,2,1,0:T(8,128)(2,1)S(1)}) custom-call(bf16[2,2,6,64,128]{4,3,2,1,0:T(8,128)(2,1)S(1)} %pad_maximum_fusion.4.refs_1_.refs_0_, bf16[2,2,6,64,128]{4,3,2,1,0:T(8,128)(2,1)S(1)} %collective-permute-done.refs_2_.refs_1_, ...), custom_call_target="tpu_custom_call" | custom-call | flops 6341787648 | bytes 2359296 | tf_op jit(solution)/shard_map/pallas_call | solution.py:159
  88.0 0.8 collective-permute-start.19
  89.1 1.0 %collective-permute-done.18 = bf16[2,2,3,64,128]{4,3,2,1,0:T(8,128)(2,1)S(1)} collective-permute-done((bf16[2,2,3,64,128]{4,3,2,1,0:T(8,128)(2,1)S(1)}, bf16[2,2,3,64,128]{4,3,2,1,0:T(8,128)(2,1)S(1)}, u32[]{:S(2)}, u32[]{:S(2)}) %collective-permute-start.18) | collective-permute-done | bytes 196640 | tf_op jit(solution)/shard_map/ppermute | solution.py:183
  90.5 0.9 slice_bitcast_fusion.2
  91.5 2.0 %collective-permute-done.19 = bf16[2,2,3,64,128]{4,3,2,1,0:T(8,128)(2,1)S(1)} collective-permute-done((bf16[2,2,3,64,128]{4,3,2,1,0:T(8,128)(2,1)S(1)}, bf16[2,2,3,64,128]{4,3,2,1,0:T(8,128)(2,1)S(1)}, u32[]{:S(2)}, u32[]{:S(2)}) %collective-permute-start.19) | collective-permute-done | bytes 196640 | tf_op jit(solution)/shard_map/ppermute | solution.py:183
  93.6 0.9 slice_bitcast_fusion
  (101 shorter events, 5.7 us)
Async XLA Ops:
  2.0 1.7 %copy-start.3 = (s32[8,4,2,27]{3,2,1,0:T(2,128)S(1)}, s32[8,4,2,27]{3,2,1,0:T(2,128)}, u32[]{:S(2)}) copy-start(s32[8,4,2,27]{3,2,1,0:T(2,128)} %param.11) | copy-start | bytes 20740
  2.0 3.3 %copy-start.4 = (bf16[4,3,9,2,9,1]{4,2,1,0,5,3:T(8,128)(2,1)S(1)}, bf16[4,3,9,2,9,1]{4,2,1,0,5,3:T(8,128)(2,1)}, u32[]{:S(2)}) copy-start(bf16[4,3,9,2,9,1]{4,2,1,0,5,3:T(8,128)(2,1)} %constant.219) | copy-start | bytes 11668
  2.1 3.9 %copy-start.2 = (bf16[18,1152]{1,0:T(8,128)(2,1)S(1)}, bf16[18,1152]{1,0:T(8,128)(2,1)}, u32[]{:S(2)}) copy-start(bf16[18,1152]{1,0:T(8,128)(2,1)} %constant.114.clone) | copy-start | bytes 124420
  2.1 10.0 %collective-permute-start = (bf16[2,2,6,64,128]{4,3,2,1,0:T(8,128)(2,1)S(1)}, bf16[2,2,6,64,128]{4,3,2,1,0:T(8,128)(2,1)S(1)}, u32[]{:S(2)}, u32[]{:S(2)}) collective-permute-start(bf16[2,2,6,64,128]{4,3,2,1,0:T(8,128)(2,1)S(1)} %pad_maximum_fusion.3), channel_id=1, source_target_pairs={{0,1},{1,0},{2,3},{3,2},{4,5},{5,4},{6,7},{7,6},{8,9},{9,8},{10,11... | collective-permute-start | bytes 1179656 | tf_op jit(solution)/shard_map/ppermute | solution.py:183
  3.6 8.0 %copy-start = (bf16[2,8,8,12,128]{4,2,3,1,0:T(8,128)(2,1)S(1)}, bf16[2,8,8,12,128]{4,2,3,1,0:T(8,128)(2,1)}, u32[]{:S(2)}) copy-start(bf16[2,8,8,12,128]{4,2,3,1,0:T(8,128)(2,1)} %param.10) | copy-start | bytes 1179652
  3.6 8.0 %copy-start.1 = (bf16[2,8,8,12,128]{4,2,3,1,0:T(8,128)(2,1)S(1)}, bf16[2,8,8,12,128]{4,2,3,1,0:T(8,128)(2,1)}, u32[]{:S(2)}) copy-start(bf16[2,8,8,12,128]{4,2,3,1,0:T(8,128)(2,1)} %param.7) | copy-start | bytes 1179652
  6.2 12.5 %collective-permute-start.2 = (bf16[2,2,6,64,128]{4,3,2,1,0:T(8,128)(2,1)S(1)}, bf16[2,2,6,64,128]{4,3,2,1,0:T(8,128)(2,1)S(1)}, u32[]{:S(2)}, u32[]{:S(2)}) collective-permute-start(bf16[2,2,6,64,128]{4,3,2,1,0:T(8,128)(2,1)S(1)} %pad_maximum_fusion.4.refs_1_.refs_0_), channel_id=1, source_target_pairs={{0,2},{2,4},{4,6},{1,3},{3,5},{5,7},{8,10},{10,12},{12,14},{9,11},... | collective-permute-start | bytes 1179656 | tf_op jit(solution)/shard_map/ppermute | solution.py:178
  9.5 19.9 %collective-permute-start.4 = (bf16[2,2,6,64,128]{4,3,2,1,0:T(8,128)(2,1)S(1)}, bf16[2,2,6,64,128]{4,3,2,1,0:T(8,128)(2,1)S(1)}, u32[]{:S(2)}, u32[]{:S(2)}) collective-permute-start(bf16[2,2,6,64,128]{4,3,2,1,0:T(8,128)(2,1)S(1)} %pad_maximum_fusion.4.refs_1_.refs_0_), channel_id=1, source_target_pairs={{2,0},{4,2},{6,4},{3,1},{5,3},{7,5},{10,8},{12,10},{14,12},{11,9},... | collective-permute-start | bytes 1179656 | tf_op jit(solution)/shard_map/ppermute | solution.py:178
  12.2 19.4 %collective-permute-start.3 = (bf16[2,2,6,64,128]{4,3,2,1,0:T(8,128)(2,1)S(1)}, bf16[2,2,6,64,128]{4,3,2,1,0:T(8,128)(2,1)S(1)}, u32[]{:S(2)}, u32[]{:S(2)}) collective-permute-start(bf16[2,2,6,64,128]{4,3,2,1,0:T(8,128)(2,1)S(1)} %collective-permute-done.refs_2_.refs_1_), channel_id=1, source_target_pairs={{0,2},{2,4},{4,6},{1,3},{3,5},{5,7},{8,10},{10,12},{12,14},{9,11},... | collective-permute-start | bytes 1179656 | tf_op jit(solution)/shard_map/ppermute | solution.py:178
  15.4 16.4 %collective-permute-start.5 = (bf16[2,2,6,64,128]{4,3,2,1,0:T(8,128)(2,1)S(1)}, bf16[2,2,6,64,128]{4,3,2,1,0:T(8,128)(2,1)S(1)}, u32[]{:S(2)}, u32[]{:S(2)}) collective-permute-start(bf16[2,2,6,64,128]{4,3,2,1,0:T(8,128)(2,1)S(1)} %collective-permute-done.refs_2_.refs_1_), channel_id=1, source_target_pairs={{2,0},{4,2},{6,4},{3,1},{5,3},{7,5},{10,8},{12,10},{14,12},{11,9},... | collective-permute-start | bytes 1179656 | tf_op jit(solution)/shard_map/ppermute | solution.py:178
  17.5 8.6 %collective-permute-start.1 = (bf16[2,2,6,64,128]{4,3,2,1,0:T(8,128)(2,1)S(1)}, bf16[2,2,6,64,128]{4,3,2,1,0:T(8,128)(2,1)S(1)}, u32[]{:S(2)}, u32[]{:S(2)}) collective-permute-start(bf16[2,2,6,64,128]{4,3,2,1,0:T(8,128)(2,1)S(1)} %pad_maximum_fusion.2), channel_id=1, source_target_pairs={{0,1},{1,0},{2,3},{3,2},{4,5},{5,4},{6,7},{7,6},{8,9},{9,8},{10,11... | collective-permute-start | bytes 1179656 | tf_op jit(solution)/shard_map/ppermute | solution.py:183
  26.1 17.9 %collective-permute-start.12 = (bf16[2,2,2,6,64,128]{5,4,3,2,0,1:T(8,128)(2,1)S(1)}, bf16[2,2,2,6,64,128]{5,4,3,2,0,1:T(8,128)(2,1)S(1)}, u32[]{:S(2)}, u32[]{:S(2)}) collective-permute-start(bf16[2,2,2,6,64,128]{5,4,3,2,0,1:T(8,128)(2,1)S(1)} %pad_maximum_fusion), channel_id=1, source_target_pairs={{0,2},{2,4},{4,6},{1,3},{3,5},{5,7},{8,10},{10,12},{12,14},{9,11},... | collective-permute-start | bytes 2359304 | tf_op jit(solution)/shard_map/ppermute | solution.py:178
  29.5 17.6 %collective-permute-start.13 = (bf16[2,2,2,6,64,128]{5,4,3,2,1,0:T(8,128)(2,1)S(1)}, bf16[2,2,2,6,64,128]{5,4,3,2,1,0:T(8,128)(2,1)S(1)}, u32[]{:S(2)}, u32[]{:S(2)}) collective-permute-start(bf16[2,2,2,6,64,128]{5,4,3,2,1,0:T(8,128)(2,1)S(1)} %copy.57.refs_0_.refs_2_), channel_id=1, source_target_pairs={{2,0},{4,2},{6,4},{3,1},{5,3},{7,5},{10,8},{12,10},{14,12},{11,9},... | collective-permute-start | bytes 2359304 | tf_op jit(solution)/shard_map/ppermute | solution.py:178
  31.8 24.8 %collective-permute-start.6 = (bf16[6,2,6,64,128]{4,3,2,1,0:T(8,128)(2,1)S(1)}, bf16[6,2,6,64,128]{4,3,2,1,0:T(8,128)(2,1)S(1)}, u32[]{:S(2)}, u32[]{:S(2)}) collective-permute-start(bf16[6,2,6,64,128]{4,3,2,1,0:T(8,128)(2,1)S(1)} %get-tuple-element.87), channel_id=1, source_target_pairs={{0,8},{8,16},{16,24},{1,9},{9,17},{17,25},{2,10},{10,18},{18,26},{... | collective-permute-start | bytes 3538952 | tf_op jit(solution)/shard_map/ppermute | solution.py:178
  38.5 18.1 %collective-permute-start.7 = (bf16[6,2,6,64,128]{4,3,2,1,0:T(8,128)(2,1)S(1)}, bf16[6,2,6,64,128]{4,3,2,1,0:T(8,128)(2,1)S(1)}, u32[]{:S(2)}, u32[]{:S(2)}) collective-permute-start(bf16[6,2,6,64,128]{4,3,2,1,0:T(8,128)(2,1)S(1)} %get-tuple-element.86), channel_id=1, source_target_pairs={{8,0},{16,8},{24,16},{9,1},{17,9},{25,17},{10,2},{18,10},{26,18},{... | collective-permute-start | bytes 3538952 | tf_op jit(solution)/shard_map/ppermute | solution.py:178
  47.3 34.1 %collective-permute-start.14 = (bf16[6,2,6,64,128]{4,3,2,1,0:T(8,128)(2,1)S(1)}, bf16[6,2,6,64,128]{4,3,2,1,0:T(8,128)(2,1)S(1)}, u32[]{:S(2)}, u32[]{:S(2)}) collective-permute-start(bf16[6,2,6,64,128]{4,3,2,1,0:T(8,128)(2,1)S(1)} %get-tuple-element.75), channel_id=1, source_target_pairs={{0,8},{8,16},{16,24},{1,9},{9,17},{17,25},{2,10},{10,18},{18,26},{... | collective-permute-start | bytes 3538952 | tf_op jit(solution)/shard_map/ppermute | solution.py:178
  54.6 26.8 %collective-permute-start.15 = (bf16[6,2,6,64,128]{4,3,2,1,0:T(8,128)(2,1)S(1)}, bf16[6,2,6,64,128]{4,3,2,1,0:T(8,128)(2,1)S(1)}, u32[]{:S(2)}, u32[]{:S(2)}) collective-permute-start(bf16[6,2,6,64,128]{4,3,2,1,0:T(8,128)(2,1)S(1)} %get-tuple-element.74), channel_id=1, source_target_pairs={{8,0},{16,8},{24,16},{9,1},{17,9},{25,17},{10,2},{18,10},{26,18},{... | collective-permute-start | bytes 3538952 | tf_op jit(solution)/shard_map/ppermute | solution.py:178
  62.4 9.1 %collective-permute-start.9 = (f32[2,6,2,128]{3,2,1,0:T(2,128)S(1)}, f32[2,6,2,128]{3,2,1,0:T(2,128)S(1)}, u32[]{:S(2)}, u32[]{:S(2)}) collective-permute-start(f32[2,6,2,128]{3,2,1,0:T(2,128)S(1)} %get-tuple-element.47.refs_10_.refs_7_), channel_id=1, source_target_pairs={{0,2},{2,4},{4,6},{1,3},{3,5},{5,7},{8,10},{10,12},{12,14},{9,11},... | collective-permute-start | bytes 36872 | tf_op jit(solution)/shard_map/ppermute | solution.py:178
  65.6 5.9 %collective-permute-start.10 = (f32[2,6,2,128]{3,2,1,0:T(2,128)S(1)}, f32[2,6,2,128]{3,2,1,0:T(2,128)S(1)}, u32[]{:S(2)}, u32[]{:S(2)}) collective-permute-start(f32[2,6,2,128]{3,2,1,0:T(2,128)S(1)} %get-tuple-element.47.refs_10_.refs_7_), channel_id=1, source_target_pairs={{2,0},{4,2},{6,4},{3,1},{5,3},{7,5},{10,8},{12,10},{14,12},{11,9},... | collective-permute-start | bytes 36872 | tf_op jit(solution)/shard_map/ppermute | solution.py:178
  70.2 18.8 %collective-permute-start.8 = (bf16[2,2,3,64,128]{4,3,2,1,0:T(8,128)(2,1)S(1)}, bf16[2,2,3,64,128]{4,3,2,1,0:T(8,128)(2,1)S(1)}, u32[]{:S(2)}, u32[]{:S(2)}) collective-permute-start(bf16[2,2,3,64,128]{4,3,2,1,0:T(8,128)(2,1)S(1)} %get-tuple-element.46), channel_id=1, source_target_pairs={{0,1},{1,0},{2,3},{3,2},{4,5},{5,4},{6,7},{7,6},{8,9},{9,8},{10,11... | collective-permute-start | bytes 589832 | tf_op jit(solution)/shard_map/ppermute | solution.py:183
  71.5 9.0 %collective-permute-start.16 = (f32[3,6,2,128]{3,2,1,0:T(2,128)S(1)}, f32[3,6,2,128]{3,2,1,0:T(2,128)S(1)}, u32[]{:S(2)}, u32[]{:S(2)}) collective-permute-start(f32[3,6,2,128]{3,2,1,0:T(2,128)S(1)} %pad_maximum_fusion.5), channel_id=1, source_target_pairs={{0,8},{8,16},{16,24},{1,9},{9,17},{17,25},{2,10},{10,18},{18,26},{... | collective-permute-start | bytes 55304 | tf_op jit(solution)/shard_map/ppermute | solution.py:178
  76.0 5.4 %collective-permute-start.17 = (f32[3,6,2,128]{3,2,1,0:T(2,128)S(1)}, f32[3,6,2,128]{3,2,1,0:T(2,128)S(1)}, u32[]{:S(2)}, u32[]{:S(2)}) collective-permute-start(f32[3,6,2,128]{3,2,1,0:T(2,128)S(1)} %pad_maximum_fusion.6), channel_id=1, source_target_pairs={{8,0},{16,8},{24,16},{9,1},{17,9},{25,17},{10,2},{18,10},{26,18},{... | collective-permute-start | bytes 55304 | tf_op jit(solution)/shard_map/ppermute | solution.py:178
  80.5 8.5 %collective-permute-start.11 = (bf16[2,2,3,64,128]{4,3,2,1,0:T(8,128)(2,1)S(1)}, bf16[2,2,3,64,128]{4,3,2,1,0:T(8,128)(2,1)S(1)}, u32[]{:S(2)}, u32[]{:S(2)}) collective-permute-start(bf16[2,2,3,64,128]{4,3,2,1,0:T(8,128)(2,1)S(1)} %get-tuple-element.49), channel_id=1, source_target_pairs={{0,1},{1,0},{2,3},{3,2},{4,5},{5,4},{6,7},{7,6},{8,9},{9,8},{10,11... | collective-permute-start | bytes 589832 | tf_op jit(solution)/shard_map/ppermute | solution.py:183
  84.3 5.8 %collective-permute-start.18 = (bf16[2,2,3,64,128]{4,3,2,1,0:T(8,128)(2,1)S(1)}, bf16[2,2,3,64,128]{4,3,2,1,0:T(8,128)(2,1)S(1)}, u32[]{:S(2)}, u32[]{:S(2)}) collective-permute-start(bf16[2,2,3,64,128]{4,3,2,1,0:T(8,128)(2,1)S(1)} %get-tuple-element.56), channel_id=1, source_target_pairs={{0,1},{1,0},{2,3},{3,2},{4,5},{5,4},{6,7},{7,6},{8,9},{9,8},{10,11... | collective-permute-start | bytes 589832 | tf_op jit(solution)/shard_map/ppermute | solution.py:183
  88.0 5.5 %collective-permute-start.19 = (bf16[2,2,3,64,128]{4,3,2,1,0:T(8,128)(2,1)S(1)}, bf16[2,2,3,64,128]{4,3,2,1,0:T(8,128)(2,1)S(1)}, u32[]{:S(2)}, u32[]{:S(2)}) collective-permute-start(bf16[2,2,3,64,128]{4,3,2,1,0:T(8,128)(2,1)S(1)} %get-tuple-element.69), channel_id=1, source_target_pairs={{0,1},{1,0},{2,3},{3,2},{4,5},{5,4},{6,7},{7,6},{8,9},{9,8},{10,11... | collective-permute-start | bytes 589832 | tf_op jit(solution)/shard_map/ppermute | solution.py:183

commit v13 on v12

--- a/solution.py
+++ b/solution.py
@@ -251,14 +251,16 @@
         ]
 
     def assemble(blocks):
-        whole = jnp.zeros((2, frames, rows, heads, columns_here, dim), jnp.bfloat16)
-        for first, pieces in blocks:
-            for b, piece in enumerate(pieces):
-                piece = piece.reshape((2, frames, -1, rows, columns_here, dim)).transpose(0, 1, 3, 2, 4, 5)
-                start = (me + size - b) % size * groups + first
-                whole = lax.dynamic_update_slice_in_dim(whole, piece, start, 3)
-        whole = jnp.transpose(whole, (0, 1, 2, 4, 3, 5))
-        return whole[0], whole[1]
+        outs = []
+        for which in range(2):
+            whole = jnp.zeros((frames, rows, heads, columns_here, dim), jnp.bfloat16)
+            for first, pieces in blocks:
+                for b, piece in enumerate(pieces):
+                    piece = piece[which].reshape((frames, -1, rows, columns_here, dim)).transpose(0, 2, 1, 3, 4)
+                    start = (me + size - b) % size * groups + first
+                    whole = lax.dynamic_update_slice_in_dim(whole, piece, start, 2)
+            outs.append(jnp.transpose(whole, (0, 1, 3, 2, 4)))
+        return tuple(outs)
 
     front_bias, back_bias = tile_biases(active, frames, columns_here, cells)
     key_here, front_bias = lax.optimization_barrier((pair_of(keys, values, 0), front_bias))

time: 96.2 us -> 96.1 us (level)
    squeeze x2 -> x0, local copies, waits for them, and re-layouts: 1.88 us -> none  [assemble(): return (whole[0], whole[1])]
  transfers between devices with their start and end apart: 20 -> 20, of which waited for: 7 -> 7; matrix products, arithmetic and copies ran while one was open for 6% -> 5% of each run, Pallas kernels for 18% -> 18%
where the time goes in v13:
time: 96.1 us; the launch traced here: 94.5 us
  starting transfers between devices  51.1 us (53%)
  waiting for transfers between devices  18.1 us (19%)
  Pallas kernels  16.7 us (17%)
  local copies, waits for them, and re-layouts  5.44 us (6%)
  between operations  1.57 us (2%)
    ppermute x14, starting transfers between devices, step_along(): lax.ppermute(tensor, axis, [(i, i + sign) for i in range(size) if 0 <= i...  45.3 us
    pallas_call x5, Pallas kernels, run(): pl.pallas_call(functools.partial(kernel, scaling, parts), grid=(count,),...  16.7 us
    ppermute x6, waiting for transfers between devices, turn(): lax.ppermute(tensor, 'head', [(i, (i + shift) % size) for i in range(size)])  11 us
    ppermute x14, waiting for transfers between devices, step_along(): lax.ppermute(tensor, axis, [(i, i + sign) for i in range(size) if 0 <= i...  7.1 us
    ppermute x6, starting transfers between devices, turn(): lax.ppermute(tensor, 'head', [(i, (i + shift) % size) for i in range(size)])  5.8 us
  transfers between devices with their start and end apart: 20, of which 7 were waited for; matrix products, arithmetic and copies ran while one was open for 5% of the time, Pallas kernels for 18%

profile of v13, /device:TPU:9, one launch (start us, length us, event | category | flops | bytes accessed | tf_op | source)
XLA Modules:
  0.0 94.5 jit_solution(15166634598074056814)
XLA Ops:
  0.7 1.3 %dynamic-slice_bitcast_fusion = (bf16[2,6,8,8,128]{4,3,1,2,0:T(8,128)(2,1)S(1)}, bf16[2,6,8,8,128]{4,3,1,2,0:T(8,128)(2,1)S(1)}, bf16[2,6,8,8,128]{4,3,1,2,0:T(8,128)(2,1)S(1)}, bf16[2,6,8,8,128]{4,3,1,2,0:T(8,128)(2,1)S(1)}) fusion(bf16[2,8,8,12,128]{4,2,3,1,0:T(8,128)(2,1)} %param.9, s32[]{:T(128)S(6)} %select_n.129, s32[]{:T(128)S(6)} %select_n.131, ...), kind=kLoop, calls=%fused_computation.54 | loop fusion | bytes 1572872 | tf_op jit(solution)/shard_map/dynamic_slice | solution.py:244
  2.1 1.3 %collective-permute-start = (bf16[2,2,6,64,128]{4,3,2,1,0:T(8,128)(2,1)S(1)}, bf16[2,2,6,64,128]{4,3,2,1,0:T(8,128)(2,1)S(1)}, u32[]{:S(2)}, u32[]{:S(2)}) collective-permute-start(bf16[2,2,6,64,128]{4,3,2,1,0:T(8,128)(2,1)S(1)} %pad_maximum_fusion.3), channel_id=1, source_target_pairs={{0,1},{1,0},{2,3},{3,2},{4,5},{5,4},{6,7},{7,6},{8,9},{9,8},{10,11... | collective-permute-start | bytes 1179656 | tf_op jit(solution)/shard_map/ppermute | solution.py:183
  6.2 3.2 %collective-permute-start.2 = (bf16[2,2,6,64,128]{4,3,2,1,0:T(8,128)(2,1)S(1)}, bf16[2,2,6,64,128]{4,3,2,1,0:T(8,128)(2,1)S(1)}, u32[]{:S(2)}, u32[]{:S(2)}) collective-permute-start(bf16[2,2,6,64,128]{4,3,2,1,0:T(8,128)(2,1)S(1)} %pad_maximum_fusion.4.refs_1_.refs_0_), channel_id=1, source_target_pairs={{0,2},{2,4},{4,6},{1,3},{3,5},{5,7},{8,10},{10,12},{12,14},{9,11},... | collective-permute-start | bytes 1179656 | tf_op jit(solution)/shard_map/ppermute | solution.py:178
  9.5 2.1 %collective-permute-start.4 = (bf16[2,2,6,64,128]{4,3,2,1,0:T(8,128)(2,1)S(1)}, bf16[2,2,6,64,128]{4,3,2,1,0:T(8,128)(2,1)S(1)}, u32[]{:S(2)}, u32[]{:S(2)}) collective-permute-start(bf16[2,2,6,64,128]{4,3,2,1,0:T(8,128)(2,1)S(1)} %pad_maximum_fusion.4.refs_1_.refs_0_), channel_id=1, source_target_pairs={{2,0},{4,2},{6,4},{3,1},{5,3},{7,5},{10,8},{12,10},{14,12},{11,9},... | collective-permute-start | bytes 1179656 | tf_op jit(solution)/shard_map/ppermute | solution.py:178
  12.2 3.2 %collective-permute-start.3 = (bf16[2,2,6,64,128]{4,3,2,1,0:T(8,128)(2,1)S(1)}, bf16[2,2,6,64,128]{4,3,2,1,0:T(8,128)(2,1)S(1)}, u32[]{:S(2)}, u32[]{:S(2)}) collective-permute-start(bf16[2,2,6,64,128]{4,3,2,1,0:T(8,128)(2,1)S(1)} %collective-permute-done.refs_2_.refs_1_), channel_id=1, source_target_pairs={{0,2},{2,4},{4,6},{1,3},{3,5},{5,7},{8,10},{10,12},{12,14},{9,11},... | collective-permute-start | bytes 1179656 | tf_op jit(solution)/shard_map/ppermute | solution.py:178
  15.4 2.1 %collective-permute-start.5 = (bf16[2,2,6,64,128]{4,3,2,1,0:T(8,128)(2,1)S(1)}, bf16[2,2,6,64,128]{4,3,2,1,0:T(8,128)(2,1)S(1)}, u32[]{:S(2)}, u32[]{:S(2)}) collective-permute-start(bf16[2,2,6,64,128]{4,3,2,1,0:T(8,128)(2,1)S(1)} %collective-permute-done.refs_2_.refs_1_), channel_id=1, source_target_pairs={{2,0},{4,2},{6,4},{3,1},{5,3},{7,5},{10,8},{12,10},{14,12},{11,9},... | collective-permute-start | bytes 1179656 | tf_op jit(solution)/shard_map/ppermute | solution.py:178
  17.5 1.3 %collective-permute-start.1 = (bf16[2,2,6,64,128]{4,3,2,1,0:T(8,128)(2,1)S(1)}, bf16[2,2,6,64,128]{4,3,2,1,0:T(8,128)(2,1)S(1)}, u32[]{:S(2)}, u32[]{:S(2)}) collective-permute-start(bf16[2,2,6,64,128]{4,3,2,1,0:T(8,128)(2,1)S(1)} %pad_maximum_fusion.2), channel_id=1, source_target_pairs={{0,1},{1,0},{2,3},{3,2},{4,5},{5,4},{6,7},{7,6},{8,9},{9,8},{10,11... | collective-permute-start | bytes 1179656 | tf_op jit(solution)/shard_map/ppermute | solution.py:183
  18.9 7.2 %collective-permute-done.1 = bf16[2,2,6,64,128]{4,3,2,1,0:T(8,128)(2,1)S(1)} collective-permute-done((bf16[2,2,6,64,128]{4,3,2,1,0:T(8,128)(2,1)S(1)}, bf16[2,2,6,64,128]{4,3,2,1,0:T(8,128)(2,1)S(1)}, u32[]{:S(2)}, u32[]{:S(2)}) %collective-permute-start.1) | collective-permute-done | bytes 393248 | tf_op jit(solution)/shard_map/ppermute | solution.py:183
  26.1 3.2 %collective-permute-start.12 = (bf16[2,2,2,6,64,128]{5,4,3,2,0,1:T(8,128)(2,1)S(1)}, bf16[2,2,2,6,64,128]{5,4,3,2,0,1:T(8,128)(2,1)S(1)}, u32[]{:S(2)}, u32[]{:S(2)}) collective-permute-start(bf16[2,2,2,6,64,128]{5,4,3,2,0,1:T(8,128)(2,1)S(1)} %pad_maximum_fusion), channel_id=1, source_target_pairs={{0,2},{2,4},{4,6},{1,3},{3,5},{5,7},{8,10},{10,12},{12,14},{9,11},... | collective-permute-start | bytes 2359304 | tf_op jit(solution)/shard_map/ppermute | solution.py:178
  29.5 2.1 %collective-permute-start.13 = (bf16[2,2,2,6,64,128]{5,4,3,2,1,0:T(8,128)(2,1)S(1)}, bf16[2,2,2,6,64,128]{5,4,3,2,1,0:T(8,128)(2,1)S(1)}, u32[]{:S(2)}, u32[]{:S(2)}) collective-permute-start(bf16[2,2,2,6,64,128]{5,4,3,2,1,0:T(8,128)(2,1)S(1)} %copy.65.refs_0_.refs_2_), channel_id=1, source_target_pairs={{2,0},{4,2},{6,4},{3,1},{5,3},{7,5},{10,8},{12,10},{14,12},{11,9},... | collective-permute-start | bytes 2359304 | tf_op jit(solution)/shard_map/ppermute | solution.py:178
  31.8 6.6 %collective-permute-start.6 = (bf16[6,2,6,64,128]{4,3,2,1,0:T(8,128)(2,1)S(1)}, bf16[6,2,6,64,128]{4,3,2,1,0:T(8,128)(2,1)S(1)}, u32[]{:S(2)}, u32[]{:S(2)}) collective-permute-start(bf16[6,2,6,64,128]{4,3,2,1,0:T(8,128)(2,1)S(1)} %get-tuple-element.83), channel_id=1, source_target_pairs={{0,8},{8,16},{16,24},{1,9},{9,17},{17,25},{2,10},{10,18},{18,26},{... | collective-permute-start | bytes 3538952 | tf_op jit(solution)/shard_map/ppermute | solution.py:178
  38.5 1.9 %collective-permute-start.7 = (bf16[6,2,6,64,128]{4,3,2,1,0:T(8,128)(2,1)S(1)}, bf16[6,2,6,64,128]{4,3,2,1,0:T(8,128)(2,1)S(1)}, u32[]{:S(2)}, u32[]{:S(2)}) collective-permute-start(bf16[6,2,6,64,128]{4,3,2,1,0:T(8,128)(2,1)S(1)} %get-tuple-element.82), channel_id=1, source_target_pairs={{8,0},{16,8},{24,16},{9,1},{17,9},{25,17},{10,2},{18,10},{26,18},{... | collective-permute-start | bytes 3538952 | tf_op jit(solution)/shard_map/ppermute | solution.py:178
  40.4 3.7 %collective-permute-done.12 = bf16[2,2,2,6,64,128]{5,4,3,2,0,1:T(8,128)(2,1)S(1)} collective-permute-done((bf16[2,2,2,6,64,128]{5,4,3,2,0,1:T(8,128)(2,1)S(1)}, bf16[2,2,2,6,64,128]{5,4,3,2,0,1:T(8,128)(2,1)S(1)}, u32[]{:S(2)}, u32[]{:S(2)}) %collective-permute-start.12) | collective-permute-done | bytes 786464 | tf_op jit(solution)/shard_map/ppermute | solution.py:178
  44.1 3.0 %collective-permute-done.13.refs_4_ = bf16[2,2,2,6,64,128]{5,4,3,2,1,0:T(8,128)(2,1)S(1)} collective-permute-done((bf16[2,2,2,6,64,128]{5,4,3,2,1,0:T(8,128)(2,1)S(1)}, bf16[2,2,2,6,64,128]{5,4,3,2,1,0:T(8,128)(2,1)S(1)}, u32[]{:S(2)}, u32[]{:S(2)}) %collective-permute-start.13) | collective-permute-done | bytes 786464 | tf_op jit(solution)/shard_map/ppermute | solution.py:178
  47.3 7.3 %collective-permute-start.14 = (bf16[6,2,6,64,128]{4,3,2,1,0:T(8,128)(2,1)S(1)}, bf16[6,2,6,64,128]{4,3,2,1,0:T(8,128)(2,1)S(1)}, u32[]{:S(2)}, u32[]{:S(2)}) collective-permute-start(bf16[6,2,6,64,128]{4,3,2,1,0:T(8,128)(2,1)S(1)} %get-tuple-element.71), channel_id=1, source_target_pairs={{0,8},{8,16},{16,24},{1,9},{9,17},{17,25},{2,10},{10,18},{18,26},{... | collective-permute-start | bytes 3538952 | tf_op jit(solution)/shard_map/ppermute | solution.py:178
  54.6 1.9 %collective-permute-start.15 = (bf16[6,2,6,64,128]{4,3,2,1,0:T(8,128)(2,1)S(1)}, bf16[6,2,6,64,128]{4,3,2,1,0:T(8,128)(2,1)S(1)}, u32[]{:S(2)}, u32[]{:S(2)}) collective-permute-start(bf16[6,2,6,64,128]{4,3,2,1,0:T(8,128)(2,1)S(1)} %get-tuple-element.70), channel_id=1, source_target_pairs={{8,0},{16,8},{24,16},{9,1},{17,9},{25,17},{10,2},{18,10},{26,18},{... | collective-permute-start | bytes 3538952 | tf_op jit(solution)/shard_map/ppermute | solution.py:178
  56.6 5.7 %shard_map.102 = (bf16[2,6,128,128]{3,2,1,0:T(8,128)(2,1)S(1)}, f32[2,6,2,128]{3,2,1,0:T(2,128)S(1)}) custom-call(bf16[2,2,2,6,64,128]{5,4,3,2,1,0:T(8,128)(2,1)S(1)} %copy.65.refs_0_.refs_2_, bf16[2,2,6,64,128]{4,3,2,1,0:T(8,128)(2,1)S(1)} %pad_maximum_fusion.4.refs_1_.refs_0_, bf16[2,2,6,64,128]{4,3,2,1,0:T(8,128)(2,1)S(1)} %collective-permute-done.refs_2_.refs_1_, ...), custom_call_target="tpu_custom_call" | custom-call | flops 6341787648 | bytes 4718592 | tf_op jit(solution)/shard_map/pallas_call | solution.py:159
  62.4 3.2 %collective-permute-start.9 = (f32[2,6,2,128]{3,2,1,0:T(2,128)S(1)}, f32[2,6,2,128]{3,2,1,0:T(2,128)S(1)}, u32[]{:S(2)}, u32[]{:S(2)}) collective-permute-start(f32[2,6,2,128]{3,2,1,0:T(2,128)S(1)} %get-tuple-element.47.refs_10_.refs_7_), channel_id=1, source_target_pairs={{0,2},{2,4},{4,6},{1,3},{3,5},{5,7},{8,10},{10,12},{12,14},{9,11},... | collective-permute-start | bytes 36872 | tf_op jit(solution)/shard_map/ppermute | solution.py:178
  65.6 2.1 %collective-permute-start.10 = (f32[2,6,2,128]{3,2,1,0:T(2,128)S(1)}, f32[2,6,2,128]{3,2,1,0:T(2,128)S(1)}, u32[]{:S(2)}, u32[]{:S(2)}) collective-permute-start(f32[2,6,2,128]{3,2,1,0:T(2,128)S(1)} %get-tuple-element.47.refs_10_.refs_7_), channel_id=1, source_target_pairs={{2,0},{4,2},{6,4},{3,1},{5,3},{7,5},{10,8},{12,10},{14,12},{11,9},... | collective-permute-start | bytes 36872 | tf_op jit(solution)/shard_map/ppermute | solution.py:178
  67.6 2.5 %shard_map.103 = (bf16[2,2,3,64,128]{4,3,2,1,0:T(8,128)(2,1)S(1)}, bf16[2,2,3,64,128]{4,3,2,1,0:T(8,128)(2,1)S(1)}) custom-call(bf16[2,2,2,6,64,128]{5,4,3,2,1,0:T(8,128)(2,1)S(1)} %copy.65.refs_0_.refs_2_, bf16[2,2,6,64,128]{4,3,2,1,0:T(8,128)(2,1)S(1)} %pad_maximum_fusion.4.refs_1_.refs_0_, ...), custom_call_target="tpu_custom_call" | custom-call | flops 4756340736 | bytes 2359296 | tf_op jit(solution)/shard_map/pallas_call | solution.py:159
  70.2 1.3 %collective-permute-start.8 = (bf16[2,2,3,64,128]{4,3,2,1,0:T(8,128)(2,1)S(1)}, bf16[2,2,3,64,128]{4,3,2,1,0:T(8,128)(2,1)S(1)}, u32[]{:S(2)}, u32[]{:S(2)}) collective-permute-start(bf16[2,2,3,64,128]{4,3,2,1,0:T(8,128)(2,1)S(1)} %get-tuple-element.46), channel_id=1, source_target_pairs={{0,1},{1,0},{2,3},{3,2},{4,5},{5,4},{6,7},{7,6},{8,9},{9,8},{10,11... | collective-permute-start | bytes 589832 | tf_op jit(solution)/shard_map/ppermute | solution.py:183
  71.5 4.5 %collective-permute-start.16 = (f32[3,6,2,128]{3,2,1,0:T(2,128)S(1)}, f32[3,6,2,128]{3,2,1,0:T(2,128)S(1)}, u32[]{:S(2)}, u32[]{:S(2)}) collective-permute-start(f32[3,6,2,128]{3,2,1,0:T(2,128)S(1)} %pad_maximum_fusion.5), channel_id=1, source_target_pairs={{0,8},{8,16},{16,24},{1,9},{9,17},{17,25},{2,10},{10,18},{18,26},{... | collective-permute-start | bytes 55304 | tf_op jit(solution)/shard_map/ppermute | solution.py:178
  76.0 1.9 %collective-permute-start.17 = (f32[3,6,2,128]{3,2,1,0:T(2,128)S(1)}, f32[3,6,2,128]{3,2,1,0:T(2,128)S(1)}, u32[]{:S(2)}, u32[]{:S(2)}) collective-permute-start(f32[3,6,2,128]{3,2,1,0:T(2,128)S(1)} %pad_maximum_fusion.6), channel_id=1, source_target_pairs={{8,0},{16,8},{24,16},{9,1},{17,9},{25,17},{10,2},{18,10},{26,18},{... | collective-permute-start | bytes 55304 | tf_op jit(solution)/shard_map/ppermute | solution.py:178
  77.9 2.6 %shard_map.104 = (bf16[2,2,3,64,128]{4,3,2,1,0:T(8,128)(2,1)S(1)}, bf16[2,2,3,64,128]{4,3,2,1,0:T(8,128)(2,1)S(1)}) custom-call(bf16[2,2,2,6,64,128]{5,4,3,2,1,0:T(8,128)(2,1)S(1)} %copy.65.refs_0_.refs_2_, bf16[2,2,6,64,128]{4,3,2,1,0:T(8,128)(2,1)S(1)} %pad_maximum_fusion.4.refs_1_.refs_0_, ...), custom_call_target="tpu_custom_call" | custom-call | flops 4756340736 | bytes 2359296 | tf_op jit(solution)/shard_map/pallas_call | solution.py:159
  80.9 0.5 collective-permute-done.17.refs_11_
  81.4 2.9 %shard_map.105 = (bf16[2,2,3,64,128]{4,3,2,1,0:T(8,128)(2,1)S(1)}, bf16[2,2,3,64,128]{4,3,2,1,0:T(8,128)(2,1)S(1)}) custom-call(bf16[2,2,6,64,128]{4,3,2,1,0:T(8,128)(2,1)S(1)} %pad_maximum_fusion.4.refs_1_.refs_0_, bf16[2,2,6,64,128]{4,3,2,1,0:T(8,128)(2,1)S(1)} %collective-permute-done.refs_2_.refs_1_, ...), custom_call_target="tpu_custom_call" | custom-call | flops 6341787648 | bytes 2359296 | tf_op jit(solution)/shard_map/pallas_call | solution.py:159
  84.3 0.8 collective-permute-start.18
  85.1 3.0 %shard_map.106 = (bf16[2,2,3,64,128]{4,3,2,1,0:T(8,128)(2,1)S(1)}, bf16[2,2,3,64,128]{4,3,2,1,0:T(8,128)(2,1)S(1)}) custom-call(bf16[2,2,6,64,128]{4,3,2,1,0:T(8,128)(2,1)S(1)} %pad_maximum_fusion.4.refs_1_.refs_0_, bf16[2,2,6,64,128]{4,3,2,1,0:T(8,128)(2,1)S(1)} %collective-permute-done.refs_2_.refs_1_, ...), custom_call_target="tpu_custom_call" | custom-call | flops 6341787648 | bytes 2359296 | tf_op jit(solution)/shard_map/pallas_call | solution.py:159
  88.1 0.8 collective-permute-start.19
  89.1 0.9 collective-permute-done.18
  90.8 2.8 %collective-permute-done.19 = bf16[2,2,3,64,128]{4,3,2,1,0:T(8,128)(2,1)S(1)} collective-permute-done((bf16[2,2,3,64,128]{4,3,2,1,0:T(8,128)(2,1)S(1)}, bf16[2,2,3,64,128]{4,3,2,1,0:T(8,128)(2,1)S(1)}, u32[]{:S(2)}, u32[]{:S(2)}) %collective-permute-start.19) | collective-permute-done | bytes 196640 | tf_op jit(solution)/shard_map/ppermute | solution.py:183
  93.7 0.7 copy-done.2
  (125 shorter events, 5.6 us)
Async XLA Ops:
  2.0 1.7 %copy-start.7 = (s32[8,4,2,27]{3,2,1,0:T(2,128)S(1)}, s32[8,4,2,27]{3,2,1,0:T(2,128)}, u32[]{:S(2)}) copy-start(s32[8,4,2,27]{3,2,1,0:T(2,128)} %param.11) | copy-start | bytes 20740
  2.0 3.3 %copy-start.8 = (bf16[4,3,9,2,9,1]{4,2,1,0,5,3:T(8,128)(2,1)S(1)}, bf16[4,3,9,2,9,1]{4,2,1,0,5,3:T(8,128)(2,1)}, u32[]{:S(2)}) copy-start(bf16[4,3,9,2,9,1]{4,2,1,0,5,3:T(8,128)(2,1)} %constant.235) | copy-start | bytes 11668
  2.1 3.9 %copy-start.6 = (bf16[18,1152]{1,0:T(8,128)(2,1)S(1)}, bf16[18,1152]{1,0:T(8,128)(2,1)}, u32[]{:S(2)}) copy-start(bf16[18,1152]{1,0:T(8,128)(2,1)} %constant.130.clone) | copy-start | bytes 124420
  2.1 10.0 %collective-permute-start = (bf16[2,2,6,64,128]{4,3,2,1,0:T(8,128)(2,1)S(1)}, bf16[2,2,6,64,128]{4,3,2,1,0:T(8,128)(2,1)S(1)}, u32[]{:S(2)}, u32[]{:S(2)}) collective-permute-start(bf16[2,2,6,64,128]{4,3,2,1,0:T(8,128)(2,1)S(1)} %pad_maximum_fusion.3), channel_id=1, source_target_pairs={{0,1},{1,0},{2,3},{3,2},{4,5},{5,4},{6,7},{7,6},{8,9},{9,8},{10,11... | collective-permute-start | bytes 1179656 | tf_op jit(solution)/shard_map/ppermute | solution.py:183
  3.6 8.0 %copy-start.4 = (bf16[2,8,8,12,128]{4,2,3,1,0:T(8,128)(2,1)S(1)}, bf16[2,8,8,12,128]{4,2,3,1,0:T(8,128)(2,1)}, u32[]{:S(2)}) copy-start(bf16[2,8,8,12,128]{4,2,3,1,0:T(8,128)(2,1)} %param.10) | copy-start | bytes 1179652
  3.6 8.0 %copy-start.5 = (bf16[2,8,8,12,128]{4,2,3,1,0:T(8,128)(2,1)S(1)}, bf16[2,8,8,12,128]{4,2,3,1,0:T(8,128)(2,1)}, u32[]{:S(2)}) copy-start(bf16[2,8,8,12,128]{4,2,3,1,0:T(8,128)(2,1)} %param.7) | copy-start | bytes 1179652
  6.2 12.5 %collective-permute-start.2 = (bf16[2,2,6,64,128]{4,3,2,1,0:T(8,128)(2,1)S(1)}, bf16[2,2,6,64,128]{4,3,2,1,0:T(8,128)(2,1)S(1)}, u32[]{:S(2)}, u32[]{:S(2)}) collective-permute-start(bf16[2,2,6,64,128]{4,3,2,1,0:T(8,128)(2,1)S(1)} %pad_maximum_fusion.4.refs_1_.refs_0_), channel_id=1, source_target_pairs={{0,2},{2,4},{4,6},{1,3},{3,5},{5,7},{8,10},{10,12},{12,14},{9,11},... | collective-permute-start | bytes 1179656 | tf_op jit(solution)/shard_map/ppermute | solution.py:178
  9.5 19.9 %collective-permute-start.4 = (bf16[2,2,6,64,128]{4,3,2,1,0:T(8,128)(2,1)S(1)}, bf16[2,2,6,64,128]{4,3,2,1,0:T(8,128)(2,1)S(1)}, u32[]{:S(2)}, u32[]{:S(2)}) collective-permute-start(bf16[2,2,6,64,128]{4,3,2,1,0:T(8,128)(2,1)S(1)} %pad_maximum_fusion.4.refs_1_.refs_0_), channel_id=1, source_target_pairs={{2,0},{4,2},{6,4},{3,1},{5,3},{7,5},{10,8},{12,10},{14,12},{11,9},... | collective-permute-start | bytes 1179656 | tf_op jit(solution)/shard_map/ppermute | solution.py:178
  12.2 19.4 %collective-permute-start.3 = (bf16[2,2,6,64,128]{4,3,2,1,0:T(8,128)(2,1)S(1)}, bf16[2,2,6,64,128]{4,3,2,1,0:T(8,128)(2,1)S(1)}, u32[]{:S(2)}, u32[]{:S(2)}) collective-permute-start(bf16[2,2,6,64,128]{4,3,2,1,0:T(8,128)(2,1)S(1)} %collective-permute-done.refs_2_.refs_1_), channel_id=1, source_target_pairs={{0,2},{2,4},{4,6},{1,3},{3,5},{5,7},{8,10},{10,12},{12,14},{9,11},... | collective-permute-start | bytes 1179656 | tf_op jit(solution)/shard_map/ppermute | solution.py:178
  15.4 16.4 %collective-permute-start.5 = (bf16[2,2,6,64,128]{4,3,2,1,0:T(8,128)(2,1)S(1)}, bf16[2,2,6,64,128]{4,3,2,1,0:T(8,128)(2,1)S(1)}, u32[]{:S(2)}, u32[]{:S(2)}) collective-permute-start(bf16[2,2,6,64,128]{4,3,2,1,0:T(8,128)(2,1)S(1)} %collective-permute-done.refs_2_.refs_1_), channel_id=1, source_target_pairs={{2,0},{4,2},{6,4},{3,1},{5,3},{7,5},{10,8},{12,10},{14,12},{11,9},... | collective-permute-start | bytes 1179656 | tf_op jit(solution)/shard_map/ppermute | solution.py:178
  17.5 8.6 %collective-permute-start.1 = (bf16[2,2,6,64,128]{4,3,2,1,0:T(8,128)(2,1)S(1)}, bf16[2,2,6,64,128]{4,3,2,1,0:T(8,128)(2,1)S(1)}, u32[]{:S(2)}, u32[]{:S(2)}) collective-permute-start(bf16[2,2,6,64,128]{4,3,2,1,0:T(8,128)(2,1)S(1)} %pad_maximum_fusion.2), channel_id=1, source_target_pairs={{0,1},{1,0},{2,3},{3,2},{4,5},{5,4},{6,7},{7,6},{8,9},{9,8},{10,11... | collective-permute-start | bytes 1179656 | tf_op jit(solution)/shard_map/ppermute | solution.py:183
  26.1 17.9 %collective-permute-start.12 = (bf16[2,2,2,6,64,128]{5,4,3,2,0,1:T(8,128)(2,1)S(1)}, bf16[2,2,2,6,64,128]{5,4,3,2,0,1:T(8,128)(2,1)S(1)}, u32[]{:S(2)}, u32[]{:S(2)}) collective-permute-start(bf16[2,2,2,6,64,128]{5,4,3,2,0,1:T(8,128)(2,1)S(1)} %pad_maximum_fusion), channel_id=1, source_target_pairs={{0,2},{2,4},{4,6},{1,3},{3,5},{5,7},{8,10},{10,12},{12,14},{9,11},... | collective-permute-start | bytes 2359304 | tf_op jit(solution)/shard_map/ppermute | solution.py:178
  29.5 17.6 %collective-permute-start.13 = (bf16[2,2,2,6,64,128]{5,4,3,2,1,0:T(8,128)(2,1)S(1)}, bf16[2,2,2,6,64,128]{5,4,3,2,1,0:T(8,128)(2,1)S(1)}, u32[]{:S(2)}, u32[]{:S(2)}) collective-permute-start(bf16[2,2,2,6,64,128]{5,4,3,2,1,0:T(8,128)(2,1)S(1)} %copy.65.refs_0_.refs_2_), channel_id=1, source_target_pairs={{2,0},{4,2},{6,4},{3,1},{5,3},{7,5},{10,8},{12,10},{14,12},{11,9},... | collective-permute-start | bytes 2359304 | tf_op jit(solution)/shard_map/ppermute | solution.py:178
  31.8 24.8 %collective-permute-start.6 = (bf16[6,2,6,64,128]{4,3,2,1,0:T(8,128)(2,1)S(1)}, bf16[6,2,6,64,128]{4,3,2,1,0:T(8,128)(2,1)S(1)}, u32[]{:S(2)}, u32[]{:S(2)}) collective-permute-start(bf16[6,2,6,64,128]{4,3,2,1,0:T(8,128)(2,1)S(1)} %get-tuple-element.83), channel_id=1, source_target_pairs={{0,8},{8,16},{16,24},{1,9},{9,17},{17,25},{2,10},{10,18},{18,26},{... | collective-permute-start | bytes 3538952 | tf_op jit(solution)/shard_map/ppermute | solution.py:178
  38.5 18.1 %collective-permute-start.7 = (bf16[6,2,6,64,128]{4,3,2,1,0:T(8,128)(2,1)S(1)}, bf16[6,2,6,64,128]{4,3,2,1,0:T(8,128)(2,1)S(1)}, u32[]{:S(2)}, u32[]{:S(2)}) collective-permute-start(bf16[6,2,6,64,128]{4,3,2,1,0:T(8,128)(2,1)S(1)} %get-tuple-element.82), channel_id=1, source_target_pairs={{8,0},{16,8},{24,16},{9,1},{17,9},{25,17},{10,2},{18,10},{26,18},{... | collective-permute-start | bytes 3538952 | tf_op jit(solution)/shard_map/ppermute | solution.py:178
  47.3 34.1 %collective-permute-start.14 = (bf16[6,2,6,64,128]{4,3,2,1,0:T(8,128)(2,1)S(1)}, bf16[6,2,6,64,128]{4,3,2,1,0:T(8,128)(2,1)S(1)}, u32[]{:S(2)}, u32[]{:S(2)}) collective-permute-start(bf16[6,2,6,64,128]{4,3,2,1,0:T(8,128)(2,1)S(1)} %get-tuple-element.71), channel_id=1, source_target_pairs={{0,8},{8,16},{16,24},{1,9},{9,17},{17,25},{2,10},{10,18},{18,26},{... | collective-permute-start | bytes 3538952 | tf_op jit(solution)/shard_map/ppermute | solution.py:178
  54.6 26.8 %collective-permute-start.15 = (bf16[6,2,6,64,128]{4,3,2,1,0:T(8,128)(2,1)S(1)}, bf16[6,2,6,64,128]{4,3,2,1,0:T(8,128)(2,1)S(1)}, u32[]{:S(2)}, u32[]{:S(2)}) collective-permute-start(bf16[6,2,6,64,128]{4,3,2,1,0:T(8,128)(2,1)S(1)} %get-tuple-element.70), channel_id=1, source_target_pairs={{8,0},{16,8},{24,16},{9,1},{17,9},{25,17},{10,2},{18,10},{26,18},{... | collective-permute-start | bytes 3538952 | tf_op jit(solution)/shard_map/ppermute | solution.py:178
  62.4 9.1 %collective-permute-start.9 = (f32[2,6,2,128]{3,2,1,0:T(2,128)S(1)}, f32[2,6,2,128]{3,2,1,0:T(2,128)S(1)}, u32[]{:S(2)}, u32[]{:S(2)}) collective-permute-start(f32[2,6,2,128]{3,2,1,0:T(2,128)S(1)} %get-tuple-element.47.refs_10_.refs_7_), channel_id=1, source_target_pairs={{0,2},{2,4},{4,6},{1,3},{3,5},{5,7},{8,10},{10,12},{12,14},{9,11},... | collective-permute-start | bytes 36872 | tf_op jit(solution)/shard_map/ppermute | solution.py:178
  65.6 5.9 %collective-permute-start.10 = (f32[2,6,2,128]{3,2,1,0:T(2,128)S(1)}, f32[2,6,2,128]{3,2,1,0:T(2,128)S(1)}, u32[]{:S(2)}, u32[]{:S(2)}) collective-permute-start(f32[2,6,2,128]{3,2,1,0:T(2,128)S(1)} %get-tuple-element.47.refs_10_.refs_7_), channel_id=1, source_target_pairs={{2,0},{4,2},{6,4},{3,1},{5,3},{7,5},{10,8},{12,10},{14,12},{11,9},... | collective-permute-start | bytes 36872 | tf_op jit(solution)/shard_map/ppermute | solution.py:178
  70.2 18.9 %collective-permute-start.8 = (bf16[2,2,3,64,128]{4,3,2,1,0:T(8,128)(2,1)S(1)}, bf16[2,2,3,64,128]{4,3,2,1,0:T(8,128)(2,1)S(1)}, u32[]{:S(2)}, u32[]{:S(2)}) collective-permute-start(bf16[2,2,3,64,128]{4,3,2,1,0:T(8,128)(2,1)S(1)} %get-tuple-element.46), channel_id=1, source_target_pairs={{0,1},{1,0},{2,3},{3,2},{4,5},{5,4},{6,7},{7,6},{8,9},{9,8},{10,11... | collective-permute-start | bytes 589832 | tf_op jit(solution)/shard_map/ppermute | solution.py:183
  71.5 9.0 %collective-permute-start.16 = (f32[3,6,2,128]{3,2,1,0:T(2,128)S(1)}, f32[3,6,2,128]{3,2,1,0:T(2,128)S(1)}, u32[]{:S(2)}, u32[]{:S(2)}) collective-permute-start(f32[3,6,2,128]{3,2,1,0:T(2,128)S(1)} %pad_maximum_fusion.5), channel_id=1, source_target_pairs={{0,8},{8,16},{16,24},{1,9},{9,17},{17,25},{2,10},{10,18},{18,26},{... | collective-permute-start | bytes 55304 | tf_op jit(solution)/shard_map/ppermute | solution.py:178
  76.0 5.4 %collective-permute-start.17 = (f32[3,6,2,128]{3,2,1,0:T(2,128)S(1)}, f32[3,6,2,128]{3,2,1,0:T(2,128)S(1)}, u32[]{:S(2)}, u32[]{:S(2)}) collective-permute-start(f32[3,6,2,128]{3,2,1,0:T(2,128)S(1)} %pad_maximum_fusion.6), channel_id=1, source_target_pairs={{8,0},{16,8},{24,16},{9,1},{17,9},{25,17},{10,2},{18,10},{26,18},{... | collective-permute-start | bytes 55304 | tf_op jit(solution)/shard_map/ppermute | solution.py:178
  80.5 8.6 %collective-permute-start.11 = (bf16[2,2,3,64,128]{4,3,2,1,0:T(8,128)(2,1)S(1)}, bf16[2,2,3,64,128]{4,3,2,1,0:T(8,128)(2,1)S(1)}, u32[]{:S(2)}, u32[]{:S(2)}) collective-permute-start(bf16[2,2,3,64,128]{4,3,2,1,0:T(8,128)(2,1)S(1)} %get-tuple-element.49), channel_id=1, source_target_pairs={{0,1},{1,0},{2,3},{3,2},{4,5},{5,4},{6,7},{7,6},{8,9},{9,8},{10,11... | collective-permute-start | bytes 589832 | tf_op jit(solution)/shard_map/ppermute | solution.py:183
  84.3 5.7 %collective-permute-start.18 = (bf16[2,2,3,64,128]{4,3,2,1,0:T(8,128)(2,1)S(1)}, bf16[2,2,3,64,128]{4,3,2,1,0:T(8,128)(2,1)S(1)}, u32[]{:S(2)}, u32[]{:S(2)}) collective-permute-start(bf16[2,2,3,64,128]{4,3,2,1,0:T(8,128)(2,1)S(1)} %get-tuple-element.56), channel_id=1, source_target_pairs={{0,1},{1,0},{2,3},{3,2},{4,5},{5,4},{6,7},{7,6},{8,9},{9,8},{10,11... | collective-permute-start | bytes 589832 | tf_op jit(solution)/shard_map/ppermute | solution.py:183
  88.1 5.5 %collective-permute-start.19 = (bf16[2,2,3,64,128]{4,3,2,1,0:T(8,128)(2,1)S(1)}, bf16[2,2,3,64,128]{4,3,2,1,0:T(8,128)(2,1)S(1)}, u32[]{:S(2)}, u32[]{:S(2)}) collective-permute-start(bf16[2,2,3,64,128]{4,3,2,1,0:T(8,128)(2,1)S(1)} %get-tuple-element.69), channel_id=1, source_target_pairs={{0,1},{1,0},{2,3},{3,2},{4,5},{5,4},{6,7},{7,6},{8,9},{9,8},{10,11... | collective-permute-start | bytes 589832 | tf_op jit(solution)/shard_map/ppermute | solution.py:183
  90.6 3.1 %copy-start.3 = (bf16[2,8,12,8,128]{4,3,2,1,0:T(8,128)(2,1)}, bf16[2,8,12,8,128]{4,3,2,1,0:T(8,128)(2,1)S(1)}, u32[]{:S(2)}) copy-start(bf16[2,8,12,8,128]{4,3,2,1,0:T(8,128)(2,1)S(1)} %bitcast_dynamic-update-slice_fusion.12) | copy-start | bytes 1179652
  90.6 3.1 %copy-start = (bf16[2,8,12,8,128]{4,3,2,1,0:T(8,128)(2,1)}, bf16[2,8,12,8,128]{4,3,2,1,0:T(8,128)(2,1)S(1)}, u32[]{:S(2)}) copy-start(bf16[2,8,12,8,128]{4,3,2,1,0:T(8,128)(2,1)S(1)} %bitcast_dynamic-update-slice_fusion.8) | copy-start | bytes 1179652
  93.6 0.7 copy-start.2
  93.7 0.8 copy-start.1

commit v14 on v12

--- a/solution.py
+++ b/solution.py
@@ -40,37 +40,38 @@
                         band[place, :] = side(row, part, at - 1, which)
 
 
-def fill_keys(parts, halo, bands):
+def fill_keys(head, parts, halo, bands):
     rows = (halo[parts : 2 * parts], halo[:parts], halo[2 * parts : 3 * parts])
     edges = halo[3 * parts :]
     frames, _, _, cells, _ = halo[0].shape
-    side = lambda row, part, at, which: rows[row][part][at, which, 0]
-    edge = lambda end, row, part, which: edges[end][3 * part + row, which, 0]
+    side = lambda row, part, at, which: rows[row][part][at, which, head]
+    edge = lambda end, row, part, which: edges[end][3 * part + row, which, head]
     fill_bands(frames, parts, cells, side, edge, bands)
 
 
-def fill_queries(halo, bands):
+def fill_queries(head, halo, bands):
     own, before, after, low, high = halo
     frames, parts, _, _, cells, _ = own.shape
-    side = lambda row, part, at, which: (before, own, after)[row][at, part, which, 0]
-    edge = lambda end, row, part, which: (low, high)[end][3 * part + row, which, 0]
+    side = lambda row, part, at, which: (before, own, after)[row][at, part, which, head]
+    edge = lambda end, row, part, which: (low, high)[end][3 * part + row, which, head]
     fill_bands(frames, parts, cells, side, edge, bands)
 
 
-def slab(parts, at, which):
+def slab(head, parts, at, which):
     if isinstance(parts, list):
-        return jnp.concatenate([part[at, which, 0] for part in parts], axis=0)
-    return jnp.concatenate([parts[at, part, which, 0] for part in range(parts.shape[1])], axis=0)
-
-
-def attend_kernel(scaling, parts, *refs):
+        return jnp.concatenate([part[at, which, head] for part in parts], axis=0)
+    return jnp.concatenate([parts[at, part, which, head] for part in range(parts.shape[1])], axis=0)
+
+
+def attend_kernel(scaling, parts, first, *refs):
+    head = pl.program_id(0) + first
     pair, halo = refs[0], refs[1 : 3 * parts + 3]
     bias, attended, stats, key_all, value_all = refs[3 * parts + 3 :]
     frames, _, tokens, _ = attended.shape
-    fill_keys(parts, halo, (key_all, value_all))
+    fill_keys(head, parts, halo, (key_all, value_all))
     windows = [pl.ds(3 * at * tokens, 9 * tokens) for at in range(frames)]
     scores = [
-        dot(slab(pair, at, 0), key_all[windows[at], :], NT) * (scaling * LOG2E) + spread(bias[at], tokens)
+        dot(slab(head, pair, at, 0), key_all[windows[at], :], NT) * (scaling * LOG2E) + spread(bias[at], tokens)
         for at in range(frames)
     ]
     highest = [jnp.max(part, axis=1, keepdims=True) for part in scores]
@@ -79,7 +80,7 @@
     sums = [dot(raised[at].astype(jnp.bfloat16), value_all[windows[at], :], NN) for at in range(frames)]
     for at in range(frames):
         out = (sums[at] * (1.0 / total[at])).astype(jnp.bfloat16)
-        grad = slab(pair, at, 1).astype(jnp.float32)
+        grad = slab(head, pair, at, 1).astype(jnp.float32)
         grad_dot = jnp.sum(grad * out.astype(jnp.float32), axis=1, keepdims=True)
         attended[at, 0] = out
         lane = lax.broadcasted_iota(jnp.int32, (tokens, 128), 1)
@@ -95,20 +96,21 @@
         out[1, at, 0] = second[own]
 
 
-def query_kernel(scaling, parts, *refs):
+def query_kernel(scaling, parts, first, *refs):
+    head = pl.program_id(0) + first
     pair, halo = refs[0], refs[1 : 3 * parts + 3]
     attended, stats, bias = refs[3 * parts + 3 : 3 * parts + 6]
     grads, (key_all, value_all) = refs[3 * parts + 6 : -2], refs[-2:]
     frames, _, tokens, _ = attended.shape
-    fill_keys(parts, halo, (key_all, value_all))
+    fill_keys(head, parts, halo, (key_all, value_all))
     windows = [pl.ds(3 * at * tokens, 9 * tokens) for at in range(frames)]
 
     def column(at, which):
         wide = jnp.broadcast_to(stats[at, 0, which : which + 1], (128, tokens))
         return jnp.transpose(wide)[:, :1]
 
-    scores = [dot(slab(pair, at, 0), key_all[windows[at], :], NT) for at in range(frames)]
-    grad_probs = [dot(slab(pair, at, 1), value_all[windows[at], :], NT) for at in range(frames)]
+    scores = [dot(slab(head, pair, at, 0), key_all[windows[at], :], NT) for at in range(frames)]
+    grad_probs = [dot(slab(head, pair, at, 1), value_all[windows[at], :], NT) for at in range(frames)]
     for at in range(frames):
         shift = spread(bias[at], tokens) - column(at, 0)
         weights = jnp.exp2(scores[at] * (scaling * LOG2E) + shift)
@@ -117,12 +119,13 @@
         store(grads, at, attended[at, 0], query_grad.astype(jnp.bfloat16))
 
 
-def back_kernel(scaling, parts, *refs):
+def back_kernel(scaling, parts, first, *refs):
+    head = pl.program_id(0) + first
     pair, halo = list(refs[:parts]), refs[parts : parts + 5]
     own_st, before_st, after_st, low_st, high_st, bias = refs[parts + 5 : parts + 11]
     grads, (query_all, grad_all) = refs[parts + 11 : -2], refs[-2:]
     frames, _, _, tokens = own_st.shape
-    fill_queries(halo, (query_all, grad_all))
+    fill_queries(head, halo, (query_all, grad_all))
 
     def stat_row(at, row, which):
         if at == 0:
@@ -136,8 +139,8 @@
         return jnp.concatenate(rows, axis=1)
 
     windows = [pl.ds(3 * at * tokens, 9 * tokens) for at in range(frames)]
-    scores = [dot(slab(pair, at, 0), query_all[windows[at], :], NT) for at in range(frames)]
-    grad_probs = [dot(slab(pair, at, 1), grad_all[windows[at], :], NT) for at in range(frames)]
+    scores = [dot(slab(head, pair, at, 0), query_all[windows[at], :], NT) for at in range(frames)]
+    grad_probs = [dot(slab(head, pair, at, 1), grad_all[windows[at], :], NT) for at in range(frames)]
     for at in range(frames):
         shift = spread(bias[at] - stat_band(at, 0), tokens)
         weights = jnp.exp2(scores[at] * (scaling * LOG2E) + shift).astype(jnp.bfloat16)
@@ -157,10 +160,13 @@
     frames, (cells, dim) = bias.shape[0], operands[0].shape[-2:]
     tokens = parts * cells
     return pl.pallas_call(
-        functools.partial(kernel, scaling, parts),
+        functools.partial(kernel, scaling, parts, first),
         grid=(count,),
         out_shape=tuple(outs),
-        in_specs=[head_spec(part.shape, first) for part in operands]
+        in_specs=[
+            pl.BlockSpec(memory_space=pltpu.VMEM) if part.ndim > 4 else head_spec(part.shape, first)
+            for part in operands
+        ]
         + [pl.BlockSpec(bias.shape, lambda head: (0,) * bias.ndim)],
         out_specs=tuple(head_spec(out.shape, 0) for out in outs),
         scratch_shapes=[pltpu.VMEM((3 * (frames + 2) * tokens, dim), jnp.bfloat16)] * 2,

time: 96.2 us -> 95.2 us (0.990)
  Pallas kernels: 16.7 us -> 15.2 us
    pallas_call x5, Pallas kernels: 16.7 us -> 15.2 us  [run(): pl.pallas_call(functools.partial(kernel, scaling, parts, first), grid=(co...]
  transfers between devices with their start and end apart: 20 -> 20, of which waited for: 7 -> 7; matrix products, arithmetic and copies ran while one was open for 6% -> 6% of each run, Pallas kernels for 18% -> 16%
where the time goes in v14:
time: 95.2 us; the launch traced here: 93.6 us
  starting transfers between devices  51.3 us (54%)
  waiting for transfers between devices  17.9 us (19%)
  Pallas kernels  15.2 us (16%)
  local copies, waits for them, and re-layouts  6.31 us (7%)
  between operations  1.37 us (1%)
    ppermute x14, starting transfers between devices, step_along(): lax.ppermute(tensor, axis, [(i, i + sign) for i in range(size) if 0 <= i...  45.3 us
    pallas_call x5, Pallas kernels, run(): pl.pallas_call(functools.partial(kernel, scaling, parts, first), grid=(co...  15.2 us
    ppermute x6, waiting for transfers between devices, turn(): lax.ppermute(tensor, 'head', [(i, (i + shift) % size) for i in range(size)])  10.7 us
    ppermute x14, waiting for transfers between devices, step_along(): lax.ppermute(tensor, axis, [(i, i + sign) for i in range(size) if 0 <= i...  7.17 us
    ppermute x6, starting transfers between devices, turn(): lax.ppermute(tensor, 'head', [(i, (i + shift) % size) for i in range(size)])  6.02 us
  transfers between devices with their start and end apart: 20, of which 7 were waited for; matrix products, arithmetic and copies ran while one was open for 6% of the time, Pallas kernels for 16%

profile of v14, /device:TPU:9, one launch (start us, length us, event | category | flops | bytes accessed | tf_op | source)
XLA Modules:
  0.0 93.6 jit_solution(9177479150656541577)
XLA Ops:
  0.7 1.3 %dynamic-slice_bitcast_fusion = (bf16[2,6,8,8,128]{4,3,1,2,0:T(8,128)(2,1)S(1)}, bf16[2,6,8,8,128]{4,3,1,2,0:T(8,128)(2,1)S(1)}, bf16[2,6,8,8,128]{4,3,1,2,0:T(8,128)(2,1)S(1)}, bf16[2,6,8,8,128]{4,3,1,2,0:T(8,128)(2,1)S(1)}) fusion(bf16[2,8,8,12,128]{4,2,3,1,0:T(8,128)(2,1)} %param.9, s32[]{:T(128)S(6)} %select_n.105, s32[]{:T(128)S(6)} %select_n.107, ...), kind=kLoop, calls=%fused_computation.66 | loop fusion | bytes 1572872 | tf_op jit(solution)/shard_map/dynamic_slice | solution.py:250
  2.1 1.3 %collective-permute-start = (bf16[2,2,6,64,128]{4,3,2,1,0:T(8,128)(2,1)S(1)}, bf16[2,2,6,64,128]{4,3,2,1,0:T(8,128)(2,1)S(1)}, u32[]{:S(2)}, u32[]{:S(2)}) collective-permute-start(bf16[2,2,6,64,128]{4,3,2,1,0:T(8,128)(2,1)S(1)} %pad_maximum_fusion.3), channel_id=1, source_target_pairs={{0,1},{1,0},{2,3},{3,2},{4,5},{5,4},{6,7},{7,6},{8,9},{9,8},{10,11... | collective-permute-start | bytes 1179656 | tf_op jit(solution)/shard_map/ppermute | solution.py:189
  6.2 3.2 %collective-permute-start.2 = (bf16[2,2,6,64,128]{4,3,2,1,0:T(8,128)(2,1)S(1)}, bf16[2,2,6,64,128]{4,3,2,1,0:T(8,128)(2,1)S(1)}, u32[]{:S(2)}, u32[]{:S(2)}) collective-permute-start(bf16[2,2,6,64,128]{4,3,2,1,0:T(8,128)(2,1)S(1)} %pad_maximum_fusion.4.refs_1_.refs_0_), channel_id=1, source_target_pairs={{0,2},{2,4},{4,6},{1,3},{3,5},{5,7},{8,10},{10,12},{12,14},{9,11},... | collective-permute-start | bytes 1179656 | tf_op jit(solution)/shard_map/ppermute | solution.py:184
  9.5 2.1 %collective-permute-start.4 = (bf16[2,2,6,64,128]{4,3,2,1,0:T(8,128)(2,1)S(1)}, bf16[2,2,6,64,128]{4,3,2,1,0:T(8,128)(2,1)S(1)}, u32[]{:S(2)}, u32[]{:S(2)}) collective-permute-start(bf16[2,2,6,64,128]{4,3,2,1,0:T(8,128)(2,1)S(1)} %pad_maximum_fusion.4.refs_1_.refs_0_), channel_id=1, source_target_pairs={{2,0},{4,2},{6,4},{3,1},{5,3},{7,5},{10,8},{12,10},{14,12},{11,9},... | collective-permute-start | bytes 1179656 | tf_op jit(solution)/shard_map/ppermute | solution.py:184
  12.2 3.2 %collective-permute-start.3 = (bf16[2,2,6,64,128]{4,3,2,1,0:T(8,128)(2,1)S(1)}, bf16[2,2,6,64,128]{4,3,2,1,0:T(8,128)(2,1)S(1)}, u32[]{:S(2)}, u32[]{:S(2)}) collective-permute-start(bf16[2,2,6,64,128]{4,3,2,1,0:T(8,128)(2,1)S(1)} %collective-permute-done.refs_2_.refs_1_), channel_id=1, source_target_pairs={{0,2},{2,4},{4,6},{1,3},{3,5},{5,7},{8,10},{10,12},{12,14},{9,11},... | collective-permute-start | bytes 1179656 | tf_op jit(solution)/shard_map/ppermute | solution.py:184
  15.4 2.1 %collective-permute-start.5 = (bf16[2,2,6,64,128]{4,3,2,1,0:T(8,128)(2,1)S(1)}, bf16[2,2,6,64,128]{4,3,2,1,0:T(8,128)(2,1)S(1)}, u32[]{:S(2)}, u32[]{:S(2)}) collective-permute-start(bf16[2,2,6,64,128]{4,3,2,1,0:T(8,128)(2,1)S(1)} %collective-permute-done.refs_2_.refs_1_), channel_id=1, source_target_pairs={{2,0},{4,2},{6,4},{3,1},{5,3},{7,5},{10,8},{12,10},{14,12},{11,9},... | collective-permute-start | bytes 1179656 | tf_op jit(solution)/shard_map/ppermute | solution.py:184
  17.5 1.3 %collective-permute-start.1 = (bf16[2,2,6,64,128]{4,3,2,1,0:T(8,128)(2,1)S(1)}, bf16[2,2,6,64,128]{4,3,2,1,0:T(8,128)(2,1)S(1)}, u32[]{:S(2)}, u32[]{:S(2)}) collective-permute-start(bf16[2,2,6,64,128]{4,3,2,1,0:T(8,128)(2,1)S(1)} %pad_maximum_fusion.2), channel_id=1, source_target_pairs={{0,1},{1,0},{2,3},{3,2},{4,5},{5,4},{6,7},{7,6},{8,9},{9,8},{10,11... | collective-permute-start | bytes 1179656 | tf_op jit(solution)/shard_map/ppermute | solution.py:189
  18.9 7.2 %collective-permute-done.1 = bf16[2,2,6,64,128]{4,3,2,1,0:T(8,128)(2,1)S(1)} collective-permute-done((bf16[2,2,6,64,128]{4,3,2,1,0:T(8,128)(2,1)S(1)}, bf16[2,2,6,64,128]{4,3,2,1,0:T(8,128)(2,1)S(1)}, u32[]{:S(2)}, u32[]{:S(2)}) %collective-permute-start.1) | collective-permute-done | bytes 393248 | tf_op jit(solution)/shard_map/ppermute | solution.py:189
  26.1 3.2 %collective-permute-start.12 = (bf16[2,2,2,6,64,128]{5,4,3,2,0,1:T(8,128)(2,1)S(1)}, bf16[2,2,2,6,64,128]{5,4,3,2,0,1:T(8,128)(2,1)S(1)}, u32[]{:S(2)}, u32[]{:S(2)}) collective-permute-start(bf16[2,2,2,6,64,128]{5,4,3,2,0,1:T(8,128)(2,1)S(1)} %pad_maximum_fusion), channel_id=1, source_target_pairs={{0,2},{2,4},{4,6},{1,3},{3,5},{5,7},{8,10},{10,12},{12,14},{9,11},... | collective-permute-start | bytes 2359304 | tf_op jit(solution)/shard_map/ppermute | solution.py:184
  29.5 2.1 %collective-permute-start.13 = (bf16[2,2,2,6,64,128]{5,4,3,2,1,0:T(8,128)(2,1)S(1)}, bf16[2,2,2,6,64,128]{5,4,3,2,1,0:T(8,128)(2,1)S(1)}, u32[]{:S(2)}, u32[]{:S(2)}) collective-permute-start(bf16[2,2,2,6,64,128]{5,4,3,2,1,0:T(8,128)(2,1)S(1)} %copy.57.refs_0_.refs_2_), channel_id=1, source_target_pairs={{2,0},{4,2},{6,4},{3,1},{5,3},{7,5},{10,8},{12,10},{14,12},{11,9},... | collective-permute-start | bytes 2359304 | tf_op jit(solution)/shard_map/ppermute | solution.py:184
  31.8 6.6 %collective-permute-start.6 = (bf16[6,2,6,64,128]{4,3,2,1,0:T(8,128)(2,1)S(1)}, bf16[6,2,6,64,128]{4,3,2,1,0:T(8,128)(2,1)S(1)}, u32[]{:S(2)}, u32[]{:S(2)}) collective-permute-start(bf16[6,2,6,64,128]{4,3,2,1,0:T(8,128)(2,1)S(1)} %get-tuple-element.87), channel_id=1, source_target_pairs={{0,8},{8,16},{16,24},{1,9},{9,17},{17,25},{2,10},{10,18},{18,26},{... | collective-permute-start | bytes 3538952 | tf_op jit(solution)/shard_map/ppermute | solution.py:184
  38.5 1.9 %collective-permute-start.7 = (bf16[6,2,6,64,128]{4,3,2,1,0:T(8,128)(2,1)S(1)}, bf16[6,2,6,64,128]{4,3,2,1,0:T(8,128)(2,1)S(1)}, u32[]{:S(2)}, u32[]{:S(2)}) collective-permute-start(bf16[6,2,6,64,128]{4,3,2,1,0:T(8,128)(2,1)S(1)} %get-tuple-element.86), channel_id=1, source_target_pairs={{8,0},{16,8},{24,16},{9,1},{17,9},{25,17},{10,2},{18,10},{26,18},{... | collective-permute-start | bytes 3538952 | tf_op jit(solution)/shard_map/ppermute | solution.py:184
  40.4 3.7 %collective-permute-done.12 = bf16[2,2,2,6,64,128]{5,4,3,2,0,1:T(8,128)(2,1)S(1)} collective-permute-done((bf16[2,2,2,6,64,128]{5,4,3,2,0,1:T(8,128)(2,1)S(1)}, bf16[2,2,2,6,64,128]{5,4,3,2,0,1:T(8,128)(2,1)S(1)}, u32[]{:S(2)}, u32[]{:S(2)}) %collective-permute-start.12) | collective-permute-done | bytes 786464 | tf_op jit(solution)/shard_map/ppermute | solution.py:184
  44.1 3.0 %collective-permute-done.13.refs_4_ = bf16[2,2,2,6,64,128]{5,4,3,2,1,0:T(8,128)(2,1)S(1)} collective-permute-done((bf16[2,2,2,6,64,128]{5,4,3,2,1,0:T(8,128)(2,1)S(1)}, bf16[2,2,2,6,64,128]{5,4,3,2,1,0:T(8,128)(2,1)S(1)}, u32[]{:S(2)}, u32[]{:S(2)}) %collective-permute-start.13) | collective-permute-done | bytes 786464 | tf_op jit(solution)/shard_map/ppermute | solution.py:184
  47.3 7.3 %collective-permute-start.14 = (bf16[6,2,6,64,128]{4,3,2,1,0:T(8,128)(2,1)S(1)}, bf16[6,2,6,64,128]{4,3,2,1,0:T(8,128)(2,1)S(1)}, u32[]{:S(2)}, u32[]{:S(2)}) collective-permute-start(bf16[6,2,6,64,128]{4,3,2,1,0:T(8,128)(2,1)S(1)} %get-tuple-element.75), channel_id=1, source_target_pairs={{0,8},{8,16},{16,24},{1,9},{9,17},{17,25},{2,10},{10,18},{18,26},{... | collective-permute-start | bytes 3538952 | tf_op jit(solution)/shard_map/ppermute | solution.py:184
  54.6 1.9 %collective-permute-start.15 = (bf16[6,2,6,64,128]{4,3,2,1,0:T(8,128)(2,1)S(1)}, bf16[6,2,6,64,128]{4,3,2,1,0:T(8,128)(2,1)S(1)}, u32[]{:S(2)}, u32[]{:S(2)}) collective-permute-start(bf16[6,2,6,64,128]{4,3,2,1,0:T(8,128)(2,1)S(1)} %get-tuple-element.74), channel_id=1, source_target_pairs={{8,0},{16,8},{24,16},{9,1},{17,9},{25,17},{10,2},{18,10},{26,18},{... | collective-permute-start | bytes 3538952 | tf_op jit(solution)/shard_map/ppermute | solution.py:184
  56.6 5.2 %shard_map.102 = (bf16[2,6,128,128]{3,2,1,0:T(8,128)(2,1)S(1)}, f32[2,6,2,128]{3,2,1,0:T(2,128)S(1)}) custom-call(bf16[2,2,2,6,64,128]{5,4,3,2,1,0:T(8,128)(2,1)S(1)} %copy.57.refs_0_.refs_2_, bf16[2,2,6,64,128]{4,3,2,1,0:T(8,128)(2,1)S(1)} %pad_maximum_fusion.4.refs_1_.refs_0_, bf16[2,2,6,64,128]{4,3,2,1,0:T(8,128)(2,1)S(1)} %collective-permute-done.refs_2_.refs_1_, ...), custom_call_target="tpu_custom_call" | custom-call | flops 6341787648 | bytes 4718592 | tf_op jit(solution)/shard_map/pallas_call | solution.py:162
  61.8 3.2 %collective-permute-start.9 = (f32[2,6,2,128]{3,2,1,0:T(2,128)S(1)}, f32[2,6,2,128]{3,2,1,0:T(2,128)S(1)}, u32[]{:S(2)}, u32[]{:S(2)}) collective-permute-start(f32[2,6,2,128]{3,2,1,0:T(2,128)S(1)} %get-tuple-element.47.refs_10_.refs_7_), channel_id=1, source_target_pairs={{0,2},{2,4},{4,6},{1,3},{3,5},{5,7},{8,10},{10,12},{12,14},{9,11},... | collective-permute-start | bytes 36872 | tf_op jit(solution)/shard_map/ppermute | solution.py:184
  65.1 2.0 %collective-permute-start.10 = (f32[2,6,2,128]{3,2,1,0:T(2,128)S(1)}, f32[2,6,2,128]{3,2,1,0:T(2,128)S(1)}, u32[]{:S(2)}, u32[]{:S(2)}) collective-permute-start(f32[2,6,2,128]{3,2,1,0:T(2,128)S(1)} %get-tuple-element.47.refs_10_.refs_7_), channel_id=1, source_target_pairs={{2,0},{4,2},{6,4},{3,1},{5,3},{7,5},{10,8},{12,10},{14,12},{11,9},... | collective-permute-start | bytes 36872 | tf_op jit(solution)/shard_map/ppermute | solution.py:184
  67.1 2.3 %shard_map.103 = (bf16[2,2,3,64,128]{4,3,2,1,0:T(8,128)(2,1)S(1)}, bf16[2,2,3,64,128]{4,3,2,1,0:T(8,128)(2,1)S(1)}) custom-call(bf16[2,2,2,6,64,128]{5,4,3,2,1,0:T(8,128)(2,1)S(1)} %copy.57.refs_0_.refs_2_, bf16[2,2,6,64,128]{4,3,2,1,0:T(8,128)(2,1)S(1)} %pad_maximum_fusion.4.refs_1_.refs_0_, ...), custom_call_target="tpu_custom_call" | custom-call | flops 4756340736 | bytes 2359296 | tf_op jit(solution)/shard_map/pallas_call | solution.py:162
  69.5 1.3 %collective-permute-start.8 = (bf16[2,2,3,64,128]{4,3,2,1,0:T(8,128)(2,1)S(1)}, bf16[2,2,3,64,128]{4,3,2,1,0:T(8,128)(2,1)S(1)}, u32[]{:S(2)}, u32[]{:S(2)}) collective-permute-start(bf16[2,2,3,64,128]{4,3,2,1,0:T(8,128)(2,1)S(1)} %get-tuple-element.46), channel_id=1, source_target_pairs={{0,1},{1,0},{2,3},{3,2},{4,5},{5,4},{6,7},{7,6},{8,9},{9,8},{10,11... | collective-permute-start | bytes 589832 | tf_op jit(solution)/shard_map/ppermute | solution.py:189
  70.8 4.5 %collective-permute-start.16 = (f32[3,6,2,128]{3,2,1,0:T(2,128)S(1)}, f32[3,6,2,128]{3,2,1,0:T(2,128)S(1)}, u32[]{:S(2)}, u32[]{:S(2)}) collective-permute-start(f32[3,6,2,128]{3,2,1,0:T(2,128)S(1)} %pad_maximum_fusion.5), channel_id=1, source_target_pairs={{0,8},{8,16},{16,24},{1,9},{9,17},{17,25},{2,10},{10,18},{18,26},{... | collective-permute-start | bytes 55304 | tf_op jit(solution)/shard_map/ppermute | solution.py:184
  75.3 1.9 %collective-permute-start.17 = (f32[3,6,2,128]{3,2,1,0:T(2,128)S(1)}, f32[3,6,2,128]{3,2,1,0:T(2,128)S(1)}, u32[]{:S(2)}, u32[]{:S(2)}) collective-permute-start(f32[3,6,2,128]{3,2,1,0:T(2,128)S(1)} %pad_maximum_fusion.6), channel_id=1, source_target_pairs={{8,0},{16,8},{24,16},{9,1},{17,9},{25,17},{10,2},{18,10},{26,18},{... | collective-permute-start | bytes 55304 | tf_op jit(solution)/shard_map/ppermute | solution.py:184
  77.2 2.3 %shard_map.104 = (bf16[2,2,3,64,128]{4,3,2,1,0:T(8,128)(2,1)S(1)}, bf16[2,2,3,64,128]{4,3,2,1,0:T(8,128)(2,1)S(1)}) custom-call(bf16[2,2,2,6,64,128]{5,4,3,2,1,0:T(8,128)(2,1)S(1)} %copy.57.refs_0_.refs_2_, bf16[2,2,6,64,128]{4,3,2,1,0:T(8,128)(2,1)S(1)} %pad_maximum_fusion.4.refs_1_.refs_0_, ...), custom_call_target="tpu_custom_call" | custom-call | flops 4756340736 | bytes 2359296 | tf_op jit(solution)/shard_map/pallas_call | solution.py:162
  79.6 0.6 collective-permute-start.11
  80.7 2.7 %shard_map.105 = (bf16[2,2,3,64,128]{4,3,2,1,0:T(8,128)(2,1)S(1)}, bf16[2,2,3,64,128]{4,3,2,1,0:T(8,128)(2,1)S(1)}) custom-call(bf16[2,2,6,64,128]{4,3,2,1,0:T(8,128)(2,1)S(1)} %pad_maximum_fusion.4.refs_1_.refs_0_, bf16[2,2,6,64,128]{4,3,2,1,0:T(8,128)(2,1)S(1)} %collective-permute-done.refs_2_.refs_1_, ...), custom_call_target="tpu_custom_call" | custom-call | flops 6341787648 | bytes 2359296 | tf_op jit(solution)/shard_map/pallas_call | solution.py:162
  84.0 2.6 %shard_map.106 = (bf16[2,2,3,64,128]{4,3,2,1,0:T(8,128)(2,1)S(1)}, bf16[2,2,3,64,128]{4,3,2,1,0:T(8,128)(2,1)S(1)}) custom-call(bf16[2,2,6,64,128]{4,3,2,1,0:T(8,128)(2,1)S(1)} %pad_maximum_fusion.4.refs_1_.refs_0_, bf16[2,2,6,64,128]{4,3,2,1,0:T(8,128)(2,1)S(1)} %collective-permute-done.refs_2_.refs_1_, ...), custom_call_target="tpu_custom_call" | custom-call | flops 6341787648 | bytes 2359296 | tf_op jit(solution)/shard_map/pallas_call | solution.py:162
  86.6 1.0 %collective-permute-start.19 = (bf16[2,2,3,64,128]{4,3,2,1,0:T(8,128)(2,1)S(1)}, bf16[2,2,3,64,128]{4,3,2,1,0:T(8,128)(2,1)S(1)}, u32[]{:S(2)}, u32[]{:S(2)}) collective-permute-start(bf16[2,2,3,64,128]{4,3,2,1,0:T(8,128)(2,1)S(1)} %get-tuple-element.69), channel_id=1, source_target_pairs={{0,1},{1,0},{2,3},{3,2},{4,5},{5,4},{6,7},{7,6},{8,9},{9,8},{10,11... | collective-permute-start | bytes 589832 | tf_op jit(solution)/shard_map/ppermute | solution.py:189
  87.8 1.6 %collective-permute-done.18 = bf16[2,2,3,64,128]{4,3,2,1,0:T(8,128)(2,1)S(1)} collective-permute-done((bf16[2,2,3,64,128]{4,3,2,1,0:T(8,128)(2,1)S(1)}, bf16[2,2,3,64,128]{4,3,2,1,0:T(8,128)(2,1)S(1)}, u32[]{:S(2)}, u32[]{:S(2)}) %collective-permute-start.18) | collective-permute-done | bytes 196640 | tf_op jit(solution)/shard_map/ppermute | solution.py:189
  89.8 0.9 %slice_bitcast_fusion.2 = (bf16[2,8,8,12,128]{4,2,3,1,0:T(8,128)(2,1)}, bf16[2,8,8,12,128]{4,2,3,1,0:T(8,128)(2,1)}) fusion(bf16[2,2,8,8,12,128]{5,3,4,2,1,0:T(8,128)(2,1)S(1)} %bitcast.182), kind=kLoop, calls=%fused_computation.12 | loop fusion | bytes 1572864 | tf_op jit(solution)/shard_map/squeeze | solution.py:267
  90.8 1.7 %collective-permute-done.19 = bf16[2,2,3,64,128]{4,3,2,1,0:T(8,128)(2,1)S(1)} collective-permute-done((bf16[2,2,3,64,128]{4,3,2,1,0:T(8,128)(2,1)S(1)}, bf16[2,2,3,64,128]{4,3,2,1,0:T(8,128)(2,1)S(1)}, u32[]{:S(2)}, u32[]{:S(2)}) %collective-permute-start.19) | collective-permute-done | bytes 196640 | tf_op jit(solution)/shard_map/ppermute | solution.py:189
  92.6 0.9 %slice_bitcast_fusion = (bf16[2,8,8,12,128]{4,2,3,1,0:T(8,128)(2,1)}, bf16[2,8,8,12,128]{4,2,3,1,0:T(8,128)(2,1)}) fusion(bf16[2,2,8,8,12,128]{5,3,4,2,1,0:T(8,128)(2,1)S(1)} %bitcast.183), kind=kLoop, calls=%fused_computation.10 | loop fusion | bytes 1572864 | tf_op jit(solution)/shard_map/squeeze | solution.py:267
  (101 shorter events, 6.0 us)
Async XLA Ops:
  2.0 1.7 %copy-start.3 = (s32[8,4,2,27]{3,2,1,0:T(2,128)S(1)}, s32[8,4,2,27]{3,2,1,0:T(2,128)}, u32[]{:S(2)}) copy-start(s32[8,4,2,27]{3,2,1,0:T(2,128)} %param.11) | copy-start | bytes 20740
  2.0 3.3 %copy-start.4 = (bf16[4,3,9,2,9,1]{4,2,1,0,5,3:T(8,128)(2,1)S(1)}, bf16[4,3,9,2,9,1]{4,2,1,0,5,3:T(8,128)(2,1)}, u32[]{:S(2)}) copy-start(bf16[4,3,9,2,9,1]{4,2,1,0,5,3:T(8,128)(2,1)} %constant.219) | copy-start | bytes 11668
  2.1 3.9 %copy-start.2 = (bf16[18,1152]{1,0:T(8,128)(2,1)S(1)}, bf16[18,1152]{1,0:T(8,128)(2,1)}, u32[]{:S(2)}) copy-start(bf16[18,1152]{1,0:T(8,128)(2,1)} %constant.114.clone) | copy-start | bytes 124420
  2.1 10.0 %collective-permute-start = (bf16[2,2,6,64,128]{4,3,2,1,0:T(8,128)(2,1)S(1)}, bf16[2,2,6,64,128]{4,3,2,1,0:T(8,128)(2,1)S(1)}, u32[]{:S(2)}, u32[]{:S(2)}) collective-permute-start(bf16[2,2,6,64,128]{4,3,2,1,0:T(8,128)(2,1)S(1)} %pad_maximum_fusion.3), channel_id=1, source_target_pairs={{0,1},{1,0},{2,3},{3,2},{4,5},{5,4},{6,7},{7,6},{8,9},{9,8},{10,11... | collective-permute-start | bytes 1179656 | tf_op jit(solution)/shard_map/ppermute | solution.py:189
  3.6 8.0 %copy-start = (bf16[2,8,8,12,128]{4,2,3,1,0:T(8,128)(2,1)S(1)}, bf16[2,8,8,12,128]{4,2,3,1,0:T(8,128)(2,1)}, u32[]{:S(2)}) copy-start(bf16[2,8,8,12,128]{4,2,3,1,0:T(8,128)(2,1)} %param.10) | copy-start | bytes 1179652
  3.6 8.0 %copy-start.1 = (bf16[2,8,8,12,128]{4,2,3,1,0:T(8,128)(2,1)S(1)}, bf16[2,8,8,12,128]{4,2,3,1,0:T(8,128)(2,1)}, u32[]{:S(2)}) copy-start(bf16[2,8,8,12,128]{4,2,3,1,0:T(8,128)(2,1)} %param.7) | copy-start | bytes 1179652
  6.2 12.5 %collective-permute-start.2 = (bf16[2,2,6,64,128]{4,3,2,1,0:T(8,128)(2,1)S(1)}, bf16[2,2,6,64,128]{4,3,2,1,0:T(8,128)(2,1)S(1)}, u32[]{:S(2)}, u32[]{:S(2)}) collective-permute-start(bf16[2,2,6,64,128]{4,3,2,1,0:T(8,128)(2,1)S(1)} %pad_maximum_fusion.4.refs_1_.refs_0_), channel_id=1, source_target_pairs={{0,2},{2,4},{4,6},{1,3},{3,5},{5,7},{8,10},{10,12},{12,14},{9,11},... | collective-permute-start | bytes 1179656 | tf_op jit(solution)/shard_map/ppermute | solution.py:184
  9.5 19.9 %collective-permute-start.4 = (bf16[2,2,6,64,128]{4,3,2,1,0:T(8,128)(2,1)S(1)}, bf16[2,2,6,64,128]{4,3,2,1,0:T(8,128)(2,1)S(1)}, u32[]{:S(2)}, u32[]{:S(2)}) collective-permute-start(bf16[2,2,6,64,128]{4,3,2,1,0:T(8,128)(2,1)S(1)} %pad_maximum_fusion.4.refs_1_.refs_0_), channel_id=1, source_target_pairs={{2,0},{4,2},{6,4},{3,1},{5,3},{7,5},{10,8},{12,10},{14,12},{11,9},... | collective-permute-start | bytes 1179656 | tf_op jit(solution)/shard_map/ppermute | solution.py:184
  12.2 19.4 %collective-permute-start.3 = (bf16[2,2,6,64,128]{4,3,2,1,0:T(8,128)(2,1)S(1)}, bf16[2,2,6,64,128]{4,3,2,1,0:T(8,128)(2,1)S(1)}, u32[]{:S(2)}, u32[]{:S(2)}) collective-permute-start(bf16[2,2,6,64,128]{4,3,2,1,0:T(8,128)(2,1)S(1)} %collective-permute-done.refs_2_.refs_1_), channel_id=1, source_target_pairs={{0,2},{2,4},{4,6},{1,3},{3,5},{5,7},{8,10},{10,12},{12,14},{9,11},... | collective-permute-start | bytes 1179656 | tf_op jit(solution)/shard_map/ppermute | solution.py:184
  15.4 16.4 %collective-permute-start.5 = (bf16[2,2,6,64,128]{4,3,2,1,0:T(8,128)(2,1)S(1)}, bf16[2,2,6,64,128]{4,3,2,1,0:T(8,128)(2,1)S(1)}, u32[]{:S(2)}, u32[]{:S(2)}) collective-permute-start(bf16[2,2,6,64,128]{4,3,2,1,0:T(8,128)(2,1)S(1)} %collective-permute-done.refs_2_.refs_1_), channel_id=1, source_target_pairs={{2,0},{4,2},{6,4},{3,1},{5,3},{7,5},{10,8},{12,10},{14,12},{11,9},... | collective-permute-start | bytes 1179656 | tf_op jit(solution)/shard_map/ppermute | solution.py:184
  17.5 8.6 %collective-permute-start.1 = (bf16[2,2,6,64,128]{4,3,2,1,0:T(8,128)(2,1)S(1)}, bf16[2,2,6,64,128]{4,3,2,1,0:T(8,128)(2,1)S(1)}, u32[]{:S(2)}, u32[]{:S(2)}) collective-permute-start(bf16[2,2,6,64,128]{4,3,2,1,0:T(8,128)(2,1)S(1)} %pad_maximum_fusion.2), channel_id=1, source_target_pairs={{0,1},{1,0},{2,3},{3,2},{4,5},{5,4},{6,7},{7,6},{8,9},{9,8},{10,11... | collective-permute-start | bytes 1179656 | tf_op jit(solution)/shard_map/ppermute | solution.py:189
  26.1 17.9 %collective-permute-start.12 = (bf16[2,2,2,6,64,128]{5,4,3,2,0,1:T(8,128)(2,1)S(1)}, bf16[2,2,2,6,64,128]{5,4,3,2,0,1:T(8,128)(2,1)S(1)}, u32[]{:S(2)}, u32[]{:S(2)}) collective-permute-start(bf16[2,2,2,6,64,128]{5,4,3,2,0,1:T(8,128)(2,1)S(1)} %pad_maximum_fusion), channel_id=1, source_target_pairs={{0,2},{2,4},{4,6},{1,3},{3,5},{5,7},{8,10},{10,12},{12,14},{9,11},... | collective-permute-start | bytes 2359304 | tf_op jit(solution)/shard_map/ppermute | solution.py:184
  29.5 17.6 %collective-permute-start.13 = (bf16[2,2,2,6,64,128]{5,4,3,2,1,0:T(8,128)(2,1)S(1)}, bf16[2,2,2,6,64,128]{5,4,3,2,1,0:T(8,128)(2,1)S(1)}, u32[]{:S(2)}, u32[]{:S(2)}) collective-permute-start(bf16[2,2,2,6,64,128]{5,4,3,2,1,0:T(8,128)(2,1)S(1)} %copy.57.refs_0_.refs_2_), channel_id=1, source_target_pairs={{2,0},{4,2},{6,4},{3,1},{5,3},{7,5},{10,8},{12,10},{14,12},{11,9},... | collective-permute-start | bytes 2359304 | tf_op jit(solution)/shard_map/ppermute | solution.py:184
  31.8 24.8 %collective-permute-start.6 = (bf16[6,2,6,64,128]{4,3,2,1,0:T(8,128)(2,1)S(1)}, bf16[6,2,6,64,128]{4,3,2,1,0:T(8,128)(2,1)S(1)}, u32[]{:S(2)}, u32[]{:S(2)}) collective-permute-start(bf16[6,2,6,64,128]{4,3,2,1,0:T(8,128)(2,1)S(1)} %get-tuple-element.87), channel_id=1, source_target_pairs={{0,8},{8,16},{16,24},{1,9},{9,17},{17,25},{2,10},{10,18},{18,26},{... | collective-permute-start | bytes 3538952 | tf_op jit(solution)/shard_map/ppermute | solution.py:184
  38.5 18.1 %collective-permute-start.7 = (bf16[6,2,6,64,128]{4,3,2,1,0:T(8,128)(2,1)S(1)}, bf16[6,2,6,64,128]{4,3,2,1,0:T(8,128)(2,1)S(1)}, u32[]{:S(2)}, u32[]{:S(2)}) collective-permute-start(bf16[6,2,6,64,128]{4,3,2,1,0:T(8,128)(2,1)S(1)} %get-tuple-element.86), channel_id=1, source_target_pairs={{8,0},{16,8},{24,16},{9,1},{17,9},{25,17},{10,2},{18,10},{26,18},{... | collective-permute-start | bytes 3538952 | tf_op jit(solution)/shard_map/ppermute | solution.py:184
  47.3 33.4 %collective-permute-start.14 = (bf16[6,2,6,64,128]{4,3,2,1,0:T(8,128)(2,1)S(1)}, bf16[6,2,6,64,128]{4,3,2,1,0:T(8,128)(2,1)S(1)}, u32[]{:S(2)}, u32[]{:S(2)}) collective-permute-start(bf16[6,2,6,64,128]{4,3,2,1,0:T(8,128)(2,1)S(1)} %get-tuple-element.75), channel_id=1, source_target_pairs={{0,8},{8,16},{16,24},{1,9},{9,17},{17,25},{2,10},{10,18},{18,26},{... | collective-permute-start | bytes 3538952 | tf_op jit(solution)/shard_map/ppermute | solution.py:184
  54.6 26.1 %collective-permute-start.15 = (bf16[6,2,6,64,128]{4,3,2,1,0:T(8,128)(2,1)S(1)}, bf16[6,2,6,64,128]{4,3,2,1,0:T(8,128)(2,1)S(1)}, u32[]{:S(2)}, u32[]{:S(2)}) collective-permute-start(bf16[6,2,6,64,128]{4,3,2,1,0:T(8,128)(2,1)S(1)} %get-tuple-element.74), channel_id=1, source_target_pairs={{8,0},{16,8},{24,16},{9,1},{17,9},{25,17},{10,2},{18,10},{26,18},{... | collective-permute-start | bytes 3538952 | tf_op jit(solution)/shard_map/ppermute | solution.py:184
  61.8 8.9 %collective-permute-start.9 = (f32[2,6,2,128]{3,2,1,0:T(2,128)S(1)}, f32[2,6,2,128]{3,2,1,0:T(2,128)S(1)}, u32[]{:S(2)}, u32[]{:S(2)}) collective-permute-start(f32[2,6,2,128]{3,2,1,0:T(2,128)S(1)} %get-tuple-element.47.refs_10_.refs_7_), channel_id=1, source_target_pairs={{0,2},{2,4},{4,6},{1,3},{3,5},{5,7},{8,10},{10,12},{12,14},{9,11},... | collective-permute-start | bytes 36872 | tf_op jit(solution)/shard_map/ppermute | solution.py:184
  65.1 5.7 %collective-permute-start.10 = (f32[2,6,2,128]{3,2,1,0:T(2,128)S(1)}, f32[2,6,2,128]{3,2,1,0:T(2,128)S(1)}, u32[]{:S(2)}, u32[]{:S(2)}) collective-permute-start(f32[2,6,2,128]{3,2,1,0:T(2,128)S(1)} %get-tuple-element.47.refs_10_.refs_7_), channel_id=1, source_target_pairs={{2,0},{4,2},{6,4},{3,1},{5,3},{7,5},{10,8},{12,10},{14,12},{11,9},... | collective-permute-start | bytes 36872 | tf_op jit(solution)/shard_map/ppermute | solution.py:184
  69.5 18.3 %collective-permute-start.8 = (bf16[2,2,3,64,128]{4,3,2,1,0:T(8,128)(2,1)S(1)}, bf16[2,2,3,64,128]{4,3,2,1,0:T(8,128)(2,1)S(1)}, u32[]{:S(2)}, u32[]{:S(2)}) collective-permute-start(bf16[2,2,3,64,128]{4,3,2,1,0:T(8,128)(2,1)S(1)} %get-tuple-element.46), channel_id=1, source_target_pairs={{0,1},{1,0},{2,3},{3,2},{4,5},{5,4},{6,7},{7,6},{8,9},{9,8},{10,11... | collective-permute-start | bytes 589832 | tf_op jit(solution)/shard_map/ppermute | solution.py:189
  70.8 8.7 %collective-permute-start.16 = (f32[3,6,2,128]{3,2,1,0:T(2,128)S(1)}, f32[3,6,2,128]{3,2,1,0:T(2,128)S(1)}, u32[]{:S(2)}, u32[]{:S(2)}) collective-permute-start(f32[3,6,2,128]{3,2,1,0:T(2,128)S(1)} %pad_maximum_fusion.5), channel_id=1, source_target_pairs={{0,8},{8,16},{16,24},{1,9},{9,17},{17,25},{2,10},{10,18},{18,26},{... | collective-permute-start | bytes 55304 | tf_op jit(solution)/shard_map/ppermute | solution.py:184
  75.3 5.4 %collective-permute-start.17 = (f32[3,6,2,128]{3,2,1,0:T(2,128)S(1)}, f32[3,6,2,128]{3,2,1,0:T(2,128)S(1)}, u32[]{:S(2)}, u32[]{:S(2)}) collective-permute-start(f32[3,6,2,128]{3,2,1,0:T(2,128)S(1)} %pad_maximum_fusion.6), channel_id=1, source_target_pairs={{8,0},{16,8},{24,16},{9,1},{17,9},{25,17},{10,2},{18,10},{26,18},{... | collective-permute-start | bytes 55304 | tf_op jit(solution)/shard_map/ppermute | solution.py:184
  79.6 8.3 %collective-permute-start.11 = (bf16[2,2,3,64,128]{4,3,2,1,0:T(8,128)(2,1)S(1)}, bf16[2,2,3,64,128]{4,3,2,1,0:T(8,128)(2,1)S(1)}, u32[]{:S(2)}, u32[]{:S(2)}) collective-permute-start(bf16[2,2,3,64,128]{4,3,2,1,0:T(8,128)(2,1)S(1)} %get-tuple-element.49), channel_id=1, source_target_pairs={{0,1},{1,0},{2,3},{3,2},{4,5},{5,4},{6,7},{7,6},{8,9},{9,8},{10,11... | collective-permute-start | bytes 589832 | tf_op jit(solution)/shard_map/ppermute | solution.py:189
  83.4 6.0 %collective-permute-start.18 = (bf16[2,2,3,64,128]{4,3,2,1,0:T(8,128)(2,1)S(1)}, bf16[2,2,3,64,128]{4,3,2,1,0:T(8,128)(2,1)S(1)}, u32[]{:S(2)}, u32[]{:S(2)}) collective-permute-start(bf16[2,2,3,64,128]{4,3,2,1,0:T(8,128)(2,1)S(1)} %get-tuple-element.56), channel_id=1, source_target_pairs={{0,1},{1,0},{2,3},{3,2},{4,5},{5,4},{6,7},{7,6},{8,9},{9,8},{10,11... | collective-permute-start | bytes 589832 | tf_op jit(solution)/shard_map/ppermute | solution.py:189
  86.6 6.0 %collective-permute-start.19 = (bf16[2,2,3,64,128]{4,3,2,1,0:T(8,128)(2,1)S(1)}, bf16[2,2,3,64,128]{4,3,2,1,0:T(8,128)(2,1)S(1)}, u32[]{:S(2)}, u32[]{:S(2)}) collective-permute-start(bf16[2,2,3,64,128]{4,3,2,1,0:T(8,128)(2,1)S(1)} %get-tuple-element.69), channel_id=1, source_target_pairs={{0,1},{1,0},{2,3},{3,2},{4,5},{5,4},{6,7},{7,6},{8,9},{9,8},{10,11... | collective-permute-start | bytes 589832 | tf_op jit(solution)/shard_map/ppermute | solution.py:189

commit v15 on v14

--- a/solution.py
+++ b/solution.py
@@ -30,14 +30,17 @@
     for at in range(frames + 2):
         for row in range(3):
             for part in range(parts):
-                place = pl.ds(((3 * at + row) * parts + part) * cells, cells)
                 for which, band in enumerate(bands):
                     if at == 0:
-                        band[place, :] = edge(0, row, part, which)
+                        band.append(edge(0, row, part, which))
                     elif at == frames + 1:
-                        band[place, :] = edge(1, row, part, which)
+                        band.append(edge(1, row, part, which))
                     else:
-                        band[place, :] = side(row, part, at - 1, which)
+                        band.append(side(row, part, at - 1, which))
+
+
+def window(band, parts, at):
+    return jnp.concatenate(band[3 * at * parts : (3 * at + 9) * parts], axis=0)
 
 
 def fill_keys(head, parts, halo, bands):
@@ -66,18 +69,18 @@
 def attend_kernel(scaling, parts, first, *refs):
     head = pl.program_id(0) + first
     pair, halo = refs[0], refs[1 : 3 * parts + 3]
-    bias, attended, stats, key_all, value_all = refs[3 * parts + 3 :]
+    bias, attended, stats = refs[3 * parts + 3 :]
+    key_all, value_all = [], []
     frames, _, tokens, _ = attended.shape
     fill_keys(head, parts, halo, (key_all, value_all))
-    windows = [pl.ds(3 * at * tokens, 9 * tokens) for at in range(frames)]
     scores = [
-        dot(slab(head, pair, at, 0), key_all[windows[at], :], NT) * (scaling * LOG2E) + spread(bias[at], tokens)
+        dot(slab(head, pair, at, 0), window(key_all, parts, at), NT) * (scaling * LOG2E) + spread(bias[at], tokens)
         for at in range(frames)
     ]
     highest = [jnp.max(part, axis=1, keepdims=True) for part in scores]
     raised = [jnp.exp2(part - top) for part, top in zip(scores, highest)]
     total = [jnp.sum(part, axis=1, keepdims=True) for part in raised]
-    sums = [dot(raised[at].astype(jnp.bfloat16), value_all[windows[at], :], NN) for at in range(frames)]
+    sums = [dot(raised[at].astype(jnp.bfloat16), window(value_all, parts, at), NN) for at in range(frames)]
     for at in range(frames):
         out = (sums[at] * (1.0 / total[at])).astype(jnp.bfloat16)
         grad = slab(head, pair, at, 1).astype(jnp.float32)
@@ -100,22 +103,22 @@
     head = pl.program_id(0) + first
     pair, halo = refs[0], refs[1 : 3 * parts + 3]
     attended, stats, bias = refs[3 * parts + 3 : 3 * parts + 6]
-    grads, (key_all, value_all) = refs[3 * parts + 6 : -2], refs[-2:]
+    grads = refs[3 * parts + 6 :]
+    key_all, value_all = [], []
     frames, _, tokens, _ = attended.shape
     fill_keys(head, parts, halo, (key_all, value_all))
-    windows = [pl.ds(3 * at * tokens, 9 * tokens) for at in range(frames)]
 
     def column(at, which):
         wide = jnp.broadcast_to(stats[at, 0, which : which + 1], (128, tokens))
         return jnp.transpose(wide)[:, :1]
 
-    scores = [dot(slab(head, pair, at, 0), key_all[windows[at], :], NT) for at in range(frames)]
-    grad_probs = [dot(slab(head, pair, at, 1), value_all[windows[at], :], NT) for at in range(frames)]
+    scores = [dot(slab(head, pair, at, 0), window(key_all, parts, at), NT) for at in range(frames)]
+    grad_probs = [dot(slab(head, pair, at, 1), window(value_all, parts, at), NT) for at in range(frames)]
     for at in range(frames):
         shift = spread(bias[at], tokens) - column(at, 0)
         weights = jnp.exp2(scores[at] * (scaling * LOG2E) + shift)
         grad_scores = (weights * (grad_probs[at] - column(at, 1))).astype(jnp.bfloat16)
-        query_grad = dot(grad_scores, key_all[windows[at], :], NN) * scaling
+        query_grad = dot(grad_scores, window(key_all, parts, at), NN) * scaling
         store(grads, at, attended[at, 0], query_grad.astype(jnp.bfloat16))
 
 
@@ -123,7 +126,8 @@
     head = pl.program_id(0) + first
     pair, halo = list(refs[:parts]), refs[parts : parts + 5]
     own_st, before_st, after_st, low_st, high_st, bias = refs[parts + 5 : parts + 11]
-    grads, (query_all, grad_all) = refs[parts + 11 : -2], refs[-2:]
+    grads = refs[parts + 11 :]
+    query_all, grad_all = [], []
     frames, _, _, tokens = own_st.shape
     fill_queries(head, halo, (query_all, grad_all))
 
@@ -138,15 +142,14 @@
         rows = [stat_row(at + step, row, which) for step in range(3) for row in range(3)]
         return jnp.concatenate(rows, axis=1)
 
-    windows = [pl.ds(3 * at * tokens, 9 * tokens) for at in range(frames)]
-    scores = [dot(slab(head, pair, at, 0), query_all[windows[at], :], NT) for at in range(frames)]
-    grad_probs = [dot(slab(head, pair, at, 1), grad_all[windows[at], :], NT) for at in range(frames)]
+    scores = [dot(slab(head, pair, at, 0), window(query_all, parts, at), NT) for at in range(frames)]
+    grad_probs = [dot(slab(head, pair, at, 1), window(grad_all, parts, at), NT) for at in range(frames)]
     for at in range(frames):
         shift = spread(bias[at] - stat_band(at, 0), tokens)
         weights = jnp.exp2(scores[at] * (scaling * LOG2E) + shift).astype(jnp.bfloat16)
         grad_scores = weights.astype(jnp.float32) * (grad_probs[at] - stat_band(at, 1))
-        key_grad = dot(grad_scores.astype(jnp.bfloat16), query_all[windows[at], :], NN) * scaling
-        value_grad = dot(weights, grad_all[windows[at], :], NN)
+        key_grad = dot(grad_scores.astype(jnp.bfloat16), window(query_all, parts, at), NN) * scaling
+        value_grad = dot(weights, window(grad_all, parts, at), NN)
         store(grads, at, key_grad.astype(jnp.bfloat16), value_grad.astype(jnp.bfloat16))
 
 
@@ -169,7 +172,6 @@
         ]
         + [pl.BlockSpec(bias.shape, lambda head: (0,) * bias.ndim)],
         out_specs=tuple(head_spec(out.shape, 0) for out in outs),
-        scratch_shapes=[pltpu.VMEM((3 * (frames + 2) * tokens, dim), jnp.bfloat16)] * 2,
         compiler_params=pltpu.CompilerParams(vmem_limit_bytes=16 * 2**20),
         cost_estimate=pl.CostEstimate(
             flops=7 * frames * count * 2 * products * tokens * 9 * tokens * dim,

time: 95.2 us -> 94.9 us (level)
  no operation moved by 1% of the time
where the time goes in v15:
time: 94.9 us; the launch traced here: 93.2 us
  starting transfers between devices  51.4 us (54%)
  waiting for transfers between devices  17.9 us (19%)
  Pallas kernels  14.7 us (15%)
  local copies, waits for them, and re-layouts  6.31 us (7%)
  between operations  1.37 us (1%)
    ppermute x14, starting transfers between devices, step_along(): lax.ppermute(tensor, axis, [(i, i + sign) for i in range(size) if 0 <= i...  45.3 us
    pallas_call x5, Pallas kernels, run(): pl.pallas_call(functools.partial(kernel, scaling, parts, first), grid=(co...  14.7 us
    ppermute x6, waiting for transfers between devices, turn(): lax.ppermute(tensor, 'head', [(i, (i + shift) % size) for i in range(size)])  10.8 us
    ppermute x14, waiting for transfers between devices, step_along(): lax.ppermute(tensor, axis, [(i, i + sign) for i in range(size) if 0 <= i...  7.08 us
    ppermute x6, starting transfers between devices, turn(): lax.ppermute(tensor, 'head', [(i, (i + shift) % size) for i in range(size)])  6.1 us
  transfers between devices with their start and end apart: 20, of which 7 were waited for; matrix products, arithmetic and copies ran while one was open for 6% of the time, Pallas kernels for 16%

profile of v15, /device:TPU:9, one launch (start us, length us, event | category | flops | bytes accessed | tf_op | source)
XLA Modules:
  0.0 93.2 jit_solution(1357464232077242098)
XLA Ops:
  0.7 1.3 %dynamic-slice_bitcast_fusion = (bf16[2,6,8,8,128]{4,3,1,2,0:T(8,128)(2,1)S(1)}, bf16[2,6,8,8,128]{4,3,1,2,0:T(8,128)(2,1)S(1)}, bf16[2,6,8,8,128]{4,3,1,2,0:T(8,128)(2,1)S(1)}, bf16[2,6,8,8,128]{4,3,1,2,0:T(8,128)(2,1)S(1)}) fusion(bf16[2,8,8,12,128]{4,2,3,1,0:T(8,128)(2,1)} %param.9, s32[]{:T(128)S(6)} %select_n.105, s32[]{:T(128)S(6)} %select_n.107, ...), kind=kLoop, calls=%fused_computation.66 | loop fusion | bytes 1572872 | tf_op jit(solution)/shard_map/dynamic_slice | solution.py:252
  2.1 1.3 %collective-permute-start = (bf16[2,2,6,64,128]{4,3,2,1,0:T(8,128)(2,1)S(1)}, bf16[2,2,6,64,128]{4,3,2,1,0:T(8,128)(2,1)S(1)}, u32[]{:S(2)}, u32[]{:S(2)}) collective-permute-start(bf16[2,2,6,64,128]{4,3,2,1,0:T(8,128)(2,1)S(1)} %pad_maximum_fusion.3), channel_id=1, source_target_pairs={{0,1},{1,0},{2,3},{3,2},{4,5},{5,4},{6,7},{7,6},{8,9},{9,8},{10,11... | collective-permute-start | bytes 1179656 | tf_op jit(solution)/shard_map/ppermute | solution.py:191
  6.2 3.2 %collective-permute-start.2 = (bf16[2,2,6,64,128]{4,3,2,1,0:T(8,128)(2,1)S(1)}, bf16[2,2,6,64,128]{4,3,2,1,0:T(8,128)(2,1)S(1)}, u32[]{:S(2)}, u32[]{:S(2)}) collective-permute-start(bf16[2,2,6,64,128]{4,3,2,1,0:T(8,128)(2,1)S(1)} %pad_maximum_fusion.4.refs_1_.refs_0_), channel_id=1, source_target_pairs={{0,2},{2,4},{4,6},{1,3},{3,5},{5,7},{8,10},{10,12},{12,14},{9,11},... | collective-permute-start | bytes 1179656 | tf_op jit(solution)/shard_map/ppermute | solution.py:186
  9.5 2.1 %collective-permute-start.4 = (bf16[2,2,6,64,128]{4,3,2,1,0:T(8,128)(2,1)S(1)}, bf16[2,2,6,64,128]{4,3,2,1,0:T(8,128)(2,1)S(1)}, u32[]{:S(2)}, u32[]{:S(2)}) collective-permute-start(bf16[2,2,6,64,128]{4,3,2,1,0:T(8,128)(2,1)S(1)} %pad_maximum_fusion.4.refs_1_.refs_0_), channel_id=1, source_target_pairs={{2,0},{4,2},{6,4},{3,1},{5,3},{7,5},{10,8},{12,10},{14,12},{11,9},... | collective-permute-start | bytes 1179656 | tf_op jit(solution)/shard_map/ppermute | solution.py:186
  12.2 3.2 %collective-permute-start.3 = (bf16[2,2,6,64,128]{4,3,2,1,0:T(8,128)(2,1)S(1)}, bf16[2,2,6,64,128]{4,3,2,1,0:T(8,128)(2,1)S(1)}, u32[]{:S(2)}, u32[]{:S(2)}) collective-permute-start(bf16[2,2,6,64,128]{4,3,2,1,0:T(8,128)(2,1)S(1)} %collective-permute-done.refs_2_.refs_1_), channel_id=1, source_target_pairs={{0,2},{2,4},{4,6},{1,3},{3,5},{5,7},{8,10},{10,12},{12,14},{9,11},... | collective-permute-start | bytes 1179656 | tf_op jit(solution)/shard_map/ppermute | solution.py:186
  15.4 2.1 %collective-permute-start.5 = (bf16[2,2,6,64,128]{4,3,2,1,0:T(8,128)(2,1)S(1)}, bf16[2,2,6,64,128]{4,3,2,1,0:T(8,128)(2,1)S(1)}, u32[]{:S(2)}, u32[]{:S(2)}) collective-permute-start(bf16[2,2,6,64,128]{4,3,2,1,0:T(8,128)(2,1)S(1)} %collective-permute-done.refs_2_.refs_1_), channel_id=1, source_target_pairs={{2,0},{4,2},{6,4},{3,1},{5,3},{7,5},{10,8},{12,10},{14,12},{11,9},... | collective-permute-start | bytes 1179656 | tf_op jit(solution)/shard_map/ppermute | solution.py:186
  17.5 1.3 %collective-permute-start.1 = (bf16[2,2,6,64,128]{4,3,2,1,0:T(8,128)(2,1)S(1)}, bf16[2,2,6,64,128]{4,3,2,1,0:T(8,128)(2,1)S(1)}, u32[]{:S(2)}, u32[]{:S(2)}) collective-permute-start(bf16[2,2,6,64,128]{4,3,2,1,0:T(8,128)(2,1)S(1)} %pad_maximum_fusion.2), channel_id=1, source_target_pairs={{0,1},{1,0},{2,3},{3,2},{4,5},{5,4},{6,7},{7,6},{8,9},{9,8},{10,11... | collective-permute-start | bytes 1179656 | tf_op jit(solution)/shard_map/ppermute | solution.py:191
  18.9 7.2 %collective-permute-done.1 = bf16[2,2,6,64,128]{4,3,2,1,0:T(8,128)(2,1)S(1)} collective-permute-done((bf16[2,2,6,64,128]{4,3,2,1,0:T(8,128)(2,1)S(1)}, bf16[2,2,6,64,128]{4,3,2,1,0:T(8,128)(2,1)S(1)}, u32[]{:S(2)}, u32[]{:S(2)}) %collective-permute-start.1) | collective-permute-done | bytes 393248 | tf_op jit(solution)/shard_map/ppermute | solution.py:191
  26.1 3.2 %collective-permute-start.12 = (bf16[2,2,2,6,64,128]{5,4,3,2,0,1:T(8,128)(2,1)S(1)}, bf16[2,2,2,6,64,128]{5,4,3,2,0,1:T(8,128)(2,1)S(1)}, u32[]{:S(2)}, u32[]{:S(2)}) collective-permute-start(bf16[2,2,2,6,64,128]{5,4,3,2,0,1:T(8,128)(2,1)S(1)} %pad_maximum_fusion), channel_id=1, source_target_pairs={{0,2},{2,4},{4,6},{1,3},{3,5},{5,7},{8,10},{10,12},{12,14},{9,11},... | collective-permute-start | bytes 2359304 | tf_op jit(solution)/shard_map/ppermute | solution.py:186
  29.5 2.1 %collective-permute-start.13 = (bf16[2,2,2,6,64,128]{5,4,3,2,1,0:T(8,128)(2,1)S(1)}, bf16[2,2,2,6,64,128]{5,4,3,2,1,0:T(8,128)(2,1)S(1)}, u32[]{:S(2)}, u32[]{:S(2)}) collective-permute-start(bf16[2,2,2,6,64,128]{5,4,3,2,1,0:T(8,128)(2,1)S(1)} %copy.57.refs_0_.refs_2_), channel_id=1, source_target_pairs={{2,0},{4,2},{6,4},{3,1},{5,3},{7,5},{10,8},{12,10},{14,12},{11,9},... | collective-permute-start | bytes 2359304 | tf_op jit(solution)/shard_map/ppermute | solution.py:186
  31.8 6.6 %collective-permute-start.6 = (bf16[6,2,6,64,128]{4,3,2,1,0:T(8,128)(2,1)S(1)}, bf16[6,2,6,64,128]{4,3,2,1,0:T(8,128)(2,1)S(1)}, u32[]{:S(2)}, u32[]{:S(2)}) collective-permute-start(bf16[6,2,6,64,128]{4,3,2,1,0:T(8,128)(2,1)S(1)} %get-tuple-element.87), channel_id=1, source_target_pairs={{0,8},{8,16},{16,24},{1,9},{9,17},{17,25},{2,10},{10,18},{18,26},{... | collective-permute-start | bytes 3538952 | tf_op jit(solution)/shard_map/ppermute | solution.py:186
  38.5 1.9 %collective-permute-start.7 = (bf16[6,2,6,64,128]{4,3,2,1,0:T(8,128)(2,1)S(1)}, bf16[6,2,6,64,128]{4,3,2,1,0:T(8,128)(2,1)S(1)}, u32[]{:S(2)}, u32[]{:S(2)}) collective-permute-start(bf16[6,2,6,64,128]{4,3,2,1,0:T(8,128)(2,1)S(1)} %get-tuple-element.86), channel_id=1, source_target_pairs={{8,0},{16,8},{24,16},{9,1},{17,9},{25,17},{10,2},{18,10},{26,18},{... | collective-permute-start | bytes 3538952 | tf_op jit(solution)/shard_map/ppermute | solution.py:186
  40.4 3.7 %collective-permute-done.12 = bf16[2,2,2,6,64,128]{5,4,3,2,0,1:T(8,128)(2,1)S(1)} collective-permute-done((bf16[2,2,2,6,64,128]{5,4,3,2,0,1:T(8,128)(2,1)S(1)}, bf16[2,2,2,6,64,128]{5,4,3,2,0,1:T(8,128)(2,1)S(1)}, u32[]{:S(2)}, u32[]{:S(2)}) %collective-permute-start.12) | collective-permute-done | bytes 786464 | tf_op jit(solution)/shard_map/ppermute | solution.py:186
  44.1 3.0 %collective-permute-done.13.refs_4_ = bf16[2,2,2,6,64,128]{5,4,3,2,1,0:T(8,128)(2,1)S(1)} collective-permute-done((bf16[2,2,2,6,64,128]{5,4,3,2,1,0:T(8,128)(2,1)S(1)}, bf16[2,2,2,6,64,128]{5,4,3,2,1,0:T(8,128)(2,1)S(1)}, u32[]{:S(2)}, u32[]{:S(2)}) %collective-permute-start.13) | collective-permute-done | bytes 786464 | tf_op jit(solution)/shard_map/ppermute | solution.py:186
  47.3 7.3 %collective-permute-start.14 = (bf16[6,2,6,64,128]{4,3,2,1,0:T(8,128)(2,1)S(1)}, bf16[6,2,6,64,128]{4,3,2,1,0:T(8,128)(2,1)S(1)}, u32[]{:S(2)}, u32[]{:S(2)}) collective-permute-start(bf16[6,2,6,64,128]{4,3,2,1,0:T(8,128)(2,1)S(1)} %get-tuple-element.75), channel_id=1, source_target_pairs={{0,8},{8,16},{16,24},{1,9},{9,17},{17,25},{2,10},{10,18},{18,26},{... | collective-permute-start | bytes 3538952 | tf_op jit(solution)/shard_map/ppermute | solution.py:186
  54.6 1.9 %collective-permute-start.15 = (bf16[6,2,6,64,128]{4,3,2,1,0:T(8,128)(2,1)S(1)}, bf16[6,2,6,64,128]{4,3,2,1,0:T(8,128)(2,1)S(1)}, u32[]{:S(2)}, u32[]{:S(2)}) collective-permute-start(bf16[6,2,6,64,128]{4,3,2,1,0:T(8,128)(2,1)S(1)} %get-tuple-element.74), channel_id=1, source_target_pairs={{8,0},{16,8},{24,16},{9,1},{17,9},{25,17},{10,2},{18,10},{26,18},{... | collective-permute-start | bytes 3538952 | tf_op jit(solution)/shard_map/ppermute | solution.py:186
  56.6 5.0 %shard_map.102 = (bf16[2,6,128,128]{3,2,1,0:T(8,128)(2,1)S(1)}, f32[2,6,2,128]{3,2,1,0:T(2,128)S(1)}) custom-call(bf16[2,2,2,6,64,128]{5,4,3,2,1,0:T(8,128)(2,1)S(1)} %copy.57.refs_0_.refs_2_, bf16[2,2,6,64,128]{4,3,2,1,0:T(8,128)(2,1)S(1)} %pad_maximum_fusion.4.refs_1_.refs_0_, bf16[2,2,6,64,128]{4,3,2,1,0:T(8,128)(2,1)S(1)} %collective-permute-done.refs_2_.refs_1_, ...), custom_call_target="tpu_custom_call" | custom-call | flops 6341787648 | bytes 4718592 | tf_op jit(solution)/shard_map/pallas_call | solution.py:165
  61.6 3.2 %collective-permute-start.9 = (f32[2,6,2,128]{3,2,1,0:T(2,128)S(1)}, f32[2,6,2,128]{3,2,1,0:T(2,128)S(1)}, u32[]{:S(2)}, u32[]{:S(2)}) collective-permute-start(f32[2,6,2,128]{3,2,1,0:T(2,128)S(1)} %get-tuple-element.47.refs_10_.refs_7_), channel_id=1, source_target_pairs={{0,2},{2,4},{4,6},{1,3},{3,5},{5,7},{8,10},{10,12},{12,14},{9,11},... | collective-permute-start | bytes 36872 | tf_op jit(solution)/shard_map/ppermute | solution.py:186
  64.8 2.1 %collective-permute-start.10 = (f32[2,6,2,128]{3,2,1,0:T(2,128)S(1)}, f32[2,6,2,128]{3,2,1,0:T(2,128)S(1)}, u32[]{:S(2)}, u32[]{:S(2)}) collective-permute-start(f32[2,6,2,128]{3,2,1,0:T(2,128)S(1)} %get-tuple-element.47.refs_10_.refs_7_), channel_id=1, source_target_pairs={{2,0},{4,2},{6,4},{3,1},{5,3},{7,5},{10,8},{12,10},{14,12},{11,9},... | collective-permute-start | bytes 36872 | tf_op jit(solution)/shard_map/ppermute | solution.py:186
  66.9 2.3 %shard_map.103 = (bf16[2,2,3,64,128]{4,3,2,1,0:T(8,128)(2,1)S(1)}, bf16[2,2,3,64,128]{4,3,2,1,0:T(8,128)(2,1)S(1)}) custom-call(bf16[2,2,2,6,64,128]{5,4,3,2,1,0:T(8,128)(2,1)S(1)} %copy.57.refs_0_.refs_2_, bf16[2,2,6,64,128]{4,3,2,1,0:T(8,128)(2,1)S(1)} %pad_maximum_fusion.4.refs_1_.refs_0_, ...), custom_call_target="tpu_custom_call" | custom-call | flops 4756340736 | bytes 2359296 | tf_op jit(solution)/shard_map/pallas_call | solution.py:165
  69.1 1.3 %collective-permute-start.8 = (bf16[2,2,3,64,128]{4,3,2,1,0:T(8,128)(2,1)S(1)}, bf16[2,2,3,64,128]{4,3,2,1,0:T(8,128)(2,1)S(1)}, u32[]{:S(2)}, u32[]{:S(2)}) collective-permute-start(bf16[2,2,3,64,128]{4,3,2,1,0:T(8,128)(2,1)S(1)} %get-tuple-element.46), channel_id=1, source_target_pairs={{0,1},{1,0},{2,3},{3,2},{4,5},{5,4},{6,7},{7,6},{8,9},{9,8},{10,11... | collective-permute-start | bytes 589832 | tf_op jit(solution)/shard_map/ppermute | solution.py:191
  70.5 4.5 %collective-permute-start.16 = (f32[3,6,2,128]{3,2,1,0:T(2,128)S(1)}, f32[3,6,2,128]{3,2,1,0:T(2,128)S(1)}, u32[]{:S(2)}, u32[]{:S(2)}) collective-permute-start(f32[3,6,2,128]{3,2,1,0:T(2,128)S(1)} %pad_maximum_fusion.5), channel_id=1, source_target_pairs={{0,8},{8,16},{16,24},{1,9},{9,17},{17,25},{2,10},{10,18},{18,26},{... | collective-permute-start | bytes 55304 | tf_op jit(solution)/shard_map/ppermute | solution.py:186
  75.0 1.9 %collective-permute-start.17 = (f32[3,6,2,128]{3,2,1,0:T(2,128)S(1)}, f32[3,6,2,128]{3,2,1,0:T(2,128)S(1)}, u32[]{:S(2)}, u32[]{:S(2)}) collective-permute-start(f32[3,6,2,128]{3,2,1,0:T(2,128)S(1)} %pad_maximum_fusion.6), channel_id=1, source_target_pairs={{8,0},{16,8},{24,16},{9,1},{17,9},{25,17},{10,2},{18,10},{26,18},{... | collective-permute-start | bytes 55304 | tf_op jit(solution)/shard_map/ppermute | solution.py:186
  76.9 2.3 %shard_map.104 = (bf16[2,2,3,64,128]{4,3,2,1,0:T(8,128)(2,1)S(1)}, bf16[2,2,3,64,128]{4,3,2,1,0:T(8,128)(2,1)S(1)}) custom-call(bf16[2,2,2,6,64,128]{5,4,3,2,1,0:T(8,128)(2,1)S(1)} %copy.57.refs_0_.refs_2_, bf16[2,2,6,64,128]{4,3,2,1,0:T(8,128)(2,1)S(1)} %pad_maximum_fusion.4.refs_1_.refs_0_, ...), custom_call_target="tpu_custom_call" | custom-call | flops 4756340736 | bytes 2359296 | tf_op jit(solution)/shard_map/pallas_call | solution.py:165
  79.2 0.7 collective-permute-start.11
  80.4 2.6 %shard_map.105 = (bf16[2,2,3,64,128]{4,3,2,1,0:T(8,128)(2,1)S(1)}, bf16[2,2,3,64,128]{4,3,2,1,0:T(8,128)(2,1)S(1)}) custom-call(bf16[2,2,6,64,128]{4,3,2,1,0:T(8,128)(2,1)S(1)} %pad_maximum_fusion.4.refs_1_.refs_0_, bf16[2,2,6,64,128]{4,3,2,1,0:T(8,128)(2,1)S(1)} %collective-permute-done.refs_2_.refs_1_, ...), custom_call_target="tpu_custom_call" | custom-call | flops 6341787648 | bytes 2359296 | tf_op jit(solution)/shard_map/pallas_call | solution.py:165
  83.6 2.6 %shard_map.106 = (bf16[2,2,3,64,128]{4,3,2,1,0:T(8,128)(2,1)S(1)}, bf16[2,2,3,64,128]{4,3,2,1,0:T(8,128)(2,1)S(1)}) custom-call(bf16[2,2,6,64,128]{4,3,2,1,0:T(8,128)(2,1)S(1)} %pad_maximum_fusion.4.refs_1_.refs_0_, bf16[2,2,6,64,128]{4,3,2,1,0:T(8,128)(2,1)S(1)} %collective-permute-done.refs_2_.refs_1_, ...), custom_call_target="tpu_custom_call" | custom-call | flops 6341787648 | bytes 2359296 | tf_op jit(solution)/shard_map/pallas_call | solution.py:165
  86.2 0.9 %collective-permute-start.19 = (bf16[2,2,3,64,128]{4,3,2,1,0:T(8,128)(2,1)S(1)}, bf16[2,2,3,64,128]{4,3,2,1,0:T(8,128)(2,1)S(1)}, u32[]{:S(2)}, u32[]{:S(2)}) collective-permute-start(bf16[2,2,3,64,128]{4,3,2,1,0:T(8,128)(2,1)S(1)} %get-tuple-element.69), channel_id=1, source_target_pairs={{0,1},{1,0},{2,3},{3,2},{4,5},{5,4},{6,7},{7,6},{8,9},{9,8},{10,11... | collective-permute-start | bytes 589832 | tf_op jit(solution)/shard_map/ppermute | solution.py:191
  87.4 1.8 %collective-permute-done.18 = bf16[2,2,3,64,128]{4,3,2,1,0:T(8,128)(2,1)S(1)} collective-permute-done((bf16[2,2,3,64,128]{4,3,2,1,0:T(8,128)(2,1)S(1)}, bf16[2,2,3,64,128]{4,3,2,1,0:T(8,128)(2,1)S(1)}, u32[]{:S(2)}, u32[]{:S(2)}) %collective-permute-start.18) | collective-permute-done | bytes 196640 | tf_op jit(solution)/shard_map/ppermute | solution.py:191
  89.5 0.9 %slice_bitcast_fusion.2 = (bf16[2,8,8,12,128]{4,2,3,1,0:T(8,128)(2,1)}, bf16[2,8,8,12,128]{4,2,3,1,0:T(8,128)(2,1)}) fusion(bf16[2,2,8,8,12,128]{5,3,4,2,1,0:T(8,128)(2,1)S(1)} %bitcast.182), kind=kLoop, calls=%fused_computation.12 | loop fusion | bytes 1572864 | tf_op jit(solution)/shard_map/squeeze | solution.py:269
  90.6 1.7 %collective-permute-done.19 = bf16[2,2,3,64,128]{4,3,2,1,0:T(8,128)(2,1)S(1)} collective-permute-done((bf16[2,2,3,64,128]{4,3,2,1,0:T(8,128)(2,1)S(1)}, bf16[2,2,3,64,128]{4,3,2,1,0:T(8,128)(2,1)S(1)}, u32[]{:S(2)}, u32[]{:S(2)}) %collective-permute-start.19) | collective-permute-done | bytes 196640 | tf_op jit(solution)/shard_map/ppermute | solution.py:191
  92.3 0.9 %slice_bitcast_fusion = (bf16[2,8,8,12,128]{4,2,3,1,0:T(8,128)(2,1)}, bf16[2,8,8,12,128]{4,2,3,1,0:T(8,128)(2,1)}) fusion(bf16[2,2,8,8,12,128]{5,3,4,2,1,0:T(8,128)(2,1)S(1)} %bitcast.183), kind=kLoop, calls=%fused_computation.10 | loop fusion | bytes 1572864 | tf_op jit(solution)/shard_map/squeeze | solution.py:269
  (101 shorter events, 6.0 us)
Async XLA Ops:
  2.0 1.7 %copy-start.3 = (s32[8,4,2,27]{3,2,1,0:T(2,128)S(1)}, s32[8,4,2,27]{3,2,1,0:T(2,128)}, u32[]{:S(2)}) copy-start(s32[8,4,2,27]{3,2,1,0:T(2,128)} %param.11) | copy-start | bytes 20740
  2.0 3.3 %copy-start.4 = (bf16[4,3,9,2,9,1]{4,2,1,0,5,3:T(8,128)(2,1)S(1)}, bf16[4,3,9,2,9,1]{4,2,1,0,5,3:T(8,128)(2,1)}, u32[]{:S(2)}) copy-start(bf16[4,3,9,2,9,1]{4,2,1,0,5,3:T(8,128)(2,1)} %constant.219) | copy-start | bytes 11668
  2.1 3.9 %copy-start.2 = (bf16[18,1152]{1,0:T(8,128)(2,1)S(1)}, bf16[18,1152]{1,0:T(8,128)(2,1)}, u32[]{:S(2)}) copy-start(bf16[18,1152]{1,0:T(8,128)(2,1)} %constant.114.clone) | copy-start | bytes 124420
  2.1 10.0 %collective-permute-start = (bf16[2,2,6,64,128]{4,3,2,1,0:T(8,128)(2,1)S(1)}, bf16[2,2,6,64,128]{4,3,2,1,0:T(8,128)(2,1)S(1)}, u32[]{:S(2)}, u32[]{:S(2)}) collective-permute-start(bf16[2,2,6,64,128]{4,3,2,1,0:T(8,128)(2,1)S(1)} %pad_maximum_fusion.3), channel_id=1, source_target_pairs={{0,1},{1,0},{2,3},{3,2},{4,5},{5,4},{6,7},{7,6},{8,9},{9,8},{10,11... | collective-permute-start | bytes 1179656 | tf_op jit(solution)/shard_map/ppermute | solution.py:191
  3.6 8.0 %copy-start = (bf16[2,8,8,12,128]{4,2,3,1,0:T(8,128)(2,1)S(1)}, bf16[2,8,8,12,128]{4,2,3,1,0:T(8,128)(2,1)}, u32[]{:S(2)}) copy-start(bf16[2,8,8,12,128]{4,2,3,1,0:T(8,128)(2,1)} %param.10) | copy-start | bytes 1179652
  3.6 8.0 %copy-start.1 = (bf16[2,8,8,12,128]{4,2,3,1,0:T(8,128)(2,1)S(1)}, bf16[2,8,8,12,128]{4,2,3,1,0:T(8,128)(2,1)}, u32[]{:S(2)}) copy-start(bf16[2,8,8,12,128]{4,2,3,1,0:T(8,128)(2,1)} %param.7) | copy-start | bytes 1179652
  6.2 12.5 %collective-permute-start.2 = (bf16[2,2,6,64,128]{4,3,2,1,0:T(8,128)(2,1)S(1)}, bf16[2,2,6,64,128]{4,3,2,1,0:T(8,128)(2,1)S(1)}, u32[]{:S(2)}, u32[]{:S(2)}) collective-permute-start(bf16[2,2,6,64,128]{4,3,2,1,0:T(8,128)(2,1)S(1)} %pad_maximum_fusion.4.refs_1_.refs_0_), channel_id=1, source_target_pairs={{0,2},{2,4},{4,6},{1,3},{3,5},{5,7},{8,10},{10,12},{12,14},{9,11},... | collective-permute-start | bytes 1179656 | tf_op jit(solution)/shard_map/ppermute | solution.py:186
  9.5 19.9 %collective-permute-start.4 = (bf16[2,2,6,64,128]{4,3,2,1,0:T(8,128)(2,1)S(1)}, bf16[2,2,6,64,128]{4,3,2,1,0:T(8,128)(2,1)S(1)}, u32[]{:S(2)}, u32[]{:S(2)}) collective-permute-start(bf16[2,2,6,64,128]{4,3,2,1,0:T(8,128)(2,1)S(1)} %pad_maximum_fusion.4.refs_1_.refs_0_), channel_id=1, source_target_pairs={{2,0},{4,2},{6,4},{3,1},{5,3},{7,5},{10,8},{12,10},{14,12},{11,9},... | collective-permute-start | bytes 1179656 | tf_op jit(solution)/shard_map/ppermute | solution.py:186
  12.2 19.4 %collective-permute-start.3 = (bf16[2,2,6,64,128]{4,3,2,1,0:T(8,128)(2,1)S(1)}, bf16[2,2,6,64,128]{4,3,2,1,0:T(8,128)(2,1)S(1)}, u32[]{:S(2)}, u32[]{:S(2)}) collective-permute-start(bf16[2,2,6,64,128]{4,3,2,1,0:T(8,128)(2,1)S(1)} %collective-permute-done.refs_2_.refs_1_), channel_id=1, source_target_pairs={{0,2},{2,4},{4,6},{1,3},{3,5},{5,7},{8,10},{10,12},{12,14},{9,11},... | collective-permute-start | bytes 1179656 | tf_op jit(solution)/shard_map/ppermute | solution.py:186
  15.4 16.4 %collective-permute-start.5 = (bf16[2,2,6,64,128]{4,3,2,1,0:T(8,128)(2,1)S(1)}, bf16[2,2,6,64,128]{4,3,2,1,0:T(8,128)(2,1)S(1)}, u32[]{:S(2)}, u32[]{:S(2)}) collective-permute-start(bf16[2,2,6,64,128]{4,3,2,1,0:T(8,128)(2,1)S(1)} %collective-permute-done.refs_2_.refs_1_), channel_id=1, source_target_pairs={{2,0},{4,2},{6,4},{3,1},{5,3},{7,5},{10,8},{12,10},{14,12},{11,9},... | collective-permute-start | bytes 1179656 | tf_op jit(solution)/shard_map/ppermute | solution.py:186
  17.5 8.6 %collective-permute-start.1 = (bf16[2,2,6,64,128]{4,3,2,1,0:T(8,128)(2,1)S(1)}, bf16[2,2,6,64,128]{4,3,2,1,0:T(8,128)(2,1)S(1)}, u32[]{:S(2)}, u32[]{:S(2)}) collective-permute-start(bf16[2,2,6,64,128]{4,3,2,1,0:T(8,128)(2,1)S(1)} %pad_maximum_fusion.2), channel_id=1, source_target_pairs={{0,1},{1,0},{2,3},{3,2},{4,5},{5,4},{6,7},{7,6},{8,9},{9,8},{10,11... | collective-permute-start | bytes 1179656 | tf_op jit(solution)/shard_map/ppermute | solution.py:191
  26.1 17.9 %collective-permute-start.12 = (bf16[2,2,2,6,64,128]{5,4,3,2,0,1:T(8,128)(2,1)S(1)}, bf16[2,2,2,6,64,128]{5,4,3,2,0,1:T(8,128)(2,1)S(1)}, u32[]{:S(2)}, u32[]{:S(2)}) collective-permute-start(bf16[2,2,2,6,64,128]{5,4,3,2,0,1:T(8,128)(2,1)S(1)} %pad_maximum_fusion), channel_id=1, source_target_pairs={{0,2},{2,4},{4,6},{1,3},{3,5},{5,7},{8,10},{10,12},{12,14},{9,11},... | collective-permute-start | bytes 2359304 | tf_op jit(solution)/shard_map/ppermute | solution.py:186
  29.5 17.6 %collective-permute-start.13 = (bf16[2,2,2,6,64,128]{5,4,3,2,1,0:T(8,128)(2,1)S(1)}, bf16[2,2,2,6,64,128]{5,4,3,2,1,0:T(8,128)(2,1)S(1)}, u32[]{:S(2)}, u32[]{:S(2)}) collective-permute-start(bf16[2,2,2,6,64,128]{5,4,3,2,1,0:T(8,128)(2,1)S(1)} %copy.57.refs_0_.refs_2_), channel_id=1, source_target_pairs={{2,0},{4,2},{6,4},{3,1},{5,3},{7,5},{10,8},{12,10},{14,12},{11,9},... | collective-permute-start | bytes 2359304 | tf_op jit(solution)/shard_map/ppermute | solution.py:186
  31.8 24.8 %collective-permute-start.6 = (bf16[6,2,6,64,128]{4,3,2,1,0:T(8,128)(2,1)S(1)}, bf16[6,2,6,64,128]{4,3,2,1,0:T(8,128)(2,1)S(1)}, u32[]{:S(2)}, u32[]{:S(2)}) collective-permute-start(bf16[6,2,6,64,128]{4,3,2,1,0:T(8,128)(2,1)S(1)} %get-tuple-element.87), channel_id=1, source_target_pairs={{0,8},{8,16},{16,24},{1,9},{9,17},{17,25},{2,10},{10,18},{18,26},{... | collective-permute-start | bytes 3538952 | tf_op jit(solution)/shard_map/ppermute | solution.py:186
  38.5 18.1 %collective-permute-start.7 = (bf16[6,2,6,64,128]{4,3,2,1,0:T(8,128)(2,1)S(1)}, bf16[6,2,6,64,128]{4,3,2,1,0:T(8,128)(2,1)S(1)}, u32[]{:S(2)}, u32[]{:S(2)}) collective-permute-start(bf16[6,2,6,64,128]{4,3,2,1,0:T(8,128)(2,1)S(1)} %get-tuple-element.86), channel_id=1, source_target_pairs={{8,0},{16,8},{24,16},{9,1},{17,9},{25,17},{10,2},{18,10},{26,18},{... | collective-permute-start | bytes 3538952 | tf_op jit(solution)/shard_map/ppermute | solution.py:186
  47.3 33.0 %collective-permute-start.14 = (bf16[6,2,6,64,128]{4,3,2,1,0:T(8,128)(2,1)S(1)}, bf16[6,2,6,64,128]{4,3,2,1,0:T(8,128)(2,1)S(1)}, u32[]{:S(2)}, u32[]{:S(2)}) collective-permute-start(bf16[6,2,6,64,128]{4,3,2,1,0:T(8,128)(2,1)S(1)} %get-tuple-element.75), channel_id=1, source_target_pairs={{0,8},{8,16},{16,24},{1,9},{9,17},{17,25},{2,10},{10,18},{18,26},{... | collective-permute-start | bytes 3538952 | tf_op jit(solution)/shard_map/ppermute | solution.py:186
  54.6 25.8 %collective-permute-start.15 = (bf16[6,2,6,64,128]{4,3,2,1,0:T(8,128)(2,1)S(1)}, bf16[6,2,6,64,128]{4,3,2,1,0:T(8,128)(2,1)S(1)}, u32[]{:S(2)}, u32[]{:S(2)}) collective-permute-start(bf16[6,2,6,64,128]{4,3,2,1,0:T(8,128)(2,1)S(1)} %get-tuple-element.74), channel_id=1, source_target_pairs={{8,0},{16,8},{24,16},{9,1},{17,9},{25,17},{10,2},{18,10},{26,18},{... | collective-permute-start | bytes 3538952 | tf_op jit(solution)/shard_map/ppermute | solution.py:186
  61.6 8.8 %collective-permute-start.9 = (f32[2,6,2,128]{3,2,1,0:T(2,128)S(1)}, f32[2,6,2,128]{3,2,1,0:T(2,128)S(1)}, u32[]{:S(2)}, u32[]{:S(2)}) collective-permute-start(f32[2,6,2,128]{3,2,1,0:T(2,128)S(1)} %get-tuple-element.47.refs_10_.refs_7_), channel_id=1, source_target_pairs={{0,2},{2,4},{4,6},{1,3},{3,5},{5,7},{8,10},{10,12},{12,14},{9,11},... | collective-permute-start | bytes 36872 | tf_op jit(solution)/shard_map/ppermute | solution.py:186
  64.8 5.6 %collective-permute-start.10 = (f32[2,6,2,128]{3,2,1,0:T(2,128)S(1)}, f32[2,6,2,128]{3,2,1,0:T(2,128)S(1)}, u32[]{:S(2)}, u32[]{:S(2)}) collective-permute-start(f32[2,6,2,128]{3,2,1,0:T(2,128)S(1)} %get-tuple-element.47.refs_10_.refs_7_), channel_id=1, source_target_pairs={{2,0},{4,2},{6,4},{3,1},{5,3},{7,5},{10,8},{12,10},{14,12},{11,9},... | collective-permute-start | bytes 36872 | tf_op jit(solution)/shard_map/ppermute | solution.py:186
  69.1 18.2 %collective-permute-start.8 = (bf16[2,2,3,64,128]{4,3,2,1,0:T(8,128)(2,1)S(1)}, bf16[2,2,3,64,128]{4,3,2,1,0:T(8,128)(2,1)S(1)}, u32[]{:S(2)}, u32[]{:S(2)}) collective-permute-start(bf16[2,2,3,64,128]{4,3,2,1,0:T(8,128)(2,1)S(1)} %get-tuple-element.46), channel_id=1, source_target_pairs={{0,1},{1,0},{2,3},{3,2},{4,5},{5,4},{6,7},{7,6},{8,9},{9,8},{10,11... | collective-permute-start | bytes 589832 | tf_op jit(solution)/shard_map/ppermute | solution.py:191
  70.5 8.8 %collective-permute-start.16 = (f32[3,6,2,128]{3,2,1,0:T(2,128)S(1)}, f32[3,6,2,128]{3,2,1,0:T(2,128)S(1)}, u32[]{:S(2)}, u32[]{:S(2)}) collective-permute-start(f32[3,6,2,128]{3,2,1,0:T(2,128)S(1)} %pad_maximum_fusion.5), channel_id=1, source_target_pairs={{0,8},{8,16},{16,24},{1,9},{9,17},{17,25},{2,10},{10,18},{18,26},{... | collective-permute-start | bytes 55304 | tf_op jit(solution)/shard_map/ppermute | solution.py:186
  75.0 5.4 %collective-permute-start.17 = (f32[3,6,2,128]{3,2,1,0:T(2,128)S(1)}, f32[3,6,2,128]{3,2,1,0:T(2,128)S(1)}, u32[]{:S(2)}, u32[]{:S(2)}) collective-permute-start(f32[3,6,2,128]{3,2,1,0:T(2,128)S(1)} %pad_maximum_fusion.6), channel_id=1, source_target_pairs={{8,0},{16,8},{24,16},{9,1},{17,9},{25,17},{10,2},{18,10},{26,18},{... | collective-permute-start | bytes 55304 | tf_op jit(solution)/shard_map/ppermute | solution.py:186
  79.2 8.1 %collective-permute-start.11 = (bf16[2,2,3,64,128]{4,3,2,1,0:T(8,128)(2,1)S(1)}, bf16[2,2,3,64,128]{4,3,2,1,0:T(8,128)(2,1)S(1)}, u32[]{:S(2)}, u32[]{:S(2)}) collective-permute-start(bf16[2,2,3,64,128]{4,3,2,1,0:T(8,128)(2,1)S(1)} %get-tuple-element.49), channel_id=1, source_target_pairs={{0,1},{1,0},{2,3},{3,2},{4,5},{5,4},{6,7},{7,6},{8,9},{9,8},{10,11... | collective-permute-start | bytes 589832 | tf_op jit(solution)/shard_map/ppermute | solution.py:191
  83.0 6.2 %collective-permute-start.18 = (bf16[2,2,3,64,128]{4,3,2,1,0:T(8,128)(2,1)S(1)}, bf16[2,2,3,64,128]{4,3,2,1,0:T(8,128)(2,1)S(1)}, u32[]{:S(2)}, u32[]{:S(2)}) collective-permute-start(bf16[2,2,3,64,128]{4,3,2,1,0:T(8,128)(2,1)S(1)} %get-tuple-element.56), channel_id=1, source_target_pairs={{0,1},{1,0},{2,3},{3,2},{4,5},{5,4},{6,7},{7,6},{8,9},{9,8},{10,11... | collective-permute-start | bytes 589832 | tf_op jit(solution)/shard_map/ppermute | solution.py:191
  86.2 6.0 %collective-permute-start.19 = (bf16[2,2,3,64,128]{4,3,2,1,0:T(8,128)(2,1)S(1)}, bf16[2,2,3,64,128]{4,3,2,1,0:T(8,128)(2,1)S(1)}, u32[]{:S(2)}, u32[]{:S(2)}) collective-permute-start(bf16[2,2,3,64,128]{4,3,2,1,0:T(8,128)(2,1)S(1)} %get-tuple-element.69), channel_id=1, source_target_pairs={{0,1},{1,0},{2,3},{3,2},{4,5},{5,4},{6,7},{7,6},{8,9},{9,8},{10,11... | collective-permute-start | bytes 589832 | tf_op jit(solution)/shard_map/ppermute | solution.py:191

commit v16 on v15

--- a/solution.py
+++ b/solution.py
@@ -274,10 +274,13 @@
     key_sent = [pair_of(keys, values, shift) for shift in range(1, size)]
     key_moved = [turn(key_sent[size - b - 1], size - b) for b in range(1, size)]
     query_held = [pair_of(queries, out_grad, shift) for shift in range(size)]
-    query_held, key_moved = lax.optimization_barrier((query_held, key_moved))
+    query_held, key_sent = lax.optimization_barrier((query_held, key_sent))
     key_far = [row_sides(part) for part in key_moved]
     query_moved = [turn(query_held[size - b], size - b) for b in range(1, size)]
     query_all = jnp.stack(query_held[:1] + query_moved, 1)
+    (far_up, far_down), *rest = key_far
+    query_all, far_up = lax.optimization_barrier((query_all, far_up))
+    key_far = [(far_up, far_down)] + rest
     query_before, query_after = row_sides(query_all)
     key_parts, sides = [key_here] + key_moved, [key_near] + key_far
     key_halo = key_parts + [before for before, _ in sides] + [after for _, after in sides]

time: 94.9 us -> 94.2 us (level)
  starting transfers between devices: 51.4 us -> 47.8 us
  waiting for transfers between devices: 17.9 us -> 21 us
    ppermute x14, waiting for transfers between devices: 7.08 us -> 14.7 us  [step_along(): lax.ppermute(tensor, axis, [(i, i + sign) for i in range(size) if 0 <= i...]
    ppermute x6, waiting for transfers between devices: 10.8 us -> 6.38 us  [turn(): lax.ppermute(tensor, 'head', [(i, (i + shift) % size) for i in range(size)])]
    ppermute x6, starting transfers between devices: 6.1 us -> 4.26 us  [turn(): lax.ppermute(tensor, 'head', [(i, (i + shift) % size) for i in range(size)])]
    ppermute x14, starting transfers between devices: 45.3 us -> 43.5 us  [step_along(): lax.ppermute(tensor, axis, [(i, i + sign) for i in range(size) if 0 <= i...]
  transfers between devices with their start and end apart: 20 -> 20, of which waited for: 7 -> 8; matrix products, arithmetic and copies ran while one was open for 6% -> 6% of each run, Pallas kernels for 16% -> 16%
where the time goes in v16:
time: 94.2 us; the launch traced here: 92.6 us
  starting transfers between devices  47.8 us (51%)
  waiting for transfers between devices  21 us (22%)
  Pallas kernels  14.7 us (16%)
  local copies, waits for them, and re-layouts  6.2 us (7%)
  between operations  1.35 us (1%)
    ppermute x14, starting transfers between devices, step_along(): lax.ppermute(tensor, axis, [(i, i + sign) for i in range(size) if 0 <= i...  43.5 us
    pallas_call x5, Pallas kernels, run(): pl.pallas_call(functools.partial(kernel, scaling, parts, first), grid=(co...  14.7 us
    ppermute x14, waiting for transfers between devices, step_along(): lax.ppermute(tensor, axis, [(i, i + sign) for i in range(size) if 0 <= i...  14.7 us
    ppermute x6, waiting for transfers between devices, turn(): lax.ppermute(tensor, 'head', [(i, (i + shift) % size) for i in range(size)])  6.38 us
    ppermute x6, starting transfers between devices, turn(): lax.ppermute(tensor, 'head', [(i, (i + shift) % size) for i in range(size)])  4.26 us
  transfers between devices with their start and end apart: 20, of which 8 were waited for; matrix products, arithmetic and copies ran while one was open for 6% of the time, Pallas kernels for 16%

profile of v16, /device:TPU:9, one launch (start us, length us, event | category | flops | bytes accessed | tf_op | source)
XLA Modules:
  0.0 92.6 jit_solution(33280573185037445)
XLA Ops:
  0.7 1.3 %dynamic-slice_bitcast_fusion = (bf16[2,6,8,8,128]{4,3,1,2,0:T(8,128)(2,1)S(1)}, bf16[2,6,8,8,128]{4,3,1,2,0:T(8,128)(2,1)S(1)}, bf16[2,6,8,8,128]{4,3,1,2,0:T(8,128)(2,1)S(1)}, bf16[2,6,8,8,128]{4,3,1,2,0:T(8,128)(2,1)S(1)}) fusion(bf16[2,8,8,12,128]{4,2,3,1,0:T(8,128)(2,1)} %param.9, s32[]{:T(128)S(6)} %select_n.105, s32[]{:T(128)S(6)} %select_n.107, ...), kind=kLoop, calls=%fused_computation.66 | loop fusion | bytes 1572872 | tf_op jit(solution)/shard_map/dynamic_slice | solution.py:252
  2.1 1.3 %collective-permute-start.1 = (bf16[2,2,6,64,128]{4,3,2,1,0:T(8,128)(2,1)S(1)}, bf16[2,2,6,64,128]{4,3,2,1,0:T(8,128)(2,1)S(1)}, u32[]{:S(2)}, u32[]{:S(2)}) collective-permute-start(bf16[2,2,6,64,128]{4,3,2,1,0:T(8,128)(2,1)S(1)} %pad_maximum_fusion.3), channel_id=1, source_target_pairs={{0,1},{1,0},{2,3},{3,2},{4,5},{5,4},{6,7},{7,6},{8,9},{9,8},{10,11... | collective-permute-start | bytes 1179656 | tf_op jit(solution)/shard_map/ppermute | solution.py:191
  6.2 3.2 %collective-permute-start.3 = (bf16[2,2,6,64,128]{4,3,2,1,0:T(8,128)(2,1)S(1)}, bf16[2,2,6,64,128]{4,3,2,1,0:T(8,128)(2,1)S(1)}, u32[]{:S(2)}, u32[]{:S(2)}) collective-permute-start(bf16[2,2,6,64,128]{4,3,2,1,0:T(8,128)(2,1)S(1)} %pad_maximum_fusion.4.refs_1_.refs_0_), channel_id=1, source_target_pairs={{0,2},{2,4},{4,6},{1,3},{3,5},{5,7},{8,10},{10,12},{12,14},{9,11},... | collective-permute-start | bytes 1179656 | tf_op jit(solution)/shard_map/ppermute | solution.py:186
  10.1 2.1 %collective-permute-start.4 = (bf16[2,2,6,64,128]{4,3,2,1,0:T(8,128)(2,1)S(1)}, bf16[2,2,6,64,128]{4,3,2,1,0:T(8,128)(2,1)S(1)}, u32[]{:S(2)}, u32[]{:S(2)}) collective-permute-start(bf16[2,2,6,64,128]{4,3,2,1,0:T(8,128)(2,1)S(1)} %pad_maximum_fusion.4.refs_1_.refs_0_), channel_id=1, source_target_pairs={{2,0},{4,2},{6,4},{3,1},{5,3},{7,5},{10,8},{12,10},{14,12},{11,9},... | collective-permute-start | bytes 1179656 | tf_op jit(solution)/shard_map/ppermute | solution.py:186
  12.3 3.2 %collective-permute-start.2 = (bf16[2,2,6,64,128]{4,3,2,1,0:T(8,128)(2,1)S(1)}, bf16[2,2,6,64,128]{4,3,2,1,0:T(8,128)(2,1)S(1)}, u32[]{:S(2)}, u32[]{:S(2)}) collective-permute-start(bf16[2,2,6,64,128]{4,3,2,1,0:T(8,128)(2,1)S(1)} %collective-permute-done.1.refs_2_.refs_1_), channel_id=1, source_target_pairs={{0,2},{2,4},{4,6},{1,3},{3,5},{5,7},{8,10},{10,12},{12,14},{9,11},... | collective-permute-start | bytes 1179656 | tf_op jit(solution)/shard_map/ppermute | solution.py:186
  15.5 2.1 %collective-permute-start.5 = (bf16[2,2,6,64,128]{4,3,2,1,0:T(8,128)(2,1)S(1)}, bf16[2,2,6,64,128]{4,3,2,1,0:T(8,128)(2,1)S(1)}, u32[]{:S(2)}, u32[]{:S(2)}) collective-permute-start(bf16[2,2,6,64,128]{4,3,2,1,0:T(8,128)(2,1)S(1)} %collective-permute-done.1.refs_2_.refs_1_), channel_id=1, source_target_pairs={{2,0},{4,2},{6,4},{3,1},{5,3},{7,5},{10,8},{12,10},{14,12},{11,9},... | collective-permute-start | bytes 1179656 | tf_op jit(solution)/shard_map/ppermute | solution.py:186
  17.8 2.9 %collective-permute-done = bf16[2,2,6,64,128]{4,3,2,1,0:T(8,128)(2,1)S(1)} collective-permute-done((bf16[2,2,6,64,128]{4,3,2,1,0:T(8,128)(2,1)S(1)}, bf16[2,2,6,64,128]{4,3,2,1,0:T(8,128)(2,1)S(1)}, u32[]{:S(2)}, u32[]{:S(2)}) %collective-permute-start) | collective-permute-done | bytes 393248 | tf_op jit(solution)/shard_map/ppermute | solution.py:191
  20.9 5.3 %collective-permute-done.2.refs_4_ = bf16[2,2,6,64,128]{4,3,2,1,0:T(8,128)(2,1)S(1)} collective-permute-done((bf16[2,2,6,64,128]{4,3,2,1,0:T(8,128)(2,1)S(1)}, bf16[2,2,6,64,128]{4,3,2,1,0:T(8,128)(2,1)S(1)}, u32[]{:S(2)}, u32[]{:S(2)}) %collective-permute-start.2) | collective-permute-done | bytes 393248 | tf_op jit(solution)/shard_map/ppermute | solution.py:186
  26.2 3.2 %collective-permute-start.12 = (bf16[2,2,2,6,64,128]{5,4,3,2,1,0:T(8,128)(2,1)S(1)}, bf16[2,2,2,6,64,128]{5,4,3,2,1,0:T(8,128)(2,1)S(1)}, u32[]{:S(2)}, u32[]{:S(2)}) collective-permute-start(bf16[2,2,2,6,64,128]{5,4,3,2,1,0:T(8,128)(2,1)S(1)} %pad_maximum_fusion.refs_0_.refs_2_), channel_id=1, source_target_pairs={{0,2},{2,4},{4,6},{1,3},{3,5},{5,7},{8,10},{10,12},{12,14},{9,11},... | collective-permute-start | bytes 2359304 | tf_op jit(solution)/shard_map/ppermute | solution.py:186
  29.5 2.1 %collective-permute-start.13 = (bf16[2,2,2,6,64,128]{5,4,3,2,1,0:T(8,128)(2,1)S(1)}, bf16[2,2,2,6,64,128]{5,4,3,2,1,0:T(8,128)(2,1)S(1)}, u32[]{:S(2)}, u32[]{:S(2)}) collective-permute-start(bf16[2,2,2,6,64,128]{5,4,3,2,1,0:T(8,128)(2,1)S(1)} %pad_maximum_fusion.refs_0_.refs_2_), channel_id=1, source_target_pairs={{2,0},{4,2},{6,4},{3,1},{5,3},{7,5},{10,8},{12,10},{14,12},{11,9},... | collective-permute-start | bytes 2359304 | tf_op jit(solution)/shard_map/ppermute | solution.py:186
  31.8 5.5 %collective-permute-start.6 = (bf16[6,2,6,64,128]{4,3,2,1,0:T(8,128)(2,1)S(1)}, bf16[6,2,6,64,128]{4,3,2,1,0:T(8,128)(2,1)S(1)}, u32[]{:S(2)}, u32[]{:S(2)}) collective-permute-start(bf16[6,2,6,64,128]{4,3,2,1,0:T(8,128)(2,1)S(1)} %get-tuple-element.89), channel_id=1, source_target_pairs={{0,8},{8,16},{16,24},{1,9},{9,17},{17,25},{2,10},{10,18},{18,26},{... | collective-permute-start | bytes 3538952 | tf_op jit(solution)/shard_map/ppermute | solution.py:186
  37.3 1.9 %collective-permute-start.7 = (bf16[6,2,6,64,128]{4,3,2,1,0:T(8,128)(2,1)S(1)}, bf16[6,2,6,64,128]{4,3,2,1,0:T(8,128)(2,1)S(1)}, u32[]{:S(2)}, u32[]{:S(2)}) collective-permute-start(bf16[6,2,6,64,128]{4,3,2,1,0:T(8,128)(2,1)S(1)} %get-tuple-element.88), channel_id=1, source_target_pairs={{8,0},{16,8},{24,16},{9,1},{17,9},{25,17},{10,2},{18,10},{26,18},{... | collective-permute-start | bytes 3538952 | tf_op jit(solution)/shard_map/ppermute | solution.py:186
  39.2 6.1 %collective-permute-done.12.refs_3_ = bf16[2,2,2,6,64,128]{5,4,3,2,1,0:T(8,128)(2,1)S(1)} collective-permute-done((bf16[2,2,2,6,64,128]{5,4,3,2,1,0:T(8,128)(2,1)S(1)}, bf16[2,2,2,6,64,128]{5,4,3,2,1,0:T(8,128)(2,1)S(1)}, u32[]{:S(2)}, u32[]{:S(2)}) %collective-permute-start.12) | collective-permute-done | bytes 786464 | tf_op jit(solution)/shard_map/ppermute | solution.py:186
  45.4 2.9 %collective-permute-done.13.refs_4_ = bf16[2,2,2,6,64,128]{5,4,3,2,1,0:T(8,128)(2,1)S(1)} collective-permute-done((bf16[2,2,2,6,64,128]{5,4,3,2,1,0:T(8,128)(2,1)S(1)}, bf16[2,2,2,6,64,128]{5,4,3,2,1,0:T(8,128)(2,1)S(1)}, u32[]{:S(2)}, u32[]{:S(2)}) %collective-permute-start.13) | collective-permute-done | bytes 786464 | tf_op jit(solution)/shard_map/ppermute | solution.py:186
  48.5 6.1 %collective-permute-start.14 = (bf16[6,2,6,64,128]{4,3,2,1,0:T(8,128)(2,1)S(1)}, bf16[6,2,6,64,128]{4,3,2,1,0:T(8,128)(2,1)S(1)}, u32[]{:S(2)}, u32[]{:S(2)}) collective-permute-start(bf16[6,2,6,64,128]{4,3,2,1,0:T(8,128)(2,1)S(1)} %get-tuple-element.77), channel_id=1, source_target_pairs={{0,8},{8,16},{16,24},{1,9},{9,17},{17,25},{2,10},{10,18},{18,26},{... | collective-permute-start | bytes 3538952 | tf_op jit(solution)/shard_map/ppermute | solution.py:186
  54.6 1.9 %collective-permute-start.15 = (bf16[6,2,6,64,128]{4,3,2,1,0:T(8,128)(2,1)S(1)}, bf16[6,2,6,64,128]{4,3,2,1,0:T(8,128)(2,1)S(1)}, u32[]{:S(2)}, u32[]{:S(2)}) collective-permute-start(bf16[6,2,6,64,128]{4,3,2,1,0:T(8,128)(2,1)S(1)} %get-tuple-element.76), channel_id=1, source_target_pairs={{8,0},{16,8},{24,16},{9,1},{17,9},{25,17},{10,2},{18,10},{26,18},{... | collective-permute-start | bytes 3538952 | tf_op jit(solution)/shard_map/ppermute | solution.py:186
  56.6 5.0 %shard_map.102 = (bf16[2,6,128,128]{3,2,1,0:T(8,128)(2,1)S(1)}, f32[2,6,2,128]{3,2,1,0:T(2,128)S(1)}) custom-call(bf16[2,2,2,6,64,128]{5,4,3,2,1,0:T(8,128)(2,1)S(1)} %pad_maximum_fusion.refs_0_.refs_2_, bf16[2,2,6,64,128]{4,3,2,1,0:T(8,128)(2,1)S(1)} %pad_maximum_fusion.4.refs_1_.refs_0_, ...), custom_call_target="tpu_custom_call" | custom-call | flops 6341787648 | bytes 4718592 | tf_op jit(solution)/shard_map/pallas_call | solution.py:165
  61.6 3.2 %collective-permute-start.9 = (f32[2,6,2,128]{3,2,1,0:T(2,128)S(1)}, f32[2,6,2,128]{3,2,1,0:T(2,128)S(1)}, u32[]{:S(2)}, u32[]{:S(2)}) collective-permute-start(f32[2,6,2,128]{3,2,1,0:T(2,128)S(1)} %get-tuple-element.49.refs_10_.refs_7_), channel_id=1, source_target_pairs={{0,2},{2,4},{4,6},{1,3},{3,5},{5,7},{8,10},{10,12},{12,14},{9,11},... | collective-permute-start | bytes 36872 | tf_op jit(solution)/shard_map/ppermute | solution.py:186
  64.8 2.1 %collective-permute-start.10 = (f32[2,6,2,128]{3,2,1,0:T(2,128)S(1)}, f32[2,6,2,128]{3,2,1,0:T(2,128)S(1)}, u32[]{:S(2)}, u32[]{:S(2)}) collective-permute-start(f32[2,6,2,128]{3,2,1,0:T(2,128)S(1)} %get-tuple-element.49.refs_10_.refs_7_), channel_id=1, source_target_pairs={{2,0},{4,2},{6,4},{3,1},{5,3},{7,5},{10,8},{12,10},{14,12},{11,9},... | collective-permute-start | bytes 36872 | tf_op jit(solution)/shard_map/ppermute | solution.py:186
  66.8 2.3 %shard_map.103 = (bf16[2,2,3,64,128]{4,3,2,1,0:T(8,128)(2,1)S(1)}, bf16[2,2,3,64,128]{4,3,2,1,0:T(8,128)(2,1)S(1)}) custom-call(bf16[2,2,2,6,64,128]{5,4,3,2,1,0:T(8,128)(2,1)S(1)} %pad_maximum_fusion.refs_0_.refs_2_, bf16[2,2,6,64,128]{4,3,2,1,0:T(8,128)(2,1)S(1)} %pad_maximum_fusion.4.refs_1_.refs_0_, ...), custom_call_target="tpu_custom_call" | custom-call | flops 4756340736 | bytes 2359296 | tf_op jit(solution)/shard_map/pallas_call | solution.py:165
  69.3 5.0 %collective-permute-start.16 = (f32[3,6,2,128]{3,2,1,0:T(2,128)S(1)}, f32[3,6,2,128]{3,2,1,0:T(2,128)S(1)}, u32[]{:S(2)}, u32[]{:S(2)}) collective-permute-start(f32[3,6,2,128]{3,2,1,0:T(2,128)S(1)} %pad_maximum_fusion.5), channel_id=1, source_target_pairs={{0,8},{8,16},{16,24},{1,9},{9,17},{17,25},{2,10},{10,18},{18,26},{... | collective-permute-start | bytes 55304 | tf_op jit(solution)/shard_map/ppermute | solution.py:186
  74.3 1.9 %collective-permute-start.17 = (f32[3,6,2,128]{3,2,1,0:T(2,128)S(1)}, f32[3,6,2,128]{3,2,1,0:T(2,128)S(1)}, u32[]{:S(2)}, u32[]{:S(2)}) collective-permute-start(f32[3,6,2,128]{3,2,1,0:T(2,128)S(1)} %pad_maximum_fusion.6), channel_id=1, source_target_pairs={{8,0},{16,8},{24,16},{9,1},{17,9},{25,17},{10,2},{18,10},{26,18},{... | collective-permute-start | bytes 55304 | tf_op jit(solution)/shard_map/ppermute | solution.py:186
  76.2 2.3 %shard_map.104 = (bf16[2,2,3,64,128]{4,3,2,1,0:T(8,128)(2,1)S(1)}, bf16[2,2,3,64,128]{4,3,2,1,0:T(8,128)(2,1)S(1)}) custom-call(bf16[2,2,2,6,64,128]{5,4,3,2,1,0:T(8,128)(2,1)S(1)} %pad_maximum_fusion.refs_0_.refs_2_, bf16[2,2,6,64,128]{4,3,2,1,0:T(8,128)(2,1)S(1)} %pad_maximum_fusion.4.refs_1_.refs_0_, ...), custom_call_target="tpu_custom_call" | custom-call | flops 4756340736 | bytes 2359296 | tf_op jit(solution)/shard_map/pallas_call | solution.py:165
  78.6 1.0 %collective-permute-start.11 = (bf16[2,2,3,64,128]{4,3,2,1,0:T(8,128)(2,1)S(1)}, bf16[2,2,3,64,128]{4,3,2,1,0:T(8,128)(2,1)S(1)}, u32[]{:S(2)}, u32[]{:S(2)}) collective-permute-start(bf16[2,2,3,64,128]{4,3,2,1,0:T(8,128)(2,1)S(1)} %get-tuple-element.51), channel_id=1, source_target_pairs={{0,1},{1,0},{2,3},{3,2},{4,5},{5,4},{6,7},{7,6},{8,9},{9,8},{10,11... | collective-permute-start | bytes 589832 | tf_op jit(solution)/shard_map/ppermute | solution.py:191
  79.7 2.6 %shard_map.105 = (bf16[2,2,3,64,128]{4,3,2,1,0:T(8,128)(2,1)S(1)}, bf16[2,2,3,64,128]{4,3,2,1,0:T(8,128)(2,1)S(1)}) custom-call(bf16[2,2,6,64,128]{4,3,2,1,0:T(8,128)(2,1)S(1)} %pad_maximum_fusion.4.refs_1_.refs_0_, bf16[2,2,6,64,128]{4,3,2,1,0:T(8,128)(2,1)S(1)} %collective-permute-done.1.refs_2_.refs_1_, ...), custom_call_target="tpu_custom_call" | custom-call | flops 6341787648 | bytes 2359296 | tf_op jit(solution)/shard_map/pallas_call | solution.py:165
  82.3 1.0 %collective-permute-start.18 = (bf16[2,2,3,64,128]{4,3,2,1,0:T(8,128)(2,1)S(1)}, bf16[2,2,3,64,128]{4,3,2,1,0:T(8,128)(2,1)S(1)}, u32[]{:S(2)}, u32[]{:S(2)}) collective-permute-start(bf16[2,2,3,64,128]{4,3,2,1,0:T(8,128)(2,1)S(1)} %get-tuple-element.58), channel_id=1, source_target_pairs={{0,1},{1,0},{2,3},{3,2},{4,5},{5,4},{6,7},{7,6},{8,9},{9,8},{10,11... | collective-permute-start | bytes 589832 | tf_op jit(solution)/shard_map/ppermute | solution.py:191
  83.3 2.6 %shard_map.106 = (bf16[2,2,3,64,128]{4,3,2,1,0:T(8,128)(2,1)S(1)}, bf16[2,2,3,64,128]{4,3,2,1,0:T(8,128)(2,1)S(1)}) custom-call(bf16[2,2,6,64,128]{4,3,2,1,0:T(8,128)(2,1)S(1)} %pad_maximum_fusion.4.refs_1_.refs_0_, bf16[2,2,6,64,128]{4,3,2,1,0:T(8,128)(2,1)S(1)} %collective-permute-done.1.refs_2_.refs_1_, ...), custom_call_target="tpu_custom_call" | custom-call | flops 6341787648 | bytes 2359296 | tf_op jit(solution)/shard_map/pallas_call | solution.py:165
  85.9 0.6 collective-permute-start.19
  86.7 1.5 %collective-permute-done.18 = bf16[2,2,3,64,128]{4,3,2,1,0:T(8,128)(2,1)S(1)} collective-permute-done((bf16[2,2,3,64,128]{4,3,2,1,0:T(8,128)(2,1)S(1)}, bf16[2,2,3,64,128]{4,3,2,1,0:T(8,128)(2,1)S(1)}, u32[]{:S(2)}, u32[]{:S(2)}) %collective-permute-start.18) | collective-permute-done | bytes 196640 | tf_op jit(solution)/shard_map/ppermute | solution.py:191
  88.6 0.9 %slice_bitcast_fusion.2 = (bf16[2,8,8,12,128]{4,2,3,1,0:T(8,128)(2,1)}, bf16[2,8,8,12,128]{4,2,3,1,0:T(8,128)(2,1)}) fusion(bf16[2,2,8,8,12,128]{5,3,4,2,1,0:T(8,128)(2,1)S(1)} %bitcast.189), kind=kLoop, calls=%fused_computation.12 | loop fusion | bytes 1572864 | tf_op jit(solution)/shard_map/squeeze | solution.py:269
  89.7 1.9 %collective-permute-done.19 = bf16[2,2,3,64,128]{4,3,2,1,0:T(8,128)(2,1)S(1)} collective-permute-done((bf16[2,2,3,64,128]{4,3,2,1,0:T(8,128)(2,1)S(1)}, bf16[2,2,3,64,128]{4,3,2,1,0:T(8,128)(2,1)S(1)}, u32[]{:S(2)}, u32[]{:S(2)}) %collective-permute-start.19) | collective-permute-done | bytes 196640 | tf_op jit(solution)/shard_map/ppermute | solution.py:191
  91.7 0.9 %slice_bitcast_fusion = (bf16[2,8,8,12,128]{4,2,3,1,0:T(8,128)(2,1)}, bf16[2,8,8,12,128]{4,2,3,1,0:T(8,128)(2,1)}) fusion(bf16[2,2,8,8,12,128]{5,3,4,2,1,0:T(8,128)(2,1)S(1)} %bitcast.190), kind=kLoop, calls=%fused_computation.10 | loop fusion | bytes 1572864 | tf_op jit(solution)/shard_map/squeeze | solution.py:269
  (99 shorter events, 5.3 us)
Async XLA Ops:
  2.0 1.7 %copy-start.3 = (s32[8,4,2,27]{3,2,1,0:T(2,128)S(1)}, s32[8,4,2,27]{3,2,1,0:T(2,128)}, u32[]{:S(2)}) copy-start(s32[8,4,2,27]{3,2,1,0:T(2,128)} %param.11) | copy-start | bytes 20740
  2.0 3.3 %copy-start.4 = (bf16[4,3,9,2,9,1]{4,2,1,0,5,3:T(8,128)(2,1)S(1)}, bf16[4,3,9,2,9,1]{4,2,1,0,5,3:T(8,128)(2,1)}, u32[]{:S(2)}) copy-start(bf16[4,3,9,2,9,1]{4,2,1,0,5,3:T(8,128)(2,1)} %constant.219) | copy-start | bytes 11668
  2.1 3.9 %copy-start.2 = (bf16[18,1152]{1,0:T(8,128)(2,1)S(1)}, bf16[18,1152]{1,0:T(8,128)(2,1)}, u32[]{:S(2)}) copy-start(bf16[18,1152]{1,0:T(8,128)(2,1)} %constant.114.clone) | copy-start | bytes 124420
  2.1 10.2 %collective-permute-start.1 = (bf16[2,2,6,64,128]{4,3,2,1,0:T(8,128)(2,1)S(1)}, bf16[2,2,6,64,128]{4,3,2,1,0:T(8,128)(2,1)S(1)}, u32[]{:S(2)}, u32[]{:S(2)}) collective-permute-start(bf16[2,2,6,64,128]{4,3,2,1,0:T(8,128)(2,1)S(1)} %pad_maximum_fusion.3), channel_id=1, source_target_pairs={{0,1},{1,0},{2,3},{3,2},{4,5},{5,4},{6,7},{7,6},{8,9},{9,8},{10,11... | collective-permute-start | bytes 1179656 | tf_op jit(solution)/shard_map/ppermute | solution.py:191
  3.6 5.9 %copy-start = (bf16[2,8,8,12,128]{4,2,3,1,0:T(8,128)(2,1)S(1)}, bf16[2,8,8,12,128]{4,2,3,1,0:T(8,128)(2,1)}, u32[]{:S(2)}) copy-start(bf16[2,8,8,12,128]{4,2,3,1,0:T(8,128)(2,1)} %param.10) | copy-start | bytes 1179652
  3.6 5.9 %copy-start.1 = (bf16[2,8,8,12,128]{4,2,3,1,0:T(8,128)(2,1)S(1)}, bf16[2,8,8,12,128]{4,2,3,1,0:T(8,128)(2,1)}, u32[]{:S(2)}) copy-start(bf16[2,8,8,12,128]{4,2,3,1,0:T(8,128)(2,1)} %param.7) | copy-start | bytes 1179652
  6.2 11.6 %collective-permute-start.3 = (bf16[2,2,6,64,128]{4,3,2,1,0:T(8,128)(2,1)S(1)}, bf16[2,2,6,64,128]{4,3,2,1,0:T(8,128)(2,1)S(1)}, u32[]{:S(2)}, u32[]{:S(2)}) collective-permute-start(bf16[2,2,6,64,128]{4,3,2,1,0:T(8,128)(2,1)S(1)} %pad_maximum_fusion.4.refs_1_.refs_0_), channel_id=1, source_target_pairs={{0,2},{2,4},{4,6},{1,3},{3,5},{5,7},{8,10},{10,12},{12,14},{9,11},... | collective-permute-start | bytes 1179656 | tf_op jit(solution)/shard_map/ppermute | solution.py:186
  9.8 10.9 %collective-permute-start = (bf16[2,2,6,64,128]{4,3,2,1,0:T(8,128)(2,1)S(1)}, bf16[2,2,6,64,128]{4,3,2,1,0:T(8,128)(2,1)S(1)}, u32[]{:S(2)}, u32[]{:S(2)}) collective-permute-start(bf16[2,2,6,64,128]{4,3,2,1,0:T(8,128)(2,1)S(1)} %pad_maximum_fusion.2), channel_id=1, source_target_pairs={{0,1},{1,0},{2,3},{3,2},{4,5},{5,4},{6,7},{7,6},{8,9},{9,8},{10,11... | collective-permute-start | bytes 1179656 | tf_op jit(solution)/shard_map/ppermute | solution.py:191
  10.1 19.3 %collective-permute-start.4 = (bf16[2,2,6,64,128]{4,3,2,1,0:T(8,128)(2,1)S(1)}, bf16[2,2,6,64,128]{4,3,2,1,0:T(8,128)(2,1)S(1)}, u32[]{:S(2)}, u32[]{:S(2)}) collective-permute-start(bf16[2,2,6,64,128]{4,3,2,1,0:T(8,128)(2,1)S(1)} %pad_maximum_fusion.4.refs_1_.refs_0_), channel_id=1, source_target_pairs={{2,0},{4,2},{6,4},{3,1},{5,3},{7,5},{10,8},{12,10},{14,12},{11,9},... | collective-permute-start | bytes 1179656 | tf_op jit(solution)/shard_map/ppermute | solution.py:186
  12.3 13.9 %collective-permute-start.2 = (bf16[2,2,6,64,128]{4,3,2,1,0:T(8,128)(2,1)S(1)}, bf16[2,2,6,64,128]{4,3,2,1,0:T(8,128)(2,1)S(1)}, u32[]{:S(2)}, u32[]{:S(2)}) collective-permute-start(bf16[2,2,6,64,128]{4,3,2,1,0:T(8,128)(2,1)S(1)} %collective-permute-done.1.refs_2_.refs_1_), channel_id=1, source_target_pairs={{0,2},{2,4},{4,6},{1,3},{3,5},{5,7},{8,10},{10,12},{12,14},{9,11},... | collective-permute-start | bytes 1179656 | tf_op jit(solution)/shard_map/ppermute | solution.py:186
  15.5 16.3 %collective-permute-start.5 = (bf16[2,2,6,64,128]{4,3,2,1,0:T(8,128)(2,1)S(1)}, bf16[2,2,6,64,128]{4,3,2,1,0:T(8,128)(2,1)S(1)}, u32[]{:S(2)}, u32[]{:S(2)}) collective-permute-start(bf16[2,2,6,64,128]{4,3,2,1,0:T(8,128)(2,1)S(1)} %collective-permute-done.1.refs_2_.refs_1_), channel_id=1, source_target_pairs={{2,0},{4,2},{6,4},{3,1},{5,3},{7,5},{10,8},{12,10},{14,12},{11,9},... | collective-permute-start | bytes 1179656 | tf_op jit(solution)/shard_map/ppermute | solution.py:186
  26.2 19.1 %collective-permute-start.12 = (bf16[2,2,2,6,64,128]{5,4,3,2,1,0:T(8,128)(2,1)S(1)}, bf16[2,2,2,6,64,128]{5,4,3,2,1,0:T(8,128)(2,1)S(1)}, u32[]{:S(2)}, u32[]{:S(2)}) collective-permute-start(bf16[2,2,2,6,64,128]{5,4,3,2,1,0:T(8,128)(2,1)S(1)} %pad_maximum_fusion.refs_0_.refs_2_), channel_id=1, source_target_pairs={{0,2},{2,4},{4,6},{1,3},{3,5},{5,7},{8,10},{10,12},{12,14},{9,11},... | collective-permute-start | bytes 2359304 | tf_op jit(solution)/shard_map/ppermute | solution.py:186
  29.5 18.8 %collective-permute-start.13 = (bf16[2,2,2,6,64,128]{5,4,3,2,1,0:T(8,128)(2,1)S(1)}, bf16[2,2,2,6,64,128]{5,4,3,2,1,0:T(8,128)(2,1)S(1)}, u32[]{:S(2)}, u32[]{:S(2)}) collective-permute-start(bf16[2,2,2,6,64,128]{5,4,3,2,1,0:T(8,128)(2,1)S(1)} %pad_maximum_fusion.refs_0_.refs_2_), channel_id=1, source_target_pairs={{2,0},{4,2},{6,4},{3,1},{5,3},{7,5},{10,8},{12,10},{14,12},{11,9},... | collective-permute-start | bytes 2359304 | tf_op jit(solution)/shard_map/ppermute | solution.py:186
  31.8 24.7 %collective-permute-start.6 = (bf16[6,2,6,64,128]{4,3,2,1,0:T(8,128)(2,1)S(1)}, bf16[6,2,6,64,128]{4,3,2,1,0:T(8,128)(2,1)S(1)}, u32[]{:S(2)}, u32[]{:S(2)}) collective-permute-start(bf16[6,2,6,64,128]{4,3,2,1,0:T(8,128)(2,1)S(1)} %get-tuple-element.89), channel_id=1, source_target_pairs={{0,8},{8,16},{16,24},{1,9},{9,17},{17,25},{2,10},{10,18},{18,26},{... | collective-permute-start | bytes 3538952 | tf_op jit(solution)/shard_map/ppermute | solution.py:186
  37.3 19.3 %collective-permute-start.7 = (bf16[6,2,6,64,128]{4,3,2,1,0:T(8,128)(2,1)S(1)}, bf16[6,2,6,64,128]{4,3,2,1,0:T(8,128)(2,1)S(1)}, u32[]{:S(2)}, u32[]{:S(2)}) collective-permute-start(bf16[6,2,6,64,128]{4,3,2,1,0:T(8,128)(2,1)S(1)} %get-tuple-element.88), channel_id=1, source_target_pairs={{8,0},{16,8},{24,16},{9,1},{17,9},{25,17},{10,2},{18,10},{26,18},{... | collective-permute-start | bytes 3538952 | tf_op jit(solution)/shard_map/ppermute | solution.py:186
  48.5 31.2 %collective-permute-start.14 = (bf16[6,2,6,64,128]{4,3,2,1,0:T(8,128)(2,1)S(1)}, bf16[6,2,6,64,128]{4,3,2,1,0:T(8,128)(2,1)S(1)}, u32[]{:S(2)}, u32[]{:S(2)}) collective-permute-start(bf16[6,2,6,64,128]{4,3,2,1,0:T(8,128)(2,1)S(1)} %get-tuple-element.77), channel_id=1, source_target_pairs={{0,8},{8,16},{16,24},{1,9},{9,17},{17,25},{2,10},{10,18},{18,26},{... | collective-permute-start | bytes 3538952 | tf_op jit(solution)/shard_map/ppermute | solution.py:186
  54.6 25.1 %collective-permute-start.15 = (bf16[6,2,6,64,128]{4,3,2,1,0:T(8,128)(2,1)S(1)}, bf16[6,2,6,64,128]{4,3,2,1,0:T(8,128)(2,1)S(1)}, u32[]{:S(2)}, u32[]{:S(2)}) collective-permute-start(bf16[6,2,6,64,128]{4,3,2,1,0:T(8,128)(2,1)S(1)} %get-tuple-element.76), channel_id=1, source_target_pairs={{8,0},{16,8},{24,16},{9,1},{17,9},{25,17},{10,2},{18,10},{26,18},{... | collective-permute-start | bytes 3538952 | tf_op jit(solution)/shard_map/ppermute | solution.py:186
  61.6 7.7 %collective-permute-start.9 = (f32[2,6,2,128]{3,2,1,0:T(2,128)S(1)}, f32[2,6,2,128]{3,2,1,0:T(2,128)S(1)}, u32[]{:S(2)}, u32[]{:S(2)}) collective-permute-start(f32[2,6,2,128]{3,2,1,0:T(2,128)S(1)} %get-tuple-element.49.refs_10_.refs_7_), channel_id=1, source_target_pairs={{0,2},{2,4},{4,6},{1,3},{3,5},{5,7},{8,10},{10,12},{12,14},{9,11},... | collective-permute-start | bytes 36872 | tf_op jit(solution)/shard_map/ppermute | solution.py:186
  64.8 4.5 %collective-permute-start.10 = (f32[2,6,2,128]{3,2,1,0:T(2,128)S(1)}, f32[2,6,2,128]{3,2,1,0:T(2,128)S(1)}, u32[]{:S(2)}, u32[]{:S(2)}) collective-permute-start(f32[2,6,2,128]{3,2,1,0:T(2,128)S(1)} %get-tuple-element.49.refs_10_.refs_7_), channel_id=1, source_target_pairs={{2,0},{4,2},{6,4},{3,1},{5,3},{7,5},{10,8},{12,10},{14,12},{11,9},... | collective-permute-start | bytes 36872 | tf_op jit(solution)/shard_map/ppermute | solution.py:186
  69.1 17.6 %collective-permute-start.8 = (bf16[2,2,3,64,128]{4,3,2,1,0:T(8,128)(2,1)S(1)}, bf16[2,2,3,64,128]{4,3,2,1,0:T(8,128)(2,1)S(1)}, u32[]{:S(2)}, u32[]{:S(2)}) collective-permute-start(bf16[2,2,3,64,128]{4,3,2,1,0:T(8,128)(2,1)S(1)} %get-tuple-element.48), channel_id=1, source_target_pairs={{0,1},{1,0},{2,3},{3,2},{4,5},{5,4},{6,7},{7,6},{8,9},{9,8},{10,11... | collective-permute-start | bytes 589832 | tf_op jit(solution)/shard_map/ppermute | solution.py:191
  69.3 9.3 %collective-permute-start.16 = (f32[3,6,2,128]{3,2,1,0:T(2,128)S(1)}, f32[3,6,2,128]{3,2,1,0:T(2,128)S(1)}, u32[]{:S(2)}, u32[]{:S(2)}) collective-permute-start(f32[3,6,2,128]{3,2,1,0:T(2,128)S(1)} %pad_maximum_fusion.5), channel_id=1, source_target_pairs={{0,8},{8,16},{16,24},{1,9},{9,17},{17,25},{2,10},{10,18},{18,26},{... | collective-permute-start | bytes 55304 | tf_op jit(solution)/shard_map/ppermute | solution.py:186
  74.3 5.4 %collective-permute-start.17 = (f32[3,6,2,128]{3,2,1,0:T(2,128)S(1)}, f32[3,6,2,128]{3,2,1,0:T(2,128)S(1)}, u32[]{:S(2)}, u32[]{:S(2)}) collective-permute-start(f32[3,6,2,128]{3,2,1,0:T(2,128)S(1)} %pad_maximum_fusion.6), channel_id=1, source_target_pairs={{8,0},{16,8},{24,16},{9,1},{17,9},{25,17},{10,2},{18,10},{26,18},{... | collective-permute-start | bytes 55304 | tf_op jit(solution)/shard_map/ppermute | solution.py:186
  78.6 8.1 %collective-permute-start.11 = (bf16[2,2,3,64,128]{4,3,2,1,0:T(8,128)(2,1)S(1)}, bf16[2,2,3,64,128]{4,3,2,1,0:T(8,128)(2,1)S(1)}, u32[]{:S(2)}, u32[]{:S(2)}) collective-permute-start(bf16[2,2,3,64,128]{4,3,2,1,0:T(8,128)(2,1)S(1)} %get-tuple-element.51), channel_id=1, source_target_pairs={{0,1},{1,0},{2,3},{3,2},{4,5},{5,4},{6,7},{7,6},{8,9},{9,8},{10,11... | collective-permute-start | bytes 589832 | tf_op jit(solution)/shard_map/ppermute | solution.py:191
  82.3 5.9 %collective-permute-start.18 = (bf16[2,2,3,64,128]{4,3,2,1,0:T(8,128)(2,1)S(1)}, bf16[2,2,3,64,128]{4,3,2,1,0:T(8,128)(2,1)S(1)}, u32[]{:S(2)}, u32[]{:S(2)}) collective-permute-start(bf16[2,2,3,64,128]{4,3,2,1,0:T(8,128)(2,1)S(1)} %get-tuple-element.58), channel_id=1, source_target_pairs={{0,1},{1,0},{2,3},{3,2},{4,5},{5,4},{6,7},{7,6},{8,9},{9,8},{10,11... | collective-permute-start | bytes 589832 | tf_op jit(solution)/shard_map/ppermute | solution.py:191
  85.9 5.7 %collective-permute-start.19 = (bf16[2,2,3,64,128]{4,3,2,1,0:T(8,128)(2,1)S(1)}, bf16[2,2,3,64,128]{4,3,2,1,0:T(8,128)(2,1)S(1)}, u32[]{:S(2)}, u32[]{:S(2)}) collective-permute-start(bf16[2,2,3,64,128]{4,3,2,1,0:T(8,128)(2,1)S(1)} %get-tuple-element.71), channel_id=1, source_target_pairs={{0,1},{1,0},{2,3},{3,2},{4,5},{5,4},{6,7},{7,6},{8,9},{9,8},{10,11... | collective-permute-start | bytes 589832 | tf_op jit(solution)/shard_map/ppermute | solution.py:191
